TPU v7x, 32 devices: a whole 2x2x4 slice. The times are simulated.
32 devices in a mesh: row: 4 (over y, x), col: 8 (over z, core).
Axes of the slice: x: 2, y: 2, z: 4, core: 2. Of those that a mesh axis runs over, the one named last changes fastest.
Arguments:
- positions: float32 [3, 2048], P(None, ('row', 'col')), may hold values from -1 to 70, as said below
- noise: float32 [8, 3, 2048], P(None, None, ('row', 'col')), may hold values from -6 to 6
Outputs:
- basis: float32 [8, 3, 2048], P(None, None, ('row', 'col'))
- residual: float32 [8, 3, 2048], P(None, None, ('row', 'col'))
- coefficients: float32 [3, 8, 8], replicated
Inputs may be any that keep to these rules, and one draw needn't show every extreme that they name: `positions`: bead k lies within 0.77 of each coordinate of its own point of a cubic lattice of spacing 2.2 with 32 by 32 points a layer, distinct beads on distinct points.
All inputs are finite; a program needn't handle non-finite values.
Results may differ from a plain program's by a relative error of at most 0.0003.
Values sent between devices are 32-bit elements; how exact they have to be, the bound alone decides.
No kernel may reach another device: no remote copies, remote signals or barrier semaphores. Data moves between devices by JAX's collectives and lax.ppermute only.
A program may use at most 64 MiB of HBM per device.

v0:
```python
import jax
import jax.numpy as jnp
from jax import lax
from jax.sharding import PartitionSpec as P


def pair_tensor(target_pos, source_pos):
    displace = target_pos[:, :, None] - source_pos[:, None, :]
    distance_sq = jnp.sum(displace * displace, axis=0)
    distance = jnp.sqrt(distance_sq)
    safe_distance = jnp.where(distance > 0, distance, 1.0)
    safe_sq = safe_distance * safe_distance
    far_iso = 0.75 / safe_distance * (1.0 + 2.0 / (3.0 * safe_sq))
    far_dir = 0.75 / safe_distance * (1.0 - 2.0 / safe_sq) / safe_sq
    near_iso = 1.0 - 9.0 * distance / 32.0
    near_dir = 3.0 / (32.0 * safe_distance)
    intersecting = distance < 2.0
    iso_part = jnp.where(intersecting, near_iso, far_iso)
    dir_part = jnp.where(intersecting, near_dir, far_dir)
    identity = jnp.eye(3, dtype=displace.dtype)
    return identity[:, :, None, None] * iso_part + dir_part * displace[:, None] * displace[None, :]


def local_gram(left, right):
    return jnp.einsum("kan,jan->kj", left, right, precision=lax.Precision.HIGHEST)


def combine(vectors, matrix):
    return jnp.einsum("kan,kj->jan", vectors, matrix, precision=lax.Precision.HIGHEST)


def lower_inverse(factor):
    return jax.scipy.linalg.solve_triangular(
        factor, jnp.eye(factor.shape[0], dtype=factor.dtype), lower=True
    )


def local(positions, noise):
    local_beads = positions.shape[1]
    total_count = 3.0 * local_beads * lax.axis_size("row") * lax.axis_size("col")
    target_pos = lax.all_gather(positions, "row", axis=1, tiled=True)
    source_pos = lax.all_gather(positions, "col", axis=1, tiled=True)

    def mobility(vectors):
        initial = jnp.zeros((vectors.shape[0], 3, target_pos.shape[1]), jnp.float32)
        source_piece = lax.all_gather(vectors, "col", axis=2, tiled=True)
        piece_width = source_piece.shape[2]
        block_count = 1
        while piece_width % block_count != 0 or piece_width // block_count > 256:
            block_count = block_count + 1
        block_width = piece_width // block_count

        def add_block(block_index, running):
            block_pos = lax.dynamic_slice_in_dim(
                source_pos, block_index * block_width, block_width, 1
            )
            block_vectors = lax.dynamic_slice_in_dim(
                source_piece, block_index * block_width, block_width, 2
            )
            tensor = pair_tensor(target_pos, block_pos)
            return running + jnp.einsum(
                "abts,kbs->kat", tensor, block_vectors, precision=lax.Precision.HIGHEST
            )

        partial_image = lax.fori_loop(0, block_count, add_block, initial)
        summed = lax.psum(partial_image, "row")
        return lax.dynamic_slice_in_dim(summed, lax.axis_index("row") * local_beads, local_beads, 2)

    start_matrix = lax.psum(local_gram(noise, noise), ("row", "col")) / total_count
    start_factor = jnp.linalg.cholesky(start_matrix)
    first = combine(noise, lower_inverse(start_factor).T)
    image = mobility(first)
    both_sums = lax.psum((local_gram(first, image), local_gram(image, image)), ("row", "col"))
    alpha_one = both_sums[0] / total_count
    residual_matrix = both_sums[1] / total_count - jnp.dot(
        alpha_one.T, alpha_one, precision=lax.Precision.HIGHEST
    )
    remainder = image - combine(first, alpha_one)
    factor_one = jnp.linalg.cholesky(residual_matrix)
    basis = combine(remainder, lower_inverse(factor_one).T)
    image = mobility(basis) - combine(first, factor_one)
    alpha_two = lax.psum(local_gram(basis, image), ("row", "col")) / total_count
    residual = image - combine(basis, alpha_two)
    return (basis, residual, jnp.stack([alpha_one, factor_one, alpha_two]))


def solution(mesh):
    return jax.shard_map(
        local,
        mesh=mesh,
        in_specs=(P(None, ("row", "col")), P(None, None, ("row", "col"))),
        out_specs=(P(None, None, ("row", "col")), P(None, None, ("row", "col")), P()),
        check_vma=False,
    )
```

profile of v0, /device:TPU:0, one launch (start us, length us, event | category | flops | bytes accessed | tf_op | source)
XLA Modules:
  0.0 227.2 jit_solution(13724578865599065862)
XLA Ops:
  0.6 0.7 copy-done
  1.5 42.0 %psum.42 = f32[8,8]{0,1:T(8,128)S(1)} all-reduce(f32[8,8]{0,1:T(8,128)S(1)} %convolution_bitcast_fusion.5), channel_id=1, replica_groups=mesh['row'=4,'col'=8] {'row','col'}, use_global_device_ids=true, to_apply=%region_0.0 | all-reduce | flops 64 | bytes 512 | tf_op jit(solution)/shard_map/psum | solution.py:69
  43.5 0.7 cholesky.44
  44.3 0.6 compare_reduce_fusion.1
  44.9 0.6 fusion.42
  45.6 0.6 custom-call.8
  46.7 16.6 %all_gather.12 = f32[8,3,512]{0,1,2:T(4,128)S(1)} all-gather(f32[8,3,64]{0,1,2:T(4,128)S(1)} %copy.38), channel_id=1, replica_groups=mesh['row'=4,'col'=8] {'col'}, dimensions={2}, use_global_device_ids=true | all-gather | bytes 55296 | tf_op jit(solution)/shard_map/all_gather | solution.py:46
  63.6 12.7 %all-gather.1 = f32[8,64,3]{1,2,0:T(4,128)S(1)} all-gather(f32[1,64,3]{1,2,0:T(4,128)S(1)} %bitcast.94), channel_id=1, replica_groups=mesh['row'=4,'col'=8] {'col'}, dimensions={0}, use_global_device_ids=true | all-gather | bytes 6912 | tf_op jit(solution)/shard_map/all_gather | solution.py:42
  76.4 8.8 %all-gather = f32[4,64,3]{1,2,0:T(4,128)S(1)} all-gather(f32[1,64,3]{1,2,0:T(4,128)S(1)} %bitcast.95), channel_id=1, replica_groups=mesh['row'=4,'col'=8] {'row'}, dimensions={0}, use_global_device_ids=true | all-gather | bytes 3840 | tf_op jit(solution)/shard_map/all_gather | solution.py:41
  85.3 5.6 %while.32 = (s32[]{:T(128)}, f32[8,3,256]{2,0,1:T(8,128)S(1)}, f32[8,3,512]{2,0,1:T(8,128)S(1)}, f32[3,256]{1,0:T(4,128)S(1)}, f32[3,512]{1,0:T(4,128)S(1)}, /*index=5*/s32[]{:T(128)}, s32[]{:T(128)}, s32[]{:T(128)}, s32[]{:T(128)}) while((s32[]{:T(128)}, f32[8,3,256]{2,0,1:T(8,128)S(1)}, f32[8,3,512]{2,0,1:T(8,128)S(1)}, ...), condition=%wide.region_5.8_spmd.clone, body=%wide.region_3.7_spmd.clone.sunk | while | flops 60567576 | bytes 4812993 | solution.py:65
  85.5 0.3 multiply_select_fusion.4
  85.9 2.2 fusion.87
  88.3 0.3 multiply_select_fusion.4
  88.8 2.2 fusion.87
  90.9 15.3 %psum.43 = f32[8,3,256]{2,0,1:T(8,128)S(1)} all-reduce(f32[8,3,256]{2,0,1:T(8,128)S(1)} %get-tuple-element.269), channel_id=1, replica_groups=mesh['row'=4,'col'=8] {'row'}, use_global_device_ids=true, to_apply=%region_6.9 | all-reduce | flops 6144 | bytes 49152 | tf_op jit(solution)/shard_map/psum | solution.py:66
  106.7 38.2 %all-reduce = (f32[8,8]{0,1:T(8,128)S(1)}, f32[8,8]{0,1:T(8,128)S(1)}) all-reduce(f32[8,8]{0,1:T(8,128)S(1)} %convolution_bitcast_fusion.3, f32[8,8]{0,1:T(8,128)S(1)} %convolution_bitcast_fusion.2), channel_id=1, replica_groups=mesh['row'=4,'col'=8] {'row','col'}, use_global_device_ids=true, to_apply=%region_7.10 | all-reduce | flops 128 | bytes 1024 | tf_op jit(solution)/shard_map/psum | solution.py:73
  145.2 0.7 cholesky.55
  145.9 0.6 compare_reduce_fusion
  146.6 0.6 fusion.53
  147.2 0.6 custom-call.9
  148.3 16.6 %all_gather.15 = f32[8,3,512]{0,1,2:T(4,128)S(1)} all-gather(f32[8,3,64]{0,1,2:T(4,128)S(1)} %copy.47), channel_id=1, replica_groups=mesh['row'=4,'col'=8] {'col'}, dimensions={2}, use_global_device_ids=true | all-gather | bytes 55296 | tf_op jit(solution)/shard_map/all_gather | solution.py:46
  164.9 0.3 copy.48
  165.2 5.7 %while.33 = (s32[]{:T(128)}, f32[8,3,256]{2,0,1:T(8,128)S(1)}, f32[8,3,512]{2,0,1:T(8,128)S(1)}, f32[3,256]{1,0:T(4,128)S(1)}, f32[3,512]{1,0:T(4,128)S(1)}, /*index=5*/s32[]{:T(128)}, s32[]{:T(128)}, s32[]{:T(128)}, s32[]{:T(128)}) while((s32[]{:T(128)}, f32[8,3,256]{2,0,1:T(8,128)S(1)}, f32[8,3,512]{2,0,1:T(8,128)S(1)}, ...), condition=%wide.region_11.14_spmd.clone, body=%wide.region_9.13_spmd.clone.sunk | while | flops 60567576 | bytes 4812993 | solution.py:65
  165.4 0.3 multiply_select_fusion.5
  165.9 2.2 fusion.91
  168.2 0.3 multiply_select_fusion.5
  168.7 2.2 fusion.91
  170.9 16.2 %psum.46 = f32[8,3,256]{2,0,1:T(8,128)S(1)} all-reduce(f32[8,3,256]{2,0,1:T(8,128)S(1)} %get-tuple-element.270), channel_id=1, replica_groups=mesh['row'=4,'col'=8] {'row'}, use_global_device_ids=true, to_apply=%region_12.15 | all-reduce | flops 6144 | bytes 49152 | tf_op jit(solution)/shard_map/psum | solution.py:66
  187.1 0.8 convolution_subtract_fusion.1
  188.1 37.7 %psum.47 = f32[8,8]{0,1:T(8,128)S(1)} all-reduce(f32[8,8]{0,1:T(8,128)S(1)} %convolution_bitcast_fusion), channel_id=1, replica_groups=mesh['row'=4,'col'=8] {'row','col'}, use_global_device_ids=true, to_apply=%region_13.16 | all-reduce | flops 64 | bytes 512 | tf_op jit(solution)/shard_map/psum | solution.py:82
  225.9 0.6 pad_maximum_fusion
  226.5 0.7 convolution_subtract_fusion
  (51 shorter events, 4.2 us)
Async XLA Ops:
  0.6 0.7 copy-start
  46.7 16.9 %copy-start.2 = (f32[3,64]{1,0:T(4,128)S(1)}, f32[3,64]{1,0:T(4,128)}, u32[]{:S(2)}) copy-start(f32[3,64]{1,0:T(4,128)} %param.9) | copy-start | bytes 2308
  148.2 78.3 %copy-start.1 = (f32[8,3,64]{2,0,1:T(8,128)}, f32[8,3,64]{2,0,1:T(8,128)S(1)}, u32[]{:S(2)}) copy-start(f32[8,3,64]{2,0,1:T(8,128)S(1)} %fusion.63) | copy-start | bytes 18436
where the time goes:
time: 228 us; the launch traced here: 227 us
  blocking collectives  204 us (89%)
  matrix products  11.9 us (5%)
  other arithmetic  8.47 us (4%)
    psum x1, blocking collectives, local(): lax.psum(local_gram(noise, noise), ('row', 'col')) / total_count  42 us
    psum x1, blocking collectives, local(): lax.psum((local_gram(first, image), local_gram(image, image)), ('row', 'c...  38.2 us
    psum x1, blocking collectives, local(): alpha_two = lax.psum(local_gram(basis, image), ('row', 'col')) / total_count  37.7 us
    all_gather x2, blocking collectives, mobility(): source_piece = lax.all_gather(vectors, 'col', axis=2, tiled=True)  33.2 us
    psum x2, blocking collectives, mobility(): summed = lax.psum(partial_image, 'row')  31.5 us
    all_gather x1, blocking collectives, local(): source_pos = lax.all_gather(positions, 'col', axis=1, tiled=True)  12.7 us
    all_gather x1, blocking collectives, local(): target_pos = lax.all_gather(positions, 'row', axis=1, tiled=True)  8.82 us
    dot_general x4, matrix products, add_block(): jnp.einsum('abts,kbs->kat', tensor, block_vectors, precision=lax.Precisio...  8.65 us

commit v1 on v0

v1 whole, which is shorter than its diff:
```python
import functools

import jax
import jax.numpy as jnp
from jax import lax
from jax.experimental import pallas as pl
from jax.experimental.pallas import tpu as pltpu
from jax.sharding import PartitionSpec as P

CORES = 2
CHUNK = 2048
F32 = jnp.float32
BF16 = jnp.bfloat16


def pack_kernel(positions, noise, block):
    beads = positions.shape[1]
    vecs = noise.shape[0]
    block[...] = jnp.zeros(block.shape, F32)
    block[:vecs, :beads] = noise[:, 0, :]
    block[:vecs, beads:] = noise[:, 1, :]
    block[vecs:, :beads] = noise[:, 2, :]
    block[vecs : vecs + 3, beads:] = positions[...]


def split_two(value):
    high = value.astype(BF16)
    return high, (value - high.astype(F32)).astype(BF16)


def matmul_nt(left, right, precision=lax.Precision.HIGHEST):
    return lax.dot_general(
        left, right, (((1,), (1,)), ((), ())), precision=precision, preferred_element_type=F32
    )


def matmul(left, right):
    return lax.dot_general(
        left, right, (((1,), (0,)), ((), ())), precision=lax.Precision.HIGHEST, preferred_element_type=F32
    )


def matmul_tn(left, right):
    return lax.dot_general(
        left, right, (((0,), (0,)), ((), ())), precision=lax.Precision.HIGHEST, preferred_element_type=F32
    )


def unpack(sources, rows, beads, wide):
    at = 0
    for ref in sources:
        for index in range(0, ref.shape[0], 2):
            one, two = ref[index], ref[index + 1]
            lanes = pl.ds(at, 2 * beads)
            half = one.shape[0] // 2
            for part in range(2):
                one_part = one[part * half : (part + 1) * half]
                two_part = two[part * half : (part + 1) * half]
                if 2 * part < rows:
                    wide[2 * part * half : (2 * part + 1) * half, lanes] = jnp.concatenate(
                        [one_part[:, :beads], two_part[:, :beads]], axis=1
                    )
                if 2 * part + 1 < rows:
                    wide[(2 * part + 1) * half : (2 * part + 2) * half, lanes] = jnp.concatenate(
                        [one_part[:, beads:], two_part[:, beads:]], axis=1
                    )
            at += 2 * beads


def fill_tensor(targets, wide, pos_row, start, high, low):
    beads = targets.shape[0]
    step = 128
    columns = [jnp.broadcast_to(targets[:, axis : axis + 1], (beads, step)) for axis in range(3)]

    def body(index, carry):
        at = pl.multiple_of(start + index * step, step)
        to = pl.ds(pl.multiple_of(index * step, step), step)
        moved = [columns[axis] - wide[pos_row + axis : pos_row + axis + 1, pl.ds(at, step)] for axis in range(3)]
        square = moved[0] * moved[0] + moved[1] * moved[1] + moved[2] * moved[2]
        inverse = lax.rsqrt(jnp.maximum(square, 1e-12))
        inverse_sq = inverse * inverse
        far_iso = inverse * (0.75 + 0.5 * inverse_sq)
        far_dir = inverse * inverse_sq * (0.75 - 1.5 * inverse_sq)
        near_iso = 1.0 - (9.0 / 32.0) * (square * inverse)
        near_dir = (3.0 / 32.0) * inverse
        near = square < 4.0
        iso = jnp.where(near, near_iso, far_iso)
        along = jnp.where(near, near_dir, far_dir)
        scaled = [along * item for item in moved]
        parts = [
            iso + scaled[0] * moved[0],
            scaled[0] * moved[1],
            scaled[0] * moved[2],
            iso + scaled[1] * moved[1],
            scaled[1] * moved[2],
            iso + scaled[2] * moved[2],
        ]
        for part, value in enumerate(parts):
            upper, lower = split_two(value)
            high[part * beads : (part + 1) * beads, to] = upper
            low[part * beads : (part + 1) * beads, to] = lower
        return carry

    lax.fori_loop(0, high.shape[1] // step, body, 0)


def apply_tensor(wide, start, high, low):
    chunk = high.shape[1]
    vectors = wide[:24, pl.ds(start, chunk)]
    upper, lower = split_two(vectors)
    both = jnp.concatenate([upper, lower], axis=0)
    first = matmul_nt(both, high[...], None)
    second = matmul_nt(upper, low[...], None)
    return first[:24] + first[24:] + second


def assemble(products, beads):
    def part(row, component):
        return products[8 * row : 8 * row + 8, component * beads : (component + 1) * beads]

    x = part(0, 0) + part(1, 1) + part(2, 2)
    y = part(0, 1) + part(1, 3) + part(2, 4)
    z = part(0, 2) + part(1, 4) + part(2, 5)
    return x, y, z


def first_kernel(count, beads, targets, *refs):
    sources, (image, wide, high, low) = refs[:count], refs[count:]
    unpack(sources, 4, beads, wide)
    total = wide.shape[1]
    chunk = high.shape[1]
    products = jnp.zeros((24, 6 * beads), F32)
    for start in range(0, total, chunk):
        fill_tensor(targets, wide, 24, start, high, low)
        products = products + apply_tensor(wide, start, high, low)
    x, y, z = assemble(products, beads)
    image[...] = jnp.zeros(image.shape, F32)
    image[:8, :beads] = x
    image[:8, beads:] = y
    image[8:, :beads] = z


def cholesky(matrix):
    size = matrix.shape[0]
    rows = lax.broadcasted_iota(jnp.int32, (size, size), 0)
    cols = lax.broadcasted_iota(jnp.int32, (size, size), 1)
    upper = matrix
    inverse = (rows == cols).astype(F32)
    scale = jnp.zeros((size, size), F32)
    for step in range(size):
        pivot_row = upper[step : step + 1, :]
        pivot = pivot_row[:, step : step + 1]
        below = rows > step
        column = jnp.broadcast_to(upper[:, step : step + 1] / pivot, (size, size))
        factor = jnp.where(below, column, 0.0)
        upper = upper - factor * pivot_row
        inverse = inverse - factor * inverse[step : step + 1, :]
        scale = jnp.where(rows == step, lax.rsqrt(pivot), scale)
    return jnp.where(rows <= cols, upper * scale, 0.0), inverse * scale


def gram_rows(left, right):
    result = matmul_nt(left[0:8, :], right[0:8, :])
    for part in range(1, 3):
        result = result + matmul_nt(left[8 * part : 8 * part + 8, :], right[8 * part : 8 * part + 8, :])
    return result


def second_kernel(count, beads, targets, own, own_image, *refs):
    sources, images = refs[:count], refs[count : 2 * count]
    basis, image, alpha_one, factor_one, partial, wide, wide_image, high, low = refs[2 * count :]
    unpack(sources, 4, beads, wide)
    unpack(images, 3, beads, wide_image)
    total = wide.shape[1]
    chunk = high.shape[1]
    products = jnp.zeros((24, 6 * beads), F32)
    for start in range(0, total, chunk):
        fill_tensor(targets, wide, 24, start, high, low)
        products = products + apply_tensor(wide_image, start, high, low)
    twice = assemble(products, beads)
    size = 3.0 * total
    start_matrix = gram_rows(wide, wide) / size
    cross = gram_rows(wide, wide_image) / size
    squared = gram_rows(wide_image, wide_image) / size
    _, inverse_zero = cholesky(start_matrix)
    alpha = matmul_nt(matmul(inverse_zero, cross), inverse_zero)
    remainder = matmul_nt(matmul(inverse_zero, squared), inverse_zero) - matmul_tn(alpha, alpha)
    factor_t, inverse_one = cholesky(remainder)
    alpha_one[...] = alpha
    factor_one[...] = factor_t.T
    gram = jnp.zeros((8, 8), F32)
    for part in range(3):
        half, side = part // 2 * 8, part % 2 * beads
        noise = own[half : half + 8, side : side + beads]
        once = own_image[half : half + 8, side : side + beads]
        first = matmul(inverse_zero, noise)
        moved = matmul(inverse_zero, once)
        moved_twice = matmul(inverse_zero, twice[part])
        vector = matmul(inverse_one, moved - matmul_tn(alpha, first))
        shifted = matmul(inverse_one, moved_twice - matmul_tn(alpha, moved)) - matmul(factor_t, first)
        basis[part] = vector
        image[part] = shifted
        gram = gram + matmul_nt(vector, shifted)
    partial[...] = gram


def last_kernel(size, count, basis, image, *refs):
    partials, (vectors, residual, alpha_two) = refs[:count], refs[count:]
    total = jnp.zeros((8, 8), F32)
    for ref in partials:
        for index in range(ref.shape[0]):
            total = total + ref[index]
    alpha = total / size
    alpha_two[...] = alpha
    for part in range(3):
        vectors[:, part, :] = basis[part]
        residual[:, part, :] = image[part] - matmul_tn(alpha, basis[part])


def call(kernel, shapes, scratch=()):
    return pl.pallas_call(
        kernel,
        out_shape=[jax.ShapeDtypeStruct(shape, F32) for shape in shapes],
        scratch_shapes=list(scratch),
        compiler_params=pltpu.CompilerParams(vmem_limit_bytes=48 * 1024 * 1024),
    )


def moved_by(value, axis, shift):
    size = lax.axis_size(axis)
    return lax.ppermute(value, axis, [(index, (index + shift) % size) for index in range(size)])


def gather(block):
    cols, rows = lax.axis_size("col"), lax.axis_size("row")
    layers = [block[None]]
    for shift in range(CORES, cols, CORES):
        layers.append(moved_by(block[None], "col", shift))
    held = jnp.concatenate(layers, axis=0)
    plane = [held]
    for shift in range(1, rows):
        plane.append(moved_by(held, "row", shift))
    held = jnp.concatenate(plane, axis=0)
    core = [(index, index ^ 1) for index in range(cols)]
    return [held, lax.ppermute(held, "col", core)]


def local(positions, noise):
    vecs, _, beads = noise.shape
    devices = lax.axis_size("row") * lax.axis_size("col")
    total = beads * devices
    chunk = min(total, CHUNK)
    targets = positions.T
    (block,) = call(pack_kernel, [(2 * vecs, 2 * beads)])(positions, noise)
    sources = gather(block)
    tensors = [pltpu.VMEM((6 * beads, chunk), BF16), pltpu.VMEM((6 * beads, chunk), BF16)]
    wide = pltpu.VMEM((4 * vecs, total), F32)
    (image,) = call(
        functools.partial(first_kernel, len(sources), beads), [(2 * vecs, 2 * beads)], [wide] + tensors
    )(targets, *sources)
    images = gather(image)
    basis, moved, alpha_one, factor_one, partial = call(
        functools.partial(second_kernel, len(sources), beads),
        [(3, vecs, beads), (3, vecs, beads), (vecs, vecs), (vecs, vecs), (vecs, vecs)],
        [wide, wide] + tensors,
    )(targets, block, image, *sources, *images)
    partials = gather(partial)
    vectors, residual, alpha_two = call(
        functools.partial(last_kernel, 3.0 * total, len(partials)),
        [(vecs, 3, beads), (vecs, 3, beads), (vecs, vecs)],
    )(basis, moved, *partials)
    return (vectors, residual, jnp.stack([alpha_one, factor_one, alpha_two]))


def solution(mesh):
    return jax.shard_map(
        local,
        mesh=mesh,
        in_specs=(P(None, ("row", "col")), P(None, None, ("row", "col"))),
        out_specs=(P(None, None, ("row", "col")), P(None, None, ("row", "col")), P()),
        check_vma=False,
    )
```

time: 228 us -> 59.3 us (0.26)
  blocking collectives: 204 us -> 0 us
  starting transfers between devices: 0 us -> 26 us
  waiting for transfers between devices: 0 us -> 20.1 us
  matrix products: 11.9 us -> 0 us
  Pallas kernels: 0 us -> 9.65 us
  other arithmetic: 8.47 us -> 0.61 us
    psum x5 -> x0, blocking collectives: 149 us -> none  [the longest x1 42 us: local(): lax.psum(local_gram(noise, noise), ('row', 'col')) / total_count]
    all_gather x4 -> x0, blocking collectives: 54.8 us -> none  [the longest x2 33.2 us: mobility(): source_piece = lax.all_gather(vectors, 'col', axis=2, tiled=True)]
    ppermute x0 -> x21, starting transfers between devices: none -> 26 us  [the longest x18 26 us: moved_by(): lax.ppermute(value, axis, [(index, (index + shift) % size) for index in r...]
    ppermute x0 -> x21, waiting for transfers between devices: none -> 20.1 us  [the longest x18 16.2 us: moved_by(): lax.ppermute(value, axis, [(index, (index + shift) % size) for index in r...]
    dot_general x14 -> x0, matrix products: 11.5 us -> none  [the longest x4 8.65 us: add_block(): jnp.einsum('abts,kbs->kat', tensor, block_vectors, precision=lax.Precisio...]
    pallas_call x0 -> x4, Pallas kernels: none -> 9.65 us  [the longest x1 6.7 us: local(): call(functools.partial(second_kernel, len(sources), beads), [(3, vecs, be...]
    another operation x11 -> x1, other arithmetic: 5.95 us -> 0.6 us  [local(): return (vectors, residual, jnp.stack([alpha_one, factor_one, alpha_two]))]
  transfers between devices with their start and end apart: 0 -> 21, of which waited for: 0 -> 18; matrix products, arithmetic and copies ran while one was open for 0% -> 0% of each run, Pallas kernels for 0% -> 0%
where the time goes in v1:
time: 59.3 us; the launch traced here: 59.1 us
  starting transfers between devices  26 us (44%)
  waiting for transfers between devices  20.1 us (34%)
  Pallas kernels  9.65 us (16%)
  local copies, waits for them, and re-layouts  2.08 us (4%)
  between operations  0.68 us (1%)
  other arithmetic  0.61 us (1%)
    ppermute x18, starting transfers between devices, moved_by(): lax.ppermute(value, axis, [(index, (index + shift) % size) for index in r...  26 us
    ppermute x18, waiting for transfers between devices, moved_by(): lax.ppermute(value, axis, [(index, (index + shift) % size) for index in r...  16.2 us
    pallas_call x1, Pallas kernels, local(): call(functools.partial(second_kernel, len(sources), beads), [(3, vecs, be...  6.7 us
    ppermute x3, waiting for transfers between devices, gather(): return [held, lax.ppermute(held, 'col', core)]  3.85 us
    pallas_call x1, Pallas kernels, local(): call(functools.partial(first_kernel, len(sources), beads), [(2 * vecs, 2...  2.62 us
    unnamed x24, local copies, waits for them, and re-layouts  2.07 us
  transfers between devices with their start and end apart: 21, of which 18 were waited for; matrix products, arithmetic and copies ran while one was open for 0% of the time, Pallas kernels for 0%

profile of v1, /device:TPU:0, one launch (start us, length us, event | category | flops | bytes accessed | tf_op | source)
XLA Modules:
  0.0 59.1 jit_solution(5877979166799401264)
XLA Ops:
  0.6 0.7 %copy.6.noise = f32[8,3,64]{2,1,0:T(4,128)S(1)} copy(f32[8,3,64]{2,0,1:T(8,128)} %param.3) | data formatting | bytes 12288 | tf_op args[1]
  1.4 3.0 %collective-permute-start = (f32[1,16,128]{2,1,0:T(8,128)S(1)}, f32[1,16,128]{2,1,0:T(8,128)S(1)}, u32[]{:S(2)}, u32[]{:S(2)}) collective-permute-start(f32[1,16,128]{2,1,0:T(8,128)S(1)} %bitcast.16), channel_id=1, source_target_pairs={{0,2},{1,3},{2,4},{3,5},{4,6},{5,7},{6,0},{7,1},{8,10},{9,11},{10,... | collective-permute-start | bytes 24584 | tf_op jit(solution)/shard_map/ppermute | solution.py:231
  4.5 2.6 %collective-permute-start.1 = (f32[1,16,128]{2,1,0:T(8,128)S(1)}, f32[1,16,128]{2,1,0:T(8,128)S(1)}, u32[]{:S(2)}, u32[]{:S(2)}) collective-permute-start(f32[1,16,128]{2,1,0:T(8,128)S(1)} %bitcast.17), channel_id=1, source_target_pairs={{0,4},{1,5},{2,6},{3,7},{4,0},{5,1},{6,2},{7,3},{8,12},{9,13},{10,... | collective-permute-start | bytes 24584 | tf_op jit(solution)/shard_map/ppermute | solution.py:231
  7.1 1.3 %collective-permute-start.2 = (f32[1,16,128]{2,1,0:T(8,128)S(1)}, f32[1,16,128]{2,1,0:T(8,128)S(1)}, u32[]{:S(2)}, u32[]{:S(2)}) collective-permute-start(f32[1,16,128]{2,1,0:T(8,128)S(1)} %bitcast.18), channel_id=1, source_target_pairs={{0,6},{1,7},{2,0},{3,1},{4,2},{5,3},{6,4},{7,5},{8,14},{9,15},{10,... | collective-permute-start | bytes 24584 | tf_op jit(solution)/shard_map/ppermute | solution.py:231
  8.4 0.7 %collective-permute-done.1 = f32[1,16,128]{2,1,0:T(8,128)S(1)} collective-permute-done((f32[1,16,128]{2,1,0:T(8,128)S(1)}, f32[1,16,128]{2,1,0:T(8,128)S(1)}, u32[]{:S(2)}, u32[]{:S(2)}) %collective-permute-start.1) | collective-permute-done | bytes 8224 | tf_op jit(solution)/shard_map/ppermute | solution.py:231
  9.1 1.6 %collective-permute-done.2 = f32[1,16,128]{2,1,0:T(8,128)S(1)} collective-permute-done((f32[1,16,128]{2,1,0:T(8,128)S(1)}, f32[1,16,128]{2,1,0:T(8,128)S(1)}, u32[]{:S(2)}, u32[]{:S(2)}) %collective-permute-start.2) | collective-permute-done | bytes 8224 | tf_op jit(solution)/shard_map/ppermute | solution.py:231
  10.7 1.5 %collective-permute-start.3 = (f32[4,16,128]{2,1,0:T(8,128)S(1)}, f32[4,16,128]{2,1,0:T(8,128)S(1)}, u32[]{:S(2)}, u32[]{:S(2)}) collective-permute-start(f32[4,16,128]{2,1,0:T(8,128)S(1)} %pad_maximum_fusion), channel_id=1, source_target_pairs={{0,8},{8,16},{16,24},{24,0},{1,9},{9,17},{17,25},{25,1},{2,10},{10... | collective-permute-start | bytes 98312 | tf_op jit(solution)/shard_map/ppermute | solution.py:231
  12.2 1.5 %collective-permute-start.4 = (f32[4,16,128]{2,1,0:T(8,128)S(1)}, f32[4,16,128]{2,1,0:T(8,128)S(1)}, u32[]{:S(2)}, u32[]{:S(2)}) collective-permute-start(f32[4,16,128]{2,1,0:T(8,128)S(1)} %pad_maximum_fusion), channel_id=1, source_target_pairs={{0,16},{8,24},{16,0},{24,8},{1,17},{9,25},{17,1},{25,9},{2,18},{10... | collective-permute-start | bytes 98312 | tf_op jit(solution)/shard_map/ppermute | solution.py:231
  13.7 1.4 %collective-permute-start.5 = (f32[4,16,128]{2,1,0:T(8,128)S(1)}, f32[4,16,128]{2,1,0:T(8,128)S(1)}, u32[]{:S(2)}, u32[]{:S(2)}) collective-permute-start(f32[4,16,128]{2,1,0:T(8,128)S(1)} %pad_maximum_fusion), channel_id=1, source_target_pairs={{0,24},{8,0},{16,8},{24,16},{1,25},{9,1},{17,9},{25,17},{2,26},{10... | collective-permute-start | bytes 98312 | tf_op jit(solution)/shard_map/ppermute | solution.py:231
  16.1 1.5 %collective-permute-done.5 = f32[4,16,128]{2,1,0:T(8,128)S(1)} collective-permute-done((f32[4,16,128]{2,1,0:T(8,128)S(1)}, f32[4,16,128]{2,1,0:T(8,128)S(1)}, u32[]{:S(2)}, u32[]{:S(2)}) %collective-permute-start.5) | collective-permute-done | bytes 32800 | tf_op jit(solution)/shard_map/ppermute | solution.py:231
  17.7 1.2 %collective-permute-done.6.refs_1_ = f32[16,16,128]{2,1,0:T(8,128)S(1)} collective-permute-done((f32[16,16,128]{2,1,0:T(8,128)S(1)}, f32[16,16,128]{2,1,0:T(8,128)S(1)}, u32[]{:S(2)}, u32[]{:S(2)}) %collective-permute-start.6) | collective-permute-done | bytes 131104 | tf_op jit(solution)/shard_map/ppermute | solution.py:245
  19.0 2.6 %shard_map.50.own_image = f32[16,128]{1,0:T(8,128)S(1)} custom-call(f32[64,3]{1,0:T(8,128)S(1)} %bitcast.10, f32[16,16,128]{2,1,0:T(8,128)S(1)} %constant_dynamic-update-slice_fusion.refs_0_, f32[16,16,128]{2,1,0:T(8,128)S(1)} %collective-permute-done.6.refs_1_), custom_call_target="tpu_custom_call" | custom-call | tf_op jit(solution)/shard_map/pallas_call | solution.py:258
  21.9 3.5 %collective-permute-start.8 = (f32[1,16,128]{2,1,0:T(8,128)S(1)}, f32[1,16,128]{2,1,0:T(8,128)S(1)}, u32[]{:S(2)}, u32[]{:S(2)}) collective-permute-start(f32[1,16,128]{2,1,0:T(8,128)S(1)} %bitcast.13), channel_id=1, source_target_pairs={{0,4},{1,5},{2,6},{3,7},{4,0},{5,1},{6,2},{7,3},{8,12},{9,13},{10,... | collective-permute-start | bytes 24584 | tf_op jit(solution)/shard_map/ppermute | solution.py:231
  25.5 1.6 %collective-permute-done.7 = f32[1,16,128]{2,1,0:T(8,128)S(1)} collective-permute-done((f32[1,16,128]{2,1,0:T(8,128)S(1)}, f32[1,16,128]{2,1,0:T(8,128)S(1)}, u32[]{:S(2)}, u32[]{:S(2)}) %collective-permute-start.7) | collective-permute-done | bytes 8224 | tf_op jit(solution)/shard_map/ppermute | solution.py:231
  27.1 1.9 %collective-permute-done.9 = f32[1,16,128]{2,1,0:T(8,128)S(1)} collective-permute-done((f32[1,16,128]{2,1,0:T(8,128)S(1)}, f32[1,16,128]{2,1,0:T(8,128)S(1)}, u32[]{:S(2)}, u32[]{:S(2)}) %collective-permute-start.9) | collective-permute-done | bytes 8224 | tf_op jit(solution)/shard_map/ppermute | solution.py:231
  29.0 1.4 %collective-permute-start.10 = (f32[4,16,128]{2,1,0:T(8,128)S(1)}, f32[4,16,128]{2,1,0:T(8,128)S(1)}, u32[]{:S(2)}, u32[]{:S(2)}) collective-permute-start(f32[4,16,128]{2,1,0:T(8,128)S(1)} %pad_maximum_fusion.1), channel_id=1, source_target_pairs={{0,8},{8,16},{16,24},{24,0},{1,9},{9,17},{17,25},{25,1},{2,10},{10... | collective-permute-start | bytes 98312 | tf_op jit(solution)/shard_map/ppermute | solution.py:231
  30.4 1.5 %collective-permute-start.11 = (f32[4,16,128]{2,1,0:T(8,128)S(1)}, f32[4,16,128]{2,1,0:T(8,128)S(1)}, u32[]{:S(2)}, u32[]{:S(2)}) collective-permute-start(f32[4,16,128]{2,1,0:T(8,128)S(1)} %pad_maximum_fusion.1), channel_id=1, source_target_pairs={{0,16},{8,24},{16,0},{24,8},{1,17},{9,25},{17,1},{25,9},{2,18},{10... | collective-permute-start | bytes 98312 | tf_op jit(solution)/shard_map/ppermute | solution.py:231
  32.5 1.4 %collective-permute-done.10 = f32[4,16,128]{2,1,0:T(8,128)S(1)} collective-permute-done((f32[4,16,128]{2,1,0:T(8,128)S(1)}, f32[4,16,128]{2,1,0:T(8,128)S(1)}, u32[]{:S(2)}, u32[]{:S(2)}) %collective-permute-start.10) | collective-permute-done | bytes 32800 | tf_op jit(solution)/shard_map/ppermute | solution.py:231
  34.3 1.5 %collective-permute-done.12 = f32[4,16,128]{2,1,0:T(8,128)S(1)} collective-permute-done((f32[4,16,128]{2,1,0:T(8,128)S(1)}, f32[4,16,128]{2,1,0:T(8,128)S(1)}, u32[]{:S(2)}, u32[]{:S(2)}) %collective-permute-start.12) | collective-permute-done | bytes 32800 | tf_op jit(solution)/shard_map/ppermute | solution.py:231
  35.8 1.3 %collective-permute-done.13.refs_3_ = f32[16,16,128]{2,1,0:T(8,128)S(1)} collective-permute-done((f32[16,16,128]{2,1,0:T(8,128)S(1)}, f32[16,16,128]{2,1,0:T(8,128)S(1)}, u32[]{:S(2)}, u32[]{:S(2)}) %collective-permute-start.13) | collective-permute-done | bytes 131104 | tf_op jit(solution)/shard_map/ppermute | solution.py:245
  37.2 6.7 %shard_map.51 = (f32[3,8,64]{2,1,0:T(8,128)S(1)}, f32[3,8,64]{2,1,0:T(8,128)S(1)}, f32[8,8]{1,0:T(8,128)S(1)}, f32[8,8]{1,0:T(8,128)S(1)}, f32[8,8]{1,0:T(8,128)S(1)}) custom-call(f32[64,3]{1,0:T(8,128)S(1)} %bitcast.11, f32[16,128]{1,0:T(8,128)S(1)} %shard_map.49.own, f32[16,128]{1,0:T(8,128)S(1)} %shard_map.50.own_image, ...), custom_call_target="tpu_custom_call" | custom-call | tf_op jit(solution)/shard_map/pallas_call | solution.py:262
  43.9 0.7 %collective-permute-start.14 = (f32[1,8,8]{2,1,0:T(8,128)S(1)}, f32[1,8,8]{2,1,0:T(8,128)S(1)}, u32[]{:S(2)}, u32[]{:S(2)}) collective-permute-start(f32[1,8,8]{2,1,0:T(8,128)S(1)} %bitcast.20), channel_id=1, source_target_pairs={{0,2},{1,3},{2,4},{3,5},{4,6},{5,7},{6,0},{7,1},{8,10},{9,11},{10,... | collective-permute-start | bytes 776 | tf_op jit(solution)/shard_map/ppermute | solution.py:231
  44.6 1.8 %collective-permute-start.15 = (f32[1,8,8]{2,1,0:T(8,128)S(1)}, f32[1,8,8]{2,1,0:T(8,128)S(1)}, u32[]{:S(2)}, u32[]{:S(2)}) collective-permute-start(f32[1,8,8]{2,1,0:T(8,128)S(1)} %bitcast.21), channel_id=1, source_target_pairs={{0,4},{1,5},{2,6},{3,7},{4,0},{5,1},{6,2},{7,3},{8,12},{9,13},{10,... | collective-permute-start | bytes 776 | tf_op jit(solution)/shard_map/ppermute | solution.py:231
  46.4 1.4 %collective-permute-start.16 = (f32[1,8,8]{2,1,0:T(8,128)S(1)}, f32[1,8,8]{2,1,0:T(8,128)S(1)}, u32[]{:S(2)}, u32[]{:S(2)}) collective-permute-start(f32[1,8,8]{2,1,0:T(8,128)S(1)} %bitcast.22), channel_id=1, source_target_pairs={{0,6},{1,7},{2,0},{3,1},{4,2},{5,3},{6,4},{7,5},{8,14},{9,15},{10,... | collective-permute-start | bytes 776 | tf_op jit(solution)/shard_map/ppermute | solution.py:231
  47.7 1.6 %collective-permute-done.14 = f32[1,8,8]{2,1,0:T(8,128)S(1)} collective-permute-done((f32[1,8,8]{2,1,0:T(8,128)S(1)}, f32[1,8,8]{2,1,0:T(8,128)S(1)}, u32[]{:S(2)}, u32[]{:S(2)}) %collective-permute-start.14) | collective-permute-done | bytes 288 | tf_op jit(solution)/shard_map/ppermute | solution.py:231
  49.3 0.7 %collective-permute-done.16 = f32[1,8,8]{2,1,0:T(8,128)S(1)} collective-permute-done((f32[1,8,8]{2,1,0:T(8,128)S(1)}, f32[1,8,8]{2,1,0:T(8,128)S(1)}, u32[]{:S(2)}, u32[]{:S(2)}) %collective-permute-start.16) | collective-permute-done | bytes 288 | tf_op jit(solution)/shard_map/ppermute | solution.py:231
  50.0 1.5 %collective-permute-start.17 = (f32[4,8,8]{2,1,0:T(8,128)S(1)}, f32[4,8,8]{2,1,0:T(8,128)S(1)}, u32[]{:S(2)}, u32[]{:S(2)}) collective-permute-start(f32[4,8,8]{2,1,0:T(8,128)S(1)} %pad_maximum_fusion.2), channel_id=1, source_target_pairs={{0,8},{8,16},{16,24},{24,0},{1,9},{9,17},{17,25},{25,1},{2,10},{10... | collective-permute-start | bytes 3080 | tf_op jit(solution)/shard_map/ppermute | solution.py:231
  52.0 1.4 %collective-permute-start.19 = (f32[4,8,8]{2,1,0:T(8,128)S(1)}, f32[4,8,8]{2,1,0:T(8,128)S(1)}, u32[]{:S(2)}, u32[]{:S(2)}) collective-permute-start(f32[4,8,8]{2,1,0:T(8,128)S(1)} %pad_maximum_fusion.2), channel_id=1, source_target_pairs={{0,24},{8,0},{16,8},{24,16},{1,25},{9,1},{17,9},{25,17},{2,26},{10... | collective-permute-start | bytes 3080 | tf_op jit(solution)/shard_map/ppermute | solution.py:231
  53.4 1.2 %collective-permute-done.17 = f32[4,8,8]{2,1,0:T(8,128)S(1)} collective-permute-done((f32[4,8,8]{2,1,0:T(8,128)S(1)}, f32[4,8,8]{2,1,0:T(8,128)S(1)}, u32[]{:S(2)}, u32[]{:S(2)}) %collective-permute-start.17) | collective-permute-done | bytes 1056 | tf_op jit(solution)/shard_map/ppermute | solution.py:231
  55.7 1.3 %collective-permute-done.20.refs_1_ = f32[16,8,8]{2,1,0:T(8,128)S(1)} collective-permute-done((f32[16,8,8]{2,1,0:T(8,128)S(1)}, f32[16,8,8]{2,1,0:T(8,128)S(1)}, u32[]{:S(2)}, u32[]{:S(2)}) %collective-permute-start.20) | collective-permute-done | bytes 4128 | tf_op jit(solution)/shard_map/ppermute | solution.py:245
  57.2 0.6 %copy.7 = f32[8,3,64]{2,0,1:T(8,128)} copy(f32[8,3,64]{2,1,0:T(4,128)S(1)} %get-tuple-element.19) | data formatting | bytes 12288
  58.5 0.6 %pad_maximum_fusion.3 = f32[3,8,8]{2,1,0:T(8,128)} fusion(f32[1,8,8]{2,1,0:T(8,128)S(1)} %bitcast.26, f32[1,8,8]{2,1,0:T(8,128)S(1)} %bitcast.25, f32[1,8,8]{2,1,0:T(8,128)S(1)} %bitcast.24), kind=kLoop, calls=%fused_computation.24 | loop fusion | flops 384 | bytes 1536 | tf_op jit(solution)/shard_map/stack | solution.py:272
  (45 shorter events, 5.0 us)
Async XLA Ops:
  0.6 0.7 %copy-start = (f32[3,64]{1,0:T(4,128)S(1)}, f32[3,64]{1,0:T(4,128)}, u32[]{:S(2)}) copy-start(f32[3,64]{1,0:T(4,128)} %positions.1) | copy-start | bytes 2308
  1.4 7.0 %collective-permute-start = (f32[1,16,128]{2,1,0:T(8,128)S(1)}, f32[1,16,128]{2,1,0:T(8,128)S(1)}, u32[]{:S(2)}, u32[]{:S(2)}) collective-permute-start(f32[1,16,128]{2,1,0:T(8,128)S(1)} %bitcast.16), channel_id=1, source_target_pairs={{0,2},{1,3},{2,4},{3,5},{4,6},{5,7},{6,0},{7,1},{8,10},{9,11},{10,... | collective-permute-start | bytes 24584 | tf_op jit(solution)/shard_map/ppermute | solution.py:231
  4.5 4.6 %collective-permute-start.1 = (f32[1,16,128]{2,1,0:T(8,128)S(1)}, f32[1,16,128]{2,1,0:T(8,128)S(1)}, u32[]{:S(2)}, u32[]{:S(2)}) collective-permute-start(f32[1,16,128]{2,1,0:T(8,128)S(1)} %bitcast.17), channel_id=1, source_target_pairs={{0,4},{1,5},{2,6},{3,7},{4,0},{5,1},{6,2},{7,3},{8,12},{9,13},{10,... | collective-permute-start | bytes 24584 | tf_op jit(solution)/shard_map/ppermute | solution.py:231
  7.1 3.7 %collective-permute-start.2 = (f32[1,16,128]{2,1,0:T(8,128)S(1)}, f32[1,16,128]{2,1,0:T(8,128)S(1)}, u32[]{:S(2)}, u32[]{:S(2)}) collective-permute-start(f32[1,16,128]{2,1,0:T(8,128)S(1)} %bitcast.18), channel_id=1, source_target_pairs={{0,6},{1,7},{2,0},{3,1},{4,2},{5,3},{6,4},{7,5},{8,14},{9,15},{10,... | collective-permute-start | bytes 24584 | tf_op jit(solution)/shard_map/ppermute | solution.py:231
  10.7 4.8 %collective-permute-start.3 = (f32[4,16,128]{2,1,0:T(8,128)S(1)}, f32[4,16,128]{2,1,0:T(8,128)S(1)}, u32[]{:S(2)}, u32[]{:S(2)}) collective-permute-start(f32[4,16,128]{2,1,0:T(8,128)S(1)} %pad_maximum_fusion), channel_id=1, source_target_pairs={{0,8},{8,16},{16,24},{24,0},{1,9},{9,17},{17,25},{25,1},{2,10},{10... | collective-permute-start | bytes 98312 | tf_op jit(solution)/shard_map/ppermute | solution.py:231
  12.2 3.9 %collective-permute-start.4 = (f32[4,16,128]{2,1,0:T(8,128)S(1)}, f32[4,16,128]{2,1,0:T(8,128)S(1)}, u32[]{:S(2)}, u32[]{:S(2)}) collective-permute-start(f32[4,16,128]{2,1,0:T(8,128)S(1)} %pad_maximum_fusion), channel_id=1, source_target_pairs={{0,16},{8,24},{16,0},{24,8},{1,17},{9,25},{17,1},{25,9},{2,18},{10... | collective-permute-start | bytes 98312 | tf_op jit(solution)/shard_map/ppermute | solution.py:231
  13.7 3.9 %collective-permute-start.5 = (f32[4,16,128]{2,1,0:T(8,128)S(1)}, f32[4,16,128]{2,1,0:T(8,128)S(1)}, u32[]{:S(2)}, u32[]{:S(2)}) collective-permute-start(f32[4,16,128]{2,1,0:T(8,128)S(1)} %pad_maximum_fusion), channel_id=1, source_target_pairs={{0,24},{8,0},{16,8},{24,16},{1,25},{9,1},{17,9},{25,17},{2,26},{10... | collective-permute-start | bytes 98312 | tf_op jit(solution)/shard_map/ppermute | solution.py:231
  17.6 1.3 %collective-permute-start.6 = (f32[16,16,128]{2,1,0:T(8,128)S(1)}, f32[16,16,128]{2,1,0:T(8,128)S(1)}, u32[]{:S(2)}, u32[]{:S(2)}) collective-permute-start(f32[16,16,128]{2,1,0:T(8,128)S(1)} %constant_dynamic-update-slice_fusion.refs_0_), channel_id=1, source_target_pairs={{0,1},{1,0},{2,3},{3,2},{4,5},{5,4},{6,7},{7,6},{8,9},{9,8},{10,11... | collective-permute-start | bytes 393224 | tf_op jit(solution)/shard_map/ppermute | solution.py:245
  21.6 5.5 %collective-permute-start.7 = (f32[1,16,128]{2,1,0:T(8,128)S(1)}, f32[1,16,128]{2,1,0:T(8,128)S(1)}, u32[]{:S(2)}, u32[]{:S(2)}) collective-permute-start(f32[1,16,128]{2,1,0:T(8,128)S(1)} %bitcast.12), channel_id=1, source_target_pairs={{0,2},{1,3},{2,4},{3,5},{4,6},{5,7},{6,0},{7,1},{8,10},{9,11},{10,... | collective-permute-start | bytes 24584 | tf_op jit(solution)/shard_map/ppermute | solution.py:231
  21.9 5.2 %collective-permute-start.8 = (f32[1,16,128]{2,1,0:T(8,128)S(1)}, f32[1,16,128]{2,1,0:T(8,128)S(1)}, u32[]{:S(2)}, u32[]{:S(2)}) collective-permute-start(f32[1,16,128]{2,1,0:T(8,128)S(1)} %bitcast.13), channel_id=1, source_target_pairs={{0,4},{1,5},{2,6},{3,7},{4,0},{5,1},{6,2},{7,3},{8,12},{9,13},{10,... | collective-permute-start | bytes 24584 | tf_op jit(solution)/shard_map/ppermute | solution.py:231
  25.4 3.7 %collective-permute-start.9 = (f32[1,16,128]{2,1,0:T(8,128)S(1)}, f32[1,16,128]{2,1,0:T(8,128)S(1)}, u32[]{:S(2)}, u32[]{:S(2)}) collective-permute-start(f32[1,16,128]{2,1,0:T(8,128)S(1)} %bitcast.14), channel_id=1, source_target_pairs={{0,6},{1,7},{2,0},{3,1},{4,2},{5,3},{6,4},{7,5},{8,14},{9,15},{10,... | collective-permute-start | bytes 24584 | tf_op jit(solution)/shard_map/ppermute | solution.py:231
  29.0 4.8 %collective-permute-start.10 = (f32[4,16,128]{2,1,0:T(8,128)S(1)}, f32[4,16,128]{2,1,0:T(8,128)S(1)}, u32[]{:S(2)}, u32[]{:S(2)}) collective-permute-start(f32[4,16,128]{2,1,0:T(8,128)S(1)} %pad_maximum_fusion.1), channel_id=1, source_target_pairs={{0,8},{8,16},{16,24},{24,0},{1,9},{9,17},{17,25},{25,1},{2,10},{10... | collective-permute-start | bytes 98312 | tf_op jit(solution)/shard_map/ppermute | solution.py:231
  30.4 3.9 %collective-permute-start.11 = (f32[4,16,128]{2,1,0:T(8,128)S(1)}, f32[4,16,128]{2,1,0:T(8,128)S(1)}, u32[]{:S(2)}, u32[]{:S(2)}) collective-permute-start(f32[4,16,128]{2,1,0:T(8,128)S(1)} %pad_maximum_fusion.1), channel_id=1, source_target_pairs={{0,16},{8,24},{16,0},{24,8},{1,17},{9,25},{17,1},{25,9},{2,18},{10... | collective-permute-start | bytes 98312 | tf_op jit(solution)/shard_map/ppermute | solution.py:231
  31.9 3.9 %collective-permute-start.12 = (f32[4,16,128]{2,1,0:T(8,128)S(1)}, f32[4,16,128]{2,1,0:T(8,128)S(1)}, u32[]{:S(2)}, u32[]{:S(2)}) collective-permute-start(f32[4,16,128]{2,1,0:T(8,128)S(1)} %pad_maximum_fusion.1), channel_id=1, source_target_pairs={{0,24},{8,0},{16,8},{24,16},{1,25},{9,1},{17,9},{25,17},{2,26},{10... | collective-permute-start | bytes 98312 | tf_op jit(solution)/shard_map/ppermute | solution.py:231
  35.8 1.3 %collective-permute-start.13 = (f32[16,16,128]{2,1,0:T(8,128)S(1)}, f32[16,16,128]{2,1,0:T(8,128)S(1)}, u32[]{:S(2)}, u32[]{:S(2)}) collective-permute-start(f32[16,16,128]{2,1,0:T(8,128)S(1)} %constant_dynamic-update-slice_fusion.7.refs_2_), channel_id=1, source_target_pairs={{0,1},{1,0},{2,3},{3,2},{4,5},{5,4},{6,7},{7,6},{8,9},{9,8},{10,11... | collective-permute-start | bytes 393224 | tf_op jit(solution)/shard_map/ppermute | solution.py:245
  43.9 5.4 %collective-permute-start.14 = (f32[1,8,8]{2,1,0:T(8,128)S(1)}, f32[1,8,8]{2,1,0:T(8,128)S(1)}, u32[]{:S(2)}, u32[]{:S(2)}) collective-permute-start(f32[1,8,8]{2,1,0:T(8,128)S(1)} %bitcast.20), channel_id=1, source_target_pairs={{0,2},{1,3},{2,4},{3,5},{4,6},{5,7},{6,0},{7,1},{8,10},{9,11},{10,... | collective-permute-start | bytes 776 | tf_op jit(solution)/shard_map/ppermute | solution.py:231
  44.6 4.7 %collective-permute-start.15 = (f32[1,8,8]{2,1,0:T(8,128)S(1)}, f32[1,8,8]{2,1,0:T(8,128)S(1)}, u32[]{:S(2)}, u32[]{:S(2)}) collective-permute-start(f32[1,8,8]{2,1,0:T(8,128)S(1)} %bitcast.21), channel_id=1, source_target_pairs={{0,4},{1,5},{2,6},{3,7},{4,0},{5,1},{6,2},{7,3},{8,12},{9,13},{10,... | collective-permute-start | bytes 776 | tf_op jit(solution)/shard_map/ppermute | solution.py:231
  46.4 3.6 %collective-permute-start.16 = (f32[1,8,8]{2,1,0:T(8,128)S(1)}, f32[1,8,8]{2,1,0:T(8,128)S(1)}, u32[]{:S(2)}, u32[]{:S(2)}) collective-permute-start(f32[1,8,8]{2,1,0:T(8,128)S(1)} %bitcast.22), channel_id=1, source_target_pairs={{0,6},{1,7},{2,0},{3,1},{4,2},{5,3},{6,4},{7,5},{8,14},{9,15},{10,... | collective-permute-start | bytes 776 | tf_op jit(solution)/shard_map/ppermute | solution.py:231
  50.0 4.6 %collective-permute-start.17 = (f32[4,8,8]{2,1,0:T(8,128)S(1)}, f32[4,8,8]{2,1,0:T(8,128)S(1)}, u32[]{:S(2)}, u32[]{:S(2)}) collective-permute-start(f32[4,8,8]{2,1,0:T(8,128)S(1)} %pad_maximum_fusion.2), channel_id=1, source_target_pairs={{0,8},{8,16},{16,24},{24,0},{1,9},{9,17},{17,25},{25,1},{2,10},{10... | collective-permute-start | bytes 3080 | tf_op jit(solution)/shard_map/ppermute | solution.py:231
  51.5 3.7 %collective-permute-start.18 = (f32[4,8,8]{2,1,0:T(8,128)S(1)}, f32[4,8,8]{2,1,0:T(8,128)S(1)}, u32[]{:S(2)}, u32[]{:S(2)}) collective-permute-start(f32[4,8,8]{2,1,0:T(8,128)S(1)} %pad_maximum_fusion.2), channel_id=1, source_target_pairs={{0,16},{8,24},{16,0},{24,8},{1,17},{9,25},{17,1},{25,9},{2,18},{10... | collective-permute-start | bytes 3080 | tf_op jit(solution)/shard_map/ppermute | solution.py:231
  52.0 3.7 %collective-permute-start.19 = (f32[4,8,8]{2,1,0:T(8,128)S(1)}, f32[4,8,8]{2,1,0:T(8,128)S(1)}, u32[]{:S(2)}, u32[]{:S(2)}) collective-permute-start(f32[4,8,8]{2,1,0:T(8,128)S(1)} %pad_maximum_fusion.2), channel_id=1, source_target_pairs={{0,24},{8,0},{16,8},{24,16},{1,25},{9,1},{17,9},{25,17},{2,26},{10... | collective-permute-start | bytes 3080 | tf_op jit(solution)/shard_map/ppermute | solution.py:231
  55.7 1.3 %collective-permute-start.20 = (f32[16,8,8]{2,1,0:T(8,128)S(1)}, f32[16,8,8]{2,1,0:T(8,128)S(1)}, u32[]{:S(2)}, u32[]{:S(2)}) collective-permute-start(f32[16,8,8]{2,1,0:T(8,128)S(1)} %constant_dynamic-update-slice_fusion.14.refs_0_), channel_id=1, source_target_pairs={{0,1},{1,0},{2,3},{3,2},{4,5},{5,4},{6,7},{7,6},{8,9},{9,8},{10,11... | collective-permute-start | bytes 12296 | tf_op jit(solution)/shard_map/ppermute | solution.py:245

commit v2 on v1

--- a/solution.py
+++ b/solution.py
@@ -7,7 +7,6 @@
 from jax.experimental.pallas import tpu as pltpu
 from jax.sharding import PartitionSpec as P
 
-CORES = 2
 CHUNK = 2048
 F32 = jnp.float32
 BF16 = jnp.bfloat16
@@ -15,11 +14,11 @@
 
 def pack_kernel(positions, noise, block):
     beads = positions.shape[1]
-    vecs = noise.shape[0]
+    vecs = noise.shape[1]
     block[...] = jnp.zeros(block.shape, F32)
-    block[:vecs, :beads] = noise[:, 0, :]
-    block[:vecs, beads:] = noise[:, 1, :]
-    block[vecs:, :beads] = noise[:, 2, :]
+    block[:vecs, :beads] = noise[0]
+    block[:vecs, beads:] = noise[1]
+    block[vecs:, :beads] = noise[2]
     block[vecs : vecs + 3, beads:] = positions[...]
 
 
@@ -168,7 +167,7 @@
 
 def second_kernel(count, beads, targets, own, own_image, *refs):
     sources, images = refs[:count], refs[count : 2 * count]
-    basis, image, alpha_one, factor_one, partial, wide, wide_image, high, low = refs[2 * count :]
+    basis, image, coefficients, partial, wide, wide_image, high, low = refs[2 * count :]
     unpack(sources, 4, beads, wide)
     unpack(images, 3, beads, wide_image)
     total = wide.shape[1]
@@ -186,8 +185,8 @@
     alpha = matmul_nt(matmul(inverse_zero, cross), inverse_zero)
     remainder = matmul_nt(matmul(inverse_zero, squared), inverse_zero) - matmul_tn(alpha, alpha)
     factor_t, inverse_one = cholesky(remainder)
-    alpha_one[...] = alpha
-    factor_one[...] = factor_t.T
+    coefficients[0] = alpha
+    coefficients[1] = factor_t.T
     gram = jnp.zeros((8, 8), F32)
     for part in range(3):
         half, side = part // 2 * 8, part % 2 * beads
@@ -204,17 +203,17 @@
     partial[...] = gram
 
 
-def last_kernel(size, count, basis, image, *refs):
-    partials, (vectors, residual, alpha_two) = refs[:count], refs[count:]
+def last_kernel(size, count, basis, image, both, *refs):
+    partials, (residual, coefficients) = refs[:count], refs[count:]
     total = jnp.zeros((8, 8), F32)
     for ref in partials:
         for index in range(ref.shape[0]):
             total = total + ref[index]
     alpha = total / size
-    alpha_two[...] = alpha
+    coefficients[0:2] = both[...]
+    coefficients[2] = alpha
     for part in range(3):
-        vectors[:, part, :] = basis[part]
-        residual[:, part, :] = image[part] - matmul_tn(alpha, basis[part])
+        residual[part] = image[part] - matmul_tn(alpha, basis[part])
 
 
 def call(kernel, shapes, scratch=()):
@@ -226,23 +225,10 @@
     )
 
 
-def moved_by(value, axis, shift):
-    size = lax.axis_size(axis)
-    return lax.ppermute(value, axis, [(index, (index + shift) % size) for index in range(size)])
-
-
 def gather(block):
-    cols, rows = lax.axis_size("col"), lax.axis_size("row")
-    layers = [block[None]]
-    for shift in range(CORES, cols, CORES):
-        layers.append(moved_by(block[None], "col", shift))
-    held = jnp.concatenate(layers, axis=0)
-    plane = [held]
-    for shift in range(1, rows):
-        plane.append(moved_by(held, "row", shift))
-    held = jnp.concatenate(plane, axis=0)
-    core = [(index, index ^ 1) for index in range(cols)]
-    return [held, lax.ppermute(held, "col", core)]
+    devices = lax.axis_size("row") * lax.axis_size("col")
+    copies = jnp.broadcast_to(block[None], (devices,) + block.shape)
+    return [lax.all_to_all(copies, ("row", "col"), 0, 0, tiled=True)]
 
 
 def local(positions, noise):
@@ -251,7 +237,7 @@
     total = beads * devices
     chunk = min(total, CHUNK)
     targets = positions.T
-    (block,) = call(pack_kernel, [(2 * vecs, 2 * beads)])(positions, noise)
+    (block,) = call(pack_kernel, [(2 * vecs, 2 * beads)])(positions, noise.transpose(1, 0, 2))
     sources = gather(block)
     tensors = [pltpu.VMEM((6 * beads, chunk), BF16), pltpu.VMEM((6 * beads, chunk), BF16)]
     wide = pltpu.VMEM((4 * vecs, total), F32)
@@ -259,17 +245,17 @@
         functools.partial(first_kernel, len(sources), beads), [(2 * vecs, 2 * beads)], [wide] + tensors
     )(targets, *sources)
     images = gather(image)
-    basis, moved, alpha_one, factor_one, partial = call(
+    basis, moved, both, partial = call(
         functools.partial(second_kernel, len(sources), beads),
-        [(3, vecs, beads), (3, vecs, beads), (vecs, vecs), (vecs, vecs), (vecs, vecs)],
+        [(3, vecs, beads), (3, vecs, beads), (2, vecs, vecs), (vecs, vecs)],
         [wide, wide] + tensors,
     )(targets, block, image, *sources, *images)
     partials = gather(partial)
-    vectors, residual, alpha_two = call(
+    residual, coefficients = call(
         functools.partial(last_kernel, 3.0 * total, len(partials)),
-        [(vecs, 3, beads), (vecs, 3, beads), (vecs, vecs)],
-    )(basis, moved, *partials)
-    return (vectors, residual, jnp.stack([alpha_one, factor_one, alpha_two]))
+        [(3, vecs, beads), (3, vecs, vecs)],
+    )(basis, moved, both, *partials)
+    return (basis.transpose(1, 0, 2), residual.transpose(1, 0, 2), coefficients)
 
 
 def solution(mesh):

time: 59.3 us -> 54.8 us (0.924)
  blocking collectives: 0 us -> 23.2 us
  starting transfers between devices: 26 us -> 7.3 us
  waiting for transfers between devices: 20.1 us -> 10.3 us
  Pallas kernels: 9.65 us -> 10.7 us
  other arithmetic: 0.61 us -> 0 us
    ppermute x21 -> x0, starting transfers between devices: 26 us -> none  [the longest x18 26 us: moved_by(): lax.ppermute(value, axis, [(index, (index + shift) % size) for index in r...]
    all_to_all x0 -> x2, blocking collectives: none -> 23.2 us  [gather(): return [lax.all_to_all(copies, ('row', 'col'), 0, 0, tiled=True)]]
    ppermute x21 -> x0, waiting for transfers between devices: 20.1 us -> none  [the longest x18 16.2 us: moved_by(): lax.ppermute(value, axis, [(index, (index + shift) % size) for index in r...]
    all_to_all x0 -> x1, waiting for transfers between devices: none -> 10.3 us  [gather(): return [lax.all_to_all(copies, ('row', 'col'), 0, 0, tiled=True)]]
    all_to_all x0 -> x1, starting transfers between devices: none -> 7.3 us  [gather(): return [lax.all_to_all(copies, ('row', 'col'), 0, 0, tiled=True)]]
    broadcast_in_dim x0 -> x3, local copies, waits for them, and re-layouts: none -> 0.78 us  [gather(): copies = jnp.broadcast_to(block[None], (devices,) + block.shape)]
    pallas_call x2, Pallas kernels: 0.33 us -> 0.94 us  [the longest x1 0.87 us: local(): call(functools.partial(last_kernel, 3.0 * total, len(partials)), [(3, vec...]
    another operation x1 -> x0, other arithmetic: 0.6 us -> none  [local(): return (vectors, residual, jnp.stack([alpha_one, factor_one, alpha_two]))]
  transfers between devices with their start and end apart: 21 -> 1, of which waited for: 18 -> 1; matrix products, arithmetic and copies ran while one was open for 0% -> 0% of each run, Pallas kernels for 0% -> 0%
where the time goes in v2:
time: 54.8 us; the launch traced here: 54.5 us
  blocking collectives  23.2 us (42%)
  Pallas kernels  10.7 us (20%)
  waiting for transfers between devices  10.3 us (19%)
  starting transfers between devices  7.3 us (13%)
  local copies, waits for them, and re-layouts  2.27 us (4%)
  between operations  0.68 us (1%)
    all_to_all x2, blocking collectives, gather(): return [lax.all_to_all(copies, ('row', 'col'), 0, 0, tiled=True)]  23.2 us
    all_to_all x1, waiting for transfers between devices, gather(): return [lax.all_to_all(copies, ('row', 'col'), 0, 0, tiled=True)]  10.3 us
    all_to_all x1, starting transfers between devices, gather(): return [lax.all_to_all(copies, ('row', 'col'), 0, 0, tiled=True)]  7.3 us
    pallas_call x1, Pallas kernels, local(): call(functools.partial(second_kernel, len(sources), beads), [(3, vecs, be...  7.18 us
    pallas_call x1, Pallas kernels, local(): call(functools.partial(first_kernel, len(sources), beads), [(2 * vecs, 2...  2.62 us
    unnamed x9, local copies, waits for them, and re-layouts  1.49 us
  transfers between devices with their start and end apart: 1, of which 1 were waited for; matrix products, arithmetic and copies ran while one was open for 0% of the time, Pallas kernels for 0%

profile of v2, /device:TPU:0, one launch (start us, length us, event | category | flops | bytes accessed | tf_op | source)
XLA Modules:
  0.0 54.5 jit_solution(14622261014928866163)
XLA Ops:
  0.6 0.0 copy-start.1
  0.6 0.7 %copy-done.1 = f32[8,3,64]{2,0,1:T(8,128)S(1)} copy-done((f32[8,3,64]{2,0,1:T(8,128)S(1)}, f32[8,3,64]{2,0,1:T(8,128)}, u32[]{:S(2)}) %copy-start.1) | copy-done | bytes 6168
  1.3 0.0 copy-start.2
  1.3 0.7 %copy-done.2 = f32[3,64]{1,0:T(4,128)S(1)} copy-done((f32[3,64]{1,0:T(4,128)S(1)}, f32[3,64]{1,0:T(4,128)}, u32[]{:S(2)}) %copy-start.2) | copy-done | bytes 792
  2.0 0.1 shard_map.49.own
  2.1 0.7 %broadcast_in_dim.6 = f32[32,16,128]{2,1,0:T(8,128)} broadcast(f32[16,128]{1,0:T(8,128)S(1)} %shard_map.49.own), dimensions={1,2} | broadcast | bytes 270336 | tf_op jit(solution)/shard_map/broadcast_in_dim | solution.py:230
  2.8 0.0 copy-start.3
  2.8 7.3 %all-to-all-start = ((f32[32,16,128]{2,1,0:T(8,128)}), f32[32,16,128]{2,1,0:T(8,128)S(1)}, u32[]{:S(2)}, u32[]{:S(2)}) async-start(f32[32,16,128]{2,1,0:T(8,128)} %broadcast_in_dim.6), calls=%async_computation | async-start | bytes 524288 | tf_op jit(solution)/shard_map/all_to_all | solution.py:231
  10.1 0.0 copy-done.3
  10.1 0.1 copy.5
  10.2 10.3 %all-to-all-done.refs_0_ = f32[32,16,128]{2,1,0:T(8,128)S(1)} async-done(((f32[32,16,128]{2,1,0:T(8,128)}), f32[32,16,128]{2,1,0:T(8,128)S(1)}, u32[]{:S(2)}, u32[]{:S(2)}) %all-to-all-start) | async-done | bytes 262176 | tf_op jit(solution)/shard_map/all_to_all | solution.py:231
  20.5 2.6 %shard_map.50.own_image = f32[16,128]{1,0:T(8,128)S(1)} custom-call(f32[64,3]{1,0:T(8,128)S(1)} %bitcast.4, f32[32,16,128]{2,1,0:T(8,128)S(1)} %all-to-all-done.refs_0_), custom_call_target="tpu_custom_call" | custom-call | tf_op jit(solution)/shard_map/pallas_call | solution.py:244
  23.1 0.1 broadcast_in_dim.7
  23.2 12.7 %all_to_all.15.refs_1_ = f32[32,16,128]{2,1,0:T(8,128)S(1)} all-to-all(f32[32,16,128]{2,1,0:T(8,128)S(1)} %broadcast_in_dim.7), channel_id=1, replica_groups=mesh['row'=4,'col'=8] {'row','col'}, dimensions={0} | all-to-all | bytes 524288 | tf_op jit(solution)/shard_map/all_to_all | solution.py:231
  35.9 7.2 %shard_map.51 = (f32[3,8,64]{2,1,0:T(8,128)}, f32[3,8,64]{2,1,0:T(8,128)S(1)}, f32[2,8,8]{2,1,0:T(8,128)S(1)}, f32[8,8]{1,0:T(8,128)S(1)}) custom-call(f32[64,3]{1,0:T(8,128)S(1)} %bitcast.5, f32[16,128]{1,0:T(8,128)S(1)} %shard_map.49.own, f32[16,128]{1,0:T(8,128)S(1)} %shard_map.50.own_image, f32[32,16,128]{2,1,0:T(8,128)S(1)} %all-to-all-done.refs_0_, ...), custom_call_target="tpu_custom_call" | custom-call | tf_op jit(solution)/shard_map/pallas_call | solution.py:248
  43.1 0.0 copy-start
  43.1 10.5 %all_to_all.16.refs_0_ = f32[32,8,8]{2,1,0:T(8,128)S(1)} all-to-all(f32[32,8,8]{2,1,0:T(8,128)S(1)} %broadcast_in_dim.8), channel_id=1, replica_groups=mesh['row'=4,'col'=8] {'row','col'}, dimensions={0} | all-to-all | bytes 16384 | tf_op jit(solution)/shard_map/all_to_all | solution.py:231
  53.6 0.0 copy-done
  53.6 0.9 %shard_map.52 = (f32[3,8,64]{2,1,0:T(8,128)}, f32[3,8,8]{2,1,0:T(8,128)}) custom-call(f32[3,8,64]{2,1,0:T(8,128)S(1)} %copy-done, f32[3,8,64]{2,1,0:T(8,128)S(1)} %get-tuple-element.10.image, f32[2,8,8]{2,1,0:T(8,128)S(1)} %get-tuple-element.11.both, f32[32,8,8]{2,1,0:T(8,128)S(1)} %all_to_all.16.refs_0_), custom_call_target="tpu_custom_call" | custom-call | tf_op jit(solution)/shard_map/pallas_call | solution.py:254
  (1 shorter events, 0.0 us)
Async XLA Ops:
  0.6 0.7 %copy-start.1 = (f32[8,3,64]{2,0,1:T(8,128)S(1)}, f32[8,3,64]{2,0,1:T(8,128)}, u32[]{:S(2)}) copy-start(f32[8,3,64]{2,0,1:T(8,128)} %param.3) | copy-start | bytes 18436
  1.3 0.7 %copy-start.2 = (f32[3,64]{1,0:T(4,128)S(1)}, f32[3,64]{1,0:T(4,128)}, u32[]{:S(2)}) copy-start(f32[3,64]{1,0:T(4,128)} %positions.1) | copy-start | bytes 2308
  2.8 7.3 %copy-start.3 = (f32[3,64]{1,0:T(4,128)S(1)}, f32[3,64]{1,0:T(4,128)}, u32[]{:S(2)}) copy-start(f32[3,64]{1,0:T(4,128)} %positions.1) | copy-start | bytes 2308
  2.8 17.7 %all-to-all-start = ((f32[32,16,128]{2,1,0:T(8,128)}), f32[32,16,128]{2,1,0:T(8,128)S(1)}, u32[]{:S(2)}, u32[]{:S(2)}) async-start(f32[32,16,128]{2,1,0:T(8,128)} %broadcast_in_dim.6), calls=%async_computation | async-start | bytes 524288 | tf_op jit(solution)/shard_map/all_to_all | solution.py:231
  43.1 10.5 %copy-start = (f32[3,8,64]{2,1,0:T(8,128)S(1)}, f32[3,8,64]{2,1,0:T(8,128)}, u32[]{:S(2)}) copy-start(f32[3,8,64]{2,1,0:T(8,128)} %get-tuple-element.9.basis) | copy-start | bytes 18436

commit v3 on v0

v3 whole, which is shorter than its diff:
```python
import functools

import jax
import jax.numpy as jnp
from jax import lax
from jax.experimental import pallas as pl
from jax.experimental.pallas import tpu as pltpu
from jax.sharding import PartitionSpec as P

CHUNK = 2048
KEPT = 8 * 1024 * 1024
F32 = jnp.float32
BF16 = jnp.bfloat16


def pack_kernel(positions, noise, blocks, held_positions, held_noise, block, sems):
    one = pltpu.make_async_copy(positions, held_positions, sems.at[0])
    two = pltpu.make_async_copy(noise, held_noise, sems.at[1])
    one.start()
    two.start()
    beads = positions.shape[1]
    vecs = noise.shape[1]
    block[...] = jnp.zeros(block.shape, F32)
    one.wait()
    two.wait()
    block[:vecs, :beads] = held_noise[0]
    block[:vecs, beads:] = held_noise[1]
    block[vecs:, :beads] = held_noise[2]
    block[vecs : vecs + 3, beads:] = held_positions[...]
    blocks[...] = jnp.broadcast_to(block[...][None], blocks.shape)


def split_two(value):
    high = value.astype(BF16)
    return high, (value - high.astype(F32)).astype(BF16)


def matmul_nt(left, right, precision=None):
    return lax.dot_general(
        left, right, (((1,), (1,)), ((), ())), precision=precision, preferred_element_type=F32
    )


def small_matmul(left, right):
    total = left[:, 0:1] * right[0:1, :]
    for k in range(1, left.shape[1]):
        total = total + left[:, k : k + 1] * right[k : k + 1, :]
    return total


def unpack(blocks, wide, beads):
    for index in range(0, blocks.shape[0], 2):
        one, two = blocks[index], blocks[index + 1]
        half = one.shape[0] // 2
        lanes = pl.ds(index * beads, 2 * beads)
        for part in range(4):
            rows = slice(part // 2 * half, (part // 2 + 1) * half)
            side = slice(part % 2 * beads, (part % 2 + 1) * beads)
            wide[part * half : (part + 1) * half, lanes] = jnp.concatenate(
                [one[rows, side], two[rows, side]], axis=1
            )


def fill_tensor(own, wide, start, high, low):
    beads = own.shape[1] // 2
    step = 128
    targets = own[8:16, beads:].T
    columns = [jnp.broadcast_to(targets[:, axis : axis + 1], (beads, step)) for axis in range(3)]

    def body(index, carry):
        at = pl.multiple_of(start + index * step, step)
        to = pl.ds(pl.multiple_of(index * step, step), step)
        moved = [columns[axis] - wide[24 + axis : 25 + axis, pl.ds(at, step)] for axis in range(3)]
        square = moved[0] * moved[0] + moved[1] * moved[1] + moved[2] * moved[2]
        inverse = lax.rsqrt(jnp.maximum(square, 1e-12))
        inverse_sq = inverse * inverse
        far_iso = inverse * (0.75 + 0.5 * inverse_sq)
        far_dir = inverse * inverse_sq * (0.75 - 1.5 * inverse_sq)
        near_iso = 1.0 - (9.0 / 32.0) * (square * inverse)
        near_dir = (3.0 / 32.0) * inverse
        near = square < 4.0
        iso = jnp.where(near, near_iso, far_iso)
        along = jnp.where(near, near_dir, far_dir)
        scaled = [along * item for item in moved]
        parts = [
            iso + scaled[0] * moved[0],
            scaled[0] * moved[1],
            scaled[0] * moved[2],
            iso + scaled[1] * moved[1],
            scaled[1] * moved[2],
            iso + scaled[2] * moved[2],
        ]
        for part, value in enumerate(parts):
            upper, lower = split_two(value)
            high[part * beads : (part + 1) * beads, to] = upper
            low[part * beads : (part + 1) * beads, to] = lower
        return carry

    lax.fori_loop(0, high.shape[1] // step, body, 0)


def apply_tensor(wide, start, high, low):
    upper, lower = split_two(wide[:, pl.ds(start, high.shape[1])])
    both = jnp.concatenate([upper, lower], axis=0)
    first = matmul_nt(both, high[...])
    second = matmul_nt(upper, low[...])
    return first[:24] + first[32:56] + second[:24]


def assemble(products, image):
    beads = image.shape[1] // 2

    def part(row, component):
        return products[8 * row : 8 * row + 8, component * beads : (component + 1) * beads]

    image[...] = jnp.zeros(image.shape, F32)
    image[:8, :beads] = part(0, 0) + part(1, 1) + part(2, 2)
    image[:8, beads:] = part(0, 1) + part(1, 3) + part(2, 4)
    image[8:, :beads] = part(0, 2) + part(1, 4) + part(2, 5)


def flat(block):
    return jnp.concatenate([block[:8], block[8:]], axis=1)


def product(own, wide_from, wide, high, low, fill):
    chunk = high.shape[1]
    total = jnp.zeros((24, high.shape[0]), F32)
    for start in range(0, wide.shape[1], chunk):
        if fill:
            fill_tensor(own, wide_from, start, high, low)
        total = total + apply_tensor(wide, start, high, low)
    return total


def first_half_kernel(own_blocks, blocks, products, high, low, wide):
    own = own_blocks[0]
    unpack(blocks, wide, own.shape[1] // 2)
    products[...] = product(own, wide, wide, high, low, True)


def second_half_kernel(own_blocks, blocks, products, images, high, low, wide, image):
    own = own_blocks[0]
    unpack(blocks, wide, own.shape[1] // 2)
    assemble(products[...] + product(own, wide, wide, high, low, True), image)
    images[...] = jnp.broadcast_to(image[...][None], images.shape)


def cholesky(matrix):
    size = matrix.shape[0]
    shape = (size, size)
    rows = lax.broadcasted_iota(jnp.int32, shape, 0)
    cols = lax.broadcasted_iota(jnp.int32, shape, 1)
    entry = {}
    for j in range(size):
        column = jnp.broadcast_to(matrix[:, j : j + 1], shape)
        for i in range(j, size):
            entry[i, j] = jnp.broadcast_to(column[i : i + 1, :], shape)
    factor_t = jnp.zeros(shape, F32)
    inverse = jnp.zeros(shape, F32)
    inverse_rows = []
    for j in range(size):
        scale = lax.rsqrt(entry[j, j])
        lower_row = entry[j, j] * scale
        entry[j, j] = scale
        for i in range(j + 1, size):
            entry[i, j] = entry[i, j] * scale
        for i in range(j + 1, size):
            for k in range(j + 1, i + 1):
                entry[i, k] = entry[i, k] - entry[i, j] * entry[k, j]
        lower_row = jnp.where(cols == j, lower_row, 0.0)
        for i in range(j + 1, size):
            lower_row = jnp.where(cols == i, entry[i, j], lower_row)
        factor_t = jnp.where(rows == j, lower_row, factor_t)
        row = jnp.where(cols == j, 1.0, 0.0)
        for k in range(j):
            row = row - entry[j, k] * inverse_rows[k]
        row = row * scale
        inverse_rows.append(row)
        inverse = jnp.where(rows == j, row, inverse)
    return factor_t, inverse


def start_kernel(size, images, own_blocks, one_blocks, two_blocks, small, own_first, own_moved, one_first, two_first, wide):
    beads = own_blocks.shape[2] // 2
    gram = jnp.zeros((8, 8), F32)
    for blocks, first in ((one_blocks, one_first), (two_blocks, two_first)):
        unpack(blocks, wide, beads)
        first[...] = wide[:24]
        for part in range(3):
            rows = wide[8 * part : 8 * part + 8]
            gram = gram + matmul_nt(rows, rows, lax.Precision.HIGHEST)
    _, inverse = cholesky(gram / size)
    for first in (one_first, two_first):
        for part in range(3):
            rows = slice(8 * part, 8 * part + 8)
            first[rows] = small_matmul(inverse, first[rows])
    own_first[...] = small_matmul(inverse, flat(own_blocks[0]))
    own_moved[...] = small_matmul(inverse, flat(images[0]))
    small[0] = inverse
    small[1] = inverse.T


def inner(first, wide):
    total = jnp.zeros((16, 16), F32)
    for part in range(3):
        rows = slice(8 * part, 8 * part + 8)
        high, low = split_two(jnp.concatenate([first[rows], wide[rows]], axis=0))
        total = total + (matmul_nt(high, high) + (matmul_nt(high, low) + matmul_nt(low, high)))
    return total


def third_half_kernel(fill, own_blocks, blocks, images, first, high, low, products, gram, wide, *more):
    own = own_blocks[0]
    beads = own.shape[1] // 2
    unpack(images, wide, beads)
    if fill:
        unpack(blocks, more[0], beads)
    products[...] = product(own, more[0] if fill else None, wide, high, low, fill)
    gram[...] = inner(first, wide)


def fourth_half_kernel(
    size, fill, own_blocks, blocks, images, first, high, low, products, gram, own_images, own_first, own_moved, small,
    basis, shifted, coefficients, partials, wide, image, *more
):
    own = own_blocks[0]
    beads = own.shape[1] // 2
    unpack(images, wide, beads)
    if fill:
        unpack(blocks, more[0], beads)
    assemble(products[...] + product(own, more[0] if fill else None, wide, high, low, fill), image)
    twice = flat(image[...])
    both = (gram[...] + inner(first, wide)) / size
    cross_t, cross, squared = both[:8, 8:], both[8:, :8], both[8:, 8:]
    factor_t, inverse = cholesky(squared - small_matmul(cross, cross_t))
    start_inverse_t = small[1]
    alpha = small_matmul(cross_t, start_inverse_t)
    factor_one_t = small_matmul(factor_t, start_inverse_t)
    vectors = small_matmul(inverse, flat(own_images[0]) - small_matmul(cross, own_first[...]))
    moved = small_matmul(inverse, twice - small_matmul(cross, own_moved[...]))
    moved = moved - small_matmul(factor_one_t, own_first[...])
    valid = lax.broadcasted_iota(jnp.int32, vectors.shape, 1) < 3 * beads
    vectors = jnp.where(valid, vectors, 0.0)
    moved = jnp.where(valid, moved, 0.0)
    partial = matmul_nt(vectors, moved, lax.Precision.HIGHEST)
    for row in range(8):
        partials[:, :, 8 * row : 8 * row + 8] = jnp.broadcast_to(
            partial[row : row + 1][None], (partials.shape[0], 1, 8)
        )
    for part in range(3):
        basis[part] = vectors[:, part * beads : (part + 1) * beads]
    shifted[...] = moved
    coefficients[0] = alpha
    coefficients[1] = factor_one_t.T


def last_kernel(size, basis, shifted, both, one_partials, two_partials, residual, coefficients, alpha):
    beads = basis.shape[2]
    total = (jnp.sum(one_partials[...], axis=0) + jnp.sum(two_partials[...], axis=0)) / size
    for row in range(8):
        alpha[row : row + 1, :] = total[:, 8 * row : 8 * row + 8]
    alpha_t = alpha[...].T
    coefficients[0:2] = both[...]
    coefficients[2] = alpha[...]
    for part in range(3):
        residual[part] = shifted[:, part * beads : (part + 1) * beads] - small_matmul(alpha_t, basis[part])


def array(*shape, dtype=F32):
    return jax.ShapeDtypeStruct(shape, dtype)


def call(kernel, outs, scratch=(), **options):
    return pl.pallas_call(
        kernel,
        out_shape=outs,
        scratch_shapes=list(scratch),
        compiler_params=pltpu.CompilerParams(vmem_limit_bytes=48 * 1024 * 1024),
        **options,
    )


def gather(copies):
    rows, cols = lax.axis_size("row"), lax.axis_size("col")
    groups = [
        [row * cols + col for row in range(rows) for col in range(core, cols, 2)] for core in range(2)
    ]
    mine = lax.all_to_all(copies, ("row", "col"), 0, 0, axis_index_groups=groups, tiled=True)
    other = lax.ppermute(mine, "col", [(col, col ^ 1) for col in range(cols)])
    return mine, other


def local(positions, noise):
    vecs, _, beads = noise.shape
    chips = lax.axis_size("row") * lax.axis_size("col") // 2
    half = beads * chips
    size = 3.0 * 2.0 * half
    keep = 2 * 2 * 2 * 6 * beads * half <= KEPT
    width = half if keep else min(half, CHUNK)
    blocks = array(chips, 2 * vecs, 2 * beads)
    wide = pltpu.VMEM((4 * vecs, half), F32)
    block = pltpu.VMEM((2 * vecs, 2 * beads), F32)
    products = array(3 * vecs, 6 * beads)
    tensors = [array(6 * beads, width, dtype=BF16)] * 2 if keep else []
    held = [] if keep else [pltpu.VMEM((6 * beads, width), BF16)] * 2
    flat_block = array(vecs, 4 * beads)

    own = call(
        pack_kernel,
        blocks,
        [pltpu.VMEM(positions.shape, F32), pltpu.VMEM((3, vecs, beads), F32), block, pltpu.SemaphoreType.DMA((2,))],
        in_specs=[pl.BlockSpec(memory_space=pltpu.HBM)] * 2,
    )(positions, noise.transpose(1, 0, 2))
    one, two = gather(own)
    one_products, *one_tensor = call(first_half_kernel, [products] + tensors, held + [wide])(own, one)
    own_images, *two_tensor = call(second_half_kernel, [blocks] + tensors, held + [wide, block])(
        own, two, one_products
    )
    one_images, two_images = gather(own_images)
    small, own_first, own_moved, one_first, two_first = call(
        functools.partial(start_kernel, size),
        [array(2, vecs, vecs), flat_block, flat_block, array(3 * vecs, half), array(3 * vecs, half)],
        [wide],
    )(own_images, own, one, two)
    fill = not keep

    one_products, gram = call(
        first_of_two(fill), [products, array(2 * vecs, 2 * vecs)], held + [wide] + [wide] * fill
    )(own, one, one_images, one_first, *one_tensor)
    basis, shifted, both, partials = call(
        second_of_two(size, fill),
        [array(3, vecs, beads), flat_block, array(2, vecs, vecs), array(chips, 1, vecs * vecs)],
        held + [wide, block] + [wide] * fill,
    )(own, two, two_images, two_first, *two_tensor, one_products, gram, own_images, own_first, own_moved, small)
    one_partials, two_partials = gather(partials)
    residual, coefficients = call(
        functools.partial(last_kernel, size),
        [array(3, vecs, beads), array(3, vecs, vecs)],
        [pltpu.VMEM((vecs, vecs), F32)],
    )(basis, shifted, both, one_partials, two_partials)
    return (basis.transpose(1, 0, 2), residual.transpose(1, 0, 2), coefficients)


def first_of_two(fill):
    if not fill:
        return functools.partial(third_half_kernel, False)

    def kernel(own, blocks, images, first, products, gram, high, low, wide, more):
        third_half_kernel(True, own, blocks, images, first, high, low, products, gram, wide, more)

    return kernel


def second_of_two(size, fill):
    if not fill:
        return functools.partial(fourth_half_kernel, size, False)

    def kernel(own, blocks, images, first, products, gram, own_images, own_first, own_moved, small, *rest):
        outs, (high, low, wide, image, more) = rest[:4], rest[4:]
        fourth_half_kernel(
            size, True, own, blocks, images, first, high, low, products, gram, own_images, own_first, own_moved,
            small, *outs, wide, image, more
        )

    return kernel


def solution(mesh):
    return jax.shard_map(
        local,
        mesh=mesh,
        in_specs=(P(None, ("row", "col")), P(None, None, ("row", "col"))),
        out_specs=(P(None, None, ("row", "col")), P(None, None, ("row", "col")), P()),
        check_vma=False,
    )
```

time: 228 us -> 48.6 us (0.21)
  blocking collectives: 204 us -> 37.1 us
  matrix products: 11.9 us -> 0 us
  other arithmetic: 8.47 us -> 0 us
  Pallas kernels: 0 us -> 7.89 us
    psum x5 -> x0, blocking collectives: 149 us -> none  [the longest x1 42 us: local(): lax.psum(local_gram(noise, noise), ('row', 'col')) / total_count]
    all_gather x4 -> x0, blocking collectives: 54.8 us -> none  [the longest x2 33.2 us: mobility(): source_piece = lax.all_gather(vectors, 'col', axis=2, tiled=True)]
    all_to_all x0 -> x3, blocking collectives: none -> 37.1 us  [gather(): lax.all_to_all(copies, ('row', 'col'), 0, 0, axis_index_groups=groups, ti...]
    dot_general x14 -> x0, matrix products: 11.5 us -> none  [the longest x4 8.65 us: add_block(): jnp.einsum('abts,kbs->kat', tensor, block_vectors, precision=lax.Precisio...]
    pallas_call x0 -> x7, Pallas kernels: none -> 7.89 us  [the longest x1 1.98 us: local(): call(second_of_two(size, fill), [array(3, vecs, beads), flat_block, array...]
    another operation x11 -> x0, other arithmetic: 5.95 us -> none  [the longest x3 1.9 us: lower_inverse(): jax.scipy.linalg.solve_triangular(factor, jnp.eye(factor.shape[0], dtype=...]
  transfers between devices with their start and end apart: 0 -> 3, of which waited for: 0 -> 1; matrix products, arithmetic and copies ran while one was open for 0% -> 0% of each run, Pallas kernels for 0% -> 7%
where the time goes in v3:
time: 48.6 us; the launch traced here: 48.3 us
  blocking collectives  37.1 us (76%)
  Pallas kernels  7.89 us (16%)
  local copies, waits for them, and re-layouts  1.38 us (3%)
  waiting for transfers between devices  1.19 us (2%)
  between operations  0.68 us (1%)
    all_to_all x3, blocking collectives, gather(): lax.all_to_all(copies, ('row', 'col'), 0, 0, axis_index_groups=groups, ti...  37.1 us
    pallas_call x1, Pallas kernels, local(): call(second_of_two(size, fill), [array(3, vecs, beads), flat_block, array...  1.98 us
    pallas_call x1, Pallas kernels, local(): call(second_half_kernel, [blocks] + tensors, held + [wide, block])  1.62 us
    pallas_call x1, Pallas kernels, local(): call(first_half_kernel, [products] + tensors, held + [wide])(own, one)  1.45 us
    unnamed x6, local copies, waits for them, and re-layouts  1.38 us
    ppermute x3, waiting for transfers between devices, gather(): other = lax.ppermute(mine, 'col', [(col, col ^ 1) for col in range(cols)])  1.19 us
    pallas_call x1, Pallas kernels, local(): call(functools.partial(start_kernel, size), [array(2, vecs, vecs), flat_b...  1.03 us
    pallas_call x1, Pallas kernels, local(): call(functools.partial(last_kernel, size), [array(3, vecs, beads), array(...  0.99 us
  transfers between devices with their start and end apart: 3, of which 1 were waited for; matrix products, arithmetic and copies ran while one was open for 0% of the time, Pallas kernels for 7%

profile of v3, /device:TPU:0, one launch (start us, length us, event | category | flops | bytes accessed | tf_op | source)
XLA Modules:
  0.0 48.3 jit_solution(15551416411157870317)
XLA Ops:
  0.6 0.0 copy-start
  0.6 0.7 %copy-done = f32[8,3,64]{2,0,1:T(8,128)S(1)} copy-done((f32[8,3,64]{2,0,1:T(8,128)S(1)}, f32[8,3,64]{2,0,1:T(8,128)}, u32[]{:S(2)}) %copy-start) | copy-done | bytes 6168
  1.3 0.0 copy-start.2
  1.3 0.7 %copy-done.2 = f32[3,64]{1,0:T(4,128)S(1)} copy-done((f32[3,64]{1,0:T(4,128)S(1)}, f32[3,64]{1,0:T(4,128)}, u32[]{:S(2)}) %copy-start.2) | copy-done | bytes 792
  2.0 0.1 shard_map.49.own_blocks
  2.1 15.8 %all_to_all.15.blocks.one_blocks = f32[16,16,128]{2,1,0:T(8,128)S(1)} all-to-all(f32[16,16,128]{2,1,0:T(8,128)S(1)} %shard_map.49.own_blocks), channel_id=1, replica_groups={{0,2,4,6,8,10,12,14,16,18,20,22,24,26,28,30},{1,3,5,7,9,11,13,15,17,19,..., dimensions={0} | all-to-all | bytes 262144 | tf_op jit(solution)/shard_map/all_to_all | solution.py:289
  17.9 0.0 collective-permute-start
  18.0 1.4 %shard_map.50 = (f32[24,384]{1,0:T(8,128)S(1)}, bf16[384,1024]{1,0:T(8,128)(2,1)S(1)}, bf16[384,1024]{1,0:T(8,128)(2,1)S(1)}) custom-call(f32[16,16,128]{2,1,0:T(8,128)S(1)} %shard_map.49.own_blocks, f32[16,16,128]{2,1,0:T(8,128)S(1)} %all_to_all.15.blocks.one_blocks), custom_call_target="tpu_custom_call" | custom-call | tf_op jit(solution)/shard_map/pallas_call | solution.py:316
  19.4 0.0 collective-permute-done.blocks.two_blocks
  19.4 1.6 %shard_map.51 = (f32[16,16,128]{2,1,0:T(8,128)S(1)}, bf16[384,1024]{1,0:T(8,128)(2,1)S(1)}, bf16[384,1024]{1,0:T(8,128)(2,1)S(1)}) custom-call(f32[16,16,128]{2,1,0:T(8,128)S(1)} %shard_map.49.own_blocks, f32[16,16,128]{2,1,0:T(8,128)S(1)} %collective-permute-done.blocks.two_blocks, f32[24,384]{1,0:T(8,128)S(1)} %get-tuple-element.22.products), custom_call_target="tpu_custom_call" | custom-call | tf_op jit(solution)/shard_map/pallas_call | solution.py:317
  21.1 11.0 %all_to_all.16.images = f32[16,16,128]{2,1,0:T(8,128)S(1)} all-to-all(f32[16,16,128]{2,1,0:T(8,128)S(1)} %get-tuple-element.23.images.own_images), channel_id=1, replica_groups={{0,2,4,6,8,10,12,14,16,18,20,22,24,26,28,30},{1,3,5,7,9,11,13,15,17,19,..., dimensions={0} | all-to-all | bytes 262144 | tf_op jit(solution)/shard_map/all_to_all | solution.py:289
  32.1 0.0 collective-permute-start.1
  32.1 1.0 %shard_map.52 = (f32[2,8,8]{2,1,0:T(8,128)S(1)}, f32[8,256]{1,0:T(8,128)S(1)}, f32[8,256]{1,0:T(8,128)S(1)}, f32[24,1024]{1,0:T(8,128)S(1)}, f32[24,1024]{1,0:T(8,128)S(1)}) custom-call(f32[16,16,128]{2,1,0:T(8,128)S(1)} %get-tuple-element.23.images.own_images, f32[16,16,128]{2,1,0:T(8,128)S(1)} %shard_map.49.own_blocks, ...), custom_call_target="tpu_custom_call" | custom-call | tf_op jit(solution)/shard_map/pallas_call | solution.py:321
  33.1 0.7 %shard_map.53 = (f32[24,384]{1,0:T(8,128)S(1)}, f32[16,16]{1,0:T(8,128)S(1)}) custom-call(f32[16,16,128]{2,1,0:T(8,128)S(1)} %shard_map.49.own_blocks, f32[16,16,128]{2,1,0:T(8,128)S(1)} %all_to_all.15.blocks.one_blocks, f32[16,16,128]{2,1,0:T(8,128)S(1)} %all_to_all.16.images, f32[24,1024]{1,0:T(8,128)S(1)} %get-tuple-element.27.first, ...), custom_call_target="tpu_custom_call" | custom-call | tf_op jit(solution)/shard_map/pallas_call | solution.py:328
  33.8 0.0 collective-permute-done.1.images
  33.8 2.0 %shard_map.54 = (f32[3,8,64]{2,1,0:T(8,128)}, f32[8,256]{1,0:T(8,128)S(1)}, f32[2,8,8]{2,1,0:T(8,128)S(1)}, f32[16,1,64]{2,1,0:T(1,128)S(1)}) custom-call(f32[16,16,128]{2,1,0:T(8,128)S(1)} %shard_map.49.own_blocks, f32[16,16,128]{2,1,0:T(8,128)S(1)} %collective-permute-done.blocks.two_blocks, f32[16,16,128]{2,1,0:T(8,128)S(1)} %collective-permute-done.1.images, ...), custom_call_target="tpu_custom_call" | custom-call | tf_op jit(solution)/shard_map/pallas_call | solution.py:331
  35.8 0.0 copy-start.1
  35.8 10.3 %all_to_all.17.one_partials = f32[16,1,64]{2,1,0:T(1,128)S(1)} all-to-all(f32[16,1,64]{2,1,0:T(1,128)S(1)} %get-tuple-element.38), channel_id=1, replica_groups={{0,2,4,6,8,10,12,14,16,18,20,22,24,26,28,30},{1,3,5,7,9,11,13,15,17,19,..., dimensions={0} | all-to-all | bytes 8192 | tf_op jit(solution)/shard_map/all_to_all | solution.py:289
  46.1 0.0 collective-permute-start.2
  46.1 1.2 %collective-permute-done.2.two_partials = f32[16,1,64]{2,1,0:T(1,128)S(1)} collective-permute-done((f32[16,1,64]{2,1,0:T(1,128)S(1)}, f32[16,1,64]{2,1,0:T(1,128)S(1)}, u32[]{:S(2)}, u32[]{:S(2)}) %collective-permute-start.2) | collective-permute-done | bytes 4128 | tf_op jit(solution)/shard_map/ppermute | solution.py:290
  47.3 0.0 copy-done.1
  47.3 1.0 %shard_map.55 = (f32[3,8,64]{2,1,0:T(8,128)}, f32[3,8,8]{2,1,0:T(8,128)}) custom-call(f32[3,8,64]{2,1,0:T(8,128)S(1)} %copy-done.1, f32[8,256]{1,0:T(8,128)S(1)} %get-tuple-element.36.shifted, f32[2,8,8]{2,1,0:T(8,128)S(1)} %get-tuple-element.37.both, f32[16,1,64]{2,1,0:T(1,128)S(1)} %all_to_all.17.one_partials, ...), custom_call_target="tpu_custom_call" | custom-call | tf_op jit(solution)/shard_map/pallas_call | solution.py:337
Async XLA Ops:
  0.6 0.7 %copy-start = (f32[8,3,64]{2,0,1:T(8,128)S(1)}, f32[8,3,64]{2,0,1:T(8,128)}, u32[]{:S(2)}) copy-start(f32[8,3,64]{2,0,1:T(8,128)} %param.3) | copy-start | bytes 18436
  1.3 0.7 %copy-start.2 = (f32[3,64]{1,0:T(4,128)S(1)}, f32[3,64]{1,0:T(4,128)}, u32[]{:S(2)}) copy-start(f32[3,64]{1,0:T(4,128)} %positions.1) | copy-start | bytes 2308
  17.9 1.5 %collective-permute-start = (f32[16,16,128]{2,1,0:T(8,128)S(1)}, f32[16,16,128]{2,1,0:T(8,128)S(1)}, u32[]{:S(2)}, u32[]{:S(2)}) collective-permute-start(f32[16,16,128]{2,1,0:T(8,128)S(1)} %all_to_all.15.blocks.one_blocks), channel_id=1, source_target_pairs={{0,1},{1,0},{2,3},{3,2},{4,5},{5,4},{6,7},{7,6},{8,9},{9,8},{10,11... | collective-permute-start | bytes 393224 | tf_op jit(solution)/shard_map/ppermute | solution.py:290
  32.1 1.7 %collective-permute-start.1 = (f32[16,16,128]{2,1,0:T(8,128)S(1)}, f32[16,16,128]{2,1,0:T(8,128)S(1)}, u32[]{:S(2)}, u32[]{:S(2)}) collective-permute-start(f32[16,16,128]{2,1,0:T(8,128)S(1)} %all_to_all.16.images), channel_id=1, source_target_pairs={{0,1},{1,0},{2,3},{3,2},{4,5},{5,4},{6,7},{7,6},{8,9},{9,8},{10,11... | collective-permute-start | bytes 393224 | tf_op jit(solution)/shard_map/ppermute | solution.py:290
  35.8 11.4 %copy-start.1 = (f32[3,8,64]{2,1,0:T(8,128)S(1)}, f32[3,8,64]{2,1,0:T(8,128)}, u32[]{:S(2)}) copy-start(f32[3,8,64]{2,1,0:T(8,128)} %get-tuple-element.35.basis) | copy-start | bytes 18436
  46.1 1.2 %collective-permute-start.2 = (f32[16,1,64]{2,1,0:T(1,128)S(1)}, f32[16,1,64]{2,1,0:T(1,128)S(1)}, u32[]{:S(2)}, u32[]{:S(2)}) collective-permute-start(f32[16,1,64]{2,1,0:T(1,128)S(1)} %all_to_all.17.one_partials), channel_id=1, source_target_pairs={{0,1},{1,0},{2,3},{3,2},{4,5},{5,4},{6,7},{7,6},{8,9},{9,8},{10,11... | collective-permute-start | bytes 12296 | tf_op jit(solution)/shard_map/ppermute | solution.py:290

commit v4 on v3

--- a/solution.py
+++ b/solution.py
@@ -283,10 +283,10 @@
 
 def gather(copies):
     rows, cols = lax.axis_size("row"), lax.axis_size("col")
-    groups = [
-        [row * cols + col for row in range(rows) for col in range(core, cols, 2)] for core in range(2)
-    ]
-    mine = lax.all_to_all(copies, ("row", "col"), 0, 0, axis_index_groups=groups, tiled=True)
+    groups = [list(range(core, cols, 2)) for core in range(2)]
+    line = lax.all_to_all(copies, "col", 0, 0, axis_index_groups=groups, tiled=True)
+    mine = lax.all_to_all(jnp.broadcast_to(line[None], (rows,) + line.shape), "row", 0, 0, tiled=True)
+    mine = mine.reshape((-1,) + copies.shape[1:])
     other = lax.ppermute(mine, "col", [(col, col ^ 1) for col in range(cols)])
     return mine, other
 
@@ -298,7 +298,8 @@
     size = 3.0 * 2.0 * half
     keep = 2 * 2 * 2 * 6 * beads * half <= KEPT
     width = half if keep else min(half, CHUNK)
-    blocks = array(chips, 2 * vecs, 2 * beads)
+    layers = lax.axis_size("col") // 2
+    blocks = array(layers, 2 * vecs, 2 * beads)
     wide = pltpu.VMEM((4 * vecs, half), F32)
     block = pltpu.VMEM((2 * vecs, 2 * beads), F32)
     products = array(3 * vecs, 6 * beads)
@@ -330,7 +331,7 @@
     )(own, one, one_images, one_first, *one_tensor)
     basis, shifted, both, partials = call(
         second_of_two(size, fill),
-        [array(3, vecs, beads), flat_block, array(2, vecs, vecs), array(chips, 1, vecs * vecs)],
+        [array(3, vecs, beads), flat_block, array(2, vecs, vecs), array(layers, 1, vecs * vecs)],
         held + [wide, block] + [wide] * fill,
     )(own, two, two_images, two_first, *two_tensor, one_products, gram, own_images, own_first, own_moved, small)
     one_partials, two_partials = gather(partials)

time: 48.6 us -> 63.5 us (1.31)
  blocking collectives: 37.1 us -> 50.6 us
  local copies, waits for them, and re-layouts: 1.38 us -> 2.09 us
  other arithmetic: 0 us -> 0.66 us
    all_to_all x3 -> x6, blocking collectives: 37.1 us -> 50.6 us  [the longest x3 27.7 us: gather(): lax.all_to_all(copies, 'col', 0, 0, axis_index_groups=groups, tiled=True)]
    all_to_all x0 -> x1, other arithmetic: none -> 0.66 us  [gather(): lax.all_to_all(jnp.broadcast_to(line[None], (rows,) + line.shape), 'row',...]
    unnamed x6 -> x9, local copies, waits for them, and re-layouts: 1.38 us -> 1.56 us
  transfers between devices with their start and end apart: 3 -> 3, of which waited for: 1 -> 1; matrix products, arithmetic and copies ran while one was open for 0% -> 0% of each run, Pallas kernels for 7% -> 5%
where the time goes in v4:
time: 63.5 us; the launch traced here: 63.1 us
  blocking collectives  50.6 us (80%)
  Pallas kernels  7.83 us (12%)
  local copies, waits for them, and re-layouts  2.09 us (3%)
  waiting for transfers between devices  1.18 us (2%)
  between operations  0.7 us (1%)
  other arithmetic  0.66 us (1%)
    all_to_all x3, blocking collectives, gather(): lax.all_to_all(copies, 'col', 0, 0, axis_index_groups=groups, tiled=True)  27.7 us
    all_to_all x3, blocking collectives, gather(): lax.all_to_all(jnp.broadcast_to(line[None], (rows,) + line.shape), 'row',...  22.9 us
    pallas_call x1, Pallas kernels, local(): call(second_of_two(size, fill), [array(3, vecs, beads), flat_block, array...  1.96 us
    pallas_call x1, Pallas kernels, local(): call(second_half_kernel, [blocks] + tensors, held + [wide, block])  1.6 us
    unnamed x9, local copies, waits for them, and re-layouts  1.56 us
    pallas_call x1, Pallas kernels, local(): call(first_half_kernel, [products] + tensors, held + [wide])(own, one)  1.45 us
  transfers between devices with their start and end apart: 3, of which 1 were waited for; matrix products, arithmetic and copies ran while one was open for 0% of the time, Pallas kernels for 5%

profile of v4, /device:TPU:0, one launch (start us, length us, event | category | flops | bytes accessed | tf_op | source)
XLA Modules:
  0.0 63.1 jit_solution(6165511859289905278)
XLA Ops:
  0.6 0.0 copy-start
  0.6 0.7 %copy-done = f32[8,3,64]{2,0,1:T(8,128)S(1)} copy-done((f32[8,3,64]{2,0,1:T(8,128)S(1)}, f32[8,3,64]{2,0,1:T(8,128)}, u32[]{:S(2)}) %copy-start) | copy-done | bytes 6168
  1.3 0.0 copy-start.2
  1.3 0.7 %copy-done.2 = f32[3,64]{1,0:T(4,128)S(1)} copy-done((f32[3,64]{1,0:T(4,128)S(1)}, f32[3,64]{1,0:T(4,128)}, u32[]{:S(2)}) %copy-start.2) | copy-done | bytes 792
  2.0 0.1 shard_map.49.own_blocks
  2.1 11.8 %all_to_all.30 = f32[4,16,128]{2,1,0:T(8,128)S(1)} all-to-all(f32[4,16,128]{2,1,0:T(8,128)S(1)} %shard_map.49.own_blocks), channel_id=1, replica_groups={{0,2,4,6},{1,3,5,7},{8,10,12,14},{9,11,13,15},{16,18,20,22},{17,19,21,2..., dimensions={0} | all-to-all | bytes 65536 | tf_op jit(solution)/shard_map/all_to_all | solution.py:287
  13.9 8.5 %all_to_all.31 = f32[4,4,16,128]{3,2,1,0:T(8,128)S(1)} all-to-all(f32[4,4,16,128]{3,2,1,0:T(8,128)S(1)} %broadcast_in_dim.8), channel_id=1, replica_groups=mesh['row'=4,'col'=8] {'row'}, dimensions={0} | all-to-all | bytes 262144 | tf_op jit(solution)/shard_map/all_to_all | solution.py:288
  22.5 0.0 collective-permute-start
  22.5 1.5 %shard_map.50 = (f32[24,384]{1,0:T(8,128)S(1)}, bf16[384,1024]{1,0:T(8,128)(2,1)S(1)}, bf16[384,1024]{1,0:T(8,128)(2,1)S(1)}) custom-call(f32[4,16,128]{2,1,0:T(8,128)S(1)} %shard_map.49.own_blocks, f32[16,16,128]{2,1,0:T(8,128)S(1)} %bitcast.11), custom_call_target="tpu_custom_call" | custom-call | tf_op jit(solution)/shard_map/pallas_call | solution.py:317
  23.9 0.0 collective-permute-done.blocks.two_blocks
  23.9 1.6 %shard_map.51 = (f32[4,16,128]{2,1,0:T(8,128)S(1)}, bf16[384,1024]{1,0:T(8,128)(2,1)S(1)}, bf16[384,1024]{1,0:T(8,128)(2,1)S(1)}) custom-call(f32[4,16,128]{2,1,0:T(8,128)S(1)} %shard_map.49.own_blocks, f32[16,16,128]{2,1,0:T(8,128)S(1)} %collective-permute-done.blocks.two_blocks, f32[24,384]{1,0:T(8,128)S(1)} %get-tuple-element.22.products), custom_call_target="tpu_custom_call" | custom-call | tf_op jit(solution)/shard_map/pallas_call | solution.py:318
  25.5 8.0 %all_to_all.32 = f32[4,16,128]{2,1,0:T(8,128)S(1)} all-to-all(f32[4,16,128]{2,1,0:T(8,128)S(1)} %get-tuple-element.23.images.own_images), channel_id=1, replica_groups={{0,2,4,6},{1,3,5,7},{8,10,12,14},{9,11,13,15},{16,18,20,22},{17,19,21,2..., dimensions={0} | all-to-all | bytes 65536 | tf_op jit(solution)/shard_map/all_to_all | solution.py:287
  33.6 7.4 %all_to_all.33 = f32[4,4,16,128]{3,2,1,0:T(8,128)S(1)} all-to-all(f32[4,4,16,128]{3,2,1,0:T(8,128)S(1)} %broadcast_in_dim.9), channel_id=1, replica_groups=mesh['row'=4,'col'=8] {'row'}, dimensions={0} | all-to-all | bytes 262144 | tf_op jit(solution)/shard_map/all_to_all | solution.py:288
  41.0 0.0 collective-permute-start.1
  41.0 1.0 %shard_map.52 = (f32[2,8,8]{2,1,0:T(8,128)S(1)}, f32[8,256]{1,0:T(8,128)S(1)}, f32[8,256]{1,0:T(8,128)S(1)}, f32[24,1024]{1,0:T(8,128)S(1)}, f32[24,1024]{1,0:T(8,128)S(1)}) custom-call(f32[4,16,128]{2,1,0:T(8,128)S(1)} %get-tuple-element.23.images.own_images, f32[4,16,128]{2,1,0:T(8,128)S(1)} %shard_map.49.own_blocks, f32[16,16,128]{2,1,0:T(8,128)S(1)} %bitcast.12, ...), custom_call_target="tpu_custom_call" | custom-call | tf_op jit(solution)/shard_map/pallas_call | solution.py:322
  42.0 0.7 %shard_map.53 = (f32[24,384]{1,0:T(8,128)S(1)}, f32[16,16]{1,0:T(8,128)S(1)}) custom-call(f32[4,16,128]{2,1,0:T(8,128)S(1)} %shard_map.49.own_blocks, f32[16,16,128]{2,1,0:T(8,128)S(1)} %bitcast.13, f32[16,16,128]{2,1,0:T(8,128)S(1)} %bitcast.15, f32[24,1024]{1,0:T(8,128)S(1)} %get-tuple-element.27.first, bf16[384,1024]{1,0:T(8,128)(2,1)S(1)} %get-tuple-element.28.high, ...), custom_call_target="tpu_custom_call" | custom-call | tf_op jit(solution)/shard_map/pallas_call | solution.py:329
  42.7 0.0 collective-permute-done.1.images
  42.7 2.0 %shard_map.54 = (f32[3,8,64]{2,1,0:T(8,128)}, f32[8,256]{1,0:T(8,128)S(1)}, f32[2,8,8]{2,1,0:T(8,128)S(1)}, f32[4,1,64]{2,1,0:T(1,128)S(1)}) custom-call(f32[4,16,128]{2,1,0:T(8,128)S(1)} %shard_map.49.own_blocks, f32[16,16,128]{2,1,0:T(8,128)S(1)} %collective-permute-done.blocks.two_blocks, f32[16,16,128]{2,1,0:T(8,128)S(1)} %collective-permute-done.1.images, ...), custom_call_target="tpu_custom_call" | custom-call | tf_op jit(solution)/shard_map/pallas_call | solution.py:332
  44.7 7.9 %all_to_all.34 = f32[4,1,64]{2,1,0:T(1,128)S(1)} all-to-all(f32[4,1,64]{2,1,0:T(1,128)S(1)} %get-tuple-element.38), channel_id=1, replica_groups={{0,2,4,6},{1,3,5,7},{8,10,12,14},{9,11,13,15},{16,18,20,22},{17,19,21,2..., dimensions={0} | all-to-all | bytes 2048 | tf_op jit(solution)/shard_map/all_to_all | solution.py:287
  52.6 0.1 reshape.23
  52.7 7.0 %all_to_all.35 = f32[4,1,256]{2,1,0:T(1,128)S(1)} all-to-all(f32[4,1,256]{2,1,0:T(1,128)S(1)} %reshape.23), channel_id=1, replica_groups=mesh['row'=4,'col'=8] {'row'}, dimensions={0} | all-to-all | bytes 8192 | tf_op jit(solution)/shard_map/all_to_all | solution.py:288
  59.7 0.5 broadcast.3
  60.2 0.7 %reduce = f32[4,256]{1,0:T(4,128)S(1)} reduce(f32[4,1,256]{2,1,0:T(1,128)S(1)} %all_to_all.35, f32[]{:T(128)} %broadcast.3), dimensions={1}, to_apply=%all_to_all.23.reduce_sub_computation | reduce | bytes 8196 | tf_op jit(solution)/shard_map/all_to_all | solution.py:288
  60.8 0.0 copy-start.1
  60.9 0.1 reshape.24
  60.9 0.0 collective-permute-start.2
  61.0 1.2 %collective-permute-done.2.two_partials = f32[16,1,64]{2,1,0:T(1,128)S(1)} collective-permute-done((f32[16,1,64]{2,1,0:T(1,128)S(1)}, f32[16,1,64]{2,1,0:T(1,128)S(1)}, u32[]{:S(2)}, u32[]{:S(2)}) %collective-permute-start.2) | collective-permute-done | bytes 4128 | tf_op jit(solution)/shard_map/ppermute | solution.py:290
  62.1 0.0 copy-done.1
  62.1 1.0 %shard_map.55 = (f32[3,8,64]{2,1,0:T(8,128)}, f32[3,8,8]{2,1,0:T(8,128)}) custom-call(f32[3,8,64]{2,1,0:T(8,128)S(1)} %copy-done.1, f32[8,256]{1,0:T(8,128)S(1)} %get-tuple-element.36.shifted, f32[2,8,8]{2,1,0:T(8,128)S(1)} %get-tuple-element.37.both, f32[16,1,64]{2,1,0:T(1,128)S(1)} %bitcast.17, f32[16,1,64]{2,1,0:T(1,128)S(1)} %collective-permute-done.2.two_partials), custom_call_target="tpu_custom_call" | custom-call | tf_op jit(solution)/shard_map/pallas_call | solution.py:338
  (3 shorter events, 0.0 us)
Async XLA Ops:
  0.6 0.7 %copy-start = (f32[8,3,64]{2,0,1:T(8,128)S(1)}, f32[8,3,64]{2,0,1:T(8,128)}, u32[]{:S(2)}) copy-start(f32[8,3,64]{2,0,1:T(8,128)} %param.3) | copy-start | bytes 18436
  1.3 0.7 %copy-start.2 = (f32[3,64]{1,0:T(4,128)S(1)}, f32[3,64]{1,0:T(4,128)}, u32[]{:S(2)}) copy-start(f32[3,64]{1,0:T(4,128)} %positions.1) | copy-start | bytes 2308
  22.5 1.5 %collective-permute-start = (f32[16,16,128]{2,1,0:T(8,128)S(1)}, f32[16,16,128]{2,1,0:T(8,128)S(1)}, u32[]{:S(2)}, u32[]{:S(2)}) collective-permute-start(f32[16,16,128]{2,1,0:T(8,128)S(1)} %bitcast.10), channel_id=1, source_target_pairs={{0,1},{1,0},{2,3},{3,2},{4,5},{5,4},{6,7},{7,6},{8,9},{9,8},{10,11... | collective-permute-start | bytes 393224 | tf_op jit(solution)/shard_map/ppermute | solution.py:290
  41.0 1.7 %collective-permute-start.1 = (f32[16,16,128]{2,1,0:T(8,128)S(1)}, f32[16,16,128]{2,1,0:T(8,128)S(1)}, u32[]{:S(2)}, u32[]{:S(2)}) collective-permute-start(f32[16,16,128]{2,1,0:T(8,128)S(1)} %bitcast.14), channel_id=1, source_target_pairs={{0,1},{1,0},{2,3},{3,2},{4,5},{5,4},{6,7},{7,6},{8,9},{9,8},{10,11... | collective-permute-start | bytes 393224 | tf_op jit(solution)/shard_map/ppermute | solution.py:290
  60.8 1.3 %copy-start.1 = (f32[3,8,64]{2,1,0:T(8,128)S(1)}, f32[3,8,64]{2,1,0:T(8,128)}, u32[]{:S(2)}) copy-start(f32[3,8,64]{2,1,0:T(8,128)} %get-tuple-element.35.basis) | copy-start | bytes 18436
  60.9 1.2 %collective-permute-start.2 = (f32[16,1,64]{2,1,0:T(1,128)S(1)}, f32[16,1,64]{2,1,0:T(1,128)S(1)}, u32[]{:S(2)}, u32[]{:S(2)}) collective-permute-start(f32[16,1,64]{2,1,0:T(1,128)S(1)} %bitcast.16), channel_id=1, source_target_pairs={{0,1},{1,0},{2,3},{3,2},{4,5},{5,4},{6,7},{7,6},{8,9},{9,8},{10,11... | collective-permute-start | bytes 12296 | tf_op jit(solution)/shard_map/ppermute | solution.py:290

commit v5 on v3

v5 whole, which is shorter than its diff:
```python
import functools

import jax
import jax.numpy as jnp
from jax import lax
from jax.experimental import pallas as pl
from jax.experimental.pallas import tpu as pltpu
from jax.sharding import PartitionSpec as P

CHUNK = 2048
KEPT = 8 * 1024 * 1024
F32 = jnp.float32
BF16 = jnp.bfloat16


def pack_kernel(rows, blocks):
    beads = rows.shape[1]
    vecs = blocks.shape[1] // 2
    upper = jnp.concatenate([rows[:vecs], rows[vecs : 2 * vecs]], axis=1)
    lower = jnp.concatenate([rows[2 * vecs : 3 * vecs], rows[3 * vecs :]], axis=1)
    blocks[:, :vecs] = jnp.broadcast_to(upper[None], (blocks.shape[0], vecs, 2 * beads))
    blocks[:, vecs:] = jnp.broadcast_to(lower[None], (blocks.shape[0], vecs, 2 * beads))


def split_two(value):
    high = value.astype(BF16)
    return high, (value - high.astype(F32)).astype(BF16)


def matmul_nt(left, right, precision=None):
    return lax.dot_general(
        left, right, (((1,), (1,)), ((), ())), precision=precision, preferred_element_type=F32
    )


def small_matmul(left, right):
    total = left[:, 0:1] * right[0:1, :]
    for k in range(1, left.shape[1]):
        total = total + left[:, k : k + 1] * right[k : k + 1, :]
    return total


def unpack(blocks, wide, beads):
    for index in range(0, blocks.shape[0], 2):
        one, two = blocks[index], blocks[index + 1]
        half = one.shape[0] // 2
        lanes = pl.ds(index * beads, 2 * beads)
        for part in range(4):
            rows = slice(part // 2 * half, (part // 2 + 1) * half)
            side = slice(part % 2 * beads, (part % 2 + 1) * beads)
            wide[part * half : (part + 1) * half, lanes] = jnp.concatenate(
                [one[rows, side], two[rows, side]], axis=1
            )


def target_columns(own):
    beads = own.shape[1] // 2
    targets = own[8:16, beads:].T
    return [jnp.broadcast_to(targets[:, axis : axis + 1], (beads, 128)) for axis in range(3)]


def fill_tensor(columns, wide, start, high, low, at):
    beads = columns[0].shape[0]
    sources = pl.ds(start, 128)
    to = pl.ds(at, 128)
    moved = [columns[axis] - wide[24 + axis : 25 + axis, sources] for axis in range(3)]
    square = moved[0] * moved[0] + moved[1] * moved[1] + moved[2] * moved[2]
    square = jnp.maximum(square, 1e-12)
    inverse = lax.rsqrt(square)
    inverse_sq = inverse * inverse
    near = square < 4.0
    iso = inverse * jnp.where(near, square * (inverse - 9.0 / 32.0), 0.75 + 0.5 * inverse_sq)
    along = inverse * jnp.where(near, 3.0 / 32.0, inverse_sq * (0.75 - 1.5 * inverse_sq))
    scaled = [along * item for item in moved]
    parts = [
        iso + scaled[0] * moved[0],
        scaled[0] * moved[1],
        scaled[0] * moved[2],
        iso + scaled[1] * moved[1],
        scaled[1] * moved[2],
        iso + scaled[2] * moved[2],
    ]
    for part, value in enumerate(parts):
        upper, lower = split_two(value)
        high[part * beads : (part + 1) * beads, to] = upper
        low[part * beads : (part + 1) * beads, to] = lower


def apply_tensor(both, high, low, at, step):
    lanes = pl.ds(at, step)
    half = both.shape[0] // 2
    first = matmul_nt(both, high[:, lanes])
    return first[:half] + first[half:] + matmul_nt(both[:half], low[:, lanes])


def split_rows(*values):
    highs, lows = zip(*[split_two(value) for value in values])
    return jnp.concatenate(highs + lows, axis=0)


def inner(both):
    half = both.shape[0] // 2
    first = matmul_nt(both, both[:half])
    return first[:half] + first[half:] + matmul_nt(both[:half], both[half:])


def assemble(products, image):
    beads = image.shape[1] // 2

    def part(row, component):
        return products[8 * row : 8 * row + 8, component * beads : (component + 1) * beads]

    image[...] = jnp.zeros(image.shape, F32)
    image[:8, :beads] = part(0, 0) + part(1, 1) + part(2, 2)
    image[:8, beads:] = part(0, 1) + part(1, 3) + part(2, 4)
    image[8:, :beads] = part(0, 2) + part(1, 4) + part(2, 5)


def flat(block):
    return jnp.concatenate([block[:8], block[8:]], axis=1)


def block_sum(matrix, row, column):
    parts = [
        matrix[row + 8 * part : row + 8 * part + 8, column + 8 * part : column + 8 * part + 8]
        for part in range(3)
    ]
    return parts[0] + parts[1] + parts[2]


def filled_product(columns, source, wide, start, width, high, low, with_gram):
    step = 256 if width % 256 == 0 else 128

    def fill(index):
        for part in range(0, step, 128):
            at = pl.multiple_of(index * step + part, 128)
            fill_tensor(columns, source, pl.multiple_of(start + at, 128), high, low, at)

    def add(index, totals):
        at = pl.multiple_of(index * step, step)
        both = split_rows(wide[:, pl.ds(pl.multiple_of(start + at, 128), step)])
        products = totals[0] + apply_tensor(both, high, low, at, step)
        if with_gram:
            return products, totals[1] + inner(both)
        return (products,)

    def body(index, totals):
        totals = add(index - 1, totals)
        fill(index)
        return totals

    totals = (jnp.zeros((32, high.shape[0]), F32),)
    if with_gram:
        totals = totals + (jnp.zeros((32, 32), F32),)
    fill(0)
    count = width // step
    totals = lax.fori_loop(1, count, body, totals)
    return add(count - 1, totals)


def first_product(own, wide, high, low):
    columns = target_columns(own)
    width = high.shape[1]
    totals = None
    for start in range(0, wide.shape[1], width):
        part = filled_product(columns, wide, wide, start, width, high, low, True)
        totals = part if totals is None else tuple(a + b for a, b in zip(totals, part))
    return totals


def first_half_kernel(own_blocks, blocks, products, gram, wide, high, low):
    own = own_blocks[0]
    unpack(blocks, wide, own.shape[1] // 2)
    products[...], gram[...] = first_product(own, wide, high, low)


def second_half_kernel(own_blocks, blocks, products, images, gram, wide, high, low, image):
    own = own_blocks[0]
    unpack(blocks, wide, own.shape[1] // 2)
    more, gram[...] = first_product(own, wide, high, low)
    assemble(products[...] + more, image)
    images[...] = jnp.broadcast_to(image[...][None], images.shape)


def cholesky(matrix):
    size = matrix.shape[0]
    shape = (size, size)
    rows = lax.broadcasted_iota(jnp.int32, shape, 0)
    cols = lax.broadcasted_iota(jnp.int32, shape, 1)
    entry = {}
    for j in range(size):
        column = jnp.broadcast_to(matrix[:, j : j + 1], shape)
        for i in range(j, size):
            entry[i, j] = jnp.broadcast_to(column[i : i + 1, :], shape)
    factor_t = jnp.zeros(shape, F32)
    inverse = jnp.zeros(shape, F32)
    inverse_rows = []
    for j in range(size):
        scale = lax.rsqrt(entry[j, j])
        lower_row = entry[j, j] * scale
        entry[j, j] = scale
        for i in range(j + 1, size):
            entry[i, j] = entry[i, j] * scale
        for i in range(j + 1, size):
            for k in range(j + 1, i + 1):
                entry[i, k] = entry[i, k] - entry[i, j] * entry[k, j]
        lower_row = jnp.where(cols == j, lower_row, 0.0)
        for i in range(j + 1, size):
            lower_row = jnp.where(cols == i, entry[i, j], lower_row)
        factor_t = jnp.where(rows == j, lower_row, factor_t)
        row = jnp.where(cols == j, 1.0, 0.0)
        for k in range(j):
            row = row - entry[j, k] * inverse_rows[k]
        row = row * scale
        inverse_rows.append(row)
        inverse = jnp.where(rows == j, row, inverse)
    return factor_t, inverse


def start_kernel(size, images, own_blocks, one_gram, two_gram, small, own_first, own_moved):
    _, inverse = cholesky(block_sum(one_gram[...] + two_gram[...], 0, 0) / size)
    own_first[...] = small_matmul(inverse, flat(own_blocks[0]))
    own_moved[...] = small_matmul(inverse, flat(images[0]))
    small[0] = inverse
    small[1] = inverse.T


def second_product(fill, own, wide, wide_image, high, low):
    width = high.shape[1]
    both = split_rows(wide_image[...])
    total = jnp.zeros((32, high.shape[0]), F32)
    for start in range(0, wide.shape[1], width):
        if fill:
            columns = target_columns(own)
            total = total + filled_product(columns, wide, wide_image, start, width, high, low, False)[0]
        else:
            total = total + apply_tensor(both, high, low, 0, width)
    return total, inner(split_rows(wide[...], wide_image[...]))


def third_half_kernel(fill, own_blocks, images, wide, high, low, products, gram, wide_image):
    own = own_blocks[0]
    unpack(images, wide_image, own.shape[1] // 2)
    products[...], gram[...] = second_product(fill, own, wide, wide_image, high, low)


def fourth_half_kernel(
    size, fill, own_blocks, images, wide, high, low, products, gram, own_images, own_first, own_moved, small,
    vectors_out, shifted, coefficients, partials, wide_image, image
):
    own = own_blocks[0]
    beads = own.shape[1] // 2
    unpack(images, wide_image, beads)
    more, more_gram = second_product(fill, own, wide, wide_image, high, low)
    both = (gram[...] + more_gram) / size
    inverse_zero, inverse_zero_t = small[0], small[1]
    cross_t = small_matmul(inverse_zero, block_sum(both, 0, 32))
    cross = small_matmul(block_sum(both, 32, 0), inverse_zero_t)
    factor_t, inverse = cholesky(block_sum(both, 32, 32) - small_matmul(cross, cross_t))
    alpha = small_matmul(cross_t, inverse_zero_t)
    factor_one_t = small_matmul(factor_t, inverse_zero_t)
    assemble(products[...] + more, image)
    first, moved = own_first[...], own_moved[...]
    vectors = small_matmul(inverse, flat(own_images[0]) - small_matmul(cross, first))
    shift = small_matmul(inverse, flat(image[...]) - small_matmul(cross, moved))
    shift = shift - small_matmul(factor_one_t, first)
    valid = lax.broadcasted_iota(jnp.int32, vectors.shape, 1) < 3 * beads
    vectors = jnp.where(valid, vectors, 0.0)
    shift = jnp.where(valid, shift, 0.0)
    partial = matmul_nt(vectors, shift, lax.Precision.HIGHEST)
    for row in range(8):
        partials[:, :, 8 * row : 8 * row + 8] = jnp.broadcast_to(
            partial[row : row + 1][None], (partials.shape[0], 1, 8)
        )
    vectors_out[...] = vectors
    shifted[...] = shift
    coefficients[0] = alpha
    coefficients[1] = factor_one_t.T


def last_kernel(size, vectors, shifted, both, partials, basis, residual, coefficients):
    beads = basis.shape[2]
    width = partials.shape[2]
    total = jnp.sum(partials[...], axis=0) / size
    spread = jnp.broadcast_to(total, (8, width))
    rows = lax.broadcasted_iota(jnp.int32, spread.shape, 0)
    cols = lax.broadcasted_iota(jnp.int32, spread.shape, 1)
    block = vectors[...]
    left = shifted[...]
    transposed = jnp.where(cols % 8 == rows, spread, 0.0)
    for k in range(8):
        column = jnp.sum(jnp.where(cols // 8 == k, transposed, 0.0), axis=1, keepdims=True)
        left = left - column * block[k : k + 1, :]
    coefficients[0:2] = both[...]
    for k in range(8):
        coefficients[2, k : k + 1, :] = total[:, 8 * k : 8 * k + 8]
    for part in range(3):
        basis[part] = block[:, part * beads : (part + 1) * beads]
        residual[part] = left[:, part * beads : (part + 1) * beads]


def array(*shape, dtype=F32):
    return jax.ShapeDtypeStruct(shape, dtype)


def call(kernel, outs, scratch=(), **options):
    return pl.pallas_call(
        kernel,
        out_shape=outs,
        scratch_shapes=list(scratch),
        compiler_params=pltpu.CompilerParams(vmem_limit_bytes=48 * 1024 * 1024),
        **options,
    )


def gather(copies):
    rows, cols = lax.axis_size("row"), lax.axis_size("col")
    groups = [
        [row * cols + col for row in range(rows) for col in range(core, cols, 2)] for core in range(2)
    ]
    mine = lax.all_to_all(copies, ("row", "col"), 0, 0, axis_index_groups=groups, tiled=True)
    other = lax.ppermute(mine, "col", [(col, col ^ 1) for col in range(cols)])
    return mine, other


def local(positions, noise):
    vecs, _, beads = noise.shape
    devices = lax.axis_size("row") * lax.axis_size("col")
    chips = devices // 2
    half = beads * chips
    size = 3.0 * 2.0 * half
    keep = 2 * 2 * 2 * 6 * beads * half <= KEPT
    width = half if keep else min(half, CHUNK)
    blocks = array(chips, 2 * vecs, 2 * beads)
    wide = array(4 * vecs, half)
    held_wide = pltpu.VMEM((4 * vecs, half), F32)
    block = pltpu.VMEM((2 * vecs, 2 * beads), F32)
    products = array(4 * vecs, 6 * beads)
    tensors = [array(6 * beads, width, dtype=BF16)] * 2 if keep else []
    held = [] if keep else [pltpu.VMEM((6 * beads, width), BF16)] * 2
    flat_block = array(vecs, 4 * beads)
    small_gram, large_gram = array(4 * vecs, 4 * vecs), array(8 * vecs, 8 * vecs)

    rows = noise.transpose(1, 0, 2).reshape(3 * vecs, beads)
    rows = jnp.concatenate([rows, jnp.pad(positions, ((0, vecs - 3), (0, 0)))], axis=0)
    own = call(pack_kernel, blocks)(rows)
    one, two = gather(own)
    one_products, one_gram, one_wide, *one_tensor = call(
        first_half_kernel, [products, small_gram, wide] + tensors, held
    )(own, one)
    own_images, two_gram, two_wide, *two_tensor = call(
        second_half_kernel, [blocks, small_gram, wide] + tensors, held + [block]
    )(own, two, one_products)
    one_images, two_images = gather(own_images)
    small, own_first, own_moved = call(
        functools.partial(start_kernel, size), [array(2, vecs, vecs), flat_block, flat_block]
    )(own_images, own, one_gram, two_gram)
    fill = not keep
    one_products, gram = call(ordered(functools.partial(third_half_kernel, fill), fill, 3, 2), [products, large_gram], held + [held_wide])(
        own, one_images, one_wide, *one_tensor
    )
    vectors, shifted, both, partials = call(
        ordered(functools.partial(fourth_half_kernel, size, fill), fill, 9, 4),
        [flat_block, flat_block, array(2, vecs, vecs), array(devices, 1, vecs * vecs)],
        held + [held_wide, block],
    )(own, two_images, two_wide, *two_tensor, one_products, gram, own_images, own_first, own_moved, small)
    partials = lax.all_to_all(partials, ("row", "col"), 0, 0, tiled=True)
    basis, residual, coefficients = call(
        functools.partial(last_kernel, size),
        [array(3, vecs, beads), array(3, vecs, beads), array(3, vecs, vecs)],
    )(vectors, shifted, both, partials)
    return (basis.transpose(1, 0, 2), residual.transpose(1, 0, 2), coefficients)


def ordered(kernel, fill, ins, outs):
    if not fill:
        return kernel

    def moved(*refs):
        scratch = refs[ins + outs :]
        kernel(*refs[:3], *scratch[:2], *refs[3 : ins + outs], *scratch[2:])

    return moved


def solution(mesh):
    return jax.shard_map(
        local,
        mesh=mesh,
        in_specs=(P(None, ("row", "col")), P(None, None, ("row", "col"))),
        out_specs=(P(None, None, ("row", "col")), P(None, None, ("row", "col")), P()),
        check_vma=False,
    )
```

time: 48.6 us -> 45.4 us (0.934)
  local copies, waits for them, and re-layouts: 1.38 us -> 0 us
  blocking collectives: 37.1 us -> 35.9 us
  waiting for transfers between devices: 1.19 us -> 0.31 us
  other arithmetic: 0 us -> 0.73 us
    all_to_all x3 -> x2, blocking collectives: 37.1 us -> 26.8 us  [gather(): lax.all_to_all(copies, ('row', 'col'), 0, 0, axis_index_groups=groups, ti...]
    all_to_all x0 -> x1, blocking collectives: none -> 9.03 us  [local(): partials = lax.all_to_all(partials, ('row', 'col'), 0, 0, tiled=True)]
    unnamed x6 -> x0, local copies, waits for them, and re-layouts: 1.38 us -> none
    ppermute x3 -> x2, waiting for transfers between devices: 1.19 us -> 0.31 us  [gather(): other = lax.ppermute(mine, 'col', [(col, col ^ 1) for col in range(cols)])]
    concatenate x0 -> x1, other arithmetic: none -> 0.73 us  [local(): jnp.concatenate([rows, jnp.pad(positions, ((0, vecs - 3), (0, 0)))], axis=0)]
    pallas_call x1, Pallas kernels: 1.03 us -> 0.34 us  [local(): call(functools.partial(start_kernel, size), [array(2, vecs, vecs), flat_b...]
    pallas_call x5, Pallas kernels: 5.86 us -> 6.42 us  [the longest x1 2.1 us: local(): call(second_half_kernel, [blocks, small_gram, wide] + tensors, held + [bl...]
  transfers between devices with their start and end apart: 3 -> 2, of which waited for: 1 -> 1; matrix products, arithmetic and copies ran while one was open for 0% -> 0% of each run, Pallas kernels for 7% -> 7%
where the time goes in v5:
time: 45.4 us; the launch traced here: 45.1 us
  blocking collectives  35.9 us (79%)
  Pallas kernels  7.56 us (17%)
  other arithmetic  0.73 us (2%)
  between operations  0.67 us (1%)
    all_to_all x2, blocking collectives, gather(): lax.all_to_all(copies, ('row', 'col'), 0, 0, axis_index_groups=groups, ti...  26.8 us
    all_to_all x1, blocking collectives, local(): partials = lax.all_to_all(partials, ('row', 'col'), 0, 0, tiled=True)  9.03 us
    pallas_call x1, Pallas kernels, local(): call(second_half_kernel, [blocks, small_gram, wide] + tensors, held + [bl...  2.1 us
    pallas_call x1, Pallas kernels, local(): call(first_half_kernel, [products, small_gram, wide] + tensors, held)  2 us
    pallas_call x1, Pallas kernels, local(): call(ordered(functools.partial(fourth_half_kernel, size, fill), fill, 9,...  1.54 us
  transfers between devices with their start and end apart: 2, of which 1 were waited for; matrix products, arithmetic and copies ran while one was open for 0% of the time, Pallas kernels for 7%

profile of v5, /device:TPU:0, one launch (start us, length us, event | category | flops | bytes accessed | tf_op | source)
XLA Modules:
  0.0 45.1 jit_solution(16522570929888734136)
XLA Ops:
  0.6 0.7 %select_maximum_fusion.rows = f32[32,64]{1,0:T(8,128)S(1)} fusion(f32[3,64]{1,0:T(4,128)} %param.2, f32[24,64]{1,0:T(8,128)} %bitcast.5), kind=kLoop, calls=%fused_computation | loop fusion | flops 6144 | bytes 15104 | tf_op jit(solution)/shard_map/concatenate | solution.py:345
  1.4 0.1 shard_map.49.own_blocks
  1.4 15.8 %all_to_all.15.blocks = f32[16,16,128]{2,1,0:T(8,128)S(1)} all-to-all(f32[16,16,128]{2,1,0:T(8,128)S(1)} %shard_map.49.own_blocks), channel_id=1, replica_groups={{0,2,4,6,8,10,12,14,16,18,20,22,24,26,28,30},{1,3,5,7,9,11,13,15,17,19,..., dimensions={0} | all-to-all | bytes 262144 | tf_op jit(solution)/shard_map/all_to_all | solution.py:321
  17.2 0.0 collective-permute-start
  17.3 2.0 %shard_map.50 = (f32[32,384]{1,0:T(8,128)S(1)}, f32[32,32]{1,0:T(8,128)S(1)}, f32[32,1024]{1,0:T(8,128)S(1)}, bf16[384,1024]{1,0:T(8,128)(2,1)S(1)}, bf16[384,1024]{1,0:T(8,128)(2,1)S(1)}) custom-call(f32[16,16,128]{2,1,0:T(8,128)S(1)} %shard_map.49.own_blocks, f32[16,16,128]{2,1,0:T(8,128)S(1)} %all_to_all.15.blocks), custom_call_target="tpu_custom_call" | custom-call | tf_op jit(solution)/shard_map/pallas_call | solution.py:348
  19.3 0.0 collective-permute-done.blocks
  19.3 2.1 %shard_map.51 = (f32[16,16,128]{2,1,0:T(8,128)S(1)}, f32[32,32]{1,0:T(8,128)S(1)}, f32[32,1024]{1,0:T(8,128)S(1)}, bf16[384,1024]{1,0:T(8,128)(2,1)S(1)}, bf16[384,1024]{1,0:T(8,128)(2,1)S(1)}) custom-call(f32[16,16,128]{2,1,0:T(8,128)S(1)} %shard_map.49.own_blocks, f32[16,16,128]{2,1,0:T(8,128)S(1)} %collective-permute-done.blocks, ...), custom_call_target="tpu_custom_call" | custom-call | tf_op jit(solution)/shard_map/pallas_call | solution.py:351
  21.4 11.0 %all_to_all.16.images = f32[16,16,128]{2,1,0:T(8,128)S(1)} all-to-all(f32[16,16,128]{2,1,0:T(8,128)S(1)} %get-tuple-element.26.images.own_images), channel_id=1, replica_groups={{0,2,4,6,8,10,12,14,16,18,20,22,24,26,28,30},{1,3,5,7,9,11,13,15,17,19,..., dimensions={0} | all-to-all | bytes 262144 | tf_op jit(solution)/shard_map/all_to_all | solution.py:321
  32.4 0.0 collective-permute-start.1
  32.4 0.3 shard_map.53
  32.8 0.7 %shard_map.52 = (f32[32,384]{1,0:T(8,128)S(1)}, f32[64,64]{1,0:T(8,128)S(1)}) custom-call(f32[16,16,128]{2,1,0:T(8,128)S(1)} %shard_map.49.own_blocks, f32[16,16,128]{2,1,0:T(8,128)S(1)} %all_to_all.16.images, f32[32,1024]{1,0:T(8,128)S(1)} %get-tuple-element.30.wide, bf16[384,1024]{1,0:T(8,128)(2,1)S(1)} %get-tuple-element.31.high, ...), custom_call_target="tpu_custom_call" | custom-call | tf_op jit(solution)/shard_map/pallas_call | solution.py:359
  33.5 0.3 collective-permute-done.1.images
  33.8 1.5 %shard_map.54 = (f32[8,256]{1,0:T(8,128)S(1)}, f32[8,256]{1,0:T(8,128)S(1)}, f32[2,8,8]{2,1,0:T(8,128)S(1)}, f32[32,1,64]{2,1,0:T(1,128)S(1)}) custom-call(f32[16,16,128]{2,1,0:T(8,128)S(1)} %shard_map.49.own_blocks, f32[16,16,128]{2,1,0:T(8,128)S(1)} %collective-permute-done.1.images, f32[32,1024]{1,0:T(8,128)S(1)} %get-tuple-element.27.wide, ...), custom_call_target="tpu_custom_call" | custom-call | tf_op jit(solution)/shard_map/pallas_call | solution.py:362
  35.3 9.0 %all_to_all.17.partials = f32[32,1,64]{2,1,0:T(1,128)S(1)} all-to-all(f32[32,1,64]{2,1,0:T(1,128)S(1)} %get-tuple-element.43), channel_id=1, replica_groups=mesh['row'=4,'col'=8] {'row','col'}, dimensions={0} | all-to-all | bytes 16384 | tf_op jit(solution)/shard_map/all_to_all | solution.py:367
  44.3 0.8 %shard_map.55 = (f32[3,8,64]{2,1,0:T(8,128)}, f32[3,8,64]{2,1,0:T(8,128)}, f32[3,8,8]{2,1,0:T(8,128)}) custom-call(f32[8,256]{1,0:T(8,128)S(1)} %get-tuple-element.40.vectors, f32[8,256]{1,0:T(8,128)S(1)} %get-tuple-element.41.shifted, f32[2,8,8]{2,1,0:T(8,128)S(1)} %get-tuple-element.42.both, f32[32,1,64]{2,1,0:T(1,128)S(1)} %all_to_all.17.partials), custom_call_target="tpu_custom_call" | custom-call | tf_op jit(solution)/shard_map/pallas_call | solution.py:368
Async XLA Ops:
  17.2 2.0 %collective-permute-start = (f32[16,16,128]{2,1,0:T(8,128)S(1)}, f32[16,16,128]{2,1,0:T(8,128)S(1)}, u32[]{:S(2)}, u32[]{:S(2)}) collective-permute-start(f32[16,16,128]{2,1,0:T(8,128)S(1)} %all_to_all.15.blocks), channel_id=1, source_target_pairs={{0,1},{1,0},{2,3},{3,2},{4,5},{5,4},{6,7},{7,6},{8,9},{9,8},{10,11... | collective-permute-start | bytes 393224 | tf_op jit(solution)/shard_map/ppermute | solution.py:322
  32.4 1.3 %collective-permute-start.1 = (f32[16,16,128]{2,1,0:T(8,128)S(1)}, f32[16,16,128]{2,1,0:T(8,128)S(1)}, u32[]{:S(2)}, u32[]{:S(2)}) collective-permute-start(f32[16,16,128]{2,1,0:T(8,128)S(1)} %all_to_all.16.images), channel_id=1, source_target_pairs={{0,1},{1,0},{2,3},{3,2},{4,5},{5,4},{6,7},{7,6},{8,9},{9,8},{10,11... | collective-permute-start | bytes 393224 | tf_op jit(solution)/shard_map/ppermute | solution.py:322

commit v6 on v5

--- a/solution.py
+++ b/solution.py
@@ -7,7 +7,7 @@
 from jax.experimental.pallas import tpu as pltpu
 from jax.sharding import PartitionSpec as P
 
-CHUNK = 2048
+CHUNK = 1024
 KEPT = 8 * 1024 * 1024
 F32 = jnp.float32
 BF16 = jnp.bfloat16
@@ -128,44 +128,33 @@
     return parts[0] + parts[1] + parts[2]
 
 
-def filled_product(columns, source, wide, start, width, high, low, with_gram):
+def filled_product(columns, source, wide, start, high, low, with_gram):
+    width = high.shape[1]
     step = 256 if width % 256 == 0 else 128
-
-    def fill(index):
-        for part in range(0, step, 128):
-            at = pl.multiple_of(index * step + part, 128)
-            fill_tensor(columns, source, pl.multiple_of(start + at, 128), high, low, at)
-
-    def add(index, totals):
-        at = pl.multiple_of(index * step, step)
+    products = jnp.zeros((32, high.shape[0]), F32)
+    for at in range(0, width, step):
+        for part in range(at, at + step, 128):
+            fill_tensor(columns, source, pl.multiple_of(start + part, 128), high, low, part)
         both = split_rows(wide[:, pl.ds(pl.multiple_of(start + at, 128), step)])
-        products = totals[0] + apply_tensor(both, high, low, at, step)
-        if with_gram:
-            return products, totals[1] + inner(both)
-        return (products,)
-
-    def body(index, totals):
-        totals = add(index - 1, totals)
-        fill(index)
-        return totals
-
-    totals = (jnp.zeros((32, high.shape[0]), F32),)
+        products = products + apply_tensor(both, high, low, at, step)
     if with_gram:
-        totals = totals + (jnp.zeros((32, 32), F32),)
-    fill(0)
-    count = width // step
-    totals = lax.fori_loop(1, count, body, totals)
-    return add(count - 1, totals)
+        both = split_rows(wide[:, pl.ds(pl.multiple_of(start, 128), width)])
+        return products, inner(both)
+    return (products,)
+
+
+def all_chunks(total, width, chunk):
+    if total == width:
+        return chunk(0)
+    body = lambda index, sums: tuple(a + b for a, b in zip(sums, chunk(index * width)))
+    return lax.fori_loop(1, total // width, body, chunk(0))
 
 
 def first_product(own, wide, high, low):
     columns = target_columns(own)
-    width = high.shape[1]
-    totals = None
-    for start in range(0, wide.shape[1], width):
-        part = filled_product(columns, wide, wide, start, width, high, low, True)
-        totals = part if totals is None else tuple(a + b for a, b in zip(totals, part))
-    return totals
+    return all_chunks(
+        wide.shape[1], high.shape[1], lambda start: filled_product(columns, wide, wide, start, high, low, True)
+    )
 
 
 def first_half_kernel(own_blocks, blocks, products, gram, wide, high, low):
@@ -226,16 +215,16 @@
 
 
 def second_product(fill, own, wide, wide_image, high, low):
-    width = high.shape[1]
-    both = split_rows(wide_image[...])
-    total = jnp.zeros((32, high.shape[0]), F32)
-    for start in range(0, wide.shape[1], width):
-        if fill:
-            columns = target_columns(own)
-            total = total + filled_product(columns, wide, wide_image, start, width, high, low, False)[0]
-        else:
-            total = total + apply_tensor(both, high, low, 0, width)
-    return total, inner(split_rows(wide[...], wide_image[...]))
+    grams = inner(split_rows(wide[...], wide_image[...]))
+    if not fill:
+        return apply_tensor(split_rows(wide_image[...]), high, low, 0, high.shape[1]), grams
+    columns = target_columns(own)
+    (products,) = all_chunks(
+        wide.shape[1],
+        high.shape[1],
+        lambda start: filled_product(columns, wide, wide_image, start, high, low, False),
+    )
+    return products, grams
 
 
 def third_half_kernel(fill, own_blocks, images, wide, high, low, products, gram, wide_image):
@@ -315,9 +304,10 @@
 
 def gather(copies):
     rows, cols = lax.axis_size("row"), lax.axis_size("col")
-    groups = [
-        [row * cols + col for row in range(rows) for col in range(core, cols, 2)] for core in range(2)
-    ]
+    groups = [[], []]
+    for row in range(rows):
+        for col in range(cols):
+            groups[(bin(row).count("1") + col // 2 + col) % 2].append(row * cols + col)
     mine = lax.all_to_all(copies, ("row", "col"), 0, 0, axis_index_groups=groups, tiled=True)
     other = lax.ppermute(mine, "col", [(col, col ^ 1) for col in range(cols)])
     return mine, other

time: 45.4 us -> 44.1 us (0.971)
  Pallas kernels: 7.56 us -> 5.49 us
    pallas_call x1, Pallas kernels: 2.1 us -> 1.24 us  [local(): call(second_half_kernel, [blocks, small_gram, wide] + tensors, held + [bl...]
    pallas_call x1, Pallas kernels: 2 us -> 1.14 us  [local(): call(first_half_kernel, [products, small_gram, wide] + tensors, held)]
  transfers between devices with their start and end apart: 2 -> 2, of which waited for: 1 -> 2; matrix products, arithmetic and copies ran while one was open for 0% -> 0% of each run, Pallas kernels for 7% -> 5%
where the time goes in v6:
time: 44.1 us; the launch traced here: 43.7 us
  blocking collectives  36.3 us (82%)
  Pallas kernels  5.49 us (12%)
  other arithmetic  0.73 us (2%)
  between operations  0.65 us (1%)
  waiting for transfers between devices  0.51 us (1%)
    all_to_all x2, blocking collectives, gather(): lax.all_to_all(copies, ('row', 'col'), 0, 0, axis_index_groups=groups, ti...  27.2 us
    all_to_all x1, blocking collectives, local(): partials = lax.all_to_all(partials, ('row', 'col'), 0, 0, tiled=True)  9.1 us
    pallas_call x1, Pallas kernels, local(): call(second_half_kernel, [blocks, small_gram, wide] + tensors, held + [bl...  1.24 us
    pallas_call x1, Pallas kernels, local(): call(ordered(functools.partial(fourth_half_kernel, size, fill), fill, 9,...  1.21 us
    pallas_call x1, Pallas kernels, local(): call(first_half_kernel, [products, small_gram, wide] + tensors, held)  1.14 us
  transfers between devices with their start and end apart: 2, of which 2 were waited for; matrix products, arithmetic and copies ran while one was open for 0% of the time, Pallas kernels for 5%

profile of v6, /device:TPU:0, one launch (start us, length us, event | category | flops | bytes accessed | tf_op | source)
XLA Modules:
  0.0 43.7 jit_solution(3947922848919140766)
XLA Ops:
  0.6 0.7 %select_maximum_fusion.rows = f32[32,64]{1,0:T(8,128)S(1)} fusion(f32[3,64]{1,0:T(4,128)} %param.2, f32[24,64]{1,0:T(8,128)} %bitcast.5), kind=kLoop, calls=%fused_computation | loop fusion | flops 6144 | bytes 15104 | tf_op jit(solution)/shard_map/concatenate | solution.py:335
  1.4 0.1 shard_map.49.own_blocks
  1.4 16.4 %all_to_all.15.blocks = f32[16,16,128]{2,1,0:T(8,128)S(1)} all-to-all(f32[16,16,128]{2,1,0:T(8,128)S(1)} %shard_map.49.own_blocks), channel_id=1, replica_groups={{0,3,4,7,9,10,13,14,17,18,21,22,24,27,28,31},{1,2,5,6,8,11,12,15,16,19,..., dimensions={0} | all-to-all | bytes 262144 | tf_op jit(solution)/shard_map/all_to_all | solution.py:311
  17.9 0.0 collective-permute-start
  17.9 1.1 %shard_map.50 = (f32[32,384]{1,0:T(8,128)S(1)}, f32[32,32]{1,0:T(8,128)S(1)}, f32[32,1024]{1,0:T(8,128)S(1)}, bf16[384,1024]{1,0:T(8,128)(2,1)S(1)}, bf16[384,1024]{1,0:T(8,128)(2,1)S(1)}) custom-call(f32[16,16,128]{2,1,0:T(8,128)S(1)} %shard_map.49.own_blocks, f32[16,16,128]{2,1,0:T(8,128)S(1)} %all_to_all.15.blocks), custom_call_target="tpu_custom_call" | custom-call | tf_op jit(solution)/shard_map/pallas_call | solution.py:338
  19.0 0.2 collective-permute-done.blocks
  19.2 1.2 %shard_map.51 = (f32[16,16,128]{2,1,0:T(8,128)S(1)}, f32[32,32]{1,0:T(8,128)S(1)}, f32[32,1024]{1,0:T(8,128)S(1)}, bf16[384,1024]{1,0:T(8,128)(2,1)S(1)}, bf16[384,1024]{1,0:T(8,128)(2,1)S(1)}) custom-call(f32[16,16,128]{2,1,0:T(8,128)S(1)} %shard_map.49.own_blocks, f32[16,16,128]{2,1,0:T(8,128)S(1)} %collective-permute-done.blocks, ...), custom_call_target="tpu_custom_call" | custom-call | tf_op jit(solution)/shard_map/pallas_call | solution.py:341
  20.5 10.8 %all_to_all.16.images = f32[16,16,128]{2,1,0:T(8,128)S(1)} all-to-all(f32[16,16,128]{2,1,0:T(8,128)S(1)} %get-tuple-element.26.images.own_images), channel_id=1, replica_groups={{0,3,4,7,9,10,13,14,17,18,21,22,24,27,28,31},{1,2,5,6,8,11,12,15,16,19,..., dimensions={0} | all-to-all | bytes 262144 | tf_op jit(solution)/shard_map/all_to_all | solution.py:311
  31.3 0.0 collective-permute-start.1
  31.3 0.3 shard_map.53
  31.6 0.7 %shard_map.52 = (f32[32,384]{1,0:T(8,128)S(1)}, f32[64,64]{1,0:T(8,128)S(1)}) custom-call(f32[16,16,128]{2,1,0:T(8,128)S(1)} %shard_map.49.own_blocks, f32[16,16,128]{2,1,0:T(8,128)S(1)} %all_to_all.16.images, f32[32,1024]{1,0:T(8,128)S(1)} %get-tuple-element.30.wide, bf16[384,1024]{1,0:T(8,128)(2,1)S(1)} %get-tuple-element.31.high, ...), custom_call_target="tpu_custom_call" | custom-call | tf_op jit(solution)/shard_map/pallas_call | solution.py:349
  32.3 0.3 collective-permute-done.1.images
  32.6 1.2 %shard_map.54 = (f32[8,256]{1,0:T(8,128)S(1)}, f32[8,256]{1,0:T(8,128)S(1)}, f32[2,8,8]{2,1,0:T(8,128)S(1)}, f32[32,1,64]{2,1,0:T(1,128)S(1)}) custom-call(f32[16,16,128]{2,1,0:T(8,128)S(1)} %shard_map.49.own_blocks, f32[16,16,128]{2,1,0:T(8,128)S(1)} %collective-permute-done.1.images, f32[32,1024]{1,0:T(8,128)S(1)} %get-tuple-element.27.wide, ...), custom_call_target="tpu_custom_call" | custom-call | tf_op jit(solution)/shard_map/pallas_call | solution.py:352
  33.8 9.1 %all_to_all.17.partials = f32[32,1,64]{2,1,0:T(1,128)S(1)} all-to-all(f32[32,1,64]{2,1,0:T(1,128)S(1)} %get-tuple-element.43), channel_id=1, replica_groups=mesh['row'=4,'col'=8] {'row','col'}, dimensions={0} | all-to-all | bytes 16384 | tf_op jit(solution)/shard_map/all_to_all | solution.py:357
  42.9 0.8 %shard_map.55 = (f32[3,8,64]{2,1,0:T(8,128)}, f32[3,8,64]{2,1,0:T(8,128)}, f32[3,8,8]{2,1,0:T(8,128)}) custom-call(f32[8,256]{1,0:T(8,128)S(1)} %get-tuple-element.40.vectors, f32[8,256]{1,0:T(8,128)S(1)} %get-tuple-element.41.shifted, f32[2,8,8]{2,1,0:T(8,128)S(1)} %get-tuple-element.42.both, f32[32,1,64]{2,1,0:T(1,128)S(1)} %all_to_all.17.partials), custom_call_target="tpu_custom_call" | custom-call | tf_op jit(solution)/shard_map/pallas_call | solution.py:358
Async XLA Ops:
  17.9 1.3 %collective-permute-start = (f32[16,16,128]{2,1,0:T(8,128)S(1)}, f32[16,16,128]{2,1,0:T(8,128)S(1)}, u32[]{:S(2)}, u32[]{:S(2)}) collective-permute-start(f32[16,16,128]{2,1,0:T(8,128)S(1)} %all_to_all.15.blocks), channel_id=1, source_target_pairs={{0,1},{1,0},{2,3},{3,2},{4,5},{5,4},{6,7},{7,6},{8,9},{9,8},{10,11... | collective-permute-start | bytes 393224 | tf_op jit(solution)/shard_map/ppermute | solution.py:312
  31.3 1.3 %collective-permute-start.1 = (f32[16,16,128]{2,1,0:T(8,128)S(1)}, f32[16,16,128]{2,1,0:T(8,128)S(1)}, u32[]{:S(2)}, u32[]{:S(2)}) collective-permute-start(f32[16,16,128]{2,1,0:T(8,128)S(1)} %all_to_all.16.images), channel_id=1, source_target_pairs={{0,1},{1,0},{2,3},{3,2},{4,5},{5,4},{6,7},{7,6},{8,9},{9,8},{10,11... | collective-permute-start | bytes 393224 | tf_op jit(solution)/shard_map/ppermute | solution.py:312

commit v7 on v6

--- a/solution.py
+++ b/solution.py
@@ -40,11 +40,12 @@
     return total
 
 
-def unpack(blocks, wide, beads):
-    for index in range(0, blocks.shape[0], 2):
-        one, two = blocks[index], blocks[index + 1]
+def unpack(arrays, wide, beads):
+    blocks = [(array, index) for array in arrays for index in range(array.shape[0])]
+    for at in range(0, len(blocks), 2):
+        one, two = [array[index] for array, index in blocks[at : at + 2]]
         half = one.shape[0] // 2
-        lanes = pl.ds(index * beads, 2 * beads)
+        lanes = pl.ds(at * beads, 2 * beads)
         for part in range(4):
             rows = slice(part // 2 * half, (part // 2 + 1) * half)
             side = slice(part % 2 * beads, (part % 2 + 1) * beads)
@@ -130,9 +131,9 @@
 
 def filled_product(columns, source, wide, start, high, low, with_gram):
     width = high.shape[1]
-    step = 256 if width % 256 == 0 else 128
     products = jnp.zeros((32, high.shape[0]), F32)
-    for at in range(0, width, step):
+    for at in range(0, width, 256):
+        step = min(256, width - at)
         for part in range(at, at + step, 128):
             fill_tensor(columns, source, pl.multiple_of(start + part, 128), high, low, part)
         both = split_rows(wide[:, pl.ds(pl.multiple_of(start + at, 128), step)])
@@ -157,18 +158,22 @@
     )
 
 
-def first_half_kernel(own_blocks, blocks, products, gram, wide, high, low):
-    own = own_blocks[0]
+def first_stage(count, earlier, last, *refs):
+    refs = list(refs)
+    own_ref, blocks, refs = refs[0], refs[1 : count + 1], refs[count + 1 :]
+    before, refs = refs[: 2 * earlier], refs[2 * earlier :]
+    out, gram, wide, high, low = refs[:5]
+    own = own_ref[0]
     unpack(blocks, wide, own.shape[1] // 2)
-    products[...], gram[...] = first_product(own, wide, high, low)
-
-
-def second_half_kernel(own_blocks, blocks, products, images, gram, wide, high, low, image):
-    own = own_blocks[0]
-    unpack(blocks, wide, own.shape[1] // 2)
-    more, gram[...] = first_product(own, wide, high, low)
-    assemble(products[...] + more, image)
-    images[...] = jnp.broadcast_to(image[...][None], images.shape)
+    products, grams = first_product(own, wide, high, low)
+    if earlier:
+        products, grams = products + before[0][...], grams + before[1][...]
+    gram[...] = grams
+    if last:
+        assemble(products, refs[5])
+        out[0] = refs[5][...]
+    else:
+        out[...] = products
 
 
 def cholesky(matrix):
@@ -206,10 +211,10 @@
     return factor_t, inverse
 
 
-def start_kernel(size, images, own_blocks, one_gram, two_gram, small, own_first, own_moved):
-    _, inverse = cholesky(block_sum(one_gram[...] + two_gram[...], 0, 0) / size)
-    own_first[...] = small_matmul(inverse, flat(own_blocks[0]))
-    own_moved[...] = small_matmul(inverse, flat(images[0]))
+def start_kernel(size, image, own_block, gram, small, own_first, own_moved):
+    _, inverse = cholesky(block_sum(gram[...], 0, 0) / size)
+    own_first[...] = small_matmul(inverse, flat(own_block[0]))
+    own_moved[...] = small_matmul(inverse, flat(image[0]))
     small[0] = inverse
     small[1] = inverse.T
 
@@ -227,31 +232,40 @@
     return products, grams
 
 
-def third_half_kernel(fill, own_blocks, images, wide, high, low, products, gram, wide_image):
-    own = own_blocks[0]
-    unpack(images, wide_image, own.shape[1] // 2)
-    products[...], gram[...] = second_product(fill, own, wide, wide_image, high, low)
-
-
-def fourth_half_kernel(
-    size, fill, own_blocks, images, wide, high, low, products, gram, own_images, own_first, own_moved, small,
-    vectors_out, shifted, coefficients, partials, wide_image, image
-):
-    own = own_blocks[0]
+def second_stage(size, count, earlier, last, fill, *refs):
+    refs = list(refs)
+    own_ref, wide, refs = refs[0], refs[1], refs[2:]
+    if not fill:
+        (high, low), refs = refs[:2], refs[2:]
+    images, refs = refs[:count], refs[count:]
+    before, refs = refs[: 2 * earlier], refs[2 * earlier :]
+    if last:
+        (own_image, own_first, own_moved, small), refs = refs[:4], refs[4:]
+    outs, refs = refs[: 4 if last else 2], refs[4 if last else 2 :]
+    if fill:
+        (high, low), refs = refs[:2], refs[2:]
+    wide_image = refs[0]
+    own = own_ref[0]
     beads = own.shape[1] // 2
     unpack(images, wide_image, beads)
-    more, more_gram = second_product(fill, own, wide, wide_image, high, low)
-    both = (gram[...] + more_gram) / size
+    products, grams = second_product(fill, own, wide, wide_image, high, low)
+    if earlier:
+        products, grams = products + before[0][...], grams + before[1][...]
+    if not last:
+        outs[0][...], outs[1][...] = products, grams
+        return
+    vectors_out, shifted, coefficients, partials = outs
+    grams = grams / size
     inverse_zero, inverse_zero_t = small[0], small[1]
-    cross_t = small_matmul(inverse_zero, block_sum(both, 0, 32))
-    cross = small_matmul(block_sum(both, 32, 0), inverse_zero_t)
-    factor_t, inverse = cholesky(block_sum(both, 32, 32) - small_matmul(cross, cross_t))
+    cross_t = small_matmul(inverse_zero, block_sum(grams, 0, 32))
+    cross = small_matmul(block_sum(grams, 32, 0), inverse_zero_t)
+    factor_t, inverse = cholesky(block_sum(grams, 32, 32) - small_matmul(cross, cross_t))
     alpha = small_matmul(cross_t, inverse_zero_t)
     factor_one_t = small_matmul(factor_t, inverse_zero_t)
-    assemble(products[...] + more, image)
+    assemble(products, refs[1])
     first, moved = own_first[...], own_moved[...]
-    vectors = small_matmul(inverse, flat(own_images[0]) - small_matmul(cross, first))
-    shift = small_matmul(inverse, flat(image[...]) - small_matmul(cross, moved))
+    vectors = small_matmul(inverse, flat(own_image[0]) - small_matmul(cross, first))
+    shift = small_matmul(inverse, flat(refs[1][...]) - small_matmul(cross, moved))
     shift = shift - small_matmul(factor_one_t, first)
     valid = lax.broadcasted_iota(jnp.int32, vectors.shape, 1) < 3 * beads
     vectors = jnp.where(valid, vectors, 0.0)
@@ -302,75 +316,104 @@
     )
 
 
-def gather(copies):
+def exchange(block, first, second):
     rows, cols = lax.axis_size("row"), lax.axis_size("col")
-    groups = [[], []]
-    for row in range(rows):
-        for col in range(cols):
-            groups[(bin(row).count("1") + col // 2 + col) % 2].append(row * cols + col)
+    layers = cols // 2
+    pairs = []
+    for chip in range(rows * layers):
+        for core, offset in enumerate((first, second)):
+            if offset is not None:
+                pairs.append((2 * chip + core, 2 * (chip ^ offset) + core))
+    return lax.ppermute(block, ("row", "col"), pairs)
+
+
+def between_cores(block):
+    cols = lax.axis_size("col")
+    return lax.ppermute(block, "col", [(col, col ^ 1) for col in range(cols)])
+
+
+ROWS, LAYERS = 4, 4
+ALONE = 1
+OFFSETS = ((3, 6), (5, 2), (4, 9), (8, 12))
+
+
+def spread(block, use):
+    rows, cols = lax.axis_size("row"), lax.axis_size("col")
+    if (rows, cols) == (ROWS, 2 * LAYERS):
+        pair = jnp.concatenate([block, between_cores(block)], axis=0)
+        one = exchange(pair, *OFFSETS[0])
+        alone = exchange(pair, None, ALONE)
+        two = exchange(pair, *OFFSETS[1])
+        three = exchange(jnp.concatenate([pair, one], axis=0), *OFFSETS[2])
+        four = exchange(jnp.concatenate([pair, one, two], axis=0), *OFFSETS[3])
+        siblings = between_cores(jnp.concatenate([alone, one, two, three], axis=0))
+        used = use(0, False, [pair, one, two, three])
+        four, used = lax.optimization_barrier((four, used))
+        last = between_cores(four)
+        used = use(1, False, [four, alone, siblings], *used)
+        return use(2, True, [last], *used)
+    groups = [[row * cols + col for row in range(rows) for col in range(core, cols, 2)] for core in range(2)]
+    copies = jnp.broadcast_to(block, (rows * cols // 2,) + block.shape[1:])
     mine = lax.all_to_all(copies, ("row", "col"), 0, 0, axis_index_groups=groups, tiled=True)
-    other = lax.ppermute(mine, "col", [(col, col ^ 1) for col in range(cols)])
-    return mine, other
+    other = between_cores(mine)
+    return use(1, True, [other], *use(0, False, [mine]))
 
 
 def local(positions, noise):
     vecs, _, beads = noise.shape
     devices = lax.axis_size("row") * lax.axis_size("col")
-    chips = devices // 2
-    half = beads * chips
-    size = 3.0 * 2.0 * half
-    keep = 2 * 2 * 2 * 6 * beads * half <= KEPT
-    width = half if keep else min(half, CHUNK)
-    blocks = array(chips, 2 * vecs, 2 * beads)
-    wide = array(4 * vecs, half)
-    held_wide = pltpu.VMEM((4 * vecs, half), F32)
-    block = pltpu.VMEM((2 * vecs, 2 * beads), F32)
+    size = 3.0 * beads * devices
+    keep = 2 * 2 * 6 * beads * beads * devices <= KEPT
+    block = array(1, 2 * vecs, 2 * beads)
+    held_block = pltpu.VMEM((2 * vecs, 2 * beads), F32)
     products = array(4 * vecs, 6 * beads)
-    tensors = [array(6 * beads, width, dtype=BF16)] * 2 if keep else []
-    held = [] if keep else [pltpu.VMEM((6 * beads, width), BF16)] * 2
     flat_block = array(vecs, 4 * beads)
     small_gram, large_gram = array(4 * vecs, 4 * vecs), array(8 * vecs, 8 * vecs)
 
     rows = noise.transpose(1, 0, 2).reshape(3 * vecs, beads)
     rows = jnp.concatenate([rows, jnp.pad(positions, ((0, vecs - 3), (0, 0)))], axis=0)
-    own = call(pack_kernel, blocks)(rows)
-    one, two = gather(own)
-    one_products, one_gram, one_wide, *one_tensor = call(
-        first_half_kernel, [products, small_gram, wide] + tensors, held
-    )(own, one)
-    own_images, two_gram, two_wide, *two_tensor = call(
-        second_half_kernel, [blocks, small_gram, wide] + tensors, held + [block]
-    )(own, two, one_products)
-    one_images, two_images = gather(own_images)
+    own = call(pack_kernel, block)(rows)
+    kept = {}
+
+    def use_first(index, last, blocks, *before):
+        total = beads * sum(item.shape[0] for item in blocks)
+        shape = (6 * beads, total if keep else min(total, CHUNK))
+        kernel = functools.partial(first_stage, len(blocks), index > 0, last)
+        outs = [block if last else products, small_gram, array(4 * vecs, total)]
+        scratch = [held_block] if last else []
+        if keep:
+            outs = outs + [array(*shape, dtype=BF16)] * 2
+        else:
+            scratch = [pltpu.VMEM(shape, BF16)] * 2 + scratch
+        *before, wide, high, low = (list(call(kernel, outs, scratch)(own, *blocks, *before)) + [None, None])[:5]
+        kept[index] = (wide, high, low) if keep else (wide,)
+        return before
+
+    image, gram = spread(own, use_first)
     small, own_first, own_moved = call(
         functools.partial(start_kernel, size), [array(2, vecs, vecs), flat_block, flat_block]
-    )(own_images, own, one_gram, two_gram)
-    fill = not keep
-    one_products, gram = call(ordered(functools.partial(third_half_kernel, fill), fill, 3, 2), [products, large_gram], held + [held_wide])(
-        own, one_images, one_wide, *one_tensor
-    )
-    vectors, shifted, both, partials = call(
-        ordered(functools.partial(fourth_half_kernel, size, fill), fill, 9, 4),
-        [flat_block, flat_block, array(2, vecs, vecs), array(devices, 1, vecs * vecs)],
-        held + [held_wide, block],
-    )(own, two_images, two_wide, *two_tensor, one_products, gram, own_images, own_first, own_moved, small)
+    )(image, own, gram)
+
+    def use_second(index, last, blocks, *before):
+        total = beads * sum(item.shape[0] for item in blocks)
+        kernel = functools.partial(second_stage, size, len(blocks), index > 0, last, not keep)
+        outs, ins = [products, large_gram], []
+        scratch = [pltpu.VMEM((4 * vecs, total), F32)]
+        if last:
+            outs = [flat_block, flat_block, array(2, vecs, vecs), array(devices, 1, vecs * vecs)]
+            ins = [image, own_first, own_moved, small]
+            scratch = scratch + [held_block]
+        if not keep:
+            scratch = [pltpu.VMEM((6 * beads, min(total, CHUNK)), BF16)] * 2 + scratch
+        return call(kernel, outs, scratch)(own, *kept[index], *blocks, *before, *ins)
+
+    vectors, shifted, both, partials = spread(image, use_second)
     partials = lax.all_to_all(partials, ("row", "col"), 0, 0, tiled=True)
     basis, residual, coefficients = call(
         functools.partial(last_kernel, size),
         [array(3, vecs, beads), array(3, vecs, beads), array(3, vecs, vecs)],
     )(vectors, shifted, both, partials)
     return (basis.transpose(1, 0, 2), residual.transpose(1, 0, 2), coefficients)
-
-
-def ordered(kernel, fill, ins, outs):
-    if not fill:
-        return kernel
-
-    def moved(*refs):
-        scratch = refs[ins + outs :]
-        kernel(*refs[:3], *scratch[:2], *refs[3 : ins + outs], *scratch[2:])
-
-    return moved
 
 
 def solution(mesh):

time: 44.1 us -> 45.8 us (1.039)
  blocking collectives: 36.3 us -> 10.7 us
  starting transfers between devices: 0.01 us -> 17.3 us
  waiting for transfers between devices: 0.51 us -> 9.49 us
  Pallas kernels: 5.49 us -> 6.52 us
    all_to_all x2 -> x0, blocking collectives: 27.2 us -> none  [gather(): lax.all_to_all(copies, ('row', 'col'), 0, 0, axis_index_groups=groups, ti...]
    ppermute x2 -> x16, starting transfers between devices: 0.01 us -> 17.3 us  [the longest x10 15.4 us: exchange(): return lax.ppermute(block, ('row', 'col'), pairs)]
    ppermute x2 -> x16, waiting for transfers between devices: 0.51 us -> 9.49 us  [the longest x10 7.78 us: exchange(): return lax.ppermute(block, ('row', 'col'), pairs)]
    all_to_all x1, blocking collectives: 9.1 us -> 10.7 us  [local(): partials = lax.all_to_all(partials, ('row', 'col'), 0, 0, tiled=True)]
    pallas_call x5 -> x7, Pallas kernels: 4.36 us -> 5.38 us  [the longest x3 2.82 us: use_first(): call(kernel, outs, scratch)(own, *blocks, *before)]
  transfers between devices with their start and end apart: 2 -> 16, of which waited for: 2 -> 9; matrix products, arithmetic and copies ran while one was open for 0% -> 0% of each run, Pallas kernels for 5% -> 8%
where the time goes in v7:
time: 45.8 us; the launch traced here: 45.5 us
  starting transfers between devices  17.3 us (38%)
  blocking collectives  10.7 us (23%)
  waiting for transfers between devices  9.49 us (21%)
  Pallas kernels  6.52 us (14%)
  other arithmetic  0.76 us (2%)
  between operations  0.72 us (2%)
    ppermute x10, starting transfers between devices, exchange(): return lax.ppermute(block, ('row', 'col'), pairs)  15.4 us
    all_to_all x1, blocking collectives, local(): partials = lax.all_to_all(partials, ('row', 'col'), 0, 0, tiled=True)  10.7 us
    ppermute x10, waiting for transfers between devices, exchange(): return lax.ppermute(block, ('row', 'col'), pairs)  7.78 us
    pallas_call x3, Pallas kernels, use_first(): call(kernel, outs, scratch)(own, *blocks, *before)  2.82 us
    pallas_call x3, Pallas kernels, use_second(): call(kernel, outs, scratch)(own, *kept[index], *blocks, *before, *ins)  2.48 us
    ppermute x6, starting transfers between devices, between_cores(): return lax.ppermute(block, 'col', [(col, col ^ 1) for col in range(cols)])  1.93 us
    ppermute x6, waiting for transfers between devices, between_cores(): return lax.ppermute(block, 'col', [(col, col ^ 1) for col in range(cols)])  1.71 us
  transfers between devices with their start and end apart: 16, of which 9 were waited for; matrix products, arithmetic and copies ran while one was open for 0% of the time, Pallas kernels for 8%

profile of v7, /device:TPU:0, one launch (start us, length us, event | category | flops | bytes accessed | tf_op | source)
XLA Modules:
  0.0 45.5 jit_solution(3807475868982260514)
XLA Ops:
  0.6 0.7 %select_maximum_fusion.rows = f32[32,64]{1,0:T(8,128)S(1)} fusion(f32[3,64]{1,0:T(4,128)} %param.2, f32[24,64]{1,0:T(8,128)} %bitcast.5), kind=kLoop, calls=%fused_computation.6 | loop fusion | flops 6144 | bytes 15104 | tf_op jit(solution)/shard_map/concatenate | solution.py:374
  1.4 0.5 collective-permute-start
  1.9 0.8 %collective-permute-done = f32[1,16,128]{2,1,0:T(8,128)S(1)} collective-permute-done((f32[1,16,128]{2,1,0:T(8,128)S(1)}, f32[1,16,128]{2,1,0:T(8,128)S(1)}, u32[]{:S(2)}, u32[]{:S(2)}) %collective-permute-start) | collective-permute-done | bytes 8224 | tf_op jit(solution)/shard_map/ppermute | solution.py:332
  2.7 4.9 %collective-permute-start.1 = (f32[2,16,128]{2,1,0:T(8,128)S(1)}, f32[2,16,128]{2,1,0:T(8,128)S(1)}, u32[]{:S(2)}, u32[]{:S(2)}) collective-permute-start(f32[2,16,128]{2,1,0:T(8,128)S(1)} %pad_maximum_fusion.6.refs_1_), channel_id=1, source_target_pairs={{0,6},{1,13},{2,4},{3,15},{4,2},{5,9},{6,0},{7,11},{8,14},{9,5},{1... | collective-permute-start | bytes 49160 | tf_op jit(solution)/shard_map/ppermute | solution.py:327
  7.7 0.5 %collective-permute-start.2 = (f32[2,16,128]{2,1,0:T(8,128)S(1)}, f32[2,16,128]{2,1,0:T(8,128)S(1)}, u32[]{:S(2)}, u32[]{:S(2)}) collective-permute-start(f32[2,16,128]{2,1,0:T(8,128)S(1)} %pad_maximum_fusion.6.refs_1_), channel_id=1, source_target_pairs={{0,10},{1,5},{2,8},{3,7},{4,14},{5,1},{6,12},{7,3},{8,2},{9,13},{1... | collective-permute-start | bytes 49160 | tf_op jit(solution)/shard_map/ppermute | solution.py:327
  8.1 0.7 %collective-permute-start.6 = (f32[2,16,128]{2,1,0:T(8,128)S(1)}, f32[2,16,128]{2,1,0:T(8,128)S(1)}, u32[]{:S(2)}, u32[]{:S(2)}) collective-permute-start(f32[2,16,128]{2,1,0:T(8,128)S(1)} %pad_maximum_fusion.6.refs_1_), channel_id=1, source_target_pairs={{1,3},{3,1},{5,7},{7,5},{9,11},{11,9},{13,15},{15,13},{17,19},{19,... | collective-permute-start | bytes 49160 | tf_op jit(solution)/shard_map/ppermute | solution.py:327
  8.8 0.6 %collective-permute-done.1.refs_2_ = f32[2,16,128]{2,1,0:T(8,128)S(1)} collective-permute-done((f32[2,16,128]{2,1,0:T(8,128)S(1)}, f32[2,16,128]{2,1,0:T(8,128)S(1)}, u32[]{:S(2)}, u32[]{:S(2)}) %collective-permute-start.1) | collective-permute-done | bytes 16416 | tf_op jit(solution)/shard_map/ppermute | solution.py:327
  9.4 1.7 %collective-permute-start.4 = (f32[4,16,128]{2,1,0:T(8,128)S(1)}, f32[4,16,128]{2,1,0:T(8,128)S(1)}, u32[]{:S(2)}, u32[]{:S(2)}) collective-permute-start(f32[4,16,128]{2,1,0:T(8,128)S(1)} %pad_maximum_fusion.4), channel_id=1, source_target_pairs={{0,8},{1,19},{2,10},{3,17},{4,12},{5,23},{6,14},{7,21},{8,0},{9,27... | collective-permute-start | bytes 98312 | tf_op jit(solution)/shard_map/ppermute | solution.py:327
  11.1 1.2 %collective-permute-done.2.refs_3_ = f32[2,16,128]{2,1,0:T(8,128)S(1)} collective-permute-done((f32[2,16,128]{2,1,0:T(8,128)S(1)}, f32[2,16,128]{2,1,0:T(8,128)S(1)}, u32[]{:S(2)}, u32[]{:S(2)}) %collective-permute-start.2) | collective-permute-done | bytes 16416 | tf_op jit(solution)/shard_map/ppermute | solution.py:327
  12.3 1.5 %collective-permute-start.3 = (f32[6,16,128]{2,1,0:T(8,128)S(1)}, f32[6,16,128]{2,1,0:T(8,128)S(1)}, u32[]{:S(2)}, u32[]{:S(2)}) collective-permute-start(f32[6,16,128]{2,1,0:T(8,128)S(1)} %pad_maximum_fusion.2), channel_id=1, source_target_pairs={{0,16},{1,25},{2,18},{3,27},{4,20},{5,29},{6,22},{7,31},{8,24},{9,... | collective-permute-start | bytes 147464 | tf_op jit(solution)/shard_map/ppermute | solution.py:327
  13.9 0.6 %collective-permute-start.7 = (f32[10,16,128]{2,1,0:T(8,128)S(1)}, f32[10,16,128]{2,1,0:T(8,128)S(1)}, u32[]{:S(2)}, u32[]{:S(2)}) collective-permute-start(f32[10,16,128]{2,1,0:T(8,128)S(1)} %pad_maximum_fusion), channel_id=1, source_target_pairs={{0,1},{1,0},{2,3},{3,2},{4,5},{5,4},{6,7},{7,6},{8,9},{9,8},{10,11... | collective-permute-start | bytes 245768 | tf_op jit(solution)/shard_map/ppermute | solution.py:332
  14.5 0.9 %shard_map.50 = (f32[32,384]{1,0:T(8,128)S(1)}, f32[32,32]{1,0:T(8,128)S(1)}, f32[32,640]{1,0:T(8,128)S(1)}, bf16[384,640]{1,0:T(8,128)(2,1)S(1)}, bf16[384,640]{1,0:T(8,128)(2,1)S(1)}) custom-call(f32[1,16,128]{2,1,0:T(8,128)S(1)} %shard_map.49.refs_0_.own_block, f32[2,16,128]{2,1,0:T(8,128)S(1)} %pad_maximum_fusion.6.refs_1_, ...), custom_call_target="tpu_custom_call" | custom-call | tf_op jit(solution)/shard_map/pallas_call | solution.py:388
  15.4 1.2 %collective-permute-done.3.refs_1_ = f32[6,16,128]{2,1,0:T(8,128)S(1)} collective-permute-done((f32[6,16,128]{2,1,0:T(8,128)S(1)}, f32[6,16,128]{2,1,0:T(8,128)S(1)}, u32[]{:S(2)}, u32[]{:S(2)}) %collective-permute-start.3) | collective-permute-done | bytes 49184 | tf_op jit(solution)/shard_map/ppermute | solution.py:327
  16.6 1.2 %shard_map.51 = (f32[32,384]{1,0:T(8,128)S(1)}, f32[32,32]{1,0:T(8,128)S(1)}, f32[32,1152]{1,0:T(8,128)S(1)}, bf16[384,1152]{1,0:T(8,128)(2,1)S(1)}, bf16[384,1152]{1,0:T(8,128)(2,1)S(1)}) custom-call(f32[1,16,128]{2,1,0:T(8,128)S(1)} %shard_map.49.refs_0_.own_block, f32[6,16,128]{2,1,0:T(8,128)S(1)} %collective-permute-done.3.refs_1_, ...), custom_call_target="tpu_custom_call" | custom-call | tf_op jit(solution)/shard_map/pallas_call | solution.py:388
  17.8 0.8 %shard_map.52 = (f32[1,16,128]{2,1,0:T(8,128)S(1)}, f32[32,32]{1,0:T(8,128)S(1)}, f32[32,384]{1,0:T(8,128)S(1)}, bf16[384,384]{1,0:T(8,128)(2,1)S(1)}, bf16[384,384]{1,0:T(8,128)(2,1)S(1)}) custom-call(f32[1,16,128]{2,1,0:T(8,128)S(1)} %shard_map.49.refs_0_.own_block, f32[6,16,128]{2,1,0:T(8,128)S(1)} %collective-permute-done.5.refs_1_, ...), custom_call_target="tpu_custom_call" | custom-call | tf_op jit(solution)/shard_map/pallas_call | solution.py:388
  18.5 0.5 %collective-permute-start.8 = (f32[1,16,128]{2,1,0:T(8,128)S(1)}, f32[1,16,128]{2,1,0:T(8,128)S(1)}, u32[]{:S(2)}, u32[]{:S(2)}) collective-permute-start(f32[1,16,128]{2,1,0:T(8,128)S(1)} %get-tuple-element.48.image.refs_7_), channel_id=1, source_target_pairs={{0,1},{1,0},{2,3},{3,2},{4,5},{5,4},{6,7},{7,6},{8,9},{9,8},{10,11... | collective-permute-start | bytes 24584 | tf_op jit(solution)/shard_map/ppermute | solution.py:332
  19.0 0.8 %collective-permute-done.8 = f32[1,16,128]{2,1,0:T(8,128)S(1)} collective-permute-done((f32[1,16,128]{2,1,0:T(8,128)S(1)}, f32[1,16,128]{2,1,0:T(8,128)S(1)}, u32[]{:S(2)}, u32[]{:S(2)}) %collective-permute-start.8) | collective-permute-done | bytes 8224 | tf_op jit(solution)/shard_map/ppermute | solution.py:332
  19.9 2.7 %collective-permute-start.9 = (f32[2,16,128]{2,1,0:T(8,128)S(1)}, f32[2,16,128]{2,1,0:T(8,128)S(1)}, u32[]{:S(2)}, u32[]{:S(2)}) collective-permute-start(f32[2,16,128]{2,1,0:T(8,128)S(1)} %constant_dynamic-update-slice_fusion.refs_4_), channel_id=1, source_target_pairs={{0,6},{1,13},{2,4},{3,15},{4,2},{5,9},{6,0},{7,11},{8,14},{9,5},{1... | collective-permute-start | bytes 49160 | tf_op jit(solution)/shard_map/ppermute | solution.py:327
  22.6 0.7 %collective-permute-start.14 = (f32[2,16,128]{2,1,0:T(8,128)S(1)}, f32[2,16,128]{2,1,0:T(8,128)S(1)}, u32[]{:S(2)}, u32[]{:S(2)}) collective-permute-start(f32[2,16,128]{2,1,0:T(8,128)S(1)} %constant_dynamic-update-slice_fusion.refs_4_), channel_id=1, source_target_pairs={{1,3},{3,1},{5,7},{7,5},{9,11},{11,9},{13,15},{15,13},{17,19},{19,... | collective-permute-start | bytes 49160 | tf_op jit(solution)/shard_map/ppermute | solution.py:327
  23.3 2.2 %collective-permute-done.9.refs_5_ = f32[2,16,128]{2,1,0:T(8,128)S(1)} collective-permute-done((f32[2,16,128]{2,1,0:T(8,128)S(1)}, f32[2,16,128]{2,1,0:T(8,128)S(1)}, u32[]{:S(2)}, u32[]{:S(2)}) %collective-permute-start.9) | collective-permute-done | bytes 16416 | tf_op jit(solution)/shard_map/ppermute | solution.py:327
  25.5 1.3 %collective-permute-start.12 = (f32[4,16,128]{2,1,0:T(8,128)S(1)}, f32[4,16,128]{2,1,0:T(8,128)S(1)}, u32[]{:S(2)}, u32[]{:S(2)}) collective-permute-start(f32[4,16,128]{2,1,0:T(8,128)S(1)} %pad_maximum_fusion.5), channel_id=1, source_target_pairs={{0,8},{1,19},{2,10},{3,17},{4,12},{5,23},{6,14},{7,21},{8,0},{9,27... | collective-permute-start | bytes 98312 | tf_op jit(solution)/shard_map/ppermute | solution.py:327
  26.8 0.5 collective-permute-done.10.refs_6_
  27.2 1.4 %collective-permute-start.11 = (f32[6,16,128]{2,1,0:T(8,128)S(1)}, f32[6,16,128]{2,1,0:T(8,128)S(1)}, u32[]{:S(2)}, u32[]{:S(2)}) collective-permute-start(f32[6,16,128]{2,1,0:T(8,128)S(1)} %pad_maximum_fusion.3), channel_id=1, source_target_pairs={{0,16},{1,25},{2,18},{3,27},{4,20},{5,29},{6,22},{7,31},{8,24},{9,... | collective-permute-start | bytes 147464 | tf_op jit(solution)/shard_map/ppermute | solution.py:327
  28.6 0.8 %collective-permute-done.12.refs_7_ = f32[4,16,128]{2,1,0:T(8,128)S(1)} collective-permute-done((f32[4,16,128]{2,1,0:T(8,128)S(1)}, f32[4,16,128]{2,1,0:T(8,128)S(1)}, u32[]{:S(2)}, u32[]{:S(2)}) %collective-permute-start.12) | collective-permute-done | bytes 32800 | tf_op jit(solution)/shard_map/ppermute | solution.py:327
  29.4 0.5 %shard_map.53 = (f32[32,384]{1,0:T(8,128)S(1)}, f32[64,64]{1,0:T(8,128)S(1)}) custom-call(f32[1,16,128]{2,1,0:T(8,128)S(1)} %shard_map.49.refs_0_.own_block, f32[32,640]{1,0:T(8,128)S(1)} %get-tuple-element.49.refs_1_, bf16[384,640]{1,0:T(8,128)(2,1)S(1)} %get-tuple-element.50.refs_2_, bf16[384,640]{1,0:T(8,128)(2,1)S(1)} %get-tuple-element.51.refs_3_, ...), custom_call_target="tpu_custom_call" | custom-call | tf_op jit(solution)/shard_map/pallas_call | solution.py:408
  30.0 1.4 %collective-permute-done.11.refs_4_ = f32[6,16,128]{2,1,0:T(8,128)S(1)} collective-permute-done((f32[6,16,128]{2,1,0:T(8,128)S(1)}, f32[6,16,128]{2,1,0:T(8,128)S(1)}, u32[]{:S(2)}, u32[]{:S(2)}) %collective-permute-start.11) | collective-permute-done | bytes 49184 | tf_op jit(solution)/shard_map/ppermute | solution.py:327
  31.3 0.4 collective-permute-start.13
  31.7 0.3 shard_map.55
  32.0 0.8 %shard_map.54 = (f32[32,384]{1,0:T(8,128)S(1)}, f32[64,64]{1,0:T(8,128)S(1)}) custom-call(f32[1,16,128]{2,1,0:T(8,128)S(1)} %shard_map.49.refs_0_.own_block, f32[32,1152]{1,0:T(8,128)S(1)} %get-tuple-element.55.refs_1_, bf16[384,1152]{1,0:T(8,128)(2,1)S(1)} %get-tuple-element.56.refs_2_, bf16[384,1152]{1,0:T(8,128)(2,1)S(1)} %get-tuple-element.57.refs_3_, ...), custom_call_target="tpu_custom_call" | custom-call | tf_op jit(solution)/shard_map/pallas_call | solution.py:408
  32.9 1.1 %shard_map.56 = (f32[8,256]{1,0:T(8,128)S(1)}, f32[8,256]{1,0:T(8,128)S(1)}, f32[2,8,8]{2,1,0:T(8,128)S(1)}, f32[32,1,64]{2,1,0:T(1,128)S(1)}) custom-call(f32[1,16,128]{2,1,0:T(8,128)S(1)} %shard_map.49.refs_0_.own_block, f32[32,384]{1,0:T(8,128)S(1)} %get-tuple-element.45.refs_1_, bf16[384,384]{1,0:T(8,128)(2,1)S(1)} %get-tuple-element.46.refs_2_, ...), custom_call_target="tpu_custom_call" | custom-call | tf_op jit(solution)/shard_map/pallas_call | solution.py:408
  34.0 10.7 %all_to_all.5.partials = f32[32,1,64]{2,1,0:T(1,128)S(1)} all-to-all(f32[32,1,64]{2,1,0:T(1,128)S(1)} %get-tuple-element.69), channel_id=1, replica_groups=mesh['row'=4,'col'=8] {'row','col'}, dimensions={0} | all-to-all | bytes 16384 | tf_op jit(solution)/shard_map/all_to_all | solution.py:411
  44.7 0.8 %shard_map.57 = (f32[3,8,64]{2,1,0:T(8,128)}, f32[3,8,64]{2,1,0:T(8,128)}, f32[3,8,8]{2,1,0:T(8,128)}) custom-call(f32[8,256]{1,0:T(8,128)S(1)} %get-tuple-element.66.vectors, f32[8,256]{1,0:T(8,128)S(1)} %get-tuple-element.67.shifted, f32[2,8,8]{2,1,0:T(8,128)S(1)} %get-tuple-element.68.both, f32[32,1,64]{2,1,0:T(1,128)S(1)} %all_to_all.5.partials), custom_call_target="tpu_custom_call" | custom-call | tf_op jit(solution)/shard_map/pallas_call | solution.py:412
  (20 shorter events, 0.2 us)
Async XLA Ops:
  1.4 1.3 %collective-permute-start = (f32[1,16,128]{2,1,0:T(8,128)S(1)}, f32[1,16,128]{2,1,0:T(8,128)S(1)}, u32[]{:S(2)}, u32[]{:S(2)}) collective-permute-start(f32[1,16,128]{2,1,0:T(8,128)S(1)} %shard_map.49.refs_0_.own_block), channel_id=1, source_target_pairs={{0,1},{1,0},{2,3},{3,2},{4,5},{5,4},{6,7},{7,6},{8,9},{9,8},{10,11... | collective-permute-start | bytes 24584 | tf_op jit(solution)/shard_map/ppermute | solution.py:332
  2.7 6.7 %collective-permute-start.1 = (f32[2,16,128]{2,1,0:T(8,128)S(1)}, f32[2,16,128]{2,1,0:T(8,128)S(1)}, u32[]{:S(2)}, u32[]{:S(2)}) collective-permute-start(f32[2,16,128]{2,1,0:T(8,128)S(1)} %pad_maximum_fusion.6.refs_1_), channel_id=1, source_target_pairs={{0,6},{1,13},{2,4},{3,15},{4,2},{5,9},{6,0},{7,11},{8,14},{9,5},{1... | collective-permute-start | bytes 49160 | tf_op jit(solution)/shard_map/ppermute | solution.py:327
  7.7 4.6 %collective-permute-start.2 = (f32[2,16,128]{2,1,0:T(8,128)S(1)}, f32[2,16,128]{2,1,0:T(8,128)S(1)}, u32[]{:S(2)}, u32[]{:S(2)}) collective-permute-start(f32[2,16,128]{2,1,0:T(8,128)S(1)} %pad_maximum_fusion.6.refs_1_), channel_id=1, source_target_pairs={{0,10},{1,5},{2,8},{3,7},{4,14},{5,1},{6,12},{7,3},{8,2},{9,13},{1... | collective-permute-start | bytes 49160 | tf_op jit(solution)/shard_map/ppermute | solution.py:327
  8.1 5.7 %collective-permute-start.6 = (f32[2,16,128]{2,1,0:T(8,128)S(1)}, f32[2,16,128]{2,1,0:T(8,128)S(1)}, u32[]{:S(2)}, u32[]{:S(2)}) collective-permute-start(f32[2,16,128]{2,1,0:T(8,128)S(1)} %pad_maximum_fusion.6.refs_1_), channel_id=1, source_target_pairs={{1,3},{3,1},{5,7},{7,5},{9,11},{11,9},{13,15},{15,13},{17,19},{19,... | collective-permute-start | bytes 49160 | tf_op jit(solution)/shard_map/ppermute | solution.py:327
  9.4 4.5 %collective-permute-start.4 = (f32[4,16,128]{2,1,0:T(8,128)S(1)}, f32[4,16,128]{2,1,0:T(8,128)S(1)}, u32[]{:S(2)}, u32[]{:S(2)}) collective-permute-start(f32[4,16,128]{2,1,0:T(8,128)S(1)} %pad_maximum_fusion.4), channel_id=1, source_target_pairs={{0,8},{1,19},{2,10},{3,17},{4,12},{5,23},{6,14},{7,21},{8,0},{9,27... | collective-permute-start | bytes 98312 | tf_op jit(solution)/shard_map/ppermute | solution.py:327
  12.3 4.2 %collective-permute-start.3 = (f32[6,16,128]{2,1,0:T(8,128)S(1)}, f32[6,16,128]{2,1,0:T(8,128)S(1)}, u32[]{:S(2)}, u32[]{:S(2)}) collective-permute-start(f32[6,16,128]{2,1,0:T(8,128)S(1)} %pad_maximum_fusion.2), channel_id=1, source_target_pairs={{0,16},{1,25},{2,18},{3,27},{4,20},{5,29},{6,22},{7,31},{8,24},{9,... | collective-permute-start | bytes 147464 | tf_op jit(solution)/shard_map/ppermute | solution.py:327
  13.9 2.7 %collective-permute-start.7 = (f32[10,16,128]{2,1,0:T(8,128)S(1)}, f32[10,16,128]{2,1,0:T(8,128)S(1)}, u32[]{:S(2)}, u32[]{:S(2)}) collective-permute-start(f32[10,16,128]{2,1,0:T(8,128)S(1)} %pad_maximum_fusion), channel_id=1, source_target_pairs={{0,1},{1,0},{2,3},{3,2},{4,5},{5,4},{6,7},{7,6},{8,9},{9,8},{10,11... | collective-permute-start | bytes 245768 | tf_op jit(solution)/shard_map/ppermute | solution.py:332
  16.5 1.2 %collective-permute-start.5 = (f32[6,16,128]{2,1,0:T(8,128)S(1)}, f32[6,16,128]{2,1,0:T(8,128)S(1)}, u32[]{:S(2)}, u32[]{:S(2)}) collective-permute-start(f32[6,16,128]{2,1,0:T(8,128)S(1)} %collective-permute-done.3.refs_1_), channel_id=1, source_target_pairs={{0,1},{1,0},{2,3},{3,2},{4,5},{5,4},{6,7},{7,6},{8,9},{9,8},{10,11... | collective-permute-start | bytes 147464 | tf_op jit(solution)/shard_map/ppermute | solution.py:332
  18.5 1.3 %collective-permute-start.8 = (f32[1,16,128]{2,1,0:T(8,128)S(1)}, f32[1,16,128]{2,1,0:T(8,128)S(1)}, u32[]{:S(2)}, u32[]{:S(2)}) collective-permute-start(f32[1,16,128]{2,1,0:T(8,128)S(1)} %get-tuple-element.48.image.refs_7_), channel_id=1, source_target_pairs={{0,1},{1,0},{2,3},{3,2},{4,5},{5,4},{6,7},{7,6},{8,9},{9,8},{10,11... | collective-permute-start | bytes 24584 | tf_op jit(solution)/shard_map/ppermute | solution.py:332
  19.9 5.6 %collective-permute-start.9 = (f32[2,16,128]{2,1,0:T(8,128)S(1)}, f32[2,16,128]{2,1,0:T(8,128)S(1)}, u32[]{:S(2)}, u32[]{:S(2)}) collective-permute-start(f32[2,16,128]{2,1,0:T(8,128)S(1)} %constant_dynamic-update-slice_fusion.refs_4_), channel_id=1, source_target_pairs={{0,6},{1,13},{2,4},{3,15},{4,2},{5,9},{6,0},{7,11},{8,14},{9,5},{1... | collective-permute-start | bytes 49160 | tf_op jit(solution)/shard_map/ppermute | solution.py:327
  22.6 4.6 %collective-permute-start.10 = (f32[2,16,128]{2,1,0:T(8,128)S(1)}, f32[2,16,128]{2,1,0:T(8,128)S(1)}, u32[]{:S(2)}, u32[]{:S(2)}) collective-permute-start(f32[2,16,128]{2,1,0:T(8,128)S(1)} %constant_dynamic-update-slice_fusion.refs_4_), channel_id=1, source_target_pairs={{0,10},{1,5},{2,8},{3,7},{4,14},{5,1},{6,12},{7,3},{8,2},{9,13},{1... | collective-permute-start | bytes 49160 | tf_op jit(solution)/shard_map/ppermute | solution.py:327
  22.6 6.0 %collective-permute-start.14 = (f32[2,16,128]{2,1,0:T(8,128)S(1)}, f32[2,16,128]{2,1,0:T(8,128)S(1)}, u32[]{:S(2)}, u32[]{:S(2)}) collective-permute-start(f32[2,16,128]{2,1,0:T(8,128)S(1)} %constant_dynamic-update-slice_fusion.refs_4_), channel_id=1, source_target_pairs={{1,3},{3,1},{5,7},{7,5},{9,11},{11,9},{13,15},{15,13},{17,19},{19,... | collective-permute-start | bytes 49160 | tf_op jit(solution)/shard_map/ppermute | solution.py:327
  25.5 3.9 %collective-permute-start.12 = (f32[4,16,128]{2,1,0:T(8,128)S(1)}, f32[4,16,128]{2,1,0:T(8,128)S(1)}, u32[]{:S(2)}, u32[]{:S(2)}) collective-permute-start(f32[4,16,128]{2,1,0:T(8,128)S(1)} %pad_maximum_fusion.5), channel_id=1, source_target_pairs={{0,8},{1,19},{2,10},{3,17},{4,12},{5,23},{6,14},{7,21},{8,0},{9,27... | collective-permute-start | bytes 98312 | tf_op jit(solution)/shard_map/ppermute | solution.py:327
  27.2 4.1 %collective-permute-start.11 = (f32[6,16,128]{2,1,0:T(8,128)S(1)}, f32[6,16,128]{2,1,0:T(8,128)S(1)}, u32[]{:S(2)}, u32[]{:S(2)}) collective-permute-start(f32[6,16,128]{2,1,0:T(8,128)S(1)} %pad_maximum_fusion.3), channel_id=1, source_target_pairs={{0,16},{1,25},{2,18},{3,27},{4,20},{5,29},{6,22},{7,31},{8,24},{9,... | collective-permute-start | bytes 147464 | tf_op jit(solution)/shard_map/ppermute | solution.py:327
  29.4 2.6 %collective-permute-start.15 = (f32[10,16,128]{2,1,0:T(8,128)S(1)}, f32[10,16,128]{2,1,0:T(8,128)S(1)}, u32[]{:S(2)}, u32[]{:S(2)}) collective-permute-start(f32[10,16,128]{2,1,0:T(8,128)S(1)} %pad_maximum_fusion.1), channel_id=1, source_target_pairs={{0,1},{1,0},{2,3},{3,2},{4,5},{5,4},{6,7},{7,6},{8,9},{9,8},{10,11... | collective-permute-start | bytes 245768 | tf_op jit(solution)/shard_map/ppermute | solution.py:332
  31.3 1.5 %collective-permute-start.13 = (f32[6,16,128]{2,1,0:T(8,128)S(1)}, f32[6,16,128]{2,1,0:T(8,128)S(1)}, u32[]{:S(2)}, u32[]{:S(2)}) collective-permute-start(f32[6,16,128]{2,1,0:T(8,128)S(1)} %collective-permute-done.11.refs_4_), channel_id=1, source_target_pairs={{0,1},{1,0},{2,3},{3,2},{4,5},{5,4},{6,7},{7,6},{8,9},{9,8},{10,11... | collective-permute-start | bytes 147464 | tf_op jit(solution)/shard_map/ppermute | solution.py:332

commit v8 on v7

--- a/solution.py
+++ b/solution.py
@@ -13,13 +13,25 @@
 BF16 = jnp.bfloat16
 
 
-def pack_kernel(rows, blocks):
-    beads = rows.shape[1]
-    vecs = blocks.shape[1] // 2
-    upper = jnp.concatenate([rows[:vecs], rows[vecs : 2 * vecs]], axis=1)
-    lower = jnp.concatenate([rows[2 * vecs : 3 * vecs], rows[3 * vecs :]], axis=1)
-    blocks[:, :vecs] = jnp.broadcast_to(upper[None], (blocks.shape[0], vecs, 2 * beads))
-    blocks[:, vecs:] = jnp.broadcast_to(lower[None], (blocks.shape[0], vecs, 2 * beads))
+def halves(block):
+    beads = block.shape[1] // 4
+    middle = beads // 2
+    parts = [block[:, part * beads : (part + 1) * beads] for part in range(4)]
+    first = jnp.concatenate([part[:, :middle] for part in parts], axis=1)
+    second = jnp.concatenate([part[:, middle:] for part in parts], axis=1)
+    return first, second
+
+
+def copy_halves(block, copies):
+    for core, half in enumerate(halves(block)):
+        copies[:, core] = jnp.broadcast_to(half[None], (copies.shape[0],) + half.shape)
+
+
+def pack_kernel(rows, block, copies):
+    vecs = block.shape[0]
+    flat = jnp.concatenate([rows[part * vecs : (part + 1) * vecs] for part in range(4)], axis=1)
+    block[...] = flat
+    copy_halves(flat, copies)
 
 
 def split_two(value):
@@ -40,23 +52,20 @@
     return total
 
 
-def unpack(arrays, wide, beads):
-    blocks = [(array, index) for array in arrays for index in range(array.shape[0])]
-    for at in range(0, len(blocks), 2):
-        one, two = [array[index] for array, index in blocks[at : at + 2]]
-        half = one.shape[0] // 2
-        lanes = pl.ds(at * beads, 2 * beads)
+def unpack(blocks, wide):
+    count, vecs, lanes = blocks.shape
+    width = lanes // 4
+    for at in range(0, count, 4):
+        four = [blocks[at + index] for index in range(4)]
         for part in range(4):
-            rows = slice(part // 2 * half, (part // 2 + 1) * half)
-            side = slice(part % 2 * beads, (part % 2 + 1) * beads)
-            wide[part * half : (part + 1) * half, lanes] = jnp.concatenate(
-                [one[rows, side], two[rows, side]], axis=1
+            wide[part * vecs : (part + 1) * vecs, pl.ds(at * width, 4 * width)] = jnp.concatenate(
+                [block[:, part * width : (part + 1) * width] for block in four], axis=1
             )
 
 
 def target_columns(own):
-    beads = own.shape[1] // 2
-    targets = own[8:16, beads:].T
+    beads = own.shape[1] // 4
+    targets = own[:, 3 * beads :].T
     return [jnp.broadcast_to(targets[:, axis : axis + 1], (beads, 128)) for axis in range(3)]
 
 
@@ -105,20 +114,16 @@
     return first[:half] + first[half:] + matmul_nt(both[:half], both[half:])
 
 
-def assemble(products, image):
-    beads = image.shape[1] // 2
+def assemble(products):
+    beads = products.shape[1] // 6
 
     def part(row, component):
         return products[8 * row : 8 * row + 8, component * beads : (component + 1) * beads]
 
-    image[...] = jnp.zeros(image.shape, F32)
-    image[:8, :beads] = part(0, 0) + part(1, 1) + part(2, 2)
-    image[:8, beads:] = part(0, 1) + part(1, 3) + part(2, 4)
-    image[8:, :beads] = part(0, 2) + part(1, 4) + part(2, 5)
-
-
-def flat(block):
-    return jnp.concatenate([block[:8], block[8:]], axis=1)
+    x = part(0, 0) + part(1, 1) + part(2, 2)
+    y = part(0, 1) + part(1, 3) + part(2, 4)
+    z = part(0, 2) + part(1, 4) + part(2, 5)
+    return jnp.concatenate([x, y, z, jnp.zeros(x.shape, F32)], axis=1)
 
 
 def block_sum(matrix, row, column):
@@ -158,22 +163,23 @@
     )
 
 
-def first_stage(count, earlier, last, *refs):
+def first_stage(last, own, blocks, *refs):
     refs = list(refs)
-    own_ref, blocks, refs = refs[0], refs[1 : count + 1], refs[count + 1 :]
-    before, refs = refs[: 2 * earlier], refs[2 * earlier :]
-    out, gram, wide, high, low = refs[:5]
-    own = own_ref[0]
-    unpack(blocks, wide, own.shape[1] // 2)
-    products, grams = first_product(own, wide, high, low)
-    if earlier:
-        products, grams = products + before[0][...], grams + before[1][...]
-    gram[...] = grams
     if last:
-        assemble(products, refs[5])
-        out[0] = refs[5][...]
+        before, refs = refs[:2], refs[2:]
+        image, copies = refs[:2]
     else:
-        out[...] = products
+        products_out, copies = refs[0], None
+    gram, wide, high, low = refs[2:6] if last else refs[1:5]
+    unpack(blocks, wide)
+    products, grams = first_product(own[...], wide, high, low)
+    if not last:
+        products_out[...], gram[...] = products, grams
+        return
+    gram[...] = grams + before[1][...]
+    block = assemble(products + before[0][...])
+    image[...] = block
+    copy_halves(block, copies)
 
 
 def cholesky(matrix):
@@ -211,10 +217,10 @@
     return factor_t, inverse
 
 
-def start_kernel(size, image, own_block, gram, small, own_first, own_moved):
+def start_kernel(size, image, own, gram, small, own_first, own_moved):
     _, inverse = cholesky(block_sum(gram[...], 0, 0) / size)
-    own_first[...] = small_matmul(inverse, flat(own_block[0]))
-    own_moved[...] = small_matmul(inverse, flat(image[0]))
+    own_first[...] = small_matmul(inverse, own[...])
+    own_moved[...] = small_matmul(inverse, image[...])
     small[0] = inverse
     small[1] = inverse.T
 
@@ -232,40 +238,35 @@
     return products, grams
 
 
-def second_stage(size, count, earlier, last, fill, *refs):
+def second_stage(size, last, fill, own, wide, *refs):
     refs = list(refs)
-    own_ref, wide, refs = refs[0], refs[1], refs[2:]
     if not fill:
         (high, low), refs = refs[:2], refs[2:]
-    images, refs = refs[:count], refs[count:]
-    before, refs = refs[: 2 * earlier], refs[2 * earlier :]
+    images, refs = refs[0], refs[1:]
     if last:
-        (own_image, own_first, own_moved, small), refs = refs[:4], refs[4:]
+        (before, before_gram, own_image, own_first, own_moved, small), refs = refs[:6], refs[6:]
     outs, refs = refs[: 4 if last else 2], refs[4 if last else 2 :]
     if fill:
         (high, low), refs = refs[:2], refs[2:]
     wide_image = refs[0]
-    own = own_ref[0]
-    beads = own.shape[1] // 2
-    unpack(images, wide_image, beads)
-    products, grams = second_product(fill, own, wide, wide_image, high, low)
-    if earlier:
-        products, grams = products + before[0][...], grams + before[1][...]
+    beads = own.shape[1] // 4
+    unpack(images, wide_image)
+    products, grams = second_product(fill, own[...], wide, wide_image, high, low)
     if not last:
         outs[0][...], outs[1][...] = products, grams
         return
     vectors_out, shifted, coefficients, partials = outs
-    grams = grams / size
+    products = products + before[...]
+    grams = (grams + before_gram[...]) / size
     inverse_zero, inverse_zero_t = small[0], small[1]
     cross_t = small_matmul(inverse_zero, block_sum(grams, 0, 32))
     cross = small_matmul(block_sum(grams, 32, 0), inverse_zero_t)
     factor_t, inverse = cholesky(block_sum(grams, 32, 32) - small_matmul(cross, cross_t))
     alpha = small_matmul(cross_t, inverse_zero_t)
     factor_one_t = small_matmul(factor_t, inverse_zero_t)
-    assemble(products, refs[1])
     first, moved = own_first[...], own_moved[...]
-    vectors = small_matmul(inverse, flat(own_image[0]) - small_matmul(cross, first))
-    shift = small_matmul(inverse, flat(refs[1][...]) - small_matmul(cross, moved))
+    vectors = small_matmul(inverse, own_image[...] - small_matmul(cross, first))
+    shift = small_matmul(inverse, assemble(products) - small_matmul(cross, moved))
     shift = shift - small_matmul(factor_one_t, first)
     valid = lax.broadcasted_iota(jnp.int32, vectors.shape, 1) < 3 * beads
     vectors = jnp.where(valid, vectors, 0.0)
@@ -316,98 +317,49 @@
     )
 
 
-def exchange(block, first, second):
-    rows, cols = lax.axis_size("row"), lax.axis_size("col")
-    layers = cols // 2
-    pairs = []
-    for chip in range(rows * layers):
-        for core, offset in enumerate((first, second)):
-            if offset is not None:
-                pairs.append((2 * chip + core, 2 * (chip ^ offset) + core))
-    return lax.ppermute(block, ("row", "col"), pairs)
-
-
-def between_cores(block):
+def gather(copies):
+    mine = lax.all_to_all(copies.reshape((-1,) + copies.shape[2:]), ("row", "col"), 0, 0, tiled=True)
     cols = lax.axis_size("col")
-    return lax.ppermute(block, "col", [(col, col ^ 1) for col in range(cols)])
-
-
-ROWS, LAYERS = 4, 4
-ALONE = 1
-OFFSETS = ((3, 6), (5, 2), (4, 9), (8, 12))
-
-
-def spread(block, use):
-    rows, cols = lax.axis_size("row"), lax.axis_size("col")
-    if (rows, cols) == (ROWS, 2 * LAYERS):
-        pair = jnp.concatenate([block, between_cores(block)], axis=0)
-        one = exchange(pair, *OFFSETS[0])
-        alone = exchange(pair, None, ALONE)
-        two = exchange(pair, *OFFSETS[1])
-        three = exchange(jnp.concatenate([pair, one], axis=0), *OFFSETS[2])
-        four = exchange(jnp.concatenate([pair, one, two], axis=0), *OFFSETS[3])
-        siblings = between_cores(jnp.concatenate([alone, one, two, three], axis=0))
-        used = use(0, False, [pair, one, two, three])
-        four, used = lax.optimization_barrier((four, used))
-        last = between_cores(four)
-        used = use(1, False, [four, alone, siblings], *used)
-        return use(2, True, [last], *used)
-    groups = [[row * cols + col for row in range(rows) for col in range(core, cols, 2)] for core in range(2)]
-    copies = jnp.broadcast_to(block, (rows * cols // 2,) + block.shape[1:])
-    mine = lax.all_to_all(copies, ("row", "col"), 0, 0, axis_index_groups=groups, tiled=True)
-    other = between_cores(mine)
-    return use(1, True, [other], *use(0, False, [mine]))
+    return mine, lax.ppermute(mine, "col", [(col, col ^ 1) for col in range(cols)])
 
 
 def local(positions, noise):
     vecs, _, beads = noise.shape
     devices = lax.axis_size("row") * lax.axis_size("col")
+    total = beads * devices // 2
     size = 3.0 * beads * devices
-    keep = 2 * 2 * 6 * beads * beads * devices <= KEPT
-    block = array(1, 2 * vecs, 2 * beads)
-    held_block = pltpu.VMEM((2 * vecs, 2 * beads), F32)
+    keep = 2 * 2 * 2 * 6 * beads * total <= KEPT
+    width = total if keep else min(total, CHUNK)
+    block = array(vecs, 4 * beads)
+    copies = array(devices // 2, 2, vecs, 2 * beads)
     products = array(4 * vecs, 6 * beads)
-    flat_block = array(vecs, 4 * beads)
     small_gram, large_gram = array(4 * vecs, 4 * vecs), array(8 * vecs, 8 * vecs)
+    wide, held_wide = array(4 * vecs, total), pltpu.VMEM((4 * vecs, total), F32)
+    kept = [array(6 * beads, width, dtype=BF16)] * 2 if keep else []
+    held = [] if keep else [pltpu.VMEM((6 * beads, width), BF16)] * 2
 
     rows = noise.transpose(1, 0, 2).reshape(3 * vecs, beads)
     rows = jnp.concatenate([rows, jnp.pad(positions, ((0, vecs - 3), (0, 0)))], axis=0)
-    own = call(pack_kernel, block)(rows)
-    kept = {}
-
-    def use_first(index, last, blocks, *before):
-        total = beads * sum(item.shape[0] for item in blocks)
-        shape = (6 * beads, total if keep else min(total, CHUNK))
-        kernel = functools.partial(first_stage, len(blocks), index > 0, last)
-        outs = [block if last else products, small_gram, array(4 * vecs, total)]
-        scratch = [held_block] if last else []
-        if keep:
-            outs = outs + [array(*shape, dtype=BF16)] * 2
-        else:
-            scratch = [pltpu.VMEM(shape, BF16)] * 2 + scratch
-        *before, wide, high, low = (list(call(kernel, outs, scratch)(own, *blocks, *before)) + [None, None])[:5]
-        kept[index] = (wide, high, low) if keep else (wide,)
-        return before
-
-    image, gram = spread(own, use_first)
+    own, own_copies = call(pack_kernel, [block, copies])(rows)
+    one, two = gather(own_copies)
+    partial, gram, one_wide, *one_tensor = call(
+        functools.partial(first_stage, False), [products, small_gram, wide] + kept, held
+    )(own, one)
+    image, images, gram, two_wide, *two_tensor = call(
+        functools.partial(first_stage, True), [block, copies, small_gram, wide] + kept, held
+    )(own, two, partial, gram)
+    one, two = gather(images)
     small, own_first, own_moved = call(
-        functools.partial(start_kernel, size), [array(2, vecs, vecs), flat_block, flat_block]
+        functools.partial(start_kernel, size), [array(2, vecs, vecs), block, block]
     )(image, own, gram)
-
-    def use_second(index, last, blocks, *before):
-        total = beads * sum(item.shape[0] for item in blocks)
-        kernel = functools.partial(second_stage, size, len(blocks), index > 0, last, not keep)
-        outs, ins = [products, large_gram], []
-        scratch = [pltpu.VMEM((4 * vecs, total), F32)]
-        if last:
-            outs = [flat_block, flat_block, array(2, vecs, vecs), array(devices, 1, vecs * vecs)]
-            ins = [image, own_first, own_moved, small]
-            scratch = scratch + [held_block]
-        if not keep:
-            scratch = [pltpu.VMEM((6 * beads, min(total, CHUNK)), BF16)] * 2 + scratch
-        return call(kernel, outs, scratch)(own, *kept[index], *blocks, *before, *ins)
-
-    vectors, shifted, both, partials = spread(image, use_second)
+    partial, gram = call(
+        functools.partial(second_stage, size, False, not keep), [products, large_gram], held + [held_wide]
+    )(own, one_wide, *one_tensor, one)
+    vectors, shifted, both, partials = call(
+        functools.partial(second_stage, size, True, not keep),
+        [block, block, array(2, vecs, vecs), array(devices, 1, vecs * vecs)],
+        held + [held_wide],
+    )(own, two_wide, *two_tensor, two, partial, gram, image, own_first, own_moved, small)
     partials = lax.all_to_all(partials, ("row", "col"), 0, 0, tiled=True)
     basis, residual, coefficients = call(
         functools.partial(last_kernel, size),

time: 45.8 us -> 42.2 us (0.921)
  blocking collectives: 10.7 us -> 34 us
  starting transfers between devices: 17.3 us -> 0.63 us
  waiting for transfers between devices: 9.49 us -> 0.03 us
  Pallas kernels: 6.52 us -> 5.86 us
    all_to_all x0 -> x2, blocking collectives: none -> 25.2 us  [gather(): lax.all_to_all(copies.reshape((-1,) + copies.shape[2:]), ('row', 'col'),...]
    ppermute x16 -> x2, starting transfers between devices: 17.3 us -> 0.63 us  [gather(): lax.ppermute(mine, 'col', [(col, col ^ 1) for col in range(cols)])]
    ppermute x16 -> x2, waiting for transfers between devices: 9.49 us -> 0.03 us  [gather(): lax.ppermute(mine, 'col', [(col, col ^ 1) for col in range(cols)])]
    all_to_all x1, blocking collectives: 10.7 us -> 8.84 us  [local(): partials = lax.all_to_all(partials, ('row', 'col'), 0, 0, tiled=True)]
    pallas_call x8 -> x6, Pallas kernels: 5.72 us -> 5.06 us  [the longest x1 1.41 us: local(): call(functools.partial(first_stage, True), [block, copies, small_gram, wi...]
  transfers between devices with their start and end apart: 16 -> 2, of which waited for: 9 -> 0; matrix products, arithmetic and copies ran while one was open for 0% -> 0% of each run, Pallas kernels for 8% -> 5%
where the time goes in v8:
time: 42.2 us; the launch traced here: 41.9 us
  blocking collectives  34 us (81%)
  Pallas kernels  5.86 us (14%)
  other arithmetic  0.73 us (2%)
  between operations  0.66 us (2%)
  starting transfers between devices  0.63 us (1%)
    all_to_all x2, blocking collectives, gather(): lax.all_to_all(copies.reshape((-1,) + copies.shape[2:]), ('row', 'col'),...  25.2 us
    all_to_all x1, blocking collectives, local(): partials = lax.all_to_all(partials, ('row', 'col'), 0, 0, tiled=True)  8.84 us
    pallas_call x1, Pallas kernels, local(): call(functools.partial(first_stage, True), [block, copies, small_gram, wi...  1.41 us
    pallas_call x1, Pallas kernels, local(): call(functools.partial(second_stage, size, True, not keep), [block, block...  1.25 us
    pallas_call x1, Pallas kernels, local(): call(functools.partial(first_stage, False), [products, small_gram, wide]...  1.21 us
  transfers between devices with their start and end apart: 2, of which 0 were waited for; matrix products, arithmetic and copies ran while one was open for 0% of the time, Pallas kernels for 5%

profile of v8, /device:TPU:0, one launch (start us, length us, event | category | flops | bytes accessed | tf_op | source)
XLA Modules:
  0.0 41.9 jit_solution(6379471701158616609)
XLA Ops:
  0.6 0.7 %select_maximum_fusion.rows = f32[32,64]{1,0:T(8,128)S(1)} fusion(f32[3,64]{1,0:T(4,128)} %param.2, f32[24,64]{1,0:T(8,128)} %bitcast.9), kind=kLoop, calls=%fused_computation | loop fusion | flops 6144 | bytes 15104 | tf_op jit(solution)/shard_map/concatenate | solution.py:342
  1.4 0.1 shard_map.49
  1.5 15.3 %all_to_all.15.blocks = f32[32,8,128]{2,1,0:T(8,128)S(1)} all-to-all(f32[32,8,128]{2,1,0:T(8,128)S(1)} %bitcast.8), channel_id=1, replica_groups=mesh['row'=4,'col'=8] {'row','col'}, dimensions={0} | all-to-all | bytes 262144 | tf_op jit(solution)/shard_map/all_to_all | solution.py:321
  16.8 0.3 collective-permute-start
  17.1 1.2 %shard_map.50 = (f32[32,384]{1,0:T(8,128)S(1)}, f32[32,32]{1,0:T(8,128)S(1)}, f32[32,1024]{1,0:T(8,128)S(1)}, bf16[384,1024]{1,0:T(8,128)(2,1)S(1)}, bf16[384,1024]{1,0:T(8,128)(2,1)S(1)}) custom-call(f32[8,256]{1,0:T(8,128)S(1)} %get-tuple-element.28.own, f32[32,8,128]{2,1,0:T(8,128)S(1)} %all_to_all.15.blocks), custom_call_target="tpu_custom_call" | custom-call | tf_op jit(solution)/shard_map/pallas_call | solution.py:345
  18.3 0.0 collective-permute-done.blocks
  18.4 1.4 %shard_map.51 = (f32[8,256]{1,0:T(8,128)S(1)}, f32[16,2,8,128]{3,2,1,0:T(8,128)S(1)}, f32[32,32]{1,0:T(8,128)S(1)}, f32[32,1024]{1,0:T(8,128)S(1)}, bf16[384,102...) custom-call(f32[8,256]{1,0:T(8,128)S(1)} %get-tuple-element.28.own, f32[32,8,128]{2,1,0:T(8,128)S(1)} %collective-permute-done.blocks, ...), custom_call_target="tpu_custom_call" | custom-call | tf_op jit(solution)/shard_map/pallas_call | solution.py:348
  19.8 9.9 %all_to_all.16.refs_2_ = f32[32,8,128]{2,1,0:T(8,128)S(1)} all-to-all(f32[32,8,128]{2,1,0:T(8,128)S(1)} %bitcast.7), channel_id=1, replica_groups=mesh['row'=4,'col'=8] {'row','col'}, dimensions={0} | all-to-all | bytes 262144 | tf_op jit(solution)/shard_map/all_to_all | solution.py:321
  29.6 0.3 collective-permute-start.1
  30.0 0.3 shard_map.53
  30.3 0.7 %shard_map.52 = (f32[32,384]{1,0:T(8,128)S(1)}, f32[64,64]{1,0:T(8,128)S(1)}) custom-call(f32[8,256]{1,0:T(8,128)S(1)} %get-tuple-element.28.own, f32[32,1024]{1,0:T(8,128)S(1)} %get-tuple-element.36.wide, bf16[384,1024]{1,0:T(8,128)(2,1)S(1)} %get-tuple-element.37.refs_0_, bf16[384,1024]{1,0:T(8,128)(2,1)S(1)} %get-tuple-element.38.refs_1_, ...), custom_call_target="tpu_custom_call" | custom-call | tf_op jit(solution)/shard_map/pallas_call | solution.py:355
  31.0 0.0 collective-permute-done.1.refs_2_
  31.0 1.2 %shard_map.54 = (f32[8,256]{1,0:T(8,128)S(1)}, f32[8,256]{1,0:T(8,128)S(1)}, f32[2,8,8]{2,1,0:T(8,128)S(1)}, f32[32,1,64]{2,1,0:T(1,128)S(1)}) custom-call(f32[8,256]{1,0:T(8,128)S(1)} %get-tuple-element.28.own, f32[32,1024]{1,0:T(8,128)S(1)} %get-tuple-element.32.wide, bf16[384,1024]{1,0:T(8,128)(2,1)S(1)} %get-tuple-element.33.refs_0_, ...), custom_call_target="tpu_custom_call" | custom-call | tf_op jit(solution)/shard_map/pallas_call | solution.py:358
  32.3 8.8 %all_to_all.17.partials = f32[32,1,64]{2,1,0:T(1,128)S(1)} all-to-all(f32[32,1,64]{2,1,0:T(1,128)S(1)} %get-tuple-element.49), channel_id=1, replica_groups=mesh['row'=4,'col'=8] {'row','col'}, dimensions={0} | all-to-all | bytes 16384 | tf_op jit(solution)/shard_map/all_to_all | solution.py:363
  41.1 0.8 %shard_map.55 = (f32[3,8,64]{2,1,0:T(8,128)}, f32[3,8,64]{2,1,0:T(8,128)}, f32[3,8,8]{2,1,0:T(8,128)}) custom-call(f32[8,256]{1,0:T(8,128)S(1)} %get-tuple-element.46.vectors, f32[8,256]{1,0:T(8,128)S(1)} %get-tuple-element.47.shifted, f32[2,8,8]{2,1,0:T(8,128)S(1)} %get-tuple-element.48.both, f32[32,1,64]{2,1,0:T(1,128)S(1)} %all_to_all.17.partials), custom_call_target="tpu_custom_call" | custom-call | tf_op jit(solution)/shard_map/pallas_call | solution.py:364
Async XLA Ops:
  16.8 1.5 %collective-permute-start = (f32[32,8,128]{2,1,0:T(8,128)S(1)}, f32[32,8,128]{2,1,0:T(8,128)S(1)}, u32[]{:S(2)}, u32[]{:S(2)}) collective-permute-start(f32[32,8,128]{2,1,0:T(8,128)S(1)} %all_to_all.15.blocks), channel_id=1, source_target_pairs={{0,1},{1,0},{2,3},{3,2},{4,5},{5,4},{6,7},{7,6},{8,9},{9,8},{10,11... | collective-permute-start | bytes 393224 | tf_op jit(solution)/shard_map/ppermute | solution.py:323
  29.6 1.4 %collective-permute-start.1 = (f32[32,8,128]{2,1,0:T(8,128)S(1)}, f32[32,8,128]{2,1,0:T(8,128)S(1)}, u32[]{:S(2)}, u32[]{:S(2)}) collective-permute-start(f32[32,8,128]{2,1,0:T(8,128)S(1)} %all_to_all.16.refs_2_), channel_id=1, source_target_pairs={{0,1},{1,0},{2,3},{3,2},{4,5},{5,4},{6,7},{7,6},{8,9},{9,8},{10,11... | collective-permute-start | bytes 393224 | tf_op jit(solution)/shard_map/ppermute | solution.py:323

commit v9 on v8

--- a/solution.py
+++ b/solution.py
@@ -71,29 +71,32 @@
 
 def fill_tensor(columns, wide, start, high, low, at):
     beads = columns[0].shape[0]
-    sources = pl.ds(start, 128)
+    block = 32 if beads % 32 == 0 else beads
+    sources = [wide[24 + axis : 25 + axis, pl.ds(start, 128)] for axis in range(3)]
     to = pl.ds(at, 128)
-    moved = [columns[axis] - wide[24 + axis : 25 + axis, sources] for axis in range(3)]
-    square = moved[0] * moved[0] + moved[1] * moved[1] + moved[2] * moved[2]
-    square = jnp.maximum(square, 1e-12)
-    inverse = lax.rsqrt(square)
-    inverse_sq = inverse * inverse
-    near = square < 4.0
-    iso = inverse * jnp.where(near, square * (inverse - 9.0 / 32.0), 0.75 + 0.5 * inverse_sq)
-    along = inverse * jnp.where(near, 3.0 / 32.0, inverse_sq * (0.75 - 1.5 * inverse_sq))
-    scaled = [along * item for item in moved]
-    parts = [
-        iso + scaled[0] * moved[0],
-        scaled[0] * moved[1],
-        scaled[0] * moved[2],
-        iso + scaled[1] * moved[1],
-        scaled[1] * moved[2],
-        iso + scaled[2] * moved[2],
-    ]
-    for part, value in enumerate(parts):
-        upper, lower = split_two(value)
-        high[part * beads : (part + 1) * beads, to] = upper
-        low[part * beads : (part + 1) * beads, to] = lower
+    for row in range(0, beads, block):
+        moved = [columns[axis][row : row + block] - sources[axis] for axis in range(3)]
+        square = moved[0] * moved[0] + moved[1] * moved[1] + moved[2] * moved[2]
+        square = jnp.maximum(square, 1e-12)
+        inverse = lax.rsqrt(square)
+        inverse_sq = inverse * inverse
+        near = square < 4.0
+        iso = inverse * jnp.where(near, square * (inverse - 9.0 / 32.0), 0.75 + 0.5 * inverse_sq)
+        along = inverse * jnp.where(near, 3.0 / 32.0, inverse_sq * (0.75 - 1.5 * inverse_sq))
+        scaled = [along * item for item in moved]
+        parts = [
+            iso + scaled[0] * moved[0],
+            scaled[0] * moved[1],
+            scaled[0] * moved[2],
+            iso + scaled[1] * moved[1],
+            scaled[1] * moved[2],
+            iso + scaled[2] * moved[2],
+        ]
+        for part, value in enumerate(parts):
+            upper, lower = split_two(value)
+            rows = slice(part * beads + row, part * beads + row + block)
+            high[rows, to] = upper
+            low[rows, to] = lower
 
 
 def apply_tensor(both, high, low, at, step):
@@ -271,11 +274,12 @@
     valid = lax.broadcasted_iota(jnp.int32, vectors.shape, 1) < 3 * beads
     vectors = jnp.where(valid, vectors, 0.0)
     shift = jnp.where(valid, shift, 0.0)
-    partial = matmul_nt(vectors, shift, lax.Precision.HIGHEST)
-    for row in range(8):
-        partials[:, :, 8 * row : 8 * row + 8] = jnp.broadcast_to(
-            partial[row : row + 1][None], (partials.shape[0], 1, 8)
-        )
+    (vector_high, vector_low), (shift_high, shift_low) = split_two(vectors), split_two(shift)
+    partial = matmul_nt(vector_high, shift_high) + (
+        matmul_nt(vector_high, shift_low) + matmul_nt(vector_low, shift_high)
+    )
+    line = jnp.concatenate([partial[row : row + 1] for row in range(8)], axis=1)
+    partials[...] = jnp.broadcast_to(line[None], partials.shape)
     vectors_out[...] = vectors
     shifted[...] = shift
     coefficients[0] = alpha

time: 42.2 us -> 42.1 us (level)
  no operation moved by 1% of the time
where the time goes in v9:
time: 42.1 us; the launch traced here: 41.9 us
  blocking collectives  34 us (81%)
  Pallas kernels  5.83 us (14%)
  other arithmetic  0.73 us (2%)
  between operations  0.66 us (2%)
  starting transfers between devices  0.63 us (1%)
    all_to_all x2, blocking collectives, gather(): lax.all_to_all(copies.reshape((-1,) + copies.shape[2:]), ('row', 'col'),...  25.2 us
    all_to_all x1, blocking collectives, local(): partials = lax.all_to_all(partials, ('row', 'col'), 0, 0, tiled=True)  8.84 us
    pallas_call x1, Pallas kernels, local(): call(functools.partial(first_stage, True), [block, copies, small_gram, wi...  1.4 us
    pallas_call x1, Pallas kernels, local(): call(functools.partial(first_stage, False), [products, small_gram, wide]...  1.22 us
    pallas_call x1, Pallas kernels, local(): call(functools.partial(second_stage, size, True, not keep), [block, block...  1.22 us
  transfers between devices with their start and end apart: 2, of which 0 were waited for; matrix products, arithmetic and copies ran while one was open for 0% of the time, Pallas kernels for 5%

profile of v9, /device:TPU:0, one launch (start us, length us, event | category | flops | bytes accessed | tf_op | source)
XLA Modules:
  0.0 41.9 jit_solution(786268634196571982)
XLA Ops:
  0.6 0.7 %select_maximum_fusion.rows = f32[32,64]{1,0:T(8,128)S(1)} fusion(f32[3,64]{1,0:T(4,128)} %param.2, f32[24,64]{1,0:T(8,128)} %bitcast.9), kind=kLoop, calls=%fused_computation | loop fusion | flops 6144 | bytes 15104 | tf_op jit(solution)/shard_map/concatenate | solution.py:346
  1.4 0.1 shard_map.49
  1.5 15.3 %all_to_all.15.blocks = f32[32,8,128]{2,1,0:T(8,128)S(1)} all-to-all(f32[32,8,128]{2,1,0:T(8,128)S(1)} %bitcast.8), channel_id=1, replica_groups=mesh['row'=4,'col'=8] {'row','col'}, dimensions={0} | all-to-all | bytes 262144 | tf_op jit(solution)/shard_map/all_to_all | solution.py:325
  16.8 0.3 collective-permute-start
  17.1 1.2 %shard_map.50 = (f32[32,384]{1,0:T(8,128)S(1)}, f32[32,32]{1,0:T(8,128)S(1)}, f32[32,1024]{1,0:T(8,128)S(1)}, bf16[384,1024]{1,0:T(8,128)(2,1)S(1)}, bf16[384,1024]{1,0:T(8,128)(2,1)S(1)}) custom-call(f32[8,256]{1,0:T(8,128)S(1)} %get-tuple-element.28.own, f32[32,8,128]{2,1,0:T(8,128)S(1)} %all_to_all.15.blocks), custom_call_target="tpu_custom_call" | custom-call | tf_op jit(solution)/shard_map/pallas_call | solution.py:349
  18.3 0.0 collective-permute-done.blocks
  18.4 1.4 %shard_map.51 = (f32[8,256]{1,0:T(8,128)S(1)}, f32[16,2,8,128]{3,2,1,0:T(8,128)S(1)}, f32[32,32]{1,0:T(8,128)S(1)}, f32[32,1024]{1,0:T(8,128)S(1)}, bf16[384,102...) custom-call(f32[8,256]{1,0:T(8,128)S(1)} %get-tuple-element.28.own, f32[32,8,128]{2,1,0:T(8,128)S(1)} %collective-permute-done.blocks, ...), custom_call_target="tpu_custom_call" | custom-call | tf_op jit(solution)/shard_map/pallas_call | solution.py:352
  19.8 9.9 %all_to_all.16.refs_2_ = f32[32,8,128]{2,1,0:T(8,128)S(1)} all-to-all(f32[32,8,128]{2,1,0:T(8,128)S(1)} %bitcast.7), channel_id=1, replica_groups=mesh['row'=4,'col'=8] {'row','col'}, dimensions={0} | all-to-all | bytes 262144 | tf_op jit(solution)/shard_map/all_to_all | solution.py:325
  29.7 0.3 collective-permute-start.1
  30.0 0.3 shard_map.53
  30.3 0.7 %shard_map.52 = (f32[32,384]{1,0:T(8,128)S(1)}, f32[64,64]{1,0:T(8,128)S(1)}) custom-call(f32[8,256]{1,0:T(8,128)S(1)} %get-tuple-element.28.own, f32[32,1024]{1,0:T(8,128)S(1)} %get-tuple-element.36.wide, bf16[384,1024]{1,0:T(8,128)(2,1)S(1)} %get-tuple-element.37.refs_0_, bf16[384,1024]{1,0:T(8,128)(2,1)S(1)} %get-tuple-element.38.refs_1_, ...), custom_call_target="tpu_custom_call" | custom-call | tf_op jit(solution)/shard_map/pallas_call | solution.py:359
  31.0 0.0 collective-permute-done.1.refs_2_
  31.0 1.2 %shard_map.54 = (f32[8,256]{1,0:T(8,128)S(1)}, f32[8,256]{1,0:T(8,128)S(1)}, f32[2,8,8]{2,1,0:T(8,128)S(1)}, f32[32,1,64]{2,1,0:T(1,128)S(1)}) custom-call(f32[8,256]{1,0:T(8,128)S(1)} %get-tuple-element.28.own, f32[32,1024]{1,0:T(8,128)S(1)} %get-tuple-element.32.wide, bf16[384,1024]{1,0:T(8,128)(2,1)S(1)} %get-tuple-element.33.refs_0_, ...), custom_call_target="tpu_custom_call" | custom-call | tf_op jit(solution)/shard_map/pallas_call | solution.py:362
  32.2 8.8 %all_to_all.17.partials = f32[32,1,64]{2,1,0:T(1,128)S(1)} all-to-all(f32[32,1,64]{2,1,0:T(1,128)S(1)} %get-tuple-element.49), channel_id=1, replica_groups=mesh['row'=4,'col'=8] {'row','col'}, dimensions={0} | all-to-all | bytes 16384 | tf_op jit(solution)/shard_map/all_to_all | solution.py:367
  41.1 0.8 %shard_map.55 = (f32[3,8,64]{2,1,0:T(8,128)}, f32[3,8,64]{2,1,0:T(8,128)}, f32[3,8,8]{2,1,0:T(8,128)}) custom-call(f32[8,256]{1,0:T(8,128)S(1)} %get-tuple-element.46.vectors, f32[8,256]{1,0:T(8,128)S(1)} %get-tuple-element.47.shifted, f32[2,8,8]{2,1,0:T(8,128)S(1)} %get-tuple-element.48.both, f32[32,1,64]{2,1,0:T(1,128)S(1)} %all_to_all.17.partials), custom_call_target="tpu_custom_call" | custom-call | tf_op jit(solution)/shard_map/pallas_call | solution.py:368
Async XLA Ops:
  16.8 1.6 %collective-permute-start = (f32[32,8,128]{2,1,0:T(8,128)S(1)}, f32[32,8,128]{2,1,0:T(8,128)S(1)}, u32[]{:S(2)}, u32[]{:S(2)}) collective-permute-start(f32[32,8,128]{2,1,0:T(8,128)S(1)} %all_to_all.15.blocks), channel_id=1, source_target_pairs={{0,1},{1,0},{2,3},{3,2},{4,5},{5,4},{6,7},{7,6},{8,9},{9,8},{10,11... | collective-permute-start | bytes 393224 | tf_op jit(solution)/shard_map/ppermute | solution.py:327
  29.7 1.4 %collective-permute-start.1 = (f32[32,8,128]{2,1,0:T(8,128)S(1)}, f32[32,8,128]{2,1,0:T(8,128)S(1)}, u32[]{:S(2)}, u32[]{:S(2)}) collective-permute-start(f32[32,8,128]{2,1,0:T(8,128)S(1)} %all_to_all.16.refs_2_), channel_id=1, source_target_pairs={{0,1},{1,0},{2,3},{3,2},{4,5},{5,4},{6,7},{7,6},{8,9},{9,8},{10,11... | collective-permute-start | bytes 393224 | tf_op jit(solution)/shard_map/ppermute | solution.py:327

commit v10 on v9

--- a/solution.py
+++ b/solution.py
@@ -13,17 +13,14 @@
 BF16 = jnp.bfloat16
 
 
-def halves(block):
+def copy_halves(block, copies, last=None):
     beads = block.shape[1] // 4
     middle = beads // 2
-    parts = [block[:, part * beads : (part + 1) * beads] for part in range(4)]
-    first = jnp.concatenate([part[:, :middle] for part in parts], axis=1)
-    second = jnp.concatenate([part[:, middle:] for part in parts], axis=1)
-    return first, second
-
-
-def copy_halves(block, copies):
-    for core, half in enumerate(halves(block)):
+    for core in range(2):
+        parts = [block[:, part * beads + core * middle : part * beads + (core + 1) * middle] for part in range(4)]
+        if last is not None:
+            parts[3] = last
+        half = jnp.concatenate(parts, axis=1)
         copies[:, core] = jnp.broadcast_to(half[None], (copies.shape[0],) + half.shape)
 
 
@@ -129,15 +126,7 @@
     return jnp.concatenate([x, y, z, jnp.zeros(x.shape, F32)], axis=1)
 
 
-def block_sum(matrix, row, column):
-    parts = [
-        matrix[row + 8 * part : row + 8 * part + 8, column + 8 * part : column + 8 * part + 8]
-        for part in range(3)
-    ]
-    return parts[0] + parts[1] + parts[2]
-
-
-def filled_product(columns, source, wide, start, high, low, with_gram):
+def filled_product(columns, source, wide, start, high, low):
     width = high.shape[1]
     products = jnp.zeros((32, high.shape[0]), F32)
     for at in range(0, width, 256):
@@ -146,43 +135,40 @@
             fill_tensor(columns, source, pl.multiple_of(start + part, 128), high, low, part)
         both = split_rows(wide[:, pl.ds(pl.multiple_of(start + at, 128), step)])
         products = products + apply_tensor(both, high, low, at, step)
-    if with_gram:
-        both = split_rows(wide[:, pl.ds(pl.multiple_of(start, 128), width)])
-        return products, inner(both)
-    return (products,)
-
-
-def all_chunks(total, width, chunk):
-    if total == width:
+    return products
+
+
+def all_filled(own, source, wide, high, low):
+    columns = target_columns(own)
+    width = high.shape[1]
+    chunk = lambda start: filled_product(columns, source, wide, start, high, low)
+    if wide.shape[1] == width:
         return chunk(0)
-    body = lambda index, sums: tuple(a + b for a, b in zip(sums, chunk(index * width)))
-    return lax.fori_loop(1, total // width, body, chunk(0))
-
-
-def first_product(own, wide, high, low):
-    columns = target_columns(own)
-    return all_chunks(
-        wide.shape[1], high.shape[1], lambda start: filled_product(columns, wide, wide, start, high, low, True)
-    )
+    body = lambda index, total: total + chunk(index * width)
+    return lax.fori_loop(1, wide.shape[1] // width, body, chunk(0))
+
+
+def without_positions(block):
+    lanes = lax.broadcasted_iota(jnp.int32, block.shape, 1)
+    return jnp.where(lanes < block.shape[1] // 4 * 3, block, 0.0)
 
 
 def first_stage(last, own, blocks, *refs):
     refs = list(refs)
     if last:
-        before, refs = refs[:2], refs[2:]
-        image, copies = refs[:2]
+        before, image, copies, wide, high, low = refs
     else:
-        products_out, copies = refs[0], None
-    gram, wide, high, low = refs[2:6] if last else refs[1:5]
+        out, wide, high, low = refs
     unpack(blocks, wide)
-    products, grams = first_product(own[...], wide, high, low)
+    products = all_filled(own[...], wide, wide, high, low)
     if not last:
-        products_out[...], gram[...] = products, grams
+        out[...] = products
         return
-    gram[...] = grams + before[1][...]
-    block = assemble(products + before[0][...])
+    block = assemble(products + before[...])
     image[...] = block
-    copy_halves(block, copies)
+    sums = inner(split_rows(without_positions(own[...]), block))
+    empty = jnp.zeros((8, block.shape[1] // 8 - 24), F32)
+    copy_halves(block, copies, jnp.concatenate([sums[:8], sums[8:, 8:], empty], axis=1))
 
 
 def cholesky(matrix):
@@ -220,70 +206,62 @@
     return factor_t, inverse
 
 
-def start_kernel(size, image, own, gram, small, own_first, own_moved):
-    _, inverse = cholesky(block_sum(gram[...], 0, 0) / size)
-    own_first[...] = small_matmul(inverse, own[...])
-    own_moved[...] = small_matmul(inverse, image[...])
-    small[0] = inverse
-    small[1] = inverse.T
-
-
 def second_product(fill, own, wide, wide_image, high, low):
-    grams = inner(split_rows(wide[...], wide_image[...]))
-    if not fill:
-        return apply_tensor(split_rows(wide_image[...]), high, low, 0, high.shape[1]), grams
-    columns = target_columns(own)
-    (products,) = all_chunks(
-        wide.shape[1],
-        high.shape[1],
-        lambda start: filled_product(columns, wide, wide_image, start, high, low, False),
-    )
-    return products, grams
-
-
-def second_stage(size, last, fill, own, wide, *refs):
+    if fill:
+        return all_filled(own, wide, wide_image, high, low)
+    return apply_tensor(split_rows(wide_image[...]), high, low, 0, high.shape[1])
+
+
+def third_stage(size, fill, own, wide, *refs):
     refs = list(refs)
     if not fill:
         (high, low), refs = refs[:2], refs[2:]
-    images, refs = refs[0], refs[1:]
-    if last:
-        (before, before_gram, own_image, own_first, own_moved, small), refs = refs[:6], refs[6:]
-    outs, refs = refs[: 4 if last else 2], refs[4 if last else 2 :]
+    images, own_image, products, vectors, known, small, coefficients = refs[:7]
     if fill:
+        high, low = refs[7:9]
+    wide_image = refs[-1]
+    unpack(images, wide_image)
+    products[...] = second_product(fill, own[...], wide, wide_image, high, low)
+    sums = wide_image[24:, :128]
+    for at in range(128, wide_image.shape[1], 128):
+        sums = sums + wide_image[24:, at : at + 128]
+    width = own.shape[1] // 8
+    sums = sum(sums[:, at : at + width] for at in range(width, 128, width)) + sums[:, :width]
+    sums = sums / size
+    _, inverse_zero = cholesky(sums[:, :8])
+    inverse_zero_t = inverse_zero.T
+    cross_t = small_matmul(inverse_zero, sums[:, 8:16])
+    cross = cross_t.T
+    factor_t, inverse = cholesky(sums[:, 16:24] - small_matmul(cross, cross_t))
+    factor_one_t = small_matmul(factor_t, inverse_zero_t)
+    first = small_matmul(inverse_zero, without_positions(own[...]))
+    moved = small_matmul(inverse_zero, own_image[...])
+    vectors[...] = small_matmul(inverse, own_image[...] - small_matmul(cross, first))
+    known[...] = small_matmul(inverse, small_matmul(cross, moved)) + small_matmul(factor_one_t, first)
+    small[...] = inverse
+    coefficients[0] = small_matmul(cross_t, inverse_zero_t)
+    coefficients[1] = factor_one_t.T
+
+
+def fourth_stage(fill, own, wide, *refs):
+    refs = list(refs)
+    if not fill:
         (high, low), refs = refs[:2], refs[2:]
-    wide_image = refs[0]
-    beads = own.shape[1] // 4
+    images, before, vectors_in, known, small, shifted, partials = refs[:7]
+    if fill:
+        high, low = refs[7:9]
+    wide_image = refs[-1]
     unpack(images, wide_image)
-    products, grams = second_product(fill, own[...], wide, wide_image, high, low)
-    if not last:
-        outs[0][...], outs[1][...] = products, grams
-        return
-    vectors_out, shifted, coefficients, partials = outs
-    products = products + before[...]
-    grams = (grams + before_gram[...]) / size
-    inverse_zero, inverse_zero_t = small[0], small[1]
-    cross_t = small_matmul(inverse_zero, block_sum(grams, 0, 32))
-    cross = small_matmul(block_sum(grams, 32, 0), inverse_zero_t)
-    factor_t, inverse = cholesky(block_sum(grams, 32, 32) - small_matmul(cross, cross_t))
-    alpha = small_matmul(cross_t, inverse_zero_t)
-    factor_one_t = small_matmul(factor_t, inverse_zero_t)
-    first, moved = own_first[...], own_moved[...]
-    vectors = small_matmul(inverse, own_image[...] - small_matmul(cross, first))
-    shift = small_matmul(inverse, assemble(products) - small_matmul(cross, moved))
-    shift = shift - small_matmul(factor_one_t, first)
-    valid = lax.broadcasted_iota(jnp.int32, vectors.shape, 1) < 3 * beads
-    vectors = jnp.where(valid, vectors, 0.0)
-    shift = jnp.where(valid, shift, 0.0)
+    products = second_product(fill, own[...], wide, wide_image, high, low) + before[...]
+    vectors = vectors_in[...]
+    shift = small_matmul(small[...], assemble(products)) - known[...]
+    shifted[...] = shift
     (vector_high, vector_low), (shift_high, shift_low) = split_two(vectors), split_two(shift)
     partial = matmul_nt(vector_high, shift_high) + (
         matmul_nt(vector_high, shift_low) + matmul_nt(vector_low, shift_high)
     )
     line = jnp.concatenate([partial[row : row + 1] for row in range(8)], axis=1)
     partials[...] = jnp.broadcast_to(line[None], partials.shape)
-    vectors_out[...] = vectors
-    shifted[...] = shift
-    coefficients[0] = alpha
-    coefficients[1] = factor_one_t.T
 
 
 def last_kernel(size, vectors, shifted, both, partials, basis, residual, coefficients):
@@ -337,7 +315,6 @@
     block = array(vecs, 4 * beads)
     copies = array(devices // 2, 2, vecs, 2 * beads)
     products = array(4 * vecs, 6 * beads)
-    small_gram, large_gram = array(4 * vecs, 4 * vecs), array(8 * vecs, 8 * vecs)
     wide, held_wide = array(4 * vecs, total), pltpu.VMEM((4 * vecs, total), F32)
     kept = [array(6 * beads, width, dtype=BF16)] * 2 if keep else []
     held = [] if keep else [pltpu.VMEM((6 * beads, width), BF16)] * 2
@@ -346,24 +323,21 @@
     rows = jnp.concatenate([rows, jnp.pad(positions, ((0, vecs - 3), (0, 0)))], axis=0)
     own, own_copies = call(pack_kernel, [block, copies])(rows)
     one, two = gather(own_copies)
-    partial, gram, one_wide, *one_tensor = call(
-        functools.partial(first_stage, False), [products, small_gram, wide] + kept, held
+    partial, one_wide, *one_tensor = call(
+        functools.partial(first_stage, False), [products, wide] + kept, held
     )(own, one)
-    image, images, gram, two_wide, *two_tensor = call(
-        functools.partial(first_stage, True), [block, copies, small_gram, wide] + kept, held
-    )(own, two, partial, gram)
+    image, images, two_wide, *two_tensor = call(
+        functools.partial(first_stage, True), [block, copies, wide] + kept, held
+    )(own, two, partial)
     one, two = gather(images)
-    small, own_first, own_moved = call(
-        functools.partial(start_kernel, size), [array(2, vecs, vecs), block, block]
-    )(image, own, gram)
-    partial, gram = call(
-        functools.partial(second_stage, size, False, not keep), [products, large_gram], held + [held_wide]
-    )(own, one_wide, *one_tensor, one)
-    vectors, shifted, both, partials = call(
-        functools.partial(second_stage, size, True, not keep),
-        [block, block, array(2, vecs, vecs), array(devices, 1, vecs * vecs)],
+    partial, vectors, known, small, both = call(
+        functools.partial(third_stage, size, not keep),
+        [products, block, block, array(vecs, vecs), array(2, vecs, vecs)],
         held + [held_wide],
-    )(own, two_wide, *two_tensor, two, partial, gram, image, own_first, own_moved, small)
+    )(own, one_wide, *one_tensor, one, image)
+    shifted, partials = call(
+        functools.partial(fourth_stage, not keep), [block, array(devices, 1, vecs * vecs)], held + [held_wide]
+    )(own, two_wide, *two_tensor, two, partial, vectors, known, small)
     partials = lax.all_to_all(partials, ("row", "col"), 0, 0, tiled=True)
     basis, residual, coefficients = call(
         functools.partial(last_kernel, size),

time: 42.1 us -> 41.8 us (level)
    pallas_call x5 -> x4, Pallas kernels: 4.88 us -> 4.56 us  [the longest x1 1.47 us: local(): call(functools.partial(first_stage, True), [block, copies, wide] + kept,...]
where the time goes in v10:
time: 41.8 us; the launch traced here: 41.6 us
  blocking collectives  34 us (81%)
  Pallas kernels  5.51 us (13%)
  other arithmetic  0.73 us (2%)
  between operations  0.68 us (2%)
  starting transfers between devices  0.63 us (2%)
    all_to_all x2, blocking collectives, gather(): lax.all_to_all(copies.reshape((-1,) + copies.shape[2:]), ('row', 'col'),...  25.2 us
    all_to_all x1, blocking collectives, local(): partials = lax.all_to_all(partials, ('row', 'col'), 0, 0, tiled=True)  8.84 us
    pallas_call x1, Pallas kernels, local(): call(functools.partial(first_stage, True), [block, copies, wide] + kept,...  1.47 us
    pallas_call x1, Pallas kernels, local(): call(functools.partial(first_stage, False), [products, wide] + kept, held)  1.13 us
    pallas_call x1, Pallas kernels, local(): call(functools.partial(third_stage, size, not keep), [products, block, bl...  1.1 us
    pallas_call x1, Pallas kernels, local(): call(functools.partial(fourth_stage, not keep), [block, array(devices, 1,...  0.86 us
  transfers between devices with their start and end apart: 2, of which 0 were waited for; matrix products, arithmetic and copies ran while one was open for 0% of the time, Pallas kernels for 5%

profile of v10, /device:TPU:0, one launch (start us, length us, event | category | flops | bytes accessed | tf_op | source)
XLA Modules:
  0.0 41.6 jit_solution(9103277129478060789)
XLA Ops:
  0.6 0.7 %select_maximum_fusion.rows = f32[32,64]{1,0:T(8,128)S(1)} fusion(f32[3,64]{1,0:T(4,128)} %param.2, f32[24,64]{1,0:T(8,128)} %bitcast.9), kind=kLoop, calls=%fused_computation | loop fusion | flops 6144 | bytes 15104 | tf_op jit(solution)/shard_map/concatenate | solution.py:323
  1.4 0.1 shard_map.49
  1.5 15.3 %all_to_all.15.blocks = f32[32,8,128]{2,1,0:T(8,128)S(1)} all-to-all(f32[32,8,128]{2,1,0:T(8,128)S(1)} %bitcast.8), channel_id=1, replica_groups=mesh['row'=4,'col'=8] {'row','col'}, dimensions={0} | all-to-all | bytes 262144 | tf_op jit(solution)/shard_map/all_to_all | solution.py:303
  16.8 0.3 collective-permute-start
  17.1 1.1 %shard_map.50 = (f32[32,384]{1,0:T(8,128)S(1)}, f32[32,1024]{1,0:T(8,128)S(1)}, bf16[384,1024]{1,0:T(8,128)(2,1)S(1)}, bf16[384,1024]{1,0:T(8,128)(2,1)S(1)}) custom-call(f32[8,256]{1,0:T(8,128)S(1)} %get-tuple-element.24.own, f32[32,8,128]{2,1,0:T(8,128)S(1)} %all_to_all.15.blocks), custom_call_target="tpu_custom_call" | custom-call | tf_op jit(solution)/shard_map/pallas_call | solution.py:326
  18.2 0.0 collective-permute-done.blocks
  18.3 1.5 %shard_map.51 = (f32[8,256]{1,0:T(8,128)S(1)}, f32[16,2,8,128]{3,2,1,0:T(8,128)S(1)}, f32[32,1024]{1,0:T(8,128)S(1)}, bf16[384,1024]{1,0:T(8,128)(2,1)S(1)}, bf16[384,1024]{1,0:T(8,128)(2,1)S(1)}) custom-call(f32[8,256]{1,0:T(8,128)S(1)} %get-tuple-element.24.own, f32[32,8,128]{2,1,0:T(8,128)S(1)} %collective-permute-done.blocks, ...), custom_call_target="tpu_custom_call" | custom-call | tf_op jit(solution)/shard_map/pallas_call | solution.py:329
  19.7 9.9 %all_to_all.16.refs_2_ = f32[32,8,128]{2,1,0:T(8,128)S(1)} all-to-all(f32[32,8,128]{2,1,0:T(8,128)S(1)} %bitcast.7), channel_id=1, replica_groups=mesh['row'=4,'col'=8] {'row','col'}, dimensions={0} | all-to-all | bytes 262144 | tf_op jit(solution)/shard_map/all_to_all | solution.py:303
  29.6 0.3 collective-permute-start.1
  29.9 1.1 %shard_map.52 = (f32[32,384]{1,0:T(8,128)S(1)}, f32[8,256]{1,0:T(8,128)S(1)}, f32[8,256]{1,0:T(8,128)S(1)}, f32[8,8]{1,0:T(8,128)S(1)}, f32[2,8,8]{2,1,0:T(8,128)S(1)}) custom-call(f32[8,256]{1,0:T(8,128)S(1)} %get-tuple-element.24.own, f32[32,1024]{1,0:T(8,128)S(1)} %get-tuple-element.26.wide, bf16[384,1024]{1,0:T(8,128)(2,1)S(1)} %get-tuple-element.27.refs_0_, ...), custom_call_target="tpu_custom_call" | custom-call | tf_op jit(solution)/shard_map/pallas_call | solution.py:333
  31.0 0.0 collective-permute-done.1.refs_2_
  31.0 0.9 %shard_map.53 = (f32[8,256]{1,0:T(8,128)S(1)}, f32[32,1,64]{2,1,0:T(1,128)S(1)}) custom-call(f32[8,256]{1,0:T(8,128)S(1)} %get-tuple-element.24.own, f32[32,1024]{1,0:T(8,128)S(1)} %get-tuple-element.33.wide, bf16[384,1024]{1,0:T(8,128)(2,1)S(1)} %get-tuple-element.34.refs_0_, bf16[384,1024]{1,0:T(8,128)(2,1)S(1)} %get-tuple-element.35.refs_1_, ...), custom_call_target="tpu_custom_call" | custom-call | tf_op jit(solution)/shard_map/pallas_call | solution.py:338
  31.9 8.8 %all_to_all.17.partials = f32[32,1,64]{2,1,0:T(1,128)S(1)} all-to-all(f32[32,1,64]{2,1,0:T(1,128)S(1)} %get-tuple-element.41), channel_id=1, replica_groups=mesh['row'=4,'col'=8] {'row','col'}, dimensions={0} | all-to-all | bytes 16384 | tf_op jit(solution)/shard_map/all_to_all | solution.py:341
  40.8 0.8 %shard_map.54 = (f32[3,8,64]{2,1,0:T(8,128)}, f32[3,8,64]{2,1,0:T(8,128)}, f32[3,8,8]{2,1,0:T(8,128)}) custom-call(f32[8,256]{1,0:T(8,128)S(1)} %get-tuple-element.32.refs_4_.vectors, f32[8,256]{1,0:T(8,128)S(1)} %get-tuple-element.39.shifted, f32[2,8,8]{2,1,0:T(8,128)S(1)} %get-tuple-element.40.both, f32[32,1,64]{2,1,0:T(1,128)S(1)} %all_to_all.17.partials), custom_call_target="tpu_custom_call" | custom-call | tf_op jit(solution)/shard_map/pallas_call | solution.py:342
Async XLA Ops:
  16.8 1.5 %collective-permute-start = (f32[32,8,128]{2,1,0:T(8,128)S(1)}, f32[32,8,128]{2,1,0:T(8,128)S(1)}, u32[]{:S(2)}, u32[]{:S(2)}) collective-permute-start(f32[32,8,128]{2,1,0:T(8,128)S(1)} %all_to_all.15.blocks), channel_id=1, source_target_pairs={{0,1},{1,0},{2,3},{3,2},{4,5},{5,4},{6,7},{7,6},{8,9},{9,8},{10,11... | collective-permute-start | bytes 393224 | tf_op jit(solution)/shard_map/ppermute | solution.py:305
  29.6 1.4 %collective-permute-start.1 = (f32[32,8,128]{2,1,0:T(8,128)S(1)}, f32[32,8,128]{2,1,0:T(8,128)S(1)}, u32[]{:S(2)}, u32[]{:S(2)}) collective-permute-start(f32[32,8,128]{2,1,0:T(8,128)S(1)} %all_to_all.16.refs_2_), channel_id=1, source_target_pairs={{0,1},{1,0},{2,3},{3,2},{4,5},{5,4},{6,7},{7,6},{8,9},{9,8},{10,11... | collective-permute-start | bytes 393224 | tf_op jit(solution)/shard_map/ppermute | solution.py:305

commit v11 on v10

--- a/solution.py
+++ b/solution.py
@@ -129,12 +129,15 @@
 def filled_product(columns, source, wide, start, high, low):
     width = high.shape[1]
     products = jnp.zeros((32, high.shape[0]), F32)
-    for at in range(0, width, 256):
-        step = min(256, width - at)
-        for part in range(at, at + step, 128):
-            fill_tensor(columns, source, pl.multiple_of(start + part, 128), high, low, part)
-        both = split_rows(wide[:, pl.ds(pl.multiple_of(start + at, 128), step)])
-        products = products + apply_tensor(both, high, low, at, step)
+    steps = [(at, min(256, width - at)) for at in range(0, width, 256)]
+    vectors = [split_rows(wide[:, pl.ds(pl.multiple_of(start + at, 128), step)]) for at, step in steps]
+    for index in range(len(steps) + 1):
+        if index < len(steps):
+            at, step = steps[index]
+            for part in range(at, at + step, 128):
+                fill_tensor(columns, source, pl.multiple_of(start + part, 128), high, low, part)
+        if index > 0:
+            products = products + apply_tensor(vectors[index - 1], high, low, *steps[index - 1])
     return products
 
 

time: 41.8 us -> 41.8 us (level)
  no operation moved by 1% of the time
where the time goes in v11:
time: 41.8 us; the launch traced here: 41.6 us
  blocking collectives  34 us (81%)
  Pallas kernels  5.51 us (13%)
  other arithmetic  0.73 us (2%)
  between operations  0.68 us (2%)
  starting transfers between devices  0.63 us (2%)
    all_to_all x2, blocking collectives, gather(): lax.all_to_all(copies.reshape((-1,) + copies.shape[2:]), ('row', 'col'),...  25.2 us
    all_to_all x1, blocking collectives, local(): partials = lax.all_to_all(partials, ('row', 'col'), 0, 0, tiled=True)  8.84 us
    pallas_call x1, Pallas kernels, local(): call(functools.partial(first_stage, True), [block, copies, wide] + kept,...  1.47 us
    pallas_call x1, Pallas kernels, local(): call(functools.partial(first_stage, False), [products, wide] + kept, held)  1.13 us
    pallas_call x1, Pallas kernels, local(): call(functools.partial(third_stage, size, not keep), [products, block, bl...  1.1 us
    pallas_call x1, Pallas kernels, local(): call(functools.partial(fourth_stage, not keep), [block, array(devices, 1,...  0.86 us
  transfers between devices with their start and end apart: 2, of which 0 were waited for; matrix products, arithmetic and copies ran while one was open for 0% of the time, Pallas kernels for 5%

profile of v11, /device:TPU:0, one launch (start us, length us, event | category | flops | bytes accessed | tf_op | source)
XLA Modules:
  0.0 41.6 jit_solution(9103277129478060789)
XLA Ops:
  0.6 0.7 %select_maximum_fusion.rows = f32[32,64]{1,0:T(8,128)S(1)} fusion(f32[3,64]{1,0:T(4,128)} %param.2, f32[24,64]{1,0:T(8,128)} %bitcast.9), kind=kLoop, calls=%fused_computation | loop fusion | flops 6144 | bytes 15104 | tf_op jit(solution)/shard_map/concatenate | solution.py:326
  1.4 0.1 shard_map.49
  1.5 15.3 %all_to_all.15.blocks = f32[32,8,128]{2,1,0:T(8,128)S(1)} all-to-all(f32[32,8,128]{2,1,0:T(8,128)S(1)} %bitcast.8), channel_id=1, replica_groups=mesh['row'=4,'col'=8] {'row','col'}, dimensions={0} | all-to-all | bytes 262144 | tf_op jit(solution)/shard_map/all_to_all | solution.py:306
  16.8 0.3 collective-permute-start
  17.1 1.1 %shard_map.50 = (f32[32,384]{1,0:T(8,128)S(1)}, f32[32,1024]{1,0:T(8,128)S(1)}, bf16[384,1024]{1,0:T(8,128)(2,1)S(1)}, bf16[384,1024]{1,0:T(8,128)(2,1)S(1)}) custom-call(f32[8,256]{1,0:T(8,128)S(1)} %get-tuple-element.24.own, f32[32,8,128]{2,1,0:T(8,128)S(1)} %all_to_all.15.blocks), custom_call_target="tpu_custom_call" | custom-call | tf_op jit(solution)/shard_map/pallas_call | solution.py:329
  18.2 0.0 collective-permute-done.blocks
  18.3 1.5 %shard_map.51 = (f32[8,256]{1,0:T(8,128)S(1)}, f32[16,2,8,128]{3,2,1,0:T(8,128)S(1)}, f32[32,1024]{1,0:T(8,128)S(1)}, bf16[384,1024]{1,0:T(8,128)(2,1)S(1)}, bf16[384,1024]{1,0:T(8,128)(2,1)S(1)}) custom-call(f32[8,256]{1,0:T(8,128)S(1)} %get-tuple-element.24.own, f32[32,8,128]{2,1,0:T(8,128)S(1)} %collective-permute-done.blocks, ...), custom_call_target="tpu_custom_call" | custom-call | tf_op jit(solution)/shard_map/pallas_call | solution.py:332
  19.7 9.9 %all_to_all.16.refs_2_ = f32[32,8,128]{2,1,0:T(8,128)S(1)} all-to-all(f32[32,8,128]{2,1,0:T(8,128)S(1)} %bitcast.7), channel_id=1, replica_groups=mesh['row'=4,'col'=8] {'row','col'}, dimensions={0} | all-to-all | bytes 262144 | tf_op jit(solution)/shard_map/all_to_all | solution.py:306
  29.6 0.3 collective-permute-start.1
  29.9 1.1 %shard_map.52 = (f32[32,384]{1,0:T(8,128)S(1)}, f32[8,256]{1,0:T(8,128)S(1)}, f32[8,256]{1,0:T(8,128)S(1)}, f32[8,8]{1,0:T(8,128)S(1)}, f32[2,8,8]{2,1,0:T(8,128)S(1)}) custom-call(f32[8,256]{1,0:T(8,128)S(1)} %get-tuple-element.24.own, f32[32,1024]{1,0:T(8,128)S(1)} %get-tuple-element.26.wide, bf16[384,1024]{1,0:T(8,128)(2,1)S(1)} %get-tuple-element.27.refs_0_, ...), custom_call_target="tpu_custom_call" | custom-call | tf_op jit(solution)/shard_map/pallas_call | solution.py:336
  31.0 0.0 collective-permute-done.1.refs_2_
  31.0 0.9 %shard_map.53 = (f32[8,256]{1,0:T(8,128)S(1)}, f32[32,1,64]{2,1,0:T(1,128)S(1)}) custom-call(f32[8,256]{1,0:T(8,128)S(1)} %get-tuple-element.24.own, f32[32,1024]{1,0:T(8,128)S(1)} %get-tuple-element.33.wide, bf16[384,1024]{1,0:T(8,128)(2,1)S(1)} %get-tuple-element.34.refs_0_, bf16[384,1024]{1,0:T(8,128)(2,1)S(1)} %get-tuple-element.35.refs_1_, ...), custom_call_target="tpu_custom_call" | custom-call | tf_op jit(solution)/shard_map/pallas_call | solution.py:341
  31.9 8.8 %all_to_all.17.partials = f32[32,1,64]{2,1,0:T(1,128)S(1)} all-to-all(f32[32,1,64]{2,1,0:T(1,128)S(1)} %get-tuple-element.41), channel_id=1, replica_groups=mesh['row'=4,'col'=8] {'row','col'}, dimensions={0} | all-to-all | bytes 16384 | tf_op jit(solution)/shard_map/all_to_all | solution.py:344
  40.8 0.8 %shard_map.54 = (f32[3,8,64]{2,1,0:T(8,128)}, f32[3,8,64]{2,1,0:T(8,128)}, f32[3,8,8]{2,1,0:T(8,128)}) custom-call(f32[8,256]{1,0:T(8,128)S(1)} %get-tuple-element.32.refs_4_.vectors, f32[8,256]{1,0:T(8,128)S(1)} %get-tuple-element.39.shifted, f32[2,8,8]{2,1,0:T(8,128)S(1)} %get-tuple-element.40.both, f32[32,1,64]{2,1,0:T(1,128)S(1)} %all_to_all.17.partials), custom_call_target="tpu_custom_call" | custom-call | tf_op jit(solution)/shard_map/pallas_call | solution.py:345
Async XLA Ops:
  16.8 1.5 %collective-permute-start = (f32[32,8,128]{2,1,0:T(8,128)S(1)}, f32[32,8,128]{2,1,0:T(8,128)S(1)}, u32[]{:S(2)}, u32[]{:S(2)}) collective-permute-start(f32[32,8,128]{2,1,0:T(8,128)S(1)} %all_to_all.15.blocks), channel_id=1, source_target_pairs={{0,1},{1,0},{2,3},{3,2},{4,5},{5,4},{6,7},{7,6},{8,9},{9,8},{10,11... | collective-permute-start | bytes 393224 | tf_op jit(solution)/shard_map/ppermute | solution.py:308
  29.6 1.4 %collective-permute-start.1 = (f32[32,8,128]{2,1,0:T(8,128)S(1)}, f32[32,8,128]{2,1,0:T(8,128)S(1)}, u32[]{:S(2)}, u32[]{:S(2)}) collective-permute-start(f32[32,8,128]{2,1,0:T(8,128)S(1)} %all_to_all.16.refs_2_), channel_id=1, source_target_pairs={{0,1},{1,0},{2,3},{3,2},{4,5},{5,4},{6,7},{7,6},{8,9},{9,8},{10,11... | collective-permute-start | bytes 393224 | tf_op jit(solution)/shard_map/ppermute | solution.py:308

commit v12 on v11

--- a/solution.py
+++ b/solution.py
@@ -302,8 +302,17 @@
     )
 
 
+def to_all(copies):
+    rows, cols = lax.axis_size("row"), lax.axis_size("col")
+    layers, middle = range(cols // 2), rows // 2
+    chips = [(row, layer) for layer in layers for row in range(middle)]
+    chips = chips + [(row, layer) for layer in reversed(layers) for row in range(middle, rows)]
+    ring = [row * cols + 2 * layer + core for row, layer in chips for core in range(2)]
+    return lax.all_to_all(copies, ("row", "col"), 0, 0, axis_index_groups=[ring], tiled=True)
+
+
 def gather(copies):
-    mine = lax.all_to_all(copies.reshape((-1,) + copies.shape[2:]), ("row", "col"), 0, 0, tiled=True)
+    mine = to_all(copies.reshape((-1,) + copies.shape[2:]))
     cols = lax.axis_size("col")
     return mine, lax.ppermute(mine, "col", [(col, col ^ 1) for col in range(cols)])
 
@@ -341,7 +350,7 @@
     shifted, partials = call(
         functools.partial(fourth_stage, not keep), [block, array(devices, 1, vecs * vecs)], held + [held_wide]
     )(own, two_wide, *two_tensor, two, partial, vectors, known, small)
-    partials = lax.all_to_all(partials, ("row", "col"), 0, 0, tiled=True)
+    partials = to_all(partials)
     basis, residual, coefficients = call(
         functools.partial(last_kernel, size),
         [array(3, vecs, beads), array(3, vecs, beads), array(3, vecs, vecs)],

time: 41.8 us -> 41.7 us (level)
  no operation moved by 1% of the time
where the time goes in v12:
time: 41.7 us; the launch traced here: 41.4 us
  blocking collectives  34 us (82%)
  Pallas kernels  5.51 us (13%)
  other arithmetic  0.73 us (2%)
  between operations  0.68 us (2%)
  starting transfers between devices  0.5 us (1%)
    all_to_all x3, blocking collectives, to_all(): lax.all_to_all(copies, ('row', 'col'), 0, 0, axis_index_groups=[ring], ti...  34 us
    pallas_call x1, Pallas kernels, local(): call(functools.partial(first_stage, True), [block, copies, wide] + kept,...  1.47 us
    pallas_call x1, Pallas kernels, local(): call(functools.partial(first_stage, False), [products, wide] + kept, held)  1.14 us
    pallas_call x1, Pallas kernels, local(): call(functools.partial(third_stage, size, not keep), [products, block, bl...  1.1 us
    pallas_call x1, Pallas kernels, local(): call(functools.partial(fourth_stage, not keep), [block, array(devices, 1,...  0.86 us
  transfers between devices with their start and end apart: 2, of which 0 were waited for; matrix products, arithmetic and copies ran while one was open for 0% of the time, Pallas kernels for 5%

profile of v12, /device:TPU:0, one launch (start us, length us, event | category | flops | bytes accessed | tf_op | source)
XLA Modules:
  0.0 41.4 jit_solution(720082505193488307)
XLA Ops:
  0.6 0.7 %select_maximum_fusion.rows = f32[32,64]{1,0:T(8,128)S(1)} fusion(f32[3,64]{1,0:T(4,128)} %param.2, f32[24,64]{1,0:T(8,128)} %bitcast.9), kind=kLoop, calls=%fused_computation | loop fusion | flops 6144 | bytes 15104 | tf_op jit(solution)/shard_map/concatenate | solution.py:335
  1.4 0.1 shard_map.49
  1.5 14.9 %all_to_all.15.blocks = f32[32,8,128]{2,1,0:T(8,128)S(1)} all-to-all(f32[32,8,128]{2,1,0:T(8,128)S(1)} %bitcast.8), channel_id=1, replica_groups={{0,1,8,9,2,3,10,11,4,5,12,13,6,7,14,15,22,23,30,31,20,21,28,29,18,19,26..., dimensions={0} | all-to-all | bytes 262144 | tf_op jit(solution)/shard_map/all_to_all | solution.py:311
  16.5 0.2 collective-permute-start
  16.7 1.1 %shard_map.50 = (f32[32,384]{1,0:T(8,128)S(1)}, f32[32,1024]{1,0:T(8,128)S(1)}, bf16[384,1024]{1,0:T(8,128)(2,1)S(1)}, bf16[384,1024]{1,0:T(8,128)(2,1)S(1)}) custom-call(f32[8,256]{1,0:T(8,128)S(1)} %get-tuple-element.24.own, f32[32,8,128]{2,1,0:T(8,128)S(1)} %all_to_all.15.blocks), custom_call_target="tpu_custom_call" | custom-call | tf_op jit(solution)/shard_map/pallas_call | solution.py:338
  17.9 0.0 collective-permute-done.blocks
  17.9 1.5 %shard_map.51 = (f32[8,256]{1,0:T(8,128)S(1)}, f32[16,2,8,128]{3,2,1,0:T(8,128)S(1)}, f32[32,1024]{1,0:T(8,128)S(1)}, bf16[384,1024]{1,0:T(8,128)(2,1)S(1)}, bf16[384,1024]{1,0:T(8,128)(2,1)S(1)}) custom-call(f32[8,256]{1,0:T(8,128)S(1)} %get-tuple-element.24.own, f32[32,8,128]{2,1,0:T(8,128)S(1)} %collective-permute-done.blocks, ...), custom_call_target="tpu_custom_call" | custom-call | tf_op jit(solution)/shard_map/pallas_call | solution.py:341
  19.3 9.9 %all_to_all.16.refs_2_ = f32[32,8,128]{2,1,0:T(8,128)S(1)} all-to-all(f32[32,8,128]{2,1,0:T(8,128)S(1)} %bitcast.7), channel_id=1, replica_groups={{0,1,8,9,2,3,10,11,4,5,12,13,6,7,14,15,22,23,30,31,20,21,28,29,18,19,26..., dimensions={0} | all-to-all | bytes 262144 | tf_op jit(solution)/shard_map/all_to_all | solution.py:311
  29.2 0.2 collective-permute-start.1
  29.5 1.1 %shard_map.52 = (f32[32,384]{1,0:T(8,128)S(1)}, f32[8,256]{1,0:T(8,128)S(1)}, f32[8,256]{1,0:T(8,128)S(1)}, f32[8,8]{1,0:T(8,128)S(1)}, f32[2,8,8]{2,1,0:T(8,128)S(1)}) custom-call(f32[8,256]{1,0:T(8,128)S(1)} %get-tuple-element.24.own, f32[32,1024]{1,0:T(8,128)S(1)} %get-tuple-element.26.wide, bf16[384,1024]{1,0:T(8,128)(2,1)S(1)} %get-tuple-element.27.refs_0_, ...), custom_call_target="tpu_custom_call" | custom-call | tf_op jit(solution)/shard_map/pallas_call | solution.py:345
  30.6 0.0 collective-permute-done.1.refs_2_
  30.6 0.9 %shard_map.53 = (f32[8,256]{1,0:T(8,128)S(1)}, f32[32,1,64]{2,1,0:T(1,128)S(1)}) custom-call(f32[8,256]{1,0:T(8,128)S(1)} %get-tuple-element.24.own, f32[32,1024]{1,0:T(8,128)S(1)} %get-tuple-element.33.wide, bf16[384,1024]{1,0:T(8,128)(2,1)S(1)} %get-tuple-element.34.refs_0_, bf16[384,1024]{1,0:T(8,128)(2,1)S(1)} %get-tuple-element.35.refs_1_, ...), custom_call_target="tpu_custom_call" | custom-call | tf_op jit(solution)/shard_map/pallas_call | solution.py:350
  31.4 9.2 %all_to_all.17.partials = f32[32,1,64]{2,1,0:T(1,128)S(1)} all-to-all(f32[32,1,64]{2,1,0:T(1,128)S(1)} %get-tuple-element.41), channel_id=1, replica_groups={{0,1,8,9,2,3,10,11,4,5,12,13,6,7,14,15,22,23,30,31,20,21,28,29,18,19,26..., dimensions={0} | all-to-all | bytes 16384 | tf_op jit(solution)/shard_map/all_to_all | solution.py:311
  40.6 0.8 %shard_map.54 = (f32[3,8,64]{2,1,0:T(8,128)}, f32[3,8,64]{2,1,0:T(8,128)}, f32[3,8,8]{2,1,0:T(8,128)}) custom-call(f32[8,256]{1,0:T(8,128)S(1)} %get-tuple-element.32.refs_4_.vectors, f32[8,256]{1,0:T(8,128)S(1)} %get-tuple-element.39.shifted, f32[2,8,8]{2,1,0:T(8,128)S(1)} %get-tuple-element.40.both, f32[32,1,64]{2,1,0:T(1,128)S(1)} %all_to_all.17.partials), custom_call_target="tpu_custom_call" | custom-call | tf_op jit(solution)/shard_map/pallas_call | solution.py:354
Async XLA Ops:
  16.5 1.4 %collective-permute-start = (f32[32,8,128]{2,1,0:T(8,128)S(1)}, f32[32,8,128]{2,1,0:T(8,128)S(1)}, u32[]{:S(2)}, u32[]{:S(2)}) collective-permute-start(f32[32,8,128]{2,1,0:T(8,128)S(1)} %all_to_all.15.blocks), channel_id=1, source_target_pairs={{0,1},{1,0},{2,3},{3,2},{4,5},{5,4},{6,7},{7,6},{8,9},{9,8},{10,11... | collective-permute-start | bytes 393224 | tf_op jit(solution)/shard_map/ppermute | solution.py:317
  29.2 1.4 %collective-permute-start.1 = (f32[32,8,128]{2,1,0:T(8,128)S(1)}, f32[32,8,128]{2,1,0:T(8,128)S(1)}, u32[]{:S(2)}, u32[]{:S(2)}) collective-permute-start(f32[32,8,128]{2,1,0:T(8,128)S(1)} %all_to_all.16.refs_2_), channel_id=1, source_target_pairs={{0,1},{1,0},{2,3},{3,2},{4,5},{5,4},{6,7},{7,6},{8,9},{9,8},{10,11... | collective-permute-start | bytes 393224 | tf_op jit(solution)/shard_map/ppermute | solution.py:317

commit v13 on v12

--- a/solution.py
+++ b/solution.py
@@ -267,37 +267,50 @@
     partials[...] = jnp.broadcast_to(line[None], partials.shape)
 
 
-def last_kernel(size, vectors, shifted, both, partials, basis, residual, coefficients):
+def last_kernel(
+    size, vectors, shifted, both, partials, basis, residual, coefficients, held_basis, held_residual, held_small, sems
+):
     beads = basis.shape[2]
     width = partials.shape[2]
+    copies = [
+        pltpu.make_async_copy(held_basis, basis, sems.at[0]),
+        pltpu.make_async_copy(held_residual, residual, sems.at[1]),
+        pltpu.make_async_copy(held_small, coefficients, sems.at[2]),
+    ]
+    block = vectors[...]
+    for part in range(3):
+        held_basis[part] = block[:, part * beads : (part + 1) * beads]
+    copies[0].start()
     total = jnp.sum(partials[...], axis=0) / size
     spread = jnp.broadcast_to(total, (8, width))
     rows = lax.broadcasted_iota(jnp.int32, spread.shape, 0)
     cols = lax.broadcasted_iota(jnp.int32, spread.shape, 1)
-    block = vectors[...]
     left = shifted[...]
     transposed = jnp.where(cols % 8 == rows, spread, 0.0)
     for k in range(8):
         column = jnp.sum(jnp.where(cols // 8 == k, transposed, 0.0), axis=1, keepdims=True)
         left = left - column * block[k : k + 1, :]
-    coefficients[0:2] = both[...]
+    for part in range(3):
+        held_residual[part] = left[:, part * beads : (part + 1) * beads]
+    copies[1].start()
+    held_small[0:2] = both[...]
     for k in range(8):
-        coefficients[2, k : k + 1, :] = total[:, 8 * k : 8 * k + 8]
-    for part in range(3):
-        basis[part] = block[:, part * beads : (part + 1) * beads]
-        residual[part] = left[:, part * beads : (part + 1) * beads]
+        held_small[2, k : k + 1, :] = total[:, 8 * k : 8 * k + 8]
+    copies[2].start()
+    for copy in copies:
+        copy.wait()
 
 
 def array(*shape, dtype=F32):
     return jax.ShapeDtypeStruct(shape, dtype)
 
 
-def call(kernel, outs, scratch=(), **options):
+def call(kernel, outs, scratch=(), fuse=None, **options):
     return pl.pallas_call(
         kernel,
         out_shape=outs,
         scratch_shapes=list(scratch),
-        compiler_params=pltpu.CompilerParams(vmem_limit_bytes=48 * 1024 * 1024),
+        compiler_params=pltpu.CompilerParams(vmem_limit_bytes=48 * 1024 * 1024, allow_input_fusion=fuse),
         **options,
     )
 
@@ -333,7 +346,7 @@
 
     rows = noise.transpose(1, 0, 2).reshape(3 * vecs, beads)
     rows = jnp.concatenate([rows, jnp.pad(positions, ((0, vecs - 3), (0, 0)))], axis=0)
-    own, own_copies = call(pack_kernel, [block, copies])(rows)
+    own, own_copies = call(pack_kernel, [block, copies], fuse=[True])(rows)
     one, two = gather(own_copies)
     partial, one_wide, *one_tensor = call(
         functools.partial(first_stage, False), [products, wide] + kept, held
@@ -351,9 +364,12 @@
         functools.partial(fourth_stage, not keep), [block, array(devices, 1, vecs * vecs)], held + [held_wide]
     )(own, two_wide, *two_tensor, two, partial, vectors, known, small)
     partials = to_all(partials)
+    outs = [array(3, vecs, beads), array(3, vecs, beads), array(3, vecs, vecs)]
     basis, residual, coefficients = call(
         functools.partial(last_kernel, size),
-        [array(3, vecs, beads), array(3, vecs, beads), array(3, vecs, vecs)],
+        outs,
+        [pltpu.VMEM(out.shape, F32) for out in outs] + [pltpu.SemaphoreType.DMA((3,))],
+        out_specs=[pl.BlockSpec(memory_space=pltpu.HBM)] * 3,
     )(vectors, shifted, both, partials)
     return (basis.transpose(1, 0, 2), residual.transpose(1, 0, 2), coefficients)
 

time: 41.7 us -> 41.7 us (level)
  no operation moved by 1% of the time
where the time goes in v13:
time: 41.7 us; the launch traced here: 41.4 us
  blocking collectives  34 us (82%)
  Pallas kernels  5.53 us (13%)
  other arithmetic  0.73 us (2%)
  between operations  0.68 us (2%)
  starting transfers between devices  0.5 us (1%)
    all_to_all x3, blocking collectives, to_all(): lax.all_to_all(copies, ('row', 'col'), 0, 0, axis_index_groups=[ring], ti...  34 us
    pallas_call x1, Pallas kernels, local(): call(functools.partial(first_stage, True), [block, copies, wide] + kept,...  1.47 us
    pallas_call x1, Pallas kernels, local(): call(functools.partial(first_stage, False), [products, wide] + kept, held)  1.14 us
    pallas_call x1, Pallas kernels, local(): call(functools.partial(third_stage, size, not keep), [products, block, bl...  1.1 us
    pallas_call x1, Pallas kernels, local(): call(functools.partial(fourth_stage, not keep), [block, array(devices, 1,...  0.86 us
  transfers between devices with their start and end apart: 2, of which 0 were waited for; matrix products, arithmetic and copies ran while one was open for 0% of the time, Pallas kernels for 5%

profile of v13, /device:TPU:0, one launch (start us, length us, event | category | flops | bytes accessed | tf_op | source)
XLA Modules:
  0.0 41.4 jit_solution(12086322464916314327)
XLA Ops:
  0.6 0.7 %select_maximum_fusion.rows = f32[32,64]{1,0:T(8,128)S(1)} fusion(f32[3,64]{1,0:T(4,128)} %param.2, f32[24,64]{1,0:T(8,128)} %bitcast.9), kind=kLoop, calls=%fused_computation | loop fusion | flops 6144 | bytes 15104 | tf_op jit(solution)/shard_map/concatenate | solution.py:348
  1.4 0.1 shard_map.49
  1.5 14.9 %all_to_all.15.blocks = f32[32,8,128]{2,1,0:T(8,128)S(1)} all-to-all(f32[32,8,128]{2,1,0:T(8,128)S(1)} %bitcast.8), channel_id=1, replica_groups={{0,1,8,9,2,3,10,11,4,5,12,13,6,7,14,15,22,23,30,31,20,21,28,29,18,19,26..., dimensions={0} | all-to-all | bytes 262144 | tf_op jit(solution)/shard_map/all_to_all | solution.py:324
  16.5 0.2 collective-permute-start
  16.7 1.1 %shard_map.50 = (f32[32,384]{1,0:T(8,128)S(1)}, f32[32,1024]{1,0:T(8,128)S(1)}, bf16[384,1024]{1,0:T(8,128)(2,1)S(1)}, bf16[384,1024]{1,0:T(8,128)(2,1)S(1)}) custom-call(f32[8,256]{1,0:T(8,128)S(1)} %get-tuple-element.24.own, f32[32,8,128]{2,1,0:T(8,128)S(1)} %all_to_all.15.blocks), custom_call_target="tpu_custom_call" | custom-call | tf_op jit(solution)/shard_map/pallas_call | solution.py:351
  17.9 0.0 collective-permute-done.blocks
  17.9 1.5 %shard_map.51 = (f32[8,256]{1,0:T(8,128)S(1)}, f32[16,2,8,128]{3,2,1,0:T(8,128)S(1)}, f32[32,1024]{1,0:T(8,128)S(1)}, bf16[384,1024]{1,0:T(8,128)(2,1)S(1)}, bf16[384,1024]{1,0:T(8,128)(2,1)S(1)}) custom-call(f32[8,256]{1,0:T(8,128)S(1)} %get-tuple-element.24.own, f32[32,8,128]{2,1,0:T(8,128)S(1)} %collective-permute-done.blocks, ...), custom_call_target="tpu_custom_call" | custom-call | tf_op jit(solution)/shard_map/pallas_call | solution.py:354
  19.3 9.9 %all_to_all.16.refs_2_ = f32[32,8,128]{2,1,0:T(8,128)S(1)} all-to-all(f32[32,8,128]{2,1,0:T(8,128)S(1)} %bitcast.7), channel_id=1, replica_groups={{0,1,8,9,2,3,10,11,4,5,12,13,6,7,14,15,22,23,30,31,20,21,28,29,18,19,26..., dimensions={0} | all-to-all | bytes 262144 | tf_op jit(solution)/shard_map/all_to_all | solution.py:324
  29.2 0.2 collective-permute-start.1
  29.5 1.1 %shard_map.52 = (f32[32,384]{1,0:T(8,128)S(1)}, f32[8,256]{1,0:T(8,128)S(1)}, f32[8,256]{1,0:T(8,128)S(1)}, f32[8,8]{1,0:T(8,128)S(1)}, f32[2,8,8]{2,1,0:T(8,128)S(1)}) custom-call(f32[8,256]{1,0:T(8,128)S(1)} %get-tuple-element.24.own, f32[32,1024]{1,0:T(8,128)S(1)} %get-tuple-element.26.wide, bf16[384,1024]{1,0:T(8,128)(2,1)S(1)} %get-tuple-element.27.refs_0_, ...), custom_call_target="tpu_custom_call" | custom-call | tf_op jit(solution)/shard_map/pallas_call | solution.py:358
  30.6 0.0 collective-permute-done.1.refs_2_
  30.6 0.9 %shard_map.53 = (f32[8,256]{1,0:T(8,128)S(1)}, f32[32,1,64]{2,1,0:T(1,128)S(1)}) custom-call(f32[8,256]{1,0:T(8,128)S(1)} %get-tuple-element.24.own, f32[32,1024]{1,0:T(8,128)S(1)} %get-tuple-element.33.wide, bf16[384,1024]{1,0:T(8,128)(2,1)S(1)} %get-tuple-element.34.refs_0_, bf16[384,1024]{1,0:T(8,128)(2,1)S(1)} %get-tuple-element.35.refs_1_, ...), custom_call_target="tpu_custom_call" | custom-call | tf_op jit(solution)/shard_map/pallas_call | solution.py:363
  31.4 9.2 %all_to_all.17.partials = f32[32,1,64]{2,1,0:T(1,128)S(1)} all-to-all(f32[32,1,64]{2,1,0:T(1,128)S(1)} %get-tuple-element.41), channel_id=1, replica_groups={{0,1,8,9,2,3,10,11,4,5,12,13,6,7,14,15,22,23,30,31,20,21,28,29,18,19,26..., dimensions={0} | all-to-all | bytes 16384 | tf_op jit(solution)/shard_map/all_to_all | solution.py:324
  40.6 0.8 %shard_map.54 = (f32[3,8,64]{2,1,0:T(8,128)}, f32[3,8,64]{2,1,0:T(8,128)}, f32[3,8,8]{2,1,0:T(8,128)}) custom-call(f32[8,256]{1,0:T(8,128)S(1)} %get-tuple-element.32.refs_4_.vectors, f32[8,256]{1,0:T(8,128)S(1)} %get-tuple-element.39.shifted, f32[2,8,8]{2,1,0:T(8,128)S(1)} %get-tuple-element.40.both, f32[32,1,64]{2,1,0:T(1,128)S(1)} %all_to_all.17.partials), custom_call_target="tpu_custom_call" | custom-call | tf_op jit(solution)/shard_map/pallas_call | solution.py:368
Async XLA Ops:
  16.5 1.4 %collective-permute-start = (f32[32,8,128]{2,1,0:T(8,128)S(1)}, f32[32,8,128]{2,1,0:T(8,128)S(1)}, u32[]{:S(2)}, u32[]{:S(2)}) collective-permute-start(f32[32,8,128]{2,1,0:T(8,128)S(1)} %all_to_all.15.blocks), channel_id=1, source_target_pairs={{0,1},{1,0},{2,3},{3,2},{4,5},{5,4},{6,7},{7,6},{8,9},{9,8},{10,11... | collective-permute-start | bytes 393224 | tf_op jit(solution)/shard_map/ppermute | solution.py:330
  29.2 1.4 %collective-permute-start.1 = (f32[32,8,128]{2,1,0:T(8,128)S(1)}, f32[32,8,128]{2,1,0:T(8,128)S(1)}, u32[]{:S(2)}, u32[]{:S(2)}) collective-permute-start(f32[32,8,128]{2,1,0:T(8,128)S(1)} %all_to_all.16.refs_2_), channel_id=1, source_target_pairs={{0,1},{1,0},{2,3},{3,2},{4,5},{5,4},{6,7},{7,6},{8,9},{9,8},{10,11... | collective-permute-start | bytes 393224 | tf_op jit(solution)/shard_map/ppermute | solution.py:330

commit v14 on v12

--- a/solution.py
+++ b/solution.py
@@ -40,6 +40,10 @@
     return lax.dot_general(
         left, right, (((1,), (1,)), ((), ())), precision=precision, preferred_element_type=F32
     )
+
+
+def matmul(left, right):
+    return lax.dot_general(left, right, (((1,), (0,)), ((), ())), preferred_element_type=F32)
 
 
 def small_matmul(left, right):
@@ -215,6 +219,61 @@
     return apply_tensor(split_rows(wide_image[...]), high, low, 0, high.shape[1])
 
 
+def spread_rows(block):
+    beads = block.shape[1] // 4
+    parts = [block[:, part * beads : (part + 1) * beads] for part in range(3)]
+    empty = jnp.zeros(parts[0].shape, F32)
+    rows = []
+    for own in range(3):
+        lanes = []
+        for one, two in ((0, 0), (0, 1), (0, 2), (1, 1), (1, 2), (2, 2)):
+            lanes.append(parts[two] if own == one else parts[one] if own == two else empty)
+        rows.append(jnp.concatenate(lanes, axis=1))
+    return jnp.concatenate(rows + [jnp.zeros(rows[0].shape, F32)], axis=0)
+
+
+def backward_stage(fill, own, wide, *refs):
+    refs = list(refs)
+    if not fill:
+        (high, low), refs = refs[:2], refs[2:]
+    image, out = refs[:2]
+    if fill:
+        high, low = refs[2:4]
+    both = split_rows(spread_rows(image[...]))
+    half = both.shape[0] // 2
+
+    def add(start):
+        first = matmul(both, high[...])
+        sums = first[:half] + first[half:] + matmul(both[:half], low[...])
+        out[:, pl.ds(start, high.shape[1])] = sums
+
+    if not fill:
+        add(0)
+        return
+    columns = target_columns(own[...])
+
+    def body(index, carry):
+        start = pl.multiple_of(index * high.shape[1], 128)
+        for at in range(0, high.shape[1], 128):
+            fill_tensor(columns, wide, pl.multiple_of(start + at, 128), high, low, at)
+        add(start)
+        return carry
+
+    lax.fori_loop(0, wide.shape[1] // high.shape[1], body, 0)
+
+
+def cross_stage(images, own_sums, other_sums, partials, wide_image):
+    unpack(images, wide_image)
+    left = split_rows(wide_image[...])
+    right = split_rows(own_sums[...] + other_sums[...])
+    half = left.shape[0] // 2
+    first = matmul_nt(left, right[:half])
+    sums = first[:half] + first[half:] + matmul_nt(left[:half], right[half:])
+    partial = sums[:8, :8] + sums[8:16, 8:16] + sums[16:24, 16:24]
+    line = jnp.concatenate([partial[row : row + 1] for row in range(8)], axis=1)
+    partials[...] = jnp.broadcast_to(line[None], partials.shape)
+
+
 def third_stage(size, fill, own, wide, *refs):
     refs = list(refs)
     if not fill:
@@ -231,58 +290,55 @@
     width = own.shape[1] // 8
     sums = sum(sums[:, at : at + width] for at in range(width, 128, width)) + sums[:, :width]
     sums = sums / size
-    _, inverse_zero = cholesky(sums[:, :8])
+    noise_sums, cross_sums, image_sums = sums[:, :8], sums[:, 8:16], sums[:, 16:24]
+    _, inverse_zero = cholesky(noise_sums)
     inverse_zero_t = inverse_zero.T
-    cross_t = small_matmul(inverse_zero, sums[:, 8:16])
+    cross_t = small_matmul(inverse_zero, cross_sums)
     cross = cross_t.T
-    factor_t, inverse = cholesky(sums[:, 16:24] - small_matmul(cross, cross_t))
+    factor_t, inverse = cholesky(image_sums - small_matmul(cross, cross_t))
     factor_one_t = small_matmul(factor_t, inverse_zero_t)
+    factor_one = factor_one_t.T
     first = small_matmul(inverse_zero, without_positions(own[...]))
     moved = small_matmul(inverse_zero, own_image[...])
+    alpha = small_matmul(cross_t, inverse_zero_t)
     vectors[...] = small_matmul(inverse, own_image[...] - small_matmul(cross, first))
     known[...] = small_matmul(inverse, small_matmul(cross, moved)) + small_matmul(factor_one_t, first)
-    small[...] = inverse
-    coefficients[0] = small_matmul(cross_t, inverse_zero_t)
-    coefficients[1] = factor_one_t.T
+    image_moved = small_matmul(image_sums, inverse_zero_t)
+    moved_image = small_matmul(inverse_zero, image_sums)
+    known_sums = small_matmul(small_matmul(cross, alpha), cross_t)
+    known_sums = known_sums - small_matmul(image_moved, cross_t) - small_matmul(cross, moved_image)
+    first_sums = small_matmul(small_matmul(inverse_zero, noise_sums), inverse_zero_t)
+    vector_first = small_matmul(inverse, cross - small_matmul(cross, first_sums))
+    small[0] = inverse
+    small[1] = inverse.T
+    small[2] = known_sums
+    small[3] = small_matmul(vector_first, factor_one)
+    coefficients[0] = alpha
+    coefficients[1] = factor_one
 
 
 def fourth_stage(fill, own, wide, *refs):
     refs = list(refs)
     if not fill:
         (high, low), refs = refs[:2], refs[2:]
-    images, before, vectors_in, known, small, shifted, partials = refs[:7]
+    images, before, known, small, shifted = refs[:5]
     if fill:
-        high, low = refs[7:9]
+        high, low = refs[5:7]
     wide_image = refs[-1]
     unpack(images, wide_image)
     products = second_product(fill, own[...], wide, wide_image, high, low) + before[...]
-    vectors = vectors_in[...]
-    shift = small_matmul(small[...], assemble(products)) - known[...]
-    shifted[...] = shift
-    (vector_high, vector_low), (shift_high, shift_low) = split_two(vectors), split_two(shift)
-    partial = matmul_nt(vector_high, shift_high) + (
-        matmul_nt(vector_high, shift_low) + matmul_nt(vector_low, shift_high)
-    )
-    line = jnp.concatenate([partial[row : row + 1] for row in range(8)], axis=1)
-    partials[...] = jnp.broadcast_to(line[None], partials.shape)
-
-
-def last_kernel(size, vectors, shifted, both, partials, basis, residual, coefficients):
+    shifted[...] = small_matmul(small[0], assemble(products)) - known[...]
+
+
+def last_kernel(size, vectors, shifted, both, small, partials, basis, residual, coefficients):
     beads = basis.shape[2]
-    width = partials.shape[2]
     total = jnp.sum(partials[...], axis=0) / size
-    spread = jnp.broadcast_to(total, (8, width))
-    rows = lax.broadcasted_iota(jnp.int32, spread.shape, 0)
-    cols = lax.broadcasted_iota(jnp.int32, spread.shape, 1)
+    sums = jnp.concatenate([total[:, 8 * k : 8 * k + 8] for k in range(8)], axis=0)
+    alpha = small_matmul(small_matmul(small[0], sums + small[2]), small[1]) - small[3]
     block = vectors[...]
-    left = shifted[...]
-    transposed = jnp.where(cols % 8 == rows, spread, 0.0)
-    for k in range(8):
-        column = jnp.sum(jnp.where(cols // 8 == k, transposed, 0.0), axis=1, keepdims=True)
-        left = left - column * block[k : k + 1, :]
+    left = shifted[...] - small_matmul(alpha.T, block)
     coefficients[0:2] = both[...]
-    for k in range(8):
-        coefficients[2, k : k + 1, :] = total[:, 8 * k : 8 * k + 8]
+    coefficients[2] = alpha
     for part in range(3):
         basis[part] = block[:, part * beads : (part + 1) * beads]
         residual[part] = left[:, part * beads : (part + 1) * beads]
@@ -311,10 +367,9 @@
     return lax.all_to_all(copies, ("row", "col"), 0, 0, axis_index_groups=[ring], tiled=True)
 
 
-def gather(copies):
-    mine = to_all(copies.reshape((-1,) + copies.shape[2:]))
+def between_cores(block):
     cols = lax.axis_size("col")
-    return mine, lax.ppermute(mine, "col", [(col, col ^ 1) for col in range(cols)])
+    return lax.ppermute(block, "col", [(col, col ^ 1) for col in range(cols)])
 
 
 def local(positions, noise):
@@ -334,27 +389,33 @@
     rows = noise.transpose(1, 0, 2).reshape(3 * vecs, beads)
     rows = jnp.concatenate([rows, jnp.pad(positions, ((0, vecs - 3), (0, 0)))], axis=0)
     own, own_copies = call(pack_kernel, [block, copies])(rows)
-    one, two = gather(own_copies)
+    one = to_all(own_copies.reshape((-1,) + own_copies.shape[2:]))
+    two = between_cores(one)
     partial, one_wide, *one_tensor = call(
         functools.partial(first_stage, False), [products, wide] + kept, held
     )(own, one)
     image, images, two_wide, *two_tensor = call(
         functools.partial(first_stage, True), [block, copies, wide] + kept, held
     )(own, two, partial)
-    one, two = gather(images)
+    backward = call(functools.partial(backward_stage, not keep), wide, held)
+    other_sums = between_cores(backward(own, two_wide, *two_tensor, image))
+    own_sums = backward(own, one_wide, *one_tensor, image)
+    one = to_all(images.reshape((-1,) + images.shape[2:]))
+    partials = call(cross_stage, array(devices, 1, vecs * vecs), [held_wide])(one, own_sums, other_sums)
+    partials = to_all(partials)
+    two = between_cores(one)
     partial, vectors, known, small, both = call(
         functools.partial(third_stage, size, not keep),
-        [products, block, block, array(vecs, vecs), array(2, vecs, vecs)],
+        [products, block, block, array(4, vecs, vecs), array(2, vecs, vecs)],
         held + [held_wide],
     )(own, one_wide, *one_tensor, one, image)
-    shifted, partials = call(
-        functools.partial(fourth_stage, not keep), [block, array(devices, 1, vecs * vecs)], held + [held_wide]
-    )(own, two_wide, *two_tensor, two, partial, vectors, known, small)
-    partials = to_all(partials)
+    shifted = call(functools.partial(fourth_stage, not keep), block, held + [held_wide])(
+        own, two_wide, *two_tensor, two, partial, known, small
+    )
     basis, residual, coefficients = call(
         functools.partial(last_kernel, size),
         [array(3, vecs, beads), array(3, vecs, beads), array(3, vecs, vecs)],
-    )(vectors, shifted, both, partials)
+    )(vectors, shifted, both, small, partials)
     return (basis.transpose(1, 0, 2), residual.transpose(1, 0, 2), coefficients)
 
 

time: 41.7 us -> 46.3 us (1.11)
  blocking collectives: 34 us -> 14.9 us
  waiting for transfers between devices: 0.01 us -> 9.02 us
  starting transfers between devices: 0.5 us -> 6.44 us
  Pallas kernels: 5.51 us -> 10.2 us
  local copies, waits for them, and re-layouts: 0 us -> 3.76 us
    all_to_all x3 -> x1, blocking collectives: 34 us -> 14.9 us  [to_all(): lax.all_to_all(copies, ('row', 'col'), 0, 0, axis_index_groups=[ring], ti...]
    all_to_all x0 -> x2, waiting for transfers between devices: none -> 9.01 us  [to_all(): lax.all_to_all(copies, ('row', 'col'), 0, 0, axis_index_groups=[ring], ti...]
    all_to_all x0 -> x2, starting transfers between devices: none -> 5.83 us  [to_all(): lax.all_to_all(copies, ('row', 'col'), 0, 0, axis_index_groups=[ring], ti...]
    unnamed x0 -> x16, local copies, waits for them, and re-layouts: none -> 3.76 us
    pallas_call x1 -> x4, Pallas kernels: 0.86 us -> 4.43 us  [the longest x1 1.57 us: local(): call(functools.partial(fourth_stage, not keep), block, held + [held_wide])]
    pallas_call x1, Pallas kernels: 0.8 us -> 1.75 us  [local(): call(functools.partial(last_kernel, size), [array(3, vecs, beads), array(...]
  transfers between devices with their start and end apart: 2 -> 5, of which waited for: 0 -> 2; matrix products, arithmetic and copies ran while one was open for 0% -> 0% of each run, Pallas kernels for 5% -> 15%
where the time goes in v14:
time: 46.3 us; the launch traced here: 45.8 us
  blocking collectives  14.9 us (32%)
  Pallas kernels  10.2 us (22%)
  waiting for transfers between devices  9.02 us (19%)
  starting transfers between devices  6.44 us (14%)
  local copies, waits for them, and re-layouts  3.76 us (8%)
  other arithmetic  0.73 us (2%)
  between operations  0.73 us (2%)
    all_to_all x1, blocking collectives, to_all(): lax.all_to_all(copies, ('row', 'col'), 0, 0, axis_index_groups=[ring], ti...  14.9 us
    all_to_all x2, waiting for transfers between devices, to_all(): lax.all_to_all(copies, ('row', 'col'), 0, 0, axis_index_groups=[ring], ti...  9.01 us
    all_to_all x2, starting transfers between devices, to_all(): lax.all_to_all(copies, ('row', 'col'), 0, 0, axis_index_groups=[ring], ti...  5.83 us
    unnamed x16, local copies, waits for them, and re-layouts  3.76 us
    pallas_call x1, Pallas kernels, local(): call(functools.partial(last_kernel, size), [array(3, vecs, beads), array(...  1.75 us
    pallas_call x1, Pallas kernels, local(): call(functools.partial(fourth_stage, not keep), block, held + [held_wide])  1.57 us
    pallas_call x1, Pallas kernels, local(): call(functools.partial(first_stage, True), [block, copies, wide] + kept,...  1.49 us
    pallas_call x1, Pallas kernels, local(): call(cross_stage, array(devices, 1, vecs * vecs), [held_wide])  1.38 us
  transfers between devices with their start and end apart: 5, of which 2 were waited for; matrix products, arithmetic and copies ran while one was open for 0% of the time, Pallas kernels for 15%

profile of v14, /device:TPU:0, one launch (start us, length us, event | category | flops | bytes accessed | tf_op | source)
XLA Modules:
  0.0 45.8 jit_solution(1015202644888093779)
XLA Ops:
  0.6 0.7 %select_maximum_fusion.rows = f32[32,64]{1,0:T(8,128)S(1)} fusion(f32[3,64]{1,0:T(4,128)} %param.2, f32[24,64]{1,0:T(8,128)} %bitcast.9), kind=kLoop, calls=%fused_computation | loop fusion | flops 6144 | bytes 15104 | tf_op jit(solution)/shard_map/concatenate | solution.py:390
  1.4 0.1 shard_map.49
  1.5 14.9 %all_to_all.15.blocks = f32[32,8,128]{2,1,0:T(8,128)S(1)} all-to-all(f32[32,8,128]{2,1,0:T(8,128)S(1)} %bitcast.8), channel_id=1, replica_groups={{0,1,8,9,2,3,10,11,4,5,12,13,6,7,14,15,22,23,30,31,20,21,28,29,18,19,26..., dimensions={0} | all-to-all | bytes 262144 | tf_op jit(solution)/shard_map/all_to_all | solution.py:367
  16.5 0.2 collective-permute-start
  16.7 1.2 %shard_map.50 = (f32[32,384]{1,0:T(8,128)S(1)}, f32[32,1024]{1,0:T(8,128)S(1)}, bf16[384,1024]{1,0:T(8,128)(2,1)S(1)}, bf16[384,1024]{1,0:T(8,128)(2,1)S(1)}) custom-call(f32[8,256]{1,0:T(8,128)S(1)} %get-tuple-element.22.own, f32[32,8,128]{2,1,0:T(8,128)S(1)} %all_to_all.15.blocks), custom_call_target="tpu_custom_call" | custom-call | tf_op jit(solution)/shard_map/pallas_call | solution.py:394
  17.9 0.0 collective-permute-done.blocks
  17.9 1.5 %shard_map.51 = (f32[8,256]{1,0:T(8,128)S(1)}, f32[16,2,8,128]{3,2,1,0:T(8,128)S(1)}, f32[32,1024]{1,0:T(8,128)S(1)}, bf16[384,1024]{1,0:T(8,128)(2,1)S(1)}, bf16[384,1024]{1,0:T(8,128)(2,1)S(1)}) custom-call(f32[8,256]{1,0:T(8,128)S(1)} %get-tuple-element.22.own, f32[32,8,128]{2,1,0:T(8,128)S(1)} %collective-permute-done.blocks, ...), custom_call_target="tpu_custom_call" | custom-call | tf_op jit(solution)/shard_map/pallas_call | solution.py:397
  19.4 0.0 copy-start
  19.4 0.6 %copy-done = f32[16,2,8,128]{3,2,1,0:T(8,128)} copy-done((f32[16,2,8,128]{3,2,1,0:T(8,128)}, f32[16,2,8,128]{3,2,1,0:T(8,128)S(1)}, u32[]{:S(2)}) %copy-start) | copy-done | bytes 131096
  20.1 2.6 %all-to-all-start.1 = ((f32[32,8,128]{2,1,0:T(8,128)}), f32[32,8,128]{2,1,0:T(8,128)S(1)}, u32[]{:S(2)}, u32[]{:S(2)}) async-start(f32[32,8,128]{2,1,0:T(8,128)} %bitcast.7), calls=%async_computation.1 | async-start | bytes 262144 | tf_op jit(solution)/shard_map/all_to_all | solution.py:367
  22.6 1.1 %shard_map.55 = f32[32,1024]{1,0:T(8,128)} custom-call(f32[8,256]{1,0:T(8,128)S(1)} %get-tuple-element.22.own, f32[32,1024]{1,0:T(8,128)S(1)} %get-tuple-element.31.wide, bf16[384,1024]{1,0:T(8,128)(2,1)S(1)} %get-tuple-element.32.refs_0_, bf16[384,1024]{1,0:T(8,128)(2,1)S(1)} %get-tuple-element.33.refs_1_, f32[8,256]{1,0:T(8,128)S(1)} %get-tuple-element.29.refs_3_.refs_2_), custom_call_target="tpu_custom_call" | custom-call | tf_op jit(solution)/shard_map/pallas_call | solution.py:401
  23.7 0.1 collective-permute-start.2
  23.8 6.7 %all-to-all-done.1.refs_2_.images = f32[32,8,128]{2,1,0:T(8,128)S(1)} async-done(((f32[32,8,128]{2,1,0:T(8,128)}), f32[32,8,128]{2,1,0:T(8,128)S(1)}, u32[]{:S(2)}, u32[]{:S(2)}) %all-to-all-start.1) | async-done | bytes 131104 | tf_op jit(solution)/shard_map/all_to_all | solution.py:367
  30.5 0.2 collective-permute-start.1
  30.7 0.4 shard_map.54.own_sums
  31.1 0.0 collective-permute-done.2.other_sums
  31.1 1.4 %shard_map.56 = f32[32,1,64]{2,1,0:T(1,128)S(1)} custom-call(f32[32,8,128]{2,1,0:T(8,128)S(1)} %all-to-all-done.1.refs_2_.images, f32[32,1024]{1,0:T(8,128)S(1)} %shard_map.54.own_sums, f32[32,1024]{1,0:T(8,128)} %collective-permute-done.2.other_sums), custom_call_target="tpu_custom_call" | custom-call | tf_op jit(solution)/shard_map/pallas_call | solution.py:404
  32.5 0.0 copy-start.3
  32.5 0.6 %copy-done.3 = f32[32,1,64]{2,1,0:T(1,128)} copy-done((f32[32,1,64]{2,1,0:T(1,128)}, f32[32,1,64]{2,1,0:T(1,128)S(1)}, u32[]{:S(2)}) %copy-start.3) | copy-done | bytes 8216
  33.1 3.3 %all-to-all-start.2 = ((f32[32,1,64]{2,1,0:T(1,128)}), f32[32,1,64]{2,1,0:T(1,128)}, u32[]{:S(2)}, u32[]{:S(2)}) async-start(f32[32,1,64]{2,1,0:T(1,128)} %copy-done.3), calls=%async_computation.2 | async-start | bytes 32768 | tf_op jit(solution)/shard_map/all_to_all | solution.py:367
  36.4 1.2 %shard_map.52 = (f32[32,384]{1,0:T(8,128)S(1)}, f32[8,256]{1,0:T(8,128)S(1)}, f32[8,256]{1,0:T(8,128)S(1)}, f32[4,8,8]{2,1,0:T(8,128)S(1)}, f32[2,8,8]{2,1,0:T(8,128)S(1)}) custom-call(f32[8,256]{1,0:T(8,128)S(1)} %get-tuple-element.22.own, f32[32,1024]{1,0:T(8,128)S(1)} %get-tuple-element.24.wide, bf16[384,1024]{1,0:T(8,128)(2,1)S(1)} %get-tuple-element.25.refs_0_, ...), custom_call_target="tpu_custom_call" | custom-call | tf_op jit(solution)/shard_map/pallas_call | solution.py:407
  37.6 0.6 %copy-done.4 = f32[8,256]{1,0:T(8,128)} copy-done((f32[8,256]{1,0:T(8,128)}, f32[8,256]{1,0:T(8,128)S(1)}, u32[]{:S(2)}) %copy-start.4) | copy-done | bytes 8216
  38.2 0.6 %copy-done.6 = f32[2,8,8]{2,1,0:T(8,128)} copy-done((f32[2,8,8]{2,1,0:T(8,128)}, f32[2,8,8]{2,1,0:T(8,128)S(1)}, u32[]{:S(2)}) %copy-start.6) | copy-done | bytes 536
  38.8 0.0 collective-permute-done.1.refs_2_
  38.8 1.6 %shard_map.53.shifted = f32[8,256]{1,0:T(8,128)S(1)} custom-call(f32[8,256]{1,0:T(8,128)S(1)} %get-tuple-element.22.own, f32[32,1024]{1,0:T(8,128)S(1)} %get-tuple-element.31.wide, bf16[384,1024]{1,0:T(8,128)(2,1)S(1)} %get-tuple-element.32.refs_0_, bf16[384,1024]{1,0:T(8,128)(2,1)S(1)} %get-tuple-element.33.refs_1_, ...), custom_call_target="tpu_custom_call" | custom-call | tf_op jit(solution)/shard_map/pallas_call | solution.py:412
  40.4 0.0 copy-start.1
  40.4 0.6 %copy-done.1 = f32[4,8,8]{2,1,0:T(8,128)} copy-done((f32[4,8,8]{2,1,0:T(8,128)}, f32[4,8,8]{2,1,0:T(8,128)S(1)}, u32[]{:S(2)}) %copy-start.1) | copy-done | bytes 1048
  41.0 2.3 %all-to-all-done.2.partials = f32[32,1,64]{2,1,0:T(1,128)} async-done(((f32[32,1,64]{2,1,0:T(1,128)}), f32[32,1,64]{2,1,0:T(1,128)}, u32[]{:S(2)}, u32[]{:S(2)}) %all-to-all-start.2) | async-done | bytes 8224 | tf_op jit(solution)/shard_map/all_to_all | solution.py:367
  43.3 0.0 copy-done.5
  43.3 0.0 copy-done.7
  43.3 0.7 %copy-done.2 = f32[4,8,8]{2,1,0:T(8,128)S(1)} copy-done((f32[4,8,8]{2,1,0:T(8,128)S(1)}, f32[4,8,8]{2,1,0:T(8,128)}, u32[]{:S(2)}) %copy-start.2) | copy-done | bytes 1048
  44.0 1.7 %shard_map.57 = (f32[3,8,64]{2,1,0:T(8,128)}, f32[3,8,64]{2,1,0:T(8,128)}, f32[3,8,8]{2,1,0:T(8,128)}) custom-call(f32[8,256]{1,0:T(8,128)S(1)} %copy-done.5, f32[8,256]{1,0:T(8,128)S(1)} %shard_map.53.shifted, f32[2,8,8]{2,1,0:T(8,128)S(1)} %copy-done.7, f32[4,8,8]{2,1,0:T(8,128)S(1)} %copy-done.2, f32[32,1,64]{2,1,0:T(1,128)} %all-to-all-done.2.partials), custom_call_target="tpu_custom_call" | custom-call | tf_op jit(solution)/shard_map/pallas_call | solution.py:415
  (5 shorter events, 0.0 us)
Async XLA Ops:
  16.5 1.4 %collective-permute-start = (f32[32,8,128]{2,1,0:T(8,128)S(1)}, f32[32,8,128]{2,1,0:T(8,128)S(1)}, u32[]{:S(2)}, u32[]{:S(2)}) collective-permute-start(f32[32,8,128]{2,1,0:T(8,128)S(1)} %all_to_all.15.blocks), channel_id=1, source_target_pairs={{0,1},{1,0},{2,3},{3,2},{4,5},{5,4},{6,7},{7,6},{8,9},{9,8},{10,11... | collective-permute-start | bytes 393224 | tf_op jit(solution)/shard_map/ppermute | solution.py:372
  19.4 0.7 %copy-start = (f32[16,2,8,128]{3,2,1,0:T(8,128)}, f32[16,2,8,128]{3,2,1,0:T(8,128)S(1)}, u32[]{:S(2)}) copy-start(f32[16,2,8,128]{3,2,1,0:T(8,128)S(1)} %get-tuple-element.28) | copy-start | bytes 393220
  20.1 10.4 %all-to-all-start.1 = ((f32[32,8,128]{2,1,0:T(8,128)}), f32[32,8,128]{2,1,0:T(8,128)S(1)}, u32[]{:S(2)}, u32[]{:S(2)}) async-start(f32[32,8,128]{2,1,0:T(8,128)} %bitcast.7), calls=%async_computation.1 | async-start | bytes 262144 | tf_op jit(solution)/shard_map/all_to_all | solution.py:367
  23.7 7.4 %collective-permute-start.2 = (f32[32,1024]{1,0:T(8,128)}, f32[32,1024]{1,0:T(8,128)}, u32[]{:S(2)}, u32[]{:S(2)}) collective-permute-start(f32[32,1024]{1,0:T(8,128)} %shard_map.55), channel_id=1, source_target_pairs={{0,1},{1,0},{2,3},{3,2},{4,5},{5,4},{6,7},{7,6},{8,9},{9,8},{10,11... | collective-permute-start | bytes 393224 | tf_op jit(solution)/shard_map/ppermute | solution.py:372
  30.5 8.3 %collective-permute-start.1 = (f32[32,8,128]{2,1,0:T(8,128)S(1)}, f32[32,8,128]{2,1,0:T(8,128)}, u32[]{:S(2)}, u32[]{:S(2)}) collective-permute-start(f32[32,8,128]{2,1,0:T(8,128)S(1)} %all-to-all-done.1.refs_2_.images), channel_id=1, source_target_pairs={{0,1},{1,0},{2,3},{3,2},{4,5},{5,4},{6,7},{7,6},{8,9},{9,8},{10,11... | collective-permute-start | bytes 393224 | tf_op jit(solution)/shard_map/ppermute | solution.py:372
  32.5 0.6 %copy-start.3 = (f32[32,1,64]{2,1,0:T(1,128)}, f32[32,1,64]{2,1,0:T(1,128)S(1)}, u32[]{:S(2)}) copy-start(f32[32,1,64]{2,1,0:T(1,128)S(1)} %shard_map.56) | copy-start | bytes 24580
  33.1 10.2 %all-to-all-start.2 = ((f32[32,1,64]{2,1,0:T(1,128)}), f32[32,1,64]{2,1,0:T(1,128)}, u32[]{:S(2)}, u32[]{:S(2)}) async-start(f32[32,1,64]{2,1,0:T(1,128)} %copy-done.3), calls=%async_computation.2 | async-start | bytes 32768 | tf_op jit(solution)/shard_map/all_to_all | solution.py:367
  37.6 0.6 %copy-start.4 = (f32[8,256]{1,0:T(8,128)}, f32[8,256]{1,0:T(8,128)S(1)}, u32[]{:S(2)}) copy-start(f32[8,256]{1,0:T(8,128)S(1)} %get-tuple-element.30.vectors) | copy-start | bytes 24580
  38.2 0.6 %copy-start.6 = (f32[2,8,8]{2,1,0:T(8,128)}, f32[2,8,8]{2,1,0:T(8,128)S(1)}, u32[]{:S(2)}) copy-start(f32[2,8,8]{2,1,0:T(8,128)S(1)} %get-tuple-element.37.both) | copy-start | bytes 1540
  38.8 4.5 %copy-start.5 = (f32[8,256]{1,0:T(8,128)S(1)}, f32[8,256]{1,0:T(8,128)}, u32[]{:S(2)}) copy-start(f32[8,256]{1,0:T(8,128)} %copy-done.4) | copy-start | bytes 24580
  38.8 4.5 %copy-start.7 = (f32[2,8,8]{2,1,0:T(8,128)S(1)}, f32[2,8,8]{2,1,0:T(8,128)}, u32[]{:S(2)}) copy-start(f32[2,8,8]{2,1,0:T(8,128)} %copy-done.6) | copy-start | bytes 1540
  40.4 0.6 %copy-start.1 = (f32[4,8,8]{2,1,0:T(8,128)}, f32[4,8,8]{2,1,0:T(8,128)S(1)}, u32[]{:S(2)}) copy-start(f32[4,8,8]{2,1,0:T(8,128)S(1)} %get-tuple-element.36.refs_5_.small) | copy-start | bytes 3076
  43.3 0.7 %copy-start.2 = (f32[4,8,8]{2,1,0:T(8,128)S(1)}, f32[4,8,8]{2,1,0:T(8,128)}, u32[]{:S(2)}) copy-start(f32[4,8,8]{2,1,0:T(8,128)} %copy-done.1) | copy-start | bytes 3076

commit v15 on v14

--- a/solution.py
+++ b/solution.py
@@ -9,6 +9,7 @@
 
 CHUNK = 1024
 KEPT = 8 * 1024 * 1024
+VMEM = 16 * 1024 * 1024
 F32 = jnp.float32
 BF16 = jnp.bfloat16
 
@@ -232,14 +233,7 @@
     return jnp.concatenate(rows + [jnp.zeros(rows[0].shape, F32)], axis=0)
 
 
-def backward_stage(fill, own, wide, *refs):
-    refs = list(refs)
-    if not fill:
-        (high, low), refs = refs[:2], refs[2:]
-    image, out = refs[:2]
-    if fill:
-        high, low = refs[2:4]
-    both = split_rows(spread_rows(image[...]))
+def backward_half(fill, own, wide, both, high, low, out):
     half = both.shape[0] // 2
 
     def add(start):
@@ -260,6 +254,18 @@
         return carry
 
     lax.fori_loop(0, wide.shape[1] // high.shape[1], body, 0)
+
+
+def backward_stage(fill, own, image, one_wide, two_wide, *refs):
+    if fill:
+        one_sums, two_sums, high, low = refs
+        tensors = [(high, low)] * 2
+    else:
+        *tensors, one_sums, two_sums = refs
+        tensors = [tensors[:2], tensors[2:]]
+    both = split_rows(spread_rows(image[...]))
+    backward_half(fill, own, two_wide, both, *tensors[1], two_sums)
+    backward_half(fill, own, one_wide, both, *tensors[0], one_sums)
 
 
 def cross_stage(images, own_sums, other_sums, partials, wide_image):
@@ -353,7 +359,7 @@
         kernel,
         out_shape=outs,
         scratch_shapes=list(scratch),
-        compiler_params=pltpu.CompilerParams(vmem_limit_bytes=48 * 1024 * 1024),
+        compiler_params=pltpu.CompilerParams(vmem_limit_bytes=VMEM),
         **options,
     )
 
@@ -397,11 +403,13 @@
     image, images, two_wide, *two_tensor = call(
         functools.partial(first_stage, True), [block, copies, wide] + kept, held
     )(own, two, partial)
-    backward = call(functools.partial(backward_stage, not keep), wide, held)
-    other_sums = between_cores(backward(own, two_wide, *two_tensor, image))
-    own_sums = backward(own, one_wide, *one_tensor, image)
+    own_sums, other_sums = call(functools.partial(backward_stage, not keep), [wide, wide], held)(
+        own, image, one_wide, two_wide, *one_tensor, *two_tensor
+    )
+    other_sums = between_cores(other_sums)
     one = to_all(images.reshape((-1,) + images.shape[2:]))
     partials = call(cross_stage, array(devices, 1, vecs * vecs), [held_wide])(one, own_sums, other_sums)
+    one, partials = lax.optimization_barrier((one, partials))
     partials = to_all(partials)
     two = between_cores(one)
     partial, vectors, known, small, both = call(

time: 46.3 us -> 46.9 us (1.013)
  local copies, waits for them, and re-layouts: 3.76 us -> 6.89 us
  Pallas kernels: 10.2 us -> 8.42 us
  waiting for transfers between devices: 9.02 us -> 8.25 us
    unnamed x16 -> x24, local copies, waits for them, and re-layouts: 3.76 us -> 6.89 us
    all_to_all x2, waiting for transfers between devices: 9.01 us -> 7 us  [to_all(): lax.all_to_all(copies, ('row', 'col'), 0, 0, axis_index_groups=[ring], ti...]
    ppermute x3, waiting for transfers between devices: 0.01 us -> 1.25 us  [between_cores(): return lax.ppermute(block, 'col', [(col, col ^ 1) for col in range(cols)])]
    pallas_call x1, Pallas kernels: 1.38 us -> 0.45 us  [local(): call(cross_stage, array(devices, 1, vecs * vecs), [held_wide])]
    pallas_call x2 -> x1, Pallas kernels: 1.48 us -> 0.67 us  [local(): call(functools.partial(backward_stage, not keep), [wide, wide], held)]
  transfers between devices with their start and end apart: 5 -> 5, of which waited for: 2 -> 3; matrix products, arithmetic and copies ran while one was open for 0% -> 0% of each run, Pallas kernels for 15% -> 10%
where the time goes in v15:
time: 46.9 us; the launch traced here: 46.3 us
  blocking collectives  14.9 us (32%)
  Pallas kernels  8.42 us (18%)
  waiting for transfers between devices  8.25 us (18%)
  local copies, waits for them, and re-layouts  6.89 us (15%)
  starting transfers between devices  6.35 us (14%)
  between operations  0.74 us (2%)
  other arithmetic  0.73 us (2%)
    all_to_all x1, blocking collectives, to_all(): lax.all_to_all(copies, ('row', 'col'), 0, 0, axis_index_groups=[ring], ti...  14.9 us
    all_to_all x2, waiting for transfers between devices, to_all(): lax.all_to_all(copies, ('row', 'col'), 0, 0, axis_index_groups=[ring], ti...  7 us
    unnamed x24, local copies, waits for them, and re-layouts  6.89 us
    all_to_all x2, starting transfers between devices, to_all(): lax.all_to_all(copies, ('row', 'col'), 0, 0, axis_index_groups=[ring], ti...  5.74 us
    pallas_call x1, Pallas kernels, local(): call(functools.partial(last_kernel, size), [array(3, vecs, beads), array(...  1.75 us
    pallas_call x1, Pallas kernels, local(): call(functools.partial(fourth_stage, not keep), block, held + [held_wide])  1.57 us
    pallas_call x1, Pallas kernels, local(): call(functools.partial(first_stage, True), [block, copies, wide] + kept,...  1.5 us
    ppermute x3, waiting for transfers between devices, between_cores(): return lax.ppermute(block, 'col', [(col, col ^ 1) for col in range(cols)])  1.25 us
  transfers between devices with their start and end apart: 5, of which 3 were waited for; matrix products, arithmetic and copies ran while one was open for 0% of the time, Pallas kernels for 10%

profile of v15, /device:TPU:0, one launch (start us, length us, event | category | flops | bytes accessed | tf_op | source)
XLA Modules:
  0.0 46.3 jit_solution(1385630592456012826)
XLA Ops:
  0.6 0.7 %select_maximum_fusion.rows = f32[32,64]{1,0:T(8,128)S(1)} fusion(f32[3,64]{1,0:T(4,128)} %param.2, f32[24,64]{1,0:T(8,128)} %bitcast.9), kind=kLoop, calls=%fused_computation | loop fusion | flops 6144 | bytes 15104 | tf_op jit(solution)/shard_map/concatenate | solution.py:396
  1.4 0.1 shard_map.49
  1.5 14.9 %all_to_all.15.blocks = f32[32,8,128]{2,1,0:T(8,128)S(1)} all-to-all(f32[32,8,128]{2,1,0:T(8,128)S(1)} %bitcast.8), channel_id=1, replica_groups={{0,1,8,9,2,3,10,11,4,5,12,13,6,7,14,15,22,23,30,31,20,21,28,29,18,19,26..., dimensions={0} | all-to-all | bytes 262144 | tf_op jit(solution)/shard_map/all_to_all | solution.py:373
  16.5 0.2 collective-permute-start
  16.7 1.2 %shard_map.50 = (f32[32,384]{1,0:T(8,128)S(1)}, f32[32,1024]{1,0:T(8,128)S(1)}, bf16[384,1024]{1,0:T(8,128)(2,1)S(1)}, bf16[384,1024]{1,0:T(8,128)(2,1)S(1)}) custom-call(f32[8,256]{1,0:T(8,128)S(1)} %get-tuple-element.26.own, f32[32,8,128]{2,1,0:T(8,128)S(1)} %all_to_all.15.blocks), custom_call_target="tpu_custom_call" | custom-call | tf_op jit(solution)/shard_map/pallas_call | solution.py:400
  17.9 0.0 collective-permute-done.blocks
  17.9 1.5 %shard_map.51 = (f32[8,256]{1,0:T(8,128)S(1)}, f32[16,2,8,128]{3,2,1,0:T(8,128)S(1)}, f32[32,1024]{1,0:T(8,128)S(1)}, bf16[384,1024]{1,0:T(8,128)(2,1)S(1)}, bf16[384,1024]{1,0:T(8,128)(2,1)S(1)}) custom-call(f32[8,256]{1,0:T(8,128)S(1)} %get-tuple-element.26.own, f32[32,8,128]{2,1,0:T(8,128)S(1)} %collective-permute-done.blocks, ...), custom_call_target="tpu_custom_call" | custom-call | tf_op jit(solution)/shard_map/pallas_call | solution.py:403
  19.4 0.0 copy-start.4
  19.4 0.6 %copy-done.4 = f32[16,2,8,128]{3,2,1,0:T(8,128)} copy-done((f32[16,2,8,128]{3,2,1,0:T(8,128)}, f32[16,2,8,128]{3,2,1,0:T(8,128)S(1)}, u32[]{:S(2)}) %copy-start.4) | copy-done | bytes 131096
  20.0 2.6 %all-to-all-start.1 = ((f32[32,8,128]{2,1,0:T(8,128)}), f32[32,8,128]{2,1,0:T(8,128)S(1)}, u32[]{:S(2)}, u32[]{:S(2)}) async-start(f32[32,8,128]{2,1,0:T(8,128)} %bitcast.7), calls=%async_computation.1 | async-start | bytes 262144 | tf_op jit(solution)/shard_map/all_to_all | solution.py:373
  22.6 0.7 %shard_map.52 = (f32[32,1024]{1,0:T(8,128)S(1)}, f32[32,1024]{1,0:T(8,128)S(1)}) custom-call(f32[8,256]{1,0:T(8,128)S(1)} %get-tuple-element.26.own, f32[8,256]{1,0:T(8,128)S(1)} %get-tuple-element.33.image.refs_3_, f32[32,1024]{1,0:T(8,128)S(1)} %get-tuple-element.28.one_wide.wide, f32[32,1024]{1,0:T(8,128)S(1)} %get-tuple-element.34.two_wide.wide, ...), custom_call_target="tpu_custom_call" | custom-call | tf_op jit(solution)/shard_map/pallas_call | solution.py:406
  23.3 0.7 %copy-done = f32[32,1024]{1,0:T(8,128)} copy-done((f32[32,1024]{1,0:T(8,128)}, f32[32,1024]{1,0:T(8,128)S(1)}, u32[]{:S(2)}) %copy-start) | copy-done | bytes 131096
  24.0 0.1 collective-permute-start.1
  24.1 1.2 %collective-permute-done.1.other_sums = f32[32,1024]{1,0:T(8,128)S(1)} collective-permute-done((f32[32,1024]{1,0:T(8,128)S(1)}, f32[32,1024]{1,0:T(8,128)S(1)}, u32[]{:S(2)}, u32[]{:S(2)}) %collective-permute-start.1) | collective-permute-done | bytes 131104 | tf_op jit(solution)/shard_map/ppermute | solution.py:378
  25.3 0.7 %copy-done.2 = f32[32,1024]{1,0:T(8,128)} copy-done((f32[32,1024]{1,0:T(8,128)}, f32[32,1024]{1,0:T(8,128)S(1)}, u32[]{:S(2)}) %copy-start.2) | copy-done | bytes 131096
  26.0 4.5 %all-to-all-done.1.images.refs_2_ = f32[32,8,128]{2,1,0:T(8,128)S(1)} async-done(((f32[32,8,128]{2,1,0:T(8,128)}), f32[32,8,128]{2,1,0:T(8,128)S(1)}, u32[]{:S(2)}, u32[]{:S(2)}) %all-to-all-start.1) | async-done | bytes 131104 | tf_op jit(solution)/shard_map/all_to_all | solution.py:373
  30.5 0.9 %copy-done.1 = f32[32,1024]{1,0:T(8,128)S(1)} copy-done((f32[32,1024]{1,0:T(8,128)S(1)}, f32[32,1024]{1,0:T(8,128)}, u32[]{:S(2)}) %copy-start.1) | copy-done | bytes 131096
  31.4 0.9 %copy-done.3 = f32[32,1024]{1,0:T(8,128)S(1)} copy-done((f32[32,1024]{1,0:T(8,128)S(1)}, f32[32,1024]{1,0:T(8,128)}, u32[]{:S(2)}) %copy-start.3) | copy-done | bytes 131096
  32.3 0.5 shard_map.53
  32.7 0.6 %copy-done.7 = f32[32,1,64]{2,1,0:T(1,128)} copy-done((f32[32,1,64]{2,1,0:T(1,128)}, f32[32,1,64]{2,1,0:T(1,128)S(1)}, u32[]{:S(2)}) %copy-start.7) | copy-done | bytes 8216
  33.3 0.2 collective-permute-start.2
  33.6 3.2 %all-to-all-start.2 = ((f32[32,1,64]{2,1,0:T(1,128)}), f32[32,1,64]{2,1,0:T(1,128)}, u32[]{:S(2)}, u32[]{:S(2)}) async-start(f32[32,1,64]{2,1,0:T(1,128)} %copy-done.7), calls=%async_computation.2 | async-start | bytes 32768 | tf_op jit(solution)/shard_map/all_to_all | solution.py:373
  36.8 1.2 %shard_map.54 = (f32[32,384]{1,0:T(8,128)S(1)}, f32[8,256]{1,0:T(8,128)S(1)}, f32[8,256]{1,0:T(8,128)S(1)}, f32[4,8,8]{2,1,0:T(8,128)S(1)}, f32[2,8,8]{2,1,0:T(8,128)S(1)}) custom-call(f32[8,256]{1,0:T(8,128)S(1)} %get-tuple-element.26.own, f32[32,1024]{1,0:T(8,128)S(1)} %get-tuple-element.28.one_wide.wide, bf16[384,1024]{1,0:T(8,128)(2,1)S(1)} %get-tuple-element.29.refs_0_, ...), custom_call_target="tpu_custom_call" | custom-call | tf_op jit(solution)/shard_map/pallas_call | solution.py:415
  38.0 0.6 %copy-done.8 = f32[8,256]{1,0:T(8,128)} copy-done((f32[8,256]{1,0:T(8,128)}, f32[8,256]{1,0:T(8,128)S(1)}, u32[]{:S(2)}) %copy-start.8) | copy-done | bytes 8216
  38.6 0.6 %copy-done.10 = f32[2,8,8]{2,1,0:T(8,128)} copy-done((f32[2,8,8]{2,1,0:T(8,128)}, f32[2,8,8]{2,1,0:T(8,128)S(1)}, u32[]{:S(2)}) %copy-start.10) | copy-done | bytes 536
  39.2 0.0 collective-permute-done.2.refs_2_
  39.2 1.6 %shard_map.55.shifted = f32[8,256]{1,0:T(8,128)S(1)} custom-call(f32[8,256]{1,0:T(8,128)S(1)} %get-tuple-element.26.own, f32[32,1024]{1,0:T(8,128)S(1)} %get-tuple-element.34.two_wide.wide, bf16[384,1024]{1,0:T(8,128)(2,1)S(1)} %get-tuple-element.35.refs_2_.refs_0_, bf16[384,1024]{1,0:T(8,128)(2,1)S(1)} %get-tuple-element.36.refs_3_.refs_1_, ...), custom_call_target="tpu_custom_call" | custom-call | tf_op jit(solution)/shard_map/pallas_call | solution.py:420
  40.8 0.6 %copy-done.5 = f32[4,8,8]{2,1,0:T(8,128)} copy-done((f32[4,8,8]{2,1,0:T(8,128)}, f32[4,8,8]{2,1,0:T(8,128)S(1)}, u32[]{:S(2)}) %copy-start.5) | copy-done | bytes 1048
  41.3 2.5 %all-to-all-done.2.partials = f32[32,1,64]{2,1,0:T(1,128)} async-done(((f32[32,1,64]{2,1,0:T(1,128)}), f32[32,1,64]{2,1,0:T(1,128)}, u32[]{:S(2)}, u32[]{:S(2)}) %all-to-all-start.2) | async-done | bytes 8224 | tf_op jit(solution)/shard_map/all_to_all | solution.py:373
  43.9 0.0 copy-done.9
  43.9 0.7 %copy-done.6 = f32[4,8,8]{2,1,0:T(8,128)S(1)} copy-done((f32[4,8,8]{2,1,0:T(8,128)S(1)}, f32[4,8,8]{2,1,0:T(8,128)}, u32[]{:S(2)}) %copy-start.6) | copy-done | bytes 1048
  44.6 1.7 %shard_map.56 = (f32[3,8,64]{2,1,0:T(8,128)}, f32[3,8,64]{2,1,0:T(8,128)}, f32[3,8,8]{2,1,0:T(8,128)}) custom-call(f32[8,256]{1,0:T(8,128)S(1)} %copy-done.9, f32[8,256]{1,0:T(8,128)S(1)} %shard_map.55.shifted, f32[2,8,8]{2,1,0:T(8,128)S(1)} %copy-done.11, f32[4,8,8]{2,1,0:T(8,128)S(1)} %copy-done.6, f32[32,1,64]{2,1,0:T(1,128)} %all-to-all-done.2.partials), custom_call_target="tpu_custom_call" | custom-call | tf_op jit(solution)/shard_map/pallas_call | solution.py:423
  (12 shorter events, 0.0 us)
Async XLA Ops:
  16.5 1.4 %collective-permute-start = (f32[32,8,128]{2,1,0:T(8,128)S(1)}, f32[32,8,128]{2,1,0:T(8,128)S(1)}, u32[]{:S(2)}, u32[]{:S(2)}) collective-permute-start(f32[32,8,128]{2,1,0:T(8,128)S(1)} %all_to_all.15.blocks), channel_id=1, source_target_pairs={{0,1},{1,0},{2,3},{3,2},{4,5},{5,4},{6,7},{7,6},{8,9},{9,8},{10,11... | collective-permute-start | bytes 393224 | tf_op jit(solution)/shard_map/ppermute | solution.py:378
  19.4 0.6 %copy-start.4 = (f32[16,2,8,128]{3,2,1,0:T(8,128)}, f32[16,2,8,128]{3,2,1,0:T(8,128)S(1)}, u32[]{:S(2)}) copy-start(f32[16,2,8,128]{3,2,1,0:T(8,128)S(1)} %get-tuple-element.32) | copy-start | bytes 393220
  20.0 10.4 %all-to-all-start.1 = ((f32[32,8,128]{2,1,0:T(8,128)}), f32[32,8,128]{2,1,0:T(8,128)S(1)}, u32[]{:S(2)}, u32[]{:S(2)}) async-start(f32[32,8,128]{2,1,0:T(8,128)} %bitcast.7), calls=%async_computation.1 | async-start | bytes 262144 | tf_op jit(solution)/shard_map/all_to_all | solution.py:373
  23.3 0.7 %copy-start = (f32[32,1024]{1,0:T(8,128)}, f32[32,1024]{1,0:T(8,128)S(1)}, u32[]{:S(2)}) copy-start(f32[32,1024]{1,0:T(8,128)S(1)} %get-tuple-element.37.own_sums) | copy-start | bytes 393220
  24.0 1.3 %collective-permute-start.1 = (f32[32,1024]{1,0:T(8,128)S(1)}, f32[32,1024]{1,0:T(8,128)S(1)}, u32[]{:S(2)}, u32[]{:S(2)}) collective-permute-start(f32[32,1024]{1,0:T(8,128)S(1)} %get-tuple-element.38), channel_id=1, source_target_pairs={{0,1},{1,0},{2,3},{3,2},{4,5},{5,4},{6,7},{7,6},{8,9},{9,8},{10,11... | collective-permute-start | bytes 393224 | tf_op jit(solution)/shard_map/ppermute | solution.py:378
  25.3 0.7 %copy-start.2 = (f32[32,1024]{1,0:T(8,128)}, f32[32,1024]{1,0:T(8,128)S(1)}, u32[]{:S(2)}) copy-start(f32[32,1024]{1,0:T(8,128)S(1)} %collective-permute-done.1.other_sums) | copy-start | bytes 393220
  30.5 0.9 %copy-start.1 = (f32[32,1024]{1,0:T(8,128)S(1)}, f32[32,1024]{1,0:T(8,128)}, u32[]{:S(2)}) copy-start(f32[32,1024]{1,0:T(8,128)} %copy-done) | copy-start | bytes 393220
  31.4 0.9 %copy-start.3 = (f32[32,1024]{1,0:T(8,128)S(1)}, f32[32,1024]{1,0:T(8,128)}, u32[]{:S(2)}) copy-start(f32[32,1024]{1,0:T(8,128)} %copy-done.2) | copy-start | bytes 393220
  32.7 0.6 %copy-start.7 = (f32[32,1,64]{2,1,0:T(1,128)}, f32[32,1,64]{2,1,0:T(1,128)S(1)}, u32[]{:S(2)}) copy-start(f32[32,1,64]{2,1,0:T(1,128)S(1)} %shard_map.53) | copy-start | bytes 24580
  33.3 5.8 %collective-permute-start.2 = (f32[32,8,128]{2,1,0:T(8,128)S(1)}, f32[32,8,128]{2,1,0:T(8,128)}, u32[]{:S(2)}, u32[]{:S(2)}) collective-permute-start(f32[32,8,128]{2,1,0:T(8,128)S(1)} %all-to-all-done.1.images.refs_2_), channel_id=1, source_target_pairs={{0,1},{1,0},{2,3},{3,2},{4,5},{5,4},{6,7},{7,6},{8,9},{9,8},{10,11... | collective-permute-start | bytes 393224 | tf_op jit(solution)/shard_map/ppermute | solution.py:378
  33.6 10.3 %all-to-all-start.2 = ((f32[32,1,64]{2,1,0:T(1,128)}), f32[32,1,64]{2,1,0:T(1,128)}, u32[]{:S(2)}, u32[]{:S(2)}) async-start(f32[32,1,64]{2,1,0:T(1,128)} %copy-done.7), calls=%async_computation.2 | async-start | bytes 32768 | tf_op jit(solution)/shard_map/all_to_all | solution.py:373
  38.0 0.6 %copy-start.8 = (f32[8,256]{1,0:T(8,128)}, f32[8,256]{1,0:T(8,128)S(1)}, u32[]{:S(2)}) copy-start(f32[8,256]{1,0:T(8,128)S(1)} %get-tuple-element.40.vectors) | copy-start | bytes 24580
  38.6 0.6 %copy-start.10 = (f32[2,8,8]{2,1,0:T(8,128)}, f32[2,8,8]{2,1,0:T(8,128)S(1)}, u32[]{:S(2)}) copy-start(f32[2,8,8]{2,1,0:T(8,128)S(1)} %get-tuple-element.44.both) | copy-start | bytes 1540
  39.2 4.7 %copy-start.9 = (f32[8,256]{1,0:T(8,128)S(1)}, f32[8,256]{1,0:T(8,128)}, u32[]{:S(2)}) copy-start(f32[8,256]{1,0:T(8,128)} %copy-done.8) | copy-start | bytes 24580
  39.2 4.7 %copy-start.11 = (f32[2,8,8]{2,1,0:T(8,128)S(1)}, f32[2,8,8]{2,1,0:T(8,128)}, u32[]{:S(2)}) copy-start(f32[2,8,8]{2,1,0:T(8,128)} %copy-done.10) | copy-start | bytes 1540
  40.7 0.6 %copy-start.5 = (f32[4,8,8]{2,1,0:T(8,128)}, f32[4,8,8]{2,1,0:T(8,128)S(1)}, u32[]{:S(2)}) copy-start(f32[4,8,8]{2,1,0:T(8,128)S(1)} %get-tuple-element.43.refs_5_.small) | copy-start | bytes 3076
  43.9 0.7 %copy-start.6 = (f32[4,8,8]{2,1,0:T(8,128)S(1)}, f32[4,8,8]{2,1,0:T(8,128)}, u32[]{:S(2)}) copy-start(f32[4,8,8]{2,1,0:T(8,128)} %copy-done.5) | copy-start | bytes 3076

commit v16 on v15

--- a/solution.py
+++ b/solution.py
@@ -8,7 +8,7 @@
 from jax.sharding import PartitionSpec as P
 
 CHUNK = 1024
-KEPT = 8 * 1024 * 1024
+KEPT = 2 * 1024 * 1024
 VMEM = 16 * 1024 * 1024
 F32 = jnp.float32
 BF16 = jnp.bfloat16
@@ -233,39 +233,34 @@
     return jnp.concatenate(rows + [jnp.zeros(rows[0].shape, F32)], axis=0)
 
 
-def backward_half(fill, own, wide, both, high, low, out):
-    half = both.shape[0] // 2
-
-    def add(start):
-        first = matmul(both, high[...])
-        sums = first[:half] + first[half:] + matmul(both[:half], low[...])
-        out[:, pl.ds(start, high.shape[1])] = sums
-
-    if not fill:
-        add(0)
+def backward_half(own, wide, both, high, low, out):
+    half, width = both.shape[0] // 2, high.shape[1]
+    columns = target_columns(own[...])
+
+    def chunk(start):
+        for at in range(0, width, 128):
+            fill_tensor(columns, wide, pl.multiple_of(start + at, 128), high, low, at)
+        for at in range(0, width, 256):
+            lanes = pl.ds(at, min(256, width - at))
+            first = matmul(both, high[:, lanes])
+            sums = first[:half] + first[half:] + matmul(both[:half], low[:, lanes])
+            out[:, pl.ds(pl.multiple_of(start + at, 128), sums.shape[1])] = sums
+
+    if wide.shape[1] == width:
+        chunk(0)
         return
-    columns = target_columns(own[...])
 
     def body(index, carry):
-        start = pl.multiple_of(index * high.shape[1], 128)
-        for at in range(0, high.shape[1], 128):
-            fill_tensor(columns, wide, pl.multiple_of(start + at, 128), high, low, at)
-        add(start)
+        chunk(pl.multiple_of(index * width, 128))
         return carry
 
-    lax.fori_loop(0, wide.shape[1] // high.shape[1], body, 0)
-
-
-def backward_stage(fill, own, image, one_wide, two_wide, *refs):
-    if fill:
-        one_sums, two_sums, high, low = refs
-        tensors = [(high, low)] * 2
-    else:
-        *tensors, one_sums, two_sums = refs
-        tensors = [tensors[:2], tensors[2:]]
+    lax.fori_loop(0, wide.shape[1] // width, body, 0)
+
+
+def backward_stage(own, image, one_wide, two_wide, one_sums, two_sums, *tensors):
     both = split_rows(spread_rows(image[...]))
-    backward_half(fill, own, two_wide, both, *tensors[1], two_sums)
-    backward_half(fill, own, one_wide, both, *tensors[0], one_sums)
+    backward_half(own, two_wide, both, *tensors[-2:], two_sums)
+    backward_half(own, one_wide, both, *tensors[:2], one_sums)
 
 
 def cross_stage(images, own_sums, other_sums, partials, wide_image):
@@ -323,16 +318,9 @@
     coefficients[1] = factor_one
 
 
-def fourth_stage(fill, own, wide, *refs):
-    refs = list(refs)
-    if not fill:
-        (high, low), refs = refs[:2], refs[2:]
-    images, before, known, small, shifted = refs[:5]
-    if fill:
-        high, low = refs[5:7]
-    wide_image = refs[-1]
+def fourth_stage(own, wide, images, before, known, small, shifted, high, low, wide_image):
     unpack(images, wide_image)
-    products = second_product(fill, own[...], wide, wide_image, high, low) + before[...]
+    products = all_filled(own[...], wide, wide_image, high, low) + before[...]
     shifted[...] = small_matmul(small[0], assemble(products)) - known[...]
 
 
@@ -383,28 +371,26 @@
     devices = lax.axis_size("row") * lax.axis_size("col")
     total = beads * devices // 2
     size = 3.0 * beads * devices
-    keep = 2 * 2 * 2 * 6 * beads * total <= KEPT
+    keep = 2 * 2 * 6 * beads * total <= KEPT
     width = total if keep else min(total, CHUNK)
     block = array(vecs, 4 * beads)
     copies = array(devices // 2, 2, vecs, 2 * beads)
     products = array(4 * vecs, 6 * beads)
     wide, held_wide = array(4 * vecs, total), pltpu.VMEM((4 * vecs, total), F32)
     kept = [array(6 * beads, width, dtype=BF16)] * 2 if keep else []
-    held = [] if keep else [pltpu.VMEM((6 * beads, width), BF16)] * 2
+    held = [pltpu.VMEM((6 * beads, width), BF16)] * 2
 
     rows = noise.transpose(1, 0, 2).reshape(3 * vecs, beads)
     rows = jnp.concatenate([rows, jnp.pad(positions, ((0, vecs - 3), (0, 0)))], axis=0)
     own, own_copies = call(pack_kernel, [block, copies])(rows)
     one = to_all(own_copies.reshape((-1,) + own_copies.shape[2:]))
     two = between_cores(one)
-    partial, one_wide, *one_tensor = call(
-        functools.partial(first_stage, False), [products, wide] + kept, held
-    )(own, one)
-    image, images, two_wide, *two_tensor = call(
-        functools.partial(first_stage, True), [block, copies, wide] + kept, held
-    )(own, two, partial)
-    own_sums, other_sums = call(functools.partial(backward_stage, not keep), [wide, wide], held)(
-        own, image, one_wide, two_wide, *one_tensor, *two_tensor
+    partial, one_wide = call(functools.partial(first_stage, False), [products, wide], held)(own, one)
+    image, images, two_wide = call(functools.partial(first_stage, True), [block, copies, wide], held)(
+        own, two, partial
+    )
+    own_sums, other_sums, *one_tensor = call(backward_stage, [wide, wide] + kept, held)(
+        own, image, one_wide, two_wide
     )
     other_sums = between_cores(other_sums)
     one = to_all(images.reshape((-1,) + images.shape[2:]))
@@ -415,11 +401,9 @@
     partial, vectors, known, small, both = call(
         functools.partial(third_stage, size, not keep),
         [products, block, block, array(4, vecs, vecs), array(2, vecs, vecs)],
-        held + [held_wide],
+        (held if not keep else []) + [held_wide],
     )(own, one_wide, *one_tensor, one, image)
-    shifted = call(functools.partial(fourth_stage, not keep), block, held + [held_wide])(
-        own, two_wide, *two_tensor, two, partial, known, small
-    )
+    shifted = call(fourth_stage, block, held + [held_wide])(own, two_wide, two, partial, known, small)
     basis, residual, coefficients = call(
         functools.partial(last_kernel, size),
         [array(3, vecs, beads), array(3, vecs, beads), array(3, vecs, vecs)],

time: 46.9 us -> 42.7 us (0.910)
  local copies, waits for them, and re-layouts: 6.89 us -> 0 us
  waiting for transfers between devices: 8.25 us -> 10.4 us
  Pallas kernels: 8.42 us -> 9.83 us
  starting transfers between devices: 6.35 us -> 5.71 us
    unnamed x24 -> x0, local copies, waits for them, and re-layouts: 6.89 us -> none
    all_to_all x2, waiting for transfers between devices: 7 us -> 9.21 us  [to_all(): lax.all_to_all(copies, ('row', 'col'), 0, 0, axis_index_groups=[ring], ti...]
    pallas_call x4, Pallas kernels: 4.9 us -> 6.42 us  [the longest x1 2.13 us: local(): call(functools.partial(first_stage, True), [block, copies, wide], held)]
    pallas_call x1, Pallas kernels: 1.75 us -> 1.03 us  [local(): call(functools.partial(last_kernel, size), [array(3, vecs, beads), array(...]
    all_to_all x2, starting transfers between devices: 5.74 us -> 5.06 us  [to_all(): lax.all_to_all(copies, ('row', 'col'), 0, 0, axis_index_groups=[ring], ti...]
    pallas_call x1, Pallas kernels: 0.45 us -> 1.06 us  [local(): call(cross_stage, array(devices, 1, vecs * vecs), [held_wide])]
  transfers between devices with their start and end apart: 5 -> 5, of which waited for: 3 -> 3; matrix products, arithmetic and copies ran while one was open for 0% -> 0% of each run, Pallas kernels for 10% -> 13%
where the time goes in v16:
time: 42.7 us; the launch traced here: 42.4 us
  blocking collectives  14.9 us (35%)
  waiting for transfers between devices  10.4 us (24%)
  Pallas kernels  9.83 us (23%)
  starting transfers between devices  5.71 us (13%)
  other arithmetic  0.73 us (2%)
  between operations  0.68 us (2%)
    all_to_all x1, blocking collectives, to_all(): lax.all_to_all(copies, ('row', 'col'), 0, 0, axis_index_groups=[ring], ti...  14.9 us
    all_to_all x2, waiting for transfers between devices, to_all(): lax.all_to_all(copies, ('row', 'col'), 0, 0, axis_index_groups=[ring], ti...  9.21 us
    all_to_all x2, starting transfers between devices, to_all(): lax.all_to_all(copies, ('row', 'col'), 0, 0, axis_index_groups=[ring], ti...  5.06 us
    pallas_call x1, Pallas kernels, local(): call(functools.partial(first_stage, True), [block, copies, wide], held)  2.13 us
    pallas_call x1, Pallas kernels, local(): call(backward_stage, [wide, wide] + kept, held)  1.93 us
    ppermute x3, waiting for transfers between devices, between_cores(): return lax.ppermute(block, 'col', [(col, col ^ 1) for col in range(cols)])  1.24 us
    pallas_call x1, Pallas kernels, local(): call(fourth_stage, block, held + [held_wide])  1.23 us
    pallas_call x1, Pallas kernels, local(): call(functools.partial(third_stage, size, not keep), [products, block, bl...  1.17 us
  transfers between devices with their start and end apart: 5, of which 3 were waited for; matrix products, arithmetic and copies ran while one was open for 0% of the time, Pallas kernels for 13%

profile of v16, /device:TPU:0, one launch (start us, length us, event | category | flops | bytes accessed | tf_op | source)
XLA Modules:
  0.0 42.4 jit_solution(1883502306888766205)
XLA Ops:
  0.6 0.7 %select_maximum_fusion.rows = f32[32,64]{1,0:T(8,128)S(1)} fusion(f32[3,64]{1,0:T(4,128)} %param.2, f32[24,64]{1,0:T(8,128)} %bitcast.8), kind=kLoop, calls=%fused_computation | loop fusion | flops 6144 | bytes 15104 | tf_op jit(solution)/shard_map/concatenate | solution.py:384
  1.4 0.1 shard_map.49
  1.5 14.9 %all_to_all.15.blocks = f32[32,8,128]{2,1,0:T(8,128)S(1)} all-to-all(f32[32,8,128]{2,1,0:T(8,128)S(1)} %bitcast.7), channel_id=1, replica_groups={{0,1,8,9,2,3,10,11,4,5,12,13,6,7,14,15,22,23,30,31,20,21,28,29,18,19,26..., dimensions={0} | all-to-all | bytes 262144 | tf_op jit(solution)/shard_map/all_to_all | solution.py:361
  16.5 0.2 collective-permute-start
  16.7 1.1 %shard_map.50 = (f32[32,384]{1,0:T(8,128)S(1)}, f32[32,1024]{1,0:T(8,128)S(1)}) custom-call(f32[8,256]{1,0:T(8,128)S(1)} %get-tuple-element.24.own, f32[32,8,128]{2,1,0:T(8,128)S(1)} %all_to_all.15.blocks), custom_call_target="tpu_custom_call" | custom-call | tf_op jit(solution)/shard_map/pallas_call | solution.py:388
  17.8 0.0 collective-permute-done.blocks
  17.9 2.1 %shard_map.51 = (f32[8,256]{1,0:T(8,128)S(1)}, f32[16,2,8,128]{3,2,1,0:T(8,128)}, f32[32,1024]{1,0:T(8,128)S(1)}) custom-call(f32[8,256]{1,0:T(8,128)S(1)} %get-tuple-element.24.own, f32[32,8,128]{2,1,0:T(8,128)S(1)} %collective-permute-done.blocks, f32[32,384]{1,0:T(8,128)S(1)} %get-tuple-element.27.refs_0_), custom_call_target="tpu_custom_call" | custom-call | tf_op jit(solution)/shard_map/pallas_call | solution.py:389
  20.0 2.6 %all-to-all-start.1 = ((f32[32,8,128]{2,1,0:T(8,128)}), f32[32,8,128]{2,1,0:T(8,128)S(1)}, u32[]{:S(2)}, u32[]{:S(2)}) async-start(f32[32,8,128]{2,1,0:T(8,128)} %bitcast.3), calls=%async_computation.1 | async-start | bytes 262144 | tf_op jit(solution)/shard_map/all_to_all | solution.py:361
  22.6 1.9 %shard_map.52 = (f32[32,1024]{1,0:T(8,128)S(1)}, f32[32,1024]{1,0:T(8,128)S(1)}, bf16[384,1024]{1,0:T(8,128)(2,1)S(1)}, bf16[384,1024]{1,0:T(8,128)(2,1)S(1)}) custom-call(f32[8,256]{1,0:T(8,128)S(1)} %get-tuple-element.24.own, f32[8,256]{1,0:T(8,128)S(1)} %get-tuple-element.28.image.refs_3_, f32[32,1024]{1,0:T(8,128)S(1)} %get-tuple-element.26.one_wide.wide, ...), custom_call_target="tpu_custom_call" | custom-call | tf_op jit(solution)/shard_map/pallas_call | solution.py:392
  24.5 0.2 collective-permute-start.1
  24.6 1.2 %collective-permute-done.1.other_sums = f32[32,1024]{1,0:T(8,128)S(1)} collective-permute-done((f32[32,1024]{1,0:T(8,128)S(1)}, f32[32,1024]{1,0:T(8,128)S(1)}, u32[]{:S(2)}, u32[]{:S(2)}) %collective-permute-start.1) | collective-permute-done | bytes 131104 | tf_op jit(solution)/shard_map/ppermute | solution.py:366
  25.9 4.5 %all-to-all-done.1.images.refs_2_ = f32[32,8,128]{2,1,0:T(8,128)S(1)} async-done(((f32[32,8,128]{2,1,0:T(8,128)}), f32[32,8,128]{2,1,0:T(8,128)S(1)}, u32[]{:S(2)}, u32[]{:S(2)}) %all-to-all-start.1) | async-done | bytes 131104 | tf_op jit(solution)/shard_map/all_to_all | solution.py:361
  30.4 1.1 %shard_map.53 = f32[32,1,64]{2,1,0:T(1,128)} custom-call(f32[32,8,128]{2,1,0:T(8,128)S(1)} %all-to-all-done.1.images.refs_2_, f32[32,1024]{1,0:T(8,128)S(1)} %get-tuple-element.33.own_sums, f32[32,1024]{1,0:T(8,128)S(1)} %collective-permute-done.1.other_sums), custom_call_target="tpu_custom_call" | custom-call | tf_op jit(solution)/shard_map/pallas_call | solution.py:397
  31.5 0.2 collective-permute-start.2
  31.7 2.5 %all-to-all-start.2 = ((f32[32,1,64]{2,1,0:T(1,128)}), f32[32,1,64]{2,1,0:T(1,128)S(1)}, u32[]{:S(2)}, u32[]{:S(2)}) async-start(f32[32,1,64]{2,1,0:T(1,128)} %shard_map.53), calls=%async_computation.2 | async-start | bytes 32768 | tf_op jit(solution)/shard_map/all_to_all | solution.py:361
  34.2 1.2 %shard_map.54 = (f32[32,384]{1,0:T(8,128)S(1)}, f32[8,256]{1,0:T(8,128)S(1)}, f32[8,256]{1,0:T(8,128)S(1)}, f32[4,8,8]{2,1,0:T(8,128)S(1)}, f32[2,8,8]{2,1,0:T(8,128)S(1)}) custom-call(f32[8,256]{1,0:T(8,128)S(1)} %get-tuple-element.24.own, f32[32,1024]{1,0:T(8,128)S(1)} %get-tuple-element.26.one_wide.wide, bf16[384,1024]{1,0:T(8,128)(2,1)S(1)} %get-tuple-element.30.refs_0_, ...), custom_call_target="tpu_custom_call" | custom-call | tf_op jit(solution)/shard_map/pallas_call | solution.py:401
  35.4 0.0 collective-permute-done.2.images
  35.4 1.2 %shard_map.55.shifted = f32[8,256]{1,0:T(8,128)S(1)} custom-call(f32[8,256]{1,0:T(8,128)S(1)} %get-tuple-element.24.own, f32[32,1024]{1,0:T(8,128)S(1)} %get-tuple-element.29.two_wide.wide, f32[32,8,128]{2,1,0:T(8,128)S(1)} %collective-permute-done.2.images, f32[32,384]{1,0:T(8,128)S(1)} %get-tuple-element.37.before, f32[8,256]{1,0:T(8,128)S(1)} %get-tuple-element.38.known, ...), custom_call_target="tpu_custom_call" | custom-call | tf_op jit(solution)/shard_map/pallas_call | solution.py:406
  36.6 4.7 %all-to-all-done.2.partials = f32[32,1,64]{2,1,0:T(1,128)S(1)} async-done(((f32[32,1,64]{2,1,0:T(1,128)}), f32[32,1,64]{2,1,0:T(1,128)S(1)}, u32[]{:S(2)}, u32[]{:S(2)}) %all-to-all-start.2) | async-done | bytes 8224 | tf_op jit(solution)/shard_map/all_to_all | solution.py:361
  41.3 1.0 %shard_map.56 = (f32[3,8,64]{2,1,0:T(8,128)}, f32[3,8,64]{2,1,0:T(8,128)}, f32[3,8,8]{2,1,0:T(8,128)}) custom-call(f32[8,256]{1,0:T(8,128)S(1)} %get-tuple-element.36.vectors, f32[8,256]{1,0:T(8,128)S(1)} %shard_map.55.shifted, f32[2,8,8]{2,1,0:T(8,128)S(1)} %get-tuple-element.40.both, f32[4,8,8]{2,1,0:T(8,128)S(1)} %get-tuple-element.39.small, ...), custom_call_target="tpu_custom_call" | custom-call | tf_op jit(solution)/shard_map/pallas_call | solution.py:407
Async XLA Ops:
  16.5 1.4 %collective-permute-start = (f32[32,8,128]{2,1,0:T(8,128)S(1)}, f32[32,8,128]{2,1,0:T(8,128)S(1)}, u32[]{:S(2)}, u32[]{:S(2)}) collective-permute-start(f32[32,8,128]{2,1,0:T(8,128)S(1)} %all_to_all.15.blocks), channel_id=1, source_target_pairs={{0,1},{1,0},{2,3},{3,2},{4,5},{5,4},{6,7},{7,6},{8,9},{9,8},{10,11... | collective-permute-start | bytes 393224 | tf_op jit(solution)/shard_map/ppermute | solution.py:366
  20.0 10.4 %all-to-all-start.1 = ((f32[32,8,128]{2,1,0:T(8,128)}), f32[32,8,128]{2,1,0:T(8,128)S(1)}, u32[]{:S(2)}, u32[]{:S(2)}) async-start(f32[32,8,128]{2,1,0:T(8,128)} %bitcast.3), calls=%async_computation.1 | async-start | bytes 262144 | tf_op jit(solution)/shard_map/all_to_all | solution.py:361
  24.5 1.4 %collective-permute-start.1 = (f32[32,1024]{1,0:T(8,128)S(1)}, f32[32,1024]{1,0:T(8,128)S(1)}, u32[]{:S(2)}, u32[]{:S(2)}) collective-permute-start(f32[32,1024]{1,0:T(8,128)S(1)} %get-tuple-element.34), channel_id=1, source_target_pairs={{0,1},{1,0},{2,3},{3,2},{4,5},{5,4},{6,7},{7,6},{8,9},{9,8},{10,11... | collective-permute-start | bytes 393224 | tf_op jit(solution)/shard_map/ppermute | solution.py:366
  31.5 3.9 %collective-permute-start.2 = (f32[32,8,128]{2,1,0:T(8,128)S(1)}, f32[32,8,128]{2,1,0:T(8,128)S(1)}, u32[]{:S(2)}, u32[]{:S(2)}) collective-permute-start(f32[32,8,128]{2,1,0:T(8,128)S(1)} %all-to-all-done.1.images.refs_2_), channel_id=1, source_target_pairs={{0,1},{1,0},{2,3},{3,2},{4,5},{5,4},{6,7},{7,6},{8,9},{9,8},{10,11... | collective-permute-start | bytes 393224 | tf_op jit(solution)/shard_map/ppermute | solution.py:366
  31.7 9.6 %all-to-all-start.2 = ((f32[32,1,64]{2,1,0:T(1,128)}), f32[32,1,64]{2,1,0:T(1,128)S(1)}, u32[]{:S(2)}, u32[]{:S(2)}) async-start(f32[32,1,64]{2,1,0:T(1,128)} %shard_map.53), calls=%async_computation.2 | async-start | bytes 32768 | tf_op jit(solution)/shard_map/all_to_all | solution.py:361

commit v17 on v12

--- a/solution.py
+++ b/solution.py
@@ -66,41 +66,32 @@
     return [jnp.broadcast_to(targets[:, axis : axis + 1], (beads, 128)) for axis in range(3)]
 
 
-def fill_tensor(columns, wide, start, high, low, at):
-    beads = columns[0].shape[0]
-    block = 32 if beads % 32 == 0 else beads
-    sources = [wide[24 + axis : 25 + axis, pl.ds(start, 128)] for axis in range(3)]
-    to = pl.ds(at, 128)
-    for row in range(0, beads, block):
-        moved = [columns[axis][row : row + block] - sources[axis] for axis in range(3)]
-        square = moved[0] * moved[0] + moved[1] * moved[1] + moved[2] * moved[2]
-        square = jnp.maximum(square, 1e-12)
-        inverse = lax.rsqrt(square)
-        inverse_sq = inverse * inverse
-        near = square < 4.0
-        iso = inverse * jnp.where(near, square * (inverse - 9.0 / 32.0), 0.75 + 0.5 * inverse_sq)
-        along = inverse * jnp.where(near, 3.0 / 32.0, inverse_sq * (0.75 - 1.5 * inverse_sq))
-        scaled = [along * item for item in moved]
-        parts = [
-            iso + scaled[0] * moved[0],
-            scaled[0] * moved[1],
-            scaled[0] * moved[2],
-            iso + scaled[1] * moved[1],
-            scaled[1] * moved[2],
-            iso + scaled[2] * moved[2],
-        ]
-        for part, value in enumerate(parts):
-            upper, lower = split_two(value)
-            rows = slice(part * beads + row, part * beads + row + block)
-            high[rows, to] = upper
-            low[rows, to] = lower
-
-
-def apply_tensor(both, high, low, at, step):
-    lanes = pl.ds(at, step)
+def tensor(columns, wide, start):
+    moved = [columns[axis] - wide[24 + axis : 25 + axis, pl.ds(start, 128)] for axis in range(3)]
+    square = moved[0] * moved[0] + moved[1] * moved[1] + moved[2] * moved[2]
+    square = jnp.maximum(square, 1e-12)
+    inverse = lax.rsqrt(square)
+    inverse_sq = inverse * inverse
+    near = square < 4.0
+    iso = inverse * jnp.where(near, square * (inverse - 9.0 / 32.0), 0.75 + 0.5 * inverse_sq)
+    along = inverse * jnp.where(near, 3.0 / 32.0, inverse_sq * (0.75 - 1.5 * inverse_sq))
+    scaled = [along * item for item in moved]
+    parts = [
+        iso + scaled[0] * moved[0],
+        scaled[0] * moved[1],
+        scaled[0] * moved[2],
+        iso + scaled[1] * moved[1],
+        scaled[1] * moved[2],
+        iso + scaled[2] * moved[2],
+    ]
+    highs, lows = zip(*[split_two(value) for value in parts])
+    return jnp.concatenate(highs, axis=0), jnp.concatenate(lows, axis=0)
+
+
+def apply_tensor(both, high, low):
     half = both.shape[0] // 2
-    first = matmul_nt(both, high[:, lanes])
-    return first[:half] + first[half:] + matmul_nt(both[:half], low[:, lanes])
+    first = matmul_nt(both, high)
+    return first[:half] + first[half:] + matmul_nt(both[:half], low)
 
 
 def split_rows(*values):
@@ -129,15 +120,17 @@
 def filled_product(columns, source, wide, start, high, low):
     width = high.shape[1]
     products = jnp.zeros((32, high.shape[0]), F32)
-    steps = [(at, min(256, width - at)) for at in range(0, width, 256)]
-    vectors = [split_rows(wide[:, pl.ds(pl.multiple_of(start + at, 128), step)]) for at, step in steps]
-    for index in range(len(steps) + 1):
-        if index < len(steps):
-            at, step = steps[index]
-            for part in range(at, at + step, 128):
-                fill_tensor(columns, source, pl.multiple_of(start + part, 128), high, low, part)
-        if index > 0:
-            products = products + apply_tensor(vectors[index - 1], high, low, *steps[index - 1])
+    for at in range(0, width, 256):
+        step = min(256, width - at)
+        lanes = pl.ds(at, step)
+        both = split_rows(wide[:, pl.ds(pl.multiple_of(start + at, 128), step)])
+        pieces = [
+            tensor(columns, source, pl.multiple_of(start + part, 128)) for part in range(at, at + step, 128)
+        ]
+        upper, lower = [jnp.concatenate(piece, axis=1) for piece in zip(*pieces)]
+        high[:, lanes] = upper
+        low[:, lanes] = lower
+        products = products + apply_tensor(both, upper, lower)
     return products
 
 
@@ -212,7 +205,7 @@
 def second_product(fill, own, wide, wide_image, high, low):
     if fill:
         return all_filled(own, wide, wide_image, high, low)
-    return apply_tensor(split_rows(wide_image[...]), high, low, 0, high.shape[1])
+    return apply_tensor(split_rows(wide_image[...]), high[...], low[...])
 
 
 def third_stage(size, fill, own, wide, *refs):

time: 41.7 us -> 41.5 us (level)
  transfers between devices with their start and end apart: 2 -> 2, of which waited for: 0 -> 1; matrix products, arithmetic and copies ran while one was open for 0% -> 0% of each run, Pallas kernels for 5% -> 5%
where the time goes in v17:
time: 41.5 us; the launch traced here: 41.2 us
  blocking collectives  34 us (82%)
  Pallas kernels  5.18 us (12%)
  other arithmetic  0.73 us (2%)
  between operations  0.68 us (2%)
  starting transfers between devices  0.5 us (1%)
    all_to_all x3, blocking collectives, to_all(): lax.all_to_all(copies, ('row', 'col'), 0, 0, axis_index_groups=[ring], ti...  34 us
    pallas_call x1, Pallas kernels, local(): call(functools.partial(first_stage, True), [block, copies, wide] + kept,...  1.3 us
    pallas_call x1, Pallas kernels, local(): call(functools.partial(third_stage, size, not keep), [products, block, bl...  1.11 us
    pallas_call x1, Pallas kernels, local(): call(functools.partial(first_stage, False), [products, wide] + kept, held)  0.97 us
    pallas_call x1, Pallas kernels, local(): call(functools.partial(fourth_stage, not keep), [block, array(devices, 1,...  0.86 us
  transfers between devices with their start and end apart: 2, of which 1 were waited for; matrix products, arithmetic and copies ran while one was open for 0% of the time, Pallas kernels for 5%

profile of v17, /device:TPU:0, one launch (start us, length us, event | category | flops | bytes accessed | tf_op | source)
XLA Modules:
  0.0 41.2 jit_solution(16582085759547667016)
XLA Ops:
  0.6 0.7 %select_maximum_fusion.rows = f32[32,64]{1,0:T(8,128)S(1)} fusion(f32[3,64]{1,0:T(4,128)} %param.2, f32[24,64]{1,0:T(8,128)} %bitcast.9), kind=kLoop, calls=%fused_computation | loop fusion | flops 6144 | bytes 15104 | tf_op jit(solution)/shard_map/concatenate | solution.py:328
  1.4 0.1 shard_map.49
  1.5 14.9 %all_to_all.15.blocks = f32[32,8,128]{2,1,0:T(8,128)S(1)} all-to-all(f32[32,8,128]{2,1,0:T(8,128)S(1)} %bitcast.8), channel_id=1, replica_groups={{0,1,8,9,2,3,10,11,4,5,12,13,6,7,14,15,22,23,30,31,20,21,28,29,18,19,26..., dimensions={0} | all-to-all | bytes 262144 | tf_op jit(solution)/shard_map/all_to_all | solution.py:304
  16.5 0.2 collective-permute-start
  16.7 1.0 %shard_map.50 = (f32[32,384]{1,0:T(8,128)S(1)}, f32[32,1024]{1,0:T(8,128)S(1)}, bf16[384,1024]{1,0:T(8,128)(2,1)S(1)}, bf16[384,1024]{1,0:T(8,128)(2,1)S(1)}) custom-call(f32[8,256]{1,0:T(8,128)S(1)} %get-tuple-element.24.own, f32[32,8,128]{2,1,0:T(8,128)S(1)} %all_to_all.15.blocks), custom_call_target="tpu_custom_call" | custom-call | tf_op jit(solution)/shard_map/pallas_call | solution.py:331
  17.7 0.1 collective-permute-done.blocks
  17.8 1.3 %shard_map.51 = (f32[8,256]{1,0:T(8,128)S(1)}, f32[16,2,8,128]{3,2,1,0:T(8,128)S(1)}, f32[32,1024]{1,0:T(8,128)S(1)}, bf16[384,1024]{1,0:T(8,128)(2,1)S(1)}, bf16[384,1024]{1,0:T(8,128)(2,1)S(1)}) custom-call(f32[8,256]{1,0:T(8,128)S(1)} %get-tuple-element.24.own, f32[32,8,128]{2,1,0:T(8,128)S(1)} %collective-permute-done.blocks, ...), custom_call_target="tpu_custom_call" | custom-call | tf_op jit(solution)/shard_map/pallas_call | solution.py:334
  19.1 9.9 %all_to_all.16.refs_2_ = f32[32,8,128]{2,1,0:T(8,128)S(1)} all-to-all(f32[32,8,128]{2,1,0:T(8,128)S(1)} %bitcast.7), channel_id=1, replica_groups={{0,1,8,9,2,3,10,11,4,5,12,13,6,7,14,15,22,23,30,31,20,21,28,29,18,19,26..., dimensions={0} | all-to-all | bytes 262144 | tf_op jit(solution)/shard_map/all_to_all | solution.py:304
  29.0 0.2 collective-permute-start.1
  29.3 1.1 %shard_map.52 = (f32[32,384]{1,0:T(8,128)S(1)}, f32[8,256]{1,0:T(8,128)S(1)}, f32[8,256]{1,0:T(8,128)S(1)}, f32[8,8]{1,0:T(8,128)S(1)}, f32[2,8,8]{2,1,0:T(8,128)S(1)}) custom-call(f32[8,256]{1,0:T(8,128)S(1)} %get-tuple-element.24.own, f32[32,1024]{1,0:T(8,128)S(1)} %get-tuple-element.26.wide, bf16[384,1024]{1,0:T(8,128)(2,1)S(1)} %get-tuple-element.27.refs_0_, ...), custom_call_target="tpu_custom_call" | custom-call | tf_op jit(solution)/shard_map/pallas_call | solution.py:338
  30.4 0.0 collective-permute-done.1.refs_2_
  30.4 0.9 %shard_map.53 = (f32[8,256]{1,0:T(8,128)S(1)}, f32[32,1,64]{2,1,0:T(1,128)S(1)}) custom-call(f32[8,256]{1,0:T(8,128)S(1)} %get-tuple-element.24.own, f32[32,1024]{1,0:T(8,128)S(1)} %get-tuple-element.33.wide, bf16[384,1024]{1,0:T(8,128)(2,1)S(1)} %get-tuple-element.34.refs_0_, bf16[384,1024]{1,0:T(8,128)(2,1)S(1)} %get-tuple-element.35.refs_1_, ...), custom_call_target="tpu_custom_call" | custom-call | tf_op jit(solution)/shard_map/pallas_call | solution.py:343
  31.3 9.2 %all_to_all.17.partials = f32[32,1,64]{2,1,0:T(1,128)S(1)} all-to-all(f32[32,1,64]{2,1,0:T(1,128)S(1)} %get-tuple-element.41), channel_id=1, replica_groups={{0,1,8,9,2,3,10,11,4,5,12,13,6,7,14,15,22,23,30,31,20,21,28,29,18,19,26..., dimensions={0} | all-to-all | bytes 16384 | tf_op jit(solution)/shard_map/all_to_all | solution.py:304
  40.4 0.8 %shard_map.54 = (f32[3,8,64]{2,1,0:T(8,128)}, f32[3,8,64]{2,1,0:T(8,128)}, f32[3,8,8]{2,1,0:T(8,128)}) custom-call(f32[8,256]{1,0:T(8,128)S(1)} %get-tuple-element.32.refs_4_.vectors, f32[8,256]{1,0:T(8,128)S(1)} %get-tuple-element.39.shifted, f32[2,8,8]{2,1,0:T(8,128)S(1)} %get-tuple-element.40.both, f32[32,1,64]{2,1,0:T(1,128)S(1)} %all_to_all.17.partials), custom_call_target="tpu_custom_call" | custom-call | tf_op jit(solution)/shard_map/pallas_call | solution.py:347
Async XLA Ops:
  16.5 1.3 %collective-permute-start = (f32[32,8,128]{2,1,0:T(8,128)S(1)}, f32[32,8,128]{2,1,0:T(8,128)S(1)}, u32[]{:S(2)}, u32[]{:S(2)}) collective-permute-start(f32[32,8,128]{2,1,0:T(8,128)S(1)} %all_to_all.15.blocks), channel_id=1, source_target_pairs={{0,1},{1,0},{2,3},{3,2},{4,5},{5,4},{6,7},{7,6},{8,9},{9,8},{10,11... | collective-permute-start | bytes 393224 | tf_op jit(solution)/shard_map/ppermute | solution.py:310
  29.0 1.4 %collective-permute-start.1 = (f32[32,8,128]{2,1,0:T(8,128)S(1)}, f32[32,8,128]{2,1,0:T(8,128)S(1)}, u32[]{:S(2)}, u32[]{:S(2)}) collective-permute-start(f32[32,8,128]{2,1,0:T(8,128)S(1)} %all_to_all.16.refs_2_), channel_id=1, source_target_pairs={{0,1},{1,0},{2,3},{3,2},{4,5},{5,4},{6,7},{7,6},{8,9},{9,8},{10,11... | collective-permute-start | bytes 393224 | tf_op jit(solution)/shard_map/ppermute | solution.py:310

commit v18 on v17

--- a/solution.py
+++ b/solution.py
@@ -297,11 +297,8 @@
 
 def to_all(copies):
     rows, cols = lax.axis_size("row"), lax.axis_size("col")
-    layers, middle = range(cols // 2), rows // 2
-    chips = [(row, layer) for layer in layers for row in range(middle)]
-    chips = chips + [(row, layer) for layer in reversed(layers) for row in range(middle, rows)]
-    ring = [row * cols + 2 * layer + core for row, layer in chips for core in range(2)]
-    return lax.all_to_all(copies, ("row", "col"), 0, 0, axis_index_groups=[ring], tiled=True)
+    order = [row * cols + 2 * layer + core for layer in range(cols // 2) for row in range(rows) for core in range(2)]
+    return lax.all_to_all(copies, ("row", "col"), 0, 0, axis_index_groups=[order], tiled=True)
 
 
 def gather(copies):

time: 41.5 us -> 41.7 us (level)
  no operation moved by 1% of the time
where the time goes in v18:
time: 41.7 us; the launch traced here: 41.5 us
  blocking collectives  34.3 us (82%)
  Pallas kernels  5.17 us (12%)
  other arithmetic  0.73 us (2%)
  between operations  0.67 us (2%)
  starting transfers between devices  0.43 us (1%)
    all_to_all x3, blocking collectives, to_all(): lax.all_to_all(copies, ('row', 'col'), 0, 0, axis_index_groups=[order], t...  34.3 us
    pallas_call x1, Pallas kernels, local(): call(functools.partial(first_stage, True), [block, copies, wide] + kept,...  1.3 us
    pallas_call x1, Pallas kernels, local(): call(functools.partial(third_stage, size, not keep), [products, block, bl...  1.1 us
    pallas_call x1, Pallas kernels, local(): call(functools.partial(first_stage, False), [products, wide] + kept, held)  0.97 us
    pallas_call x1, Pallas kernels, local(): call(functools.partial(fourth_stage, not keep), [block, array(devices, 1,...  0.85 us
  transfers between devices with their start and end apart: 2, of which 1 were waited for; matrix products, arithmetic and copies ran while one was open for 0% of the time, Pallas kernels for 5%

profile of v18, /device:TPU:0, one launch (start us, length us, event | category | flops | bytes accessed | tf_op | source)
XLA Modules:
  0.0 41.5 jit_solution(13809018002476174506)
XLA Ops:
  0.6 0.7 %select_maximum_fusion.rows = f32[32,64]{1,0:T(8,128)S(1)} fusion(f32[3,64]{1,0:T(4,128)} %param.2, f32[24,64]{1,0:T(8,128)} %bitcast.9), kind=kLoop, calls=%fused_computation | loop fusion | flops 6144 | bytes 15104 | tf_op jit(solution)/shard_map/concatenate | solution.py:325
  1.4 0.1 shard_map.49
  1.5 15.3 %all_to_all.15.blocks = f32[32,8,128]{2,1,0:T(8,128)S(1)} all-to-all(f32[32,8,128]{2,1,0:T(8,128)S(1)} %bitcast.8), channel_id=1, replica_groups={{0,1,8,9,16,17,24,25,2,3,10,11,18,19,26,27,4,5,12,13,20,21,28,29,6,7,14..., dimensions={0} | all-to-all | bytes 262144 | tf_op jit(solution)/shard_map/all_to_all | solution.py:301
  16.8 0.2 collective-permute-start
  17.1 1.0 %shard_map.50 = (f32[32,384]{1,0:T(8,128)S(1)}, f32[32,1024]{1,0:T(8,128)S(1)}, bf16[384,1024]{1,0:T(8,128)(2,1)S(1)}, bf16[384,1024]{1,0:T(8,128)(2,1)S(1)}) custom-call(f32[8,256]{1,0:T(8,128)S(1)} %get-tuple-element.24.own, f32[32,8,128]{2,1,0:T(8,128)S(1)} %all_to_all.15.blocks), custom_call_target="tpu_custom_call" | custom-call | tf_op jit(solution)/shard_map/pallas_call | solution.py:328
  18.0 0.2 collective-permute-done.blocks
  18.2 1.3 %shard_map.51 = (f32[8,256]{1,0:T(8,128)S(1)}, f32[16,2,8,128]{3,2,1,0:T(8,128)S(1)}, f32[32,1024]{1,0:T(8,128)S(1)}, bf16[384,1024]{1,0:T(8,128)(2,1)S(1)}, bf16[384,1024]{1,0:T(8,128)(2,1)S(1)}) custom-call(f32[8,256]{1,0:T(8,128)S(1)} %get-tuple-element.24.own, f32[32,8,128]{2,1,0:T(8,128)S(1)} %collective-permute-done.blocks, ...), custom_call_target="tpu_custom_call" | custom-call | tf_op jit(solution)/shard_map/pallas_call | solution.py:331
  19.5 10.0 %all_to_all.16.refs_2_ = f32[32,8,128]{2,1,0:T(8,128)S(1)} all-to-all(f32[32,8,128]{2,1,0:T(8,128)S(1)} %bitcast.7), channel_id=1, replica_groups={{0,1,8,9,16,17,24,25,2,3,10,11,18,19,26,27,4,5,12,13,20,21,28,29,6,7,14..., dimensions={0} | all-to-all | bytes 262144 | tf_op jit(solution)/shard_map/all_to_all | solution.py:301
  29.5 0.2 collective-permute-start.1
  29.7 1.1 %shard_map.52 = (f32[32,384]{1,0:T(8,128)S(1)}, f32[8,256]{1,0:T(8,128)S(1)}, f32[8,256]{1,0:T(8,128)S(1)}, f32[8,8]{1,0:T(8,128)S(1)}, f32[2,8,8]{2,1,0:T(8,128)S(1)}) custom-call(f32[8,256]{1,0:T(8,128)S(1)} %get-tuple-element.24.own, f32[32,1024]{1,0:T(8,128)S(1)} %get-tuple-element.26.wide, bf16[384,1024]{1,0:T(8,128)(2,1)S(1)} %get-tuple-element.27.refs_0_, ...), custom_call_target="tpu_custom_call" | custom-call | tf_op jit(solution)/shard_map/pallas_call | solution.py:335
  30.8 0.0 collective-permute-done.1.refs_2_
  30.9 0.9 %shard_map.53 = (f32[8,256]{1,0:T(8,128)S(1)}, f32[32,1,64]{2,1,0:T(1,128)S(1)}) custom-call(f32[8,256]{1,0:T(8,128)S(1)} %get-tuple-element.24.own, f32[32,1024]{1,0:T(8,128)S(1)} %get-tuple-element.33.wide, bf16[384,1024]{1,0:T(8,128)(2,1)S(1)} %get-tuple-element.34.refs_0_, bf16[384,1024]{1,0:T(8,128)(2,1)S(1)} %get-tuple-element.35.refs_1_, ...), custom_call_target="tpu_custom_call" | custom-call | tf_op jit(solution)/shard_map/pallas_call | solution.py:340
  31.7 8.9 %all_to_all.17.partials = f32[32,1,64]{2,1,0:T(1,128)S(1)} all-to-all(f32[32,1,64]{2,1,0:T(1,128)S(1)} %get-tuple-element.41), channel_id=1, replica_groups={{0,1,8,9,16,17,24,25,2,3,10,11,18,19,26,27,4,5,12,13,20,21,28,29,6,7,14..., dimensions={0} | all-to-all | bytes 16384 | tf_op jit(solution)/shard_map/all_to_all | solution.py:301
  40.7 0.8 %shard_map.54 = (f32[3,8,64]{2,1,0:T(8,128)}, f32[3,8,64]{2,1,0:T(8,128)}, f32[3,8,8]{2,1,0:T(8,128)}) custom-call(f32[8,256]{1,0:T(8,128)S(1)} %get-tuple-element.32.refs_4_.vectors, f32[8,256]{1,0:T(8,128)S(1)} %get-tuple-element.39.shifted, f32[2,8,8]{2,1,0:T(8,128)S(1)} %get-tuple-element.40.both, f32[32,1,64]{2,1,0:T(1,128)S(1)} %all_to_all.17.partials), custom_call_target="tpu_custom_call" | custom-call | tf_op jit(solution)/shard_map/pallas_call | solution.py:344
Async XLA Ops:
  16.8 1.3 %collective-permute-start = (f32[32,8,128]{2,1,0:T(8,128)S(1)}, f32[32,8,128]{2,1,0:T(8,128)S(1)}, u32[]{:S(2)}, u32[]{:S(2)}) collective-permute-start(f32[32,8,128]{2,1,0:T(8,128)S(1)} %all_to_all.15.blocks), channel_id=1, source_target_pairs={{0,1},{1,0},{2,3},{3,2},{4,5},{5,4},{6,7},{7,6},{8,9},{9,8},{10,11... | collective-permute-start | bytes 393224 | tf_op jit(solution)/shard_map/ppermute | solution.py:307
  29.5 1.3 %collective-permute-start.1 = (f32[32,8,128]{2,1,0:T(8,128)S(1)}, f32[32,8,128]{2,1,0:T(8,128)S(1)}, u32[]{:S(2)}, u32[]{:S(2)}) collective-permute-start(f32[32,8,128]{2,1,0:T(8,128)S(1)} %all_to_all.16.refs_2_), channel_id=1, source_target_pairs={{0,1},{1,0},{2,3},{3,2},{4,5},{5,4},{6,7},{7,6},{8,9},{9,8},{10,11... | collective-permute-start | bytes 393224 | tf_op jit(solution)/shard_map/ppermute | solution.py:307

commit v19 on v18

--- a/solution.py
+++ b/solution.py
@@ -13,14 +13,14 @@
 BF16 = jnp.bfloat16
 
 
-def copy_halves(block, copies, last=None):
+def copy_halves(block, copies, extra=None):
     beads = block.shape[1] // 4
     middle = beads // 2
     for core in range(2):
         parts = [block[:, part * beads + core * middle : part * beads + (core + 1) * middle] for part in range(4)]
-        if last is not None:
-            parts[3] = last
         half = jnp.concatenate(parts, axis=1)
+        if extra is not None:
+            half = half + extra
         copies[:, core] = jnp.broadcast_to(half[None], (copies.shape[0],) + half.shape)
 
 
@@ -99,10 +99,8 @@
     return jnp.concatenate(highs + lows, axis=0)
 
 
-def inner(both):
-    half = both.shape[0] // 2
-    first = matmul_nt(both, both[:half])
-    return first[:half] + first[half:] + matmul_nt(both[:half], both[half:])
+def inner(left, right):
+    return [jnp.sum(left * right[row : row + 1], axis=1, keepdims=True) for row in range(right.shape[0])]
 
 
 def assemble(products):
@@ -162,9 +160,13 @@
         return
     block = assemble(products + before[...])
     image[...] = block
-    sums = inner(split_rows(without_positions(own[...]), block))
-    empty = jnp.zeros((8, block.shape[1] // 8 - 24), F32)
-    copy_halves(block, copies, jnp.concatenate([sums[:8], sums[8:, 8:], empty], axis=1))
+    noise = without_positions(own[...])
+    columns = inner(noise, noise) + inner(noise, block) + inner(block, block)
+    lanes = lax.broadcasted_iota(jnp.int32, (block.shape[0], block.shape[1] // 2), 1)
+    sums = jnp.zeros(lanes.shape, F32)
+    for index, column in enumerate(columns):
+        sums = jnp.where(lanes == block.shape[1] // 8 * 3 + index, column, sums)
+    copy_halves(block, copies, sums)
 
 
 def cholesky(matrix):
@@ -252,11 +254,12 @@
     vectors = vectors_in[...]
     shift = small_matmul(small[...], assemble(products)) - known[...]
     shifted[...] = shift
-    (vector_high, vector_low), (shift_high, shift_low) = split_two(vectors), split_two(shift)
-    partial = matmul_nt(vector_high, shift_high) + (
-        matmul_nt(vector_high, shift_low) + matmul_nt(vector_low, shift_high)
-    )
-    line = jnp.concatenate([partial[row : row + 1] for row in range(8)], axis=1)
+    lanes = lax.broadcasted_iota(jnp.int32, (8, partials.shape[2]), 1)
+    rows = lax.broadcasted_iota(jnp.int32, lanes.shape, 0)
+    line = jnp.zeros(lanes.shape, F32)
+    for row, column in enumerate(inner(shift, vectors)):
+        line = jnp.where(lanes == 8 * row + rows, column, line)
+    line = jnp.sum(line, axis=0, keepdims=True)
     partials[...] = jnp.broadcast_to(line[None], partials.shape)
 
 
@@ -296,9 +299,7 @@
 
 
 def to_all(copies):
-    rows, cols = lax.axis_size("row"), lax.axis_size("col")
-    order = [row * cols + 2 * layer + core for layer in range(cols // 2) for row in range(rows) for core in range(2)]
-    return lax.all_to_all(copies, ("row", "col"), 0, 0, axis_index_groups=[order], tiled=True)
+    return lax.all_to_all(copies, ("row", "col"), 0, 0, tiled=True)
 
 
 def gather(copies):

time: 41.7 us -> 41.3 us (level)
  no operation moved by 1% of the time
where the time goes in v19:
time: 41.3 us; the launch traced here: 41 us
  blocking collectives  34 us (82%)
  Pallas kernels  4.93 us (12%)
  other arithmetic  0.73 us (2%)
  between operations  0.67 us (2%)
  starting transfers between devices  0.63 us (2%)
    all_to_all x3, blocking collectives, to_all(): return lax.all_to_all(copies, ('row', 'col'), 0, 0, tiled=True)  34 us
    pallas_call x1, Pallas kernels, local(): call(functools.partial(first_stage, True), [block, copies, wide] + kept,...  1.16 us
    pallas_call x1, Pallas kernels, local(): call(functools.partial(third_stage, size, not keep), [products, block, bl...  1.11 us
    pallas_call x1, Pallas kernels, local(): call(functools.partial(first_stage, False), [products, wide] + kept, held)  0.97 us
  transfers between devices with their start and end apart: 2, of which 1 were waited for; matrix products, arithmetic and copies ran while one was open for 0% of the time, Pallas kernels for 5%

profile of v19, /device:TPU:0, one launch (start us, length us, event | category | flops | bytes accessed | tf_op | source)
XLA Modules:
  0.0 41.0 jit_solution(4558521107591385272)
XLA Ops:
  0.6 0.7 %select_maximum_fusion.rows = f32[32,64]{1,0:T(8,128)S(1)} fusion(f32[3,64]{1,0:T(4,128)} %param.2, f32[24,64]{1,0:T(8,128)} %bitcast.9), kind=kLoop, calls=%fused_computation | loop fusion | flops 6144 | bytes 15104 | tf_op jit(solution)/shard_map/concatenate | solution.py:326
  1.4 0.1 shard_map.49
  1.5 15.3 %all_to_all.15.blocks = f32[32,8,128]{2,1,0:T(8,128)S(1)} all-to-all(f32[32,8,128]{2,1,0:T(8,128)S(1)} %bitcast.8), channel_id=1, replica_groups=mesh['row'=4,'col'=8] {'row','col'}, dimensions={0} | all-to-all | bytes 262144 | tf_op jit(solution)/shard_map/all_to_all | solution.py:302
  16.8 0.3 collective-permute-start
  17.1 1.0 %shard_map.50 = (f32[32,384]{1,0:T(8,128)S(1)}, f32[32,1024]{1,0:T(8,128)S(1)}, bf16[384,1024]{1,0:T(8,128)(2,1)S(1)}, bf16[384,1024]{1,0:T(8,128)(2,1)S(1)}) custom-call(f32[8,256]{1,0:T(8,128)S(1)} %get-tuple-element.24.own, f32[32,8,128]{2,1,0:T(8,128)S(1)} %all_to_all.15.blocks), custom_call_target="tpu_custom_call" | custom-call | tf_op jit(solution)/shard_map/pallas_call | solution.py:329
  18.1 0.1 collective-permute-done.blocks
  18.1 1.2 %shard_map.51 = (f32[8,256]{1,0:T(8,128)S(1)}, f32[16,2,8,128]{3,2,1,0:T(8,128)S(1)}, f32[32,1024]{1,0:T(8,128)S(1)}, bf16[384,1024]{1,0:T(8,128)(2,1)S(1)}, bf16[384,1024]{1,0:T(8,128)(2,1)S(1)}) custom-call(f32[8,256]{1,0:T(8,128)S(1)} %get-tuple-element.24.own, f32[32,8,128]{2,1,0:T(8,128)S(1)} %collective-permute-done.blocks, ...), custom_call_target="tpu_custom_call" | custom-call | tf_op jit(solution)/shard_map/pallas_call | solution.py:332
  19.3 9.9 %all_to_all.16.refs_2_ = f32[32,8,128]{2,1,0:T(8,128)S(1)} all-to-all(f32[32,8,128]{2,1,0:T(8,128)S(1)} %bitcast.7), channel_id=1, replica_groups=mesh['row'=4,'col'=8] {'row','col'}, dimensions={0} | all-to-all | bytes 262144 | tf_op jit(solution)/shard_map/all_to_all | solution.py:302
  29.2 0.3 collective-permute-start.1
  29.5 1.1 %shard_map.52 = (f32[32,384]{1,0:T(8,128)S(1)}, f32[8,256]{1,0:T(8,128)S(1)}, f32[8,256]{1,0:T(8,128)S(1)}, f32[8,8]{1,0:T(8,128)S(1)}, f32[2,8,8]{2,1,0:T(8,128)S(1)}) custom-call(f32[8,256]{1,0:T(8,128)S(1)} %get-tuple-element.24.own, f32[32,1024]{1,0:T(8,128)S(1)} %get-tuple-element.26.wide, bf16[384,1024]{1,0:T(8,128)(2,1)S(1)} %get-tuple-element.27.refs_0_, ...), custom_call_target="tpu_custom_call" | custom-call | tf_op jit(solution)/shard_map/pallas_call | solution.py:336
  30.6 0.0 collective-permute-done.1.refs_2_
  30.6 0.7 %shard_map.53 = (f32[8,256]{1,0:T(8,128)S(1)}, f32[32,1,64]{2,1,0:T(1,128)S(1)}) custom-call(f32[8,256]{1,0:T(8,128)S(1)} %get-tuple-element.24.own, f32[32,1024]{1,0:T(8,128)S(1)} %get-tuple-element.33.wide, bf16[384,1024]{1,0:T(8,128)(2,1)S(1)} %get-tuple-element.34.refs_0_, bf16[384,1024]{1,0:T(8,128)(2,1)S(1)} %get-tuple-element.35.refs_1_, ...), custom_call_target="tpu_custom_call" | custom-call | tf_op jit(solution)/shard_map/pallas_call | solution.py:341
  31.4 8.8 %all_to_all.17.partials = f32[32,1,64]{2,1,0:T(1,128)S(1)} all-to-all(f32[32,1,64]{2,1,0:T(1,128)S(1)} %get-tuple-element.41), channel_id=1, replica_groups=mesh['row'=4,'col'=8] {'row','col'}, dimensions={0} | all-to-all | bytes 16384 | tf_op jit(solution)/shard_map/all_to_all | solution.py:302
  40.2 0.8 %shard_map.54 = (f32[3,8,64]{2,1,0:T(8,128)}, f32[3,8,64]{2,1,0:T(8,128)}, f32[3,8,8]{2,1,0:T(8,128)}) custom-call(f32[8,256]{1,0:T(8,128)S(1)} %get-tuple-element.32.refs_4_.vectors, f32[8,256]{1,0:T(8,128)S(1)} %get-tuple-element.39.shifted, f32[2,8,8]{2,1,0:T(8,128)S(1)} %get-tuple-element.40.both, f32[32,1,64]{2,1,0:T(1,128)S(1)} %all_to_all.17.partials), custom_call_target="tpu_custom_call" | custom-call | tf_op jit(solution)/shard_map/pallas_call | solution.py:345
Async XLA Ops:
  16.8 1.3 %collective-permute-start = (f32[32,8,128]{2,1,0:T(8,128)S(1)}, f32[32,8,128]{2,1,0:T(8,128)S(1)}, u32[]{:S(2)}, u32[]{:S(2)}) collective-permute-start(f32[32,8,128]{2,1,0:T(8,128)S(1)} %all_to_all.15.blocks), channel_id=1, source_target_pairs={{0,1},{1,0},{2,3},{3,2},{4,5},{5,4},{6,7},{7,6},{8,9},{9,8},{10,11... | collective-permute-start | bytes 393224 | tf_op jit(solution)/shard_map/ppermute | solution.py:308
  29.2 1.4 %collective-permute-start.1 = (f32[32,8,128]{2,1,0:T(8,128)S(1)}, f32[32,8,128]{2,1,0:T(8,128)S(1)}, u32[]{:S(2)}, u32[]{:S(2)}) collective-permute-start(f32[32,8,128]{2,1,0:T(8,128)S(1)} %all_to_all.16.refs_2_), channel_id=1, source_target_pairs={{0,1},{1,0},{2,3},{3,2},{4,5},{5,4},{6,7},{7,6},{8,9},{9,8},{10,11... | collective-permute-start | bytes 393224 | tf_op jit(solution)/shard_map/ppermute | solution.py:308

commit v20 on v19

--- a/solution.py
+++ b/solution.py
@@ -147,26 +147,40 @@
     return jnp.where(lanes < block.shape[1] // 4 * 3, block, 0.0)
 
 
-def first_stage(last, own, blocks, *refs):
+def row_sums(wide):
+    total = jnp.zeros((wide.shape[0], wide.shape[0]), F32)
+    for at in range(0, wide.shape[1], CHUNK):
+        both = split_rows(wide[:, at : min(at + CHUNK, wide.shape[1])])
+        half = both.shape[0] // 2
+        first, second = matmul_nt(both, both[:half]), matmul_nt(both, both[half:])
+        total = total + ((first[:half] + first[half:]) + (second[:half] + second[half:]))
+    return total
+
+
+def first_stage(size, last, own, blocks, *refs):
     refs = list(refs)
     if last:
-        before, image, copies, wide, high, low = refs
+        before, before_sums, first_out, image, copies, wide, high, low = refs
     else:
-        out, wide, high, low = refs
+        out, sums_out, wide, high, low = refs
     unpack(blocks, wide)
+    sums = row_sums(wide)
     products = all_filled(own[...], wide, wide, high, low)
     if not last:
-        out[...] = products
+        out[...], sums_out[...] = products, sums
         return
-    block = assemble(products + before[...])
+    sums = (sums + before_sums[...]) / size
+    _, inverse = cholesky(sums[:8, :8] + sums[8:16, 8:16] + sums[16:24, 16:24])
+    first = small_matmul(inverse, without_positions(own[...]))
+    block = small_matmul(inverse, assemble(products + before[...]))
+    first_out[...] = first
     image[...] = block
-    noise = without_positions(own[...])
-    columns = inner(noise, noise) + inner(noise, block) + inner(block, block)
+    columns = inner(first, block) + inner(block, block)
     lanes = lax.broadcasted_iota(jnp.int32, (block.shape[0], block.shape[1] // 2), 1)
-    sums = jnp.zeros(lanes.shape, F32)
+    shares = jnp.zeros(lanes.shape, F32)
     for index, column in enumerate(columns):
-        sums = jnp.where(lanes == block.shape[1] // 8 * 3 + index, column, sums)
-    copy_halves(block, copies, sums)
+        shares = jnp.where(lanes == block.shape[1] // 8 * 3 + index, column, shares)
+    copy_halves(block, copies, shares)
 
 
 def cholesky(matrix):
@@ -214,9 +228,9 @@
     refs = list(refs)
     if not fill:
         (high, low), refs = refs[:2], refs[2:]
-    images, own_image, products, vectors, known, small, coefficients = refs[:7]
+    images, own_first, own_image, products, vectors, known, small, coefficients = refs[:8]
     if fill:
-        high, low = refs[7:9]
+        high, low = refs[8:10]
     wide_image = refs[-1]
     unpack(images, wide_image)
     products[...] = second_product(fill, own[...], wide, wide_image, high, low)
@@ -226,19 +240,15 @@
     width = own.shape[1] // 8
     sums = sum(sums[:, at : at + width] for at in range(width, 128, width)) + sums[:, :width]
     sums = sums / size
-    _, inverse_zero = cholesky(sums[:, :8])
-    inverse_zero_t = inverse_zero.T
-    cross_t = small_matmul(inverse_zero, sums[:, 8:16])
-    cross = cross_t.T
-    factor_t, inverse = cholesky(sums[:, 16:24] - small_matmul(cross, cross_t))
-    factor_one_t = small_matmul(factor_t, inverse_zero_t)
-    first = small_matmul(inverse_zero, without_positions(own[...]))
-    moved = small_matmul(inverse_zero, own_image[...])
-    vectors[...] = small_matmul(inverse, own_image[...] - small_matmul(cross, first))
-    known[...] = small_matmul(inverse, small_matmul(cross, moved)) + small_matmul(factor_one_t, first)
+    alpha = sums[:, :8]
+    alpha_t = alpha.T
+    factor_t, inverse = cholesky(sums[:, 8:16] - small_matmul(alpha_t, alpha))
+    first, image = own_first[...], own_image[...]
+    vectors[...] = small_matmul(inverse, image - small_matmul(alpha_t, first))
+    known[...] = small_matmul(inverse, small_matmul(alpha_t, image)) + small_matmul(factor_t, first)
     small[...] = inverse
-    coefficients[0] = small_matmul(cross_t, inverse_zero_t)
-    coefficients[1] = factor_one_t.T
+    coefficients[0] = alpha
+    coefficients[1] = factor_t.T
 
 
 def fourth_stage(fill, own, wide, *refs):
@@ -326,18 +336,18 @@
     rows = jnp.concatenate([rows, jnp.pad(positions, ((0, vecs - 3), (0, 0)))], axis=0)
     own, own_copies = call(pack_kernel, [block, copies])(rows)
     one, two = gather(own_copies)
-    partial, one_wide, *one_tensor = call(
-        functools.partial(first_stage, False), [products, wide] + kept, held
+    partial, sums, one_wide, *one_tensor = call(
+        functools.partial(first_stage, size, False), [products, array(4 * vecs, 4 * vecs), wide] + kept, held
     )(own, one)
-    image, images, two_wide, *two_tensor = call(
-        functools.partial(first_stage, True), [block, copies, wide] + kept, held
-    )(own, two, partial)
+    first, image, images, two_wide, *two_tensor = call(
+        functools.partial(first_stage, size, True), [block, block, copies, wide] + kept, held
+    )(own, two, partial, sums)
     one, two = gather(images)
     partial, vectors, known, small, both = call(
         functools.partial(third_stage, size, not keep),
         [products, block, block, array(vecs, vecs), array(2, vecs, vecs)],
         held + [held_wide],
-    )(own, one_wide, *one_tensor, one, image)
+    )(own, one_wide, *one_tensor, one, first, image)
     shifted, partials = call(
         functools.partial(fourth_stage, not keep), [block, array(devices, 1, vecs * vecs)], held + [held_wide]
     )(own, two_wide, *two_tensor, two, partial, vectors, known, small)

time: 41.3 us -> 41.3 us (level)
  no operation moved by 1% of the time
where the time goes in v20:
time: 41.3 us; the launch traced here: 41.1 us
  blocking collectives  34 us (82%)
  Pallas kernels  4.88 us (12%)
  other arithmetic  0.73 us (2%)
  between operations  0.67 us (2%)
  starting transfers between devices  0.63 us (2%)
    all_to_all x3, blocking collectives, to_all(): return lax.all_to_all(copies, ('row', 'col'), 0, 0, tiled=True)  34 us
    pallas_call x1, Pallas kernels, local(): call(functools.partial(first_stage, size, True), [block, block, copies, w...  1.32 us
    pallas_call x1, Pallas kernels, local(): call(functools.partial(first_stage, size, False), [products, array(4 * ve...  1.02 us
    pallas_call x1, Pallas kernels, local(): call(functools.partial(third_stage, size, not keep), [products, block, bl...  0.85 us
  transfers between devices with their start and end apart: 2, of which 1 were waited for; matrix products, arithmetic and copies ran while one was open for 0% of the time, Pallas kernels for 5%

profile of v20, /device:TPU:0, one launch (start us, length us, event | category | flops | bytes accessed | tf_op | source)
XLA Modules:
  0.0 41.1 jit_solution(2239822340715299135)
XLA Ops:
  0.6 0.7 %select_maximum_fusion.rows = f32[32,64]{1,0:T(8,128)S(1)} fusion(f32[3,64]{1,0:T(4,128)} %param.2, f32[24,64]{1,0:T(8,128)} %bitcast.9), kind=kLoop, calls=%fused_computation | loop fusion | flops 6144 | bytes 15104 | tf_op jit(solution)/shard_map/concatenate | solution.py:336
  1.4 0.1 shard_map.49
  1.5 15.3 %all_to_all.15.blocks = f32[32,8,128]{2,1,0:T(8,128)S(1)} all-to-all(f32[32,8,128]{2,1,0:T(8,128)S(1)} %bitcast.8), channel_id=1, replica_groups=mesh['row'=4,'col'=8] {'row','col'}, dimensions={0} | all-to-all | bytes 262144 | tf_op jit(solution)/shard_map/all_to_all | solution.py:312
  16.8 0.3 collective-permute-start
  17.1 1.0 %shard_map.50 = (f32[32,384]{1,0:T(8,128)S(1)}, f32[32,32]{1,0:T(8,128)S(1)}, f32[32,1024]{1,0:T(8,128)S(1)}, bf16[384,1024]{1,0:T(8,128)(2,1)S(1)}, bf16[384,1024]{1,0:T(8,128)(2,1)S(1)}) custom-call(f32[8,256]{1,0:T(8,128)S(1)} %get-tuple-element.26.own, f32[32,8,128]{2,1,0:T(8,128)S(1)} %all_to_all.15.blocks), custom_call_target="tpu_custom_call" | custom-call | tf_op jit(solution)/shard_map/pallas_call | solution.py:339
  18.1 0.0 collective-permute-done.blocks
  18.1 1.3 %shard_map.51 = (f32[8,256]{1,0:T(8,128)S(1)}, f32[8,256]{1,0:T(8,128)S(1)}, f32[16,2,8,128]{3,2,1,0:T(8,128)S(1)}, f32[32,1024]{1,0:T(8,128)S(1)}, bf16[384,102...) custom-call(f32[8,256]{1,0:T(8,128)S(1)} %get-tuple-element.26.own, f32[32,8,128]{2,1,0:T(8,128)S(1)} %collective-permute-done.blocks, ...), custom_call_target="tpu_custom_call" | custom-call | tf_op jit(solution)/shard_map/pallas_call | solution.py:342
  19.5 9.9 %all_to_all.16.refs_2_ = f32[32,8,128]{2,1,0:T(8,128)S(1)} all-to-all(f32[32,8,128]{2,1,0:T(8,128)S(1)} %bitcast.7), channel_id=1, replica_groups=mesh['row'=4,'col'=8] {'row','col'}, dimensions={0} | all-to-all | bytes 262144 | tf_op jit(solution)/shard_map/all_to_all | solution.py:312
  29.3 0.3 collective-permute-start.1
  29.7 0.8 %shard_map.52 = (f32[32,384]{1,0:T(8,128)S(1)}, f32[8,256]{1,0:T(8,128)S(1)}, f32[8,256]{1,0:T(8,128)S(1)}, f32[8,8]{1,0:T(8,128)S(1)}, f32[2,8,8]{2,1,0:T(8,128)S(1)}) custom-call(f32[8,256]{1,0:T(8,128)S(1)} %get-tuple-element.26.own, f32[32,1024]{1,0:T(8,128)S(1)} %get-tuple-element.28.wide, bf16[384,1024]{1,0:T(8,128)(2,1)S(1)} %get-tuple-element.29.refs_0_, ...), custom_call_target="tpu_custom_call" | custom-call | tf_op jit(solution)/shard_map/pallas_call | solution.py:346
  30.5 0.2 collective-permute-done.1.refs_2_
  30.7 0.7 %shard_map.53 = (f32[8,256]{1,0:T(8,128)S(1)}, f32[32,1,64]{2,1,0:T(1,128)S(1)}) custom-call(f32[8,256]{1,0:T(8,128)S(1)} %get-tuple-element.26.own, f32[32,1024]{1,0:T(8,128)S(1)} %get-tuple-element.37.wide, bf16[384,1024]{1,0:T(8,128)(2,1)S(1)} %get-tuple-element.38.refs_0_, bf16[384,1024]{1,0:T(8,128)(2,1)S(1)} %get-tuple-element.39.refs_1_, ...), custom_call_target="tpu_custom_call" | custom-call | tf_op jit(solution)/shard_map/pallas_call | solution.py:351
  31.5 8.8 %all_to_all.17.partials = f32[32,1,64]{2,1,0:T(1,128)S(1)} all-to-all(f32[32,1,64]{2,1,0:T(1,128)S(1)} %get-tuple-element.45), channel_id=1, replica_groups=mesh['row'=4,'col'=8] {'row','col'}, dimensions={0} | all-to-all | bytes 16384 | tf_op jit(solution)/shard_map/all_to_all | solution.py:312
  40.3 0.8 %shard_map.54 = (f32[3,8,64]{2,1,0:T(8,128)}, f32[3,8,64]{2,1,0:T(8,128)}, f32[3,8,8]{2,1,0:T(8,128)}) custom-call(f32[8,256]{1,0:T(8,128)S(1)} %get-tuple-element.36.refs_4_.vectors, f32[8,256]{1,0:T(8,128)S(1)} %get-tuple-element.43.shifted, f32[2,8,8]{2,1,0:T(8,128)S(1)} %get-tuple-element.44.both, f32[32,1,64]{2,1,0:T(1,128)S(1)} %all_to_all.17.partials), custom_call_target="tpu_custom_call" | custom-call | tf_op jit(solution)/shard_map/pallas_call | solution.py:355
Async XLA Ops:
  16.8 1.3 %collective-permute-start = (f32[32,8,128]{2,1,0:T(8,128)S(1)}, f32[32,8,128]{2,1,0:T(8,128)S(1)}, u32[]{:S(2)}, u32[]{:S(2)}) collective-permute-start(f32[32,8,128]{2,1,0:T(8,128)S(1)} %all_to_all.15.blocks), channel_id=1, source_target_pairs={{0,1},{1,0},{2,3},{3,2},{4,5},{5,4},{6,7},{7,6},{8,9},{9,8},{10,11... | collective-permute-start | bytes 393224 | tf_op jit(solution)/shard_map/ppermute | solution.py:318
  29.3 1.3 %collective-permute-start.1 = (f32[32,8,128]{2,1,0:T(8,128)S(1)}, f32[32,8,128]{2,1,0:T(8,128)S(1)}, u32[]{:S(2)}, u32[]{:S(2)}) collective-permute-start(f32[32,8,128]{2,1,0:T(8,128)S(1)} %all_to_all.16.refs_2_), channel_id=1, source_target_pairs={{0,1},{1,0},{2,3},{3,2},{4,5},{5,4},{6,7},{7,6},{8,9},{9,8},{10,11... | collective-permute-start | bytes 393224 | tf_op jit(solution)/shard_map/ppermute | solution.py:318

commit v21 on v20

--- a/solution.py
+++ b/solution.py
@@ -24,11 +24,21 @@
         copies[:, core] = jnp.broadcast_to(half[None], (copies.shape[0],) + half.shape)
 
 
-def pack_kernel(rows, block, copies):
-    vecs = block.shape[0]
-    flat = jnp.concatenate([rows[part * vecs : (part + 1) * vecs] for part in range(4)], axis=1)
-    block[...] = flat
-    copy_halves(flat, copies)
+def pack_kernel(positions, noise, block, copies, held_positions, held_noise, sems):
+    reads = [
+        pltpu.make_async_copy(positions, held_positions, sems.at[0]),
+        pltpu.make_async_copy(noise, held_noise, sems.at[1]),
+    ]
+    for read in reads:
+        read.start()
+    beads = block.shape[1] // 4
+    block[...] = jnp.zeros(block.shape, F32)
+    for read in reads:
+        read.wait()
+    for part in range(3):
+        block[:, part * beads : (part + 1) * beads] = held_noise[part]
+    block[:3, 3 * beads :] = held_positions[...]
+    copy_halves(block[...], copies)
 
 
 def split_two(value):
@@ -332,9 +342,15 @@
     kept = [array(6 * beads, width, dtype=BF16)] * 2 if keep else []
     held = [] if keep else [pltpu.VMEM((6 * beads, width), BF16)] * 2
 
-    rows = noise.transpose(1, 0, 2).reshape(3 * vecs, beads)
-    rows = jnp.concatenate([rows, jnp.pad(positions, ((0, vecs - 3), (0, 0)))], axis=0)
-    own, own_copies = call(pack_kernel, [block, copies])(rows)
+    arguments = [
+        pltpu.with_memory_space_constraint(item, pltpu.HBM) for item in (positions, noise.transpose(1, 0, 2))
+    ]
+    own, own_copies = call(
+        pack_kernel,
+        [block, copies],
+        [pltpu.VMEM(item.shape, F32) for item in arguments] + [pltpu.SemaphoreType.DMA((2,))],
+        in_specs=[pl.BlockSpec(memory_space=pltpu.HBM)] * 2,
+    )(*arguments)
     one, two = gather(own_copies)
     partial, sums, one_wide, *one_tensor = call(
         functools.partial(first_stage, size, False), [products, array(4 * vecs, 4 * vecs), wide] + kept, held

time: 41.3 us -> 41.4 us (level)
  Pallas kernels: 4.88 us -> 5.62 us
  other arithmetic: 0.73 us -> 0 us
    pallas_call x1, Pallas kernels: 0.15 us -> 0.89 us  [local(): call(pack_kernel, [block, copies], [pltpu.VMEM(item.shape, F32) for item...]
    concatenate x1 -> x0, other arithmetic: 0.73 us -> none  [local(): jnp.concatenate([rows, jnp.pad(positions, ((0, vecs - 3), (0, 0)))], axis=0)]
where the time goes in v21:
time: 41.4 us; the launch traced here: 41.1 us
  blocking collectives  34 us (82%)
  Pallas kernels  5.62 us (14%)
  between operations  0.67 us (2%)
  starting transfers between devices  0.63 us (2%)
    all_to_all x3, blocking collectives, to_all(): return lax.all_to_all(copies, ('row', 'col'), 0, 0, tiled=True)  34 us
    pallas_call x1, Pallas kernels, local(): call(functools.partial(first_stage, size, True), [block, block, copies, w...  1.32 us
    pallas_call x1, Pallas kernels, local(): call(functools.partial(first_stage, size, False), [products, array(4 * ve...  1.02 us
    pallas_call x1, Pallas kernels, local(): call(pack_kernel, [block, copies], [pltpu.VMEM(item.shape, F32) for item...  0.89 us
    pallas_call x1, Pallas kernels, local(): call(functools.partial(third_stage, size, not keep), [products, block, bl...  0.85 us
  transfers between devices with their start and end apart: 2, of which 1 were waited for; matrix products, arithmetic and copies ran while one was open for 0% of the time, Pallas kernels for 5%

profile of v21, /device:TPU:0, one launch (start us, length us, event | category | flops | bytes accessed | tf_op | source)
XLA Modules:
  0.0 41.1 jit_solution(10204628195242975311)
XLA Ops:
  0.6 0.9 %shard_map.49 = (f32[8,256]{1,0:T(8,128)S(1)}, f32[16,2,8,128]{3,2,1,0:T(8,128)S(1)}) custom-call(f32[3,64]{1,0:T(4,128)} %positions.1, f32[3,8,64]{2,1,0:T(8,128)} %bitcast.7), custom_call_target="tpu_custom_call" | custom-call | tf_op jit(solution)/shard_map/pallas_call | solution.py:348
  1.5 15.3 %all_to_all.15.blocks = f32[32,8,128]{2,1,0:T(8,128)S(1)} all-to-all(f32[32,8,128]{2,1,0:T(8,128)S(1)} %bitcast.6), channel_id=1, replica_groups=mesh['row'=4,'col'=8] {'row','col'}, dimensions={0} | all-to-all | bytes 262144 | tf_op jit(solution)/shard_map/all_to_all | solution.py:322
  16.8 0.3 collective-permute-start
  17.1 1.0 %shard_map.50 = (f32[32,384]{1,0:T(8,128)S(1)}, f32[32,32]{1,0:T(8,128)S(1)}, f32[32,1024]{1,0:T(8,128)S(1)}, bf16[384,1024]{1,0:T(8,128)(2,1)S(1)}, bf16[384,1024]{1,0:T(8,128)(2,1)S(1)}) custom-call(f32[8,256]{1,0:T(8,128)S(1)} %get-tuple-element.26.own, f32[32,8,128]{2,1,0:T(8,128)S(1)} %all_to_all.15.blocks), custom_call_target="tpu_custom_call" | custom-call | tf_op jit(solution)/shard_map/pallas_call | solution.py:355
  18.2 0.0 collective-permute-done.blocks
  18.2 1.3 %shard_map.51 = (f32[8,256]{1,0:T(8,128)S(1)}, f32[8,256]{1,0:T(8,128)S(1)}, f32[16,2,8,128]{3,2,1,0:T(8,128)S(1)}, f32[32,1024]{1,0:T(8,128)S(1)}, bf16[384,102...) custom-call(f32[8,256]{1,0:T(8,128)S(1)} %get-tuple-element.26.own, f32[32,8,128]{2,1,0:T(8,128)S(1)} %collective-permute-done.blocks, ...), custom_call_target="tpu_custom_call" | custom-call | tf_op jit(solution)/shard_map/pallas_call | solution.py:358
  19.5 9.9 %all_to_all.16.refs_2_ = f32[32,8,128]{2,1,0:T(8,128)S(1)} all-to-all(f32[32,8,128]{2,1,0:T(8,128)S(1)} %bitcast.5), channel_id=1, replica_groups=mesh['row'=4,'col'=8] {'row','col'}, dimensions={0} | all-to-all | bytes 262144 | tf_op jit(solution)/shard_map/all_to_all | solution.py:322
  29.4 0.3 collective-permute-start.1
  29.7 0.8 %shard_map.52 = (f32[32,384]{1,0:T(8,128)S(1)}, f32[8,256]{1,0:T(8,128)S(1)}, f32[8,256]{1,0:T(8,128)S(1)}, f32[8,8]{1,0:T(8,128)S(1)}, f32[2,8,8]{2,1,0:T(8,128)S(1)}) custom-call(f32[8,256]{1,0:T(8,128)S(1)} %get-tuple-element.26.own, f32[32,1024]{1,0:T(8,128)S(1)} %get-tuple-element.28.wide, bf16[384,1024]{1,0:T(8,128)(2,1)S(1)} %get-tuple-element.29.refs_0_, ...), custom_call_target="tpu_custom_call" | custom-call | tf_op jit(solution)/shard_map/pallas_call | solution.py:362
  30.5 0.2 collective-permute-done.1.refs_2_
  30.7 0.7 %shard_map.53 = (f32[8,256]{1,0:T(8,128)S(1)}, f32[32,1,64]{2,1,0:T(1,128)S(1)}) custom-call(f32[8,256]{1,0:T(8,128)S(1)} %get-tuple-element.26.own, f32[32,1024]{1,0:T(8,128)S(1)} %get-tuple-element.37.wide, bf16[384,1024]{1,0:T(8,128)(2,1)S(1)} %get-tuple-element.38.refs_0_, bf16[384,1024]{1,0:T(8,128)(2,1)S(1)} %get-tuple-element.39.refs_1_, ...), custom_call_target="tpu_custom_call" | custom-call | tf_op jit(solution)/shard_map/pallas_call | solution.py:367
  31.5 8.8 %all_to_all.17.partials = f32[32,1,64]{2,1,0:T(1,128)S(1)} all-to-all(f32[32,1,64]{2,1,0:T(1,128)S(1)} %get-tuple-element.45), channel_id=1, replica_groups=mesh['row'=4,'col'=8] {'row','col'}, dimensions={0} | all-to-all | bytes 16384 | tf_op jit(solution)/shard_map/all_to_all | solution.py:322
  40.3 0.8 %shard_map.54 = (f32[3,8,64]{2,1,0:T(8,128)}, f32[3,8,64]{2,1,0:T(8,128)}, f32[3,8,8]{2,1,0:T(8,128)}) custom-call(f32[8,256]{1,0:T(8,128)S(1)} %get-tuple-element.36.refs_4_.vectors, f32[8,256]{1,0:T(8,128)S(1)} %get-tuple-element.43.shifted, f32[2,8,8]{2,1,0:T(8,128)S(1)} %get-tuple-element.44.both, f32[32,1,64]{2,1,0:T(1,128)S(1)} %all_to_all.17.partials), custom_call_target="tpu_custom_call" | custom-call | tf_op jit(solution)/shard_map/pallas_call | solution.py:371
Async XLA Ops:
  16.8 1.3 %collective-permute-start = (f32[32,8,128]{2,1,0:T(8,128)S(1)}, f32[32,8,128]{2,1,0:T(8,128)S(1)}, u32[]{:S(2)}, u32[]{:S(2)}) collective-permute-start(f32[32,8,128]{2,1,0:T(8,128)S(1)} %all_to_all.15.blocks), channel_id=1, source_target_pairs={{0,1},{1,0},{2,3},{3,2},{4,5},{5,4},{6,7},{7,6},{8,9},{9,8},{10,11... | collective-permute-start | bytes 393224 | tf_op jit(solution)/shard_map/ppermute | solution.py:328
  29.4 1.3 %collective-permute-start.1 = (f32[32,8,128]{2,1,0:T(8,128)S(1)}, f32[32,8,128]{2,1,0:T(8,128)S(1)}, u32[]{:S(2)}, u32[]{:S(2)}) collective-permute-start(f32[32,8,128]{2,1,0:T(8,128)S(1)} %all_to_all.16.refs_2_), channel_id=1, source_target_pairs={{0,1},{1,0},{2,3},{3,2},{4,5},{5,4},{6,7},{7,6},{8,9},{9,8},{10,11... | collective-permute-start | bytes 393224 | tf_op jit(solution)/shard_map/ppermute | solution.py:328

commit v22 on v21

--- a/solution.py
+++ b/solution.py
@@ -128,8 +128,8 @@
 def filled_product(columns, source, wide, start, high, low):
     width = high.shape[1]
     products = jnp.zeros((32, high.shape[0]), F32)
-    for at in range(0, width, 256):
-        step = min(256, width - at)
+    for at in range(0, width, 512):
+        step = min(512, width - at)
         lanes = pl.ds(at, step)
         both = split_rows(wide[:, pl.ds(pl.multiple_of(start + at, 128), step)])
         pieces = [

time: 41.4 us -> 41.3 us (level)
  no operation moved by 1% of the time
where the time goes in v22:
time: 41.3 us; the launch traced here: 41.1 us
  blocking collectives  34 us (82%)
  Pallas kernels  5.59 us (14%)
  between operations  0.67 us (2%)
  starting transfers between devices  0.63 us (2%)
    all_to_all x3, blocking collectives, to_all(): return lax.all_to_all(copies, ('row', 'col'), 0, 0, tiled=True)  34 us
    pallas_call x1, Pallas kernels, local(): call(functools.partial(first_stage, size, True), [block, block, copies, w...  1.28 us
    pallas_call x1, Pallas kernels, local(): call(functools.partial(first_stage, size, False), [products, array(4 * ve...  1.03 us
    pallas_call x1, Pallas kernels, local(): call(pack_kernel, [block, copies], [pltpu.VMEM(item.shape, F32) for item...  0.89 us
    pallas_call x1, Pallas kernels, local(): call(functools.partial(third_stage, size, not keep), [products, block, bl...  0.85 us
  transfers between devices with their start and end apart: 2, of which 1 were waited for; matrix products, arithmetic and copies ran while one was open for 0% of the time, Pallas kernels for 5%

profile of v22, /device:TPU:0, one launch (start us, length us, event | category | flops | bytes accessed | tf_op | source)
XLA Modules:
  0.0 41.1 jit_solution(15567116662082321054)
XLA Ops:
  0.6 0.9 %shard_map.49 = (f32[8,256]{1,0:T(8,128)S(1)}, f32[16,2,8,128]{3,2,1,0:T(8,128)S(1)}) custom-call(f32[3,64]{1,0:T(4,128)} %positions.1, f32[3,8,64]{2,1,0:T(8,128)} %bitcast.7), custom_call_target="tpu_custom_call" | custom-call | tf_op jit(solution)/shard_map/pallas_call | solution.py:348
  1.5 15.3 %all_to_all.15.blocks = f32[32,8,128]{2,1,0:T(8,128)S(1)} all-to-all(f32[32,8,128]{2,1,0:T(8,128)S(1)} %bitcast.6), channel_id=1, replica_groups=mesh['row'=4,'col'=8] {'row','col'}, dimensions={0} | all-to-all | bytes 262144 | tf_op jit(solution)/shard_map/all_to_all | solution.py:322
  16.8 0.3 collective-permute-start
  17.1 1.0 %shard_map.50 = (f32[32,384]{1,0:T(8,128)S(1)}, f32[32,32]{1,0:T(8,128)S(1)}, f32[32,1024]{1,0:T(8,128)S(1)}, bf16[384,1024]{1,0:T(8,128)(2,1)S(1)}, bf16[384,1024]{1,0:T(8,128)(2,1)S(1)}) custom-call(f32[8,256]{1,0:T(8,128)S(1)} %get-tuple-element.26.own, f32[32,8,128]{2,1,0:T(8,128)S(1)} %all_to_all.15.blocks), custom_call_target="tpu_custom_call" | custom-call | tf_op jit(solution)/shard_map/pallas_call | solution.py:355
  18.2 0.0 collective-permute-done.blocks
  18.2 1.3 %shard_map.51 = (f32[8,256]{1,0:T(8,128)S(1)}, f32[8,256]{1,0:T(8,128)S(1)}, f32[16,2,8,128]{3,2,1,0:T(8,128)S(1)}, f32[32,1024]{1,0:T(8,128)S(1)}, bf16[384,102...) custom-call(f32[8,256]{1,0:T(8,128)S(1)} %get-tuple-element.26.own, f32[32,8,128]{2,1,0:T(8,128)S(1)} %collective-permute-done.blocks, ...), custom_call_target="tpu_custom_call" | custom-call | tf_op jit(solution)/shard_map/pallas_call | solution.py:358
  19.5 9.9 %all_to_all.16.refs_2_ = f32[32,8,128]{2,1,0:T(8,128)S(1)} all-to-all(f32[32,8,128]{2,1,0:T(8,128)S(1)} %bitcast.5), channel_id=1, replica_groups=mesh['row'=4,'col'=8] {'row','col'}, dimensions={0} | all-to-all | bytes 262144 | tf_op jit(solution)/shard_map/all_to_all | solution.py:322
  29.3 0.3 collective-permute-start.1
  29.7 0.8 %shard_map.52 = (f32[32,384]{1,0:T(8,128)S(1)}, f32[8,256]{1,0:T(8,128)S(1)}, f32[8,256]{1,0:T(8,128)S(1)}, f32[8,8]{1,0:T(8,128)S(1)}, f32[2,8,8]{2,1,0:T(8,128)S(1)}) custom-call(f32[8,256]{1,0:T(8,128)S(1)} %get-tuple-element.26.own, f32[32,1024]{1,0:T(8,128)S(1)} %get-tuple-element.28.wide, bf16[384,1024]{1,0:T(8,128)(2,1)S(1)} %get-tuple-element.29.refs_0_, ...), custom_call_target="tpu_custom_call" | custom-call | tf_op jit(solution)/shard_map/pallas_call | solution.py:362
  30.5 0.2 collective-permute-done.1.refs_2_
  30.7 0.7 %shard_map.53 = (f32[8,256]{1,0:T(8,128)S(1)}, f32[32,1,64]{2,1,0:T(1,128)S(1)}) custom-call(f32[8,256]{1,0:T(8,128)S(1)} %get-tuple-element.26.own, f32[32,1024]{1,0:T(8,128)S(1)} %get-tuple-element.37.wide, bf16[384,1024]{1,0:T(8,128)(2,1)S(1)} %get-tuple-element.38.refs_0_, bf16[384,1024]{1,0:T(8,128)(2,1)S(1)} %get-tuple-element.39.refs_1_, ...), custom_call_target="tpu_custom_call" | custom-call | tf_op jit(solution)/shard_map/pallas_call | solution.py:367
  31.4 8.8 %all_to_all.17.partials = f32[32,1,64]{2,1,0:T(1,128)S(1)} all-to-all(f32[32,1,64]{2,1,0:T(1,128)S(1)} %get-tuple-element.45), channel_id=1, replica_groups=mesh['row'=4,'col'=8] {'row','col'}, dimensions={0} | all-to-all | bytes 16384 | tf_op jit(solution)/shard_map/all_to_all | solution.py:322
  40.3 0.8 %shard_map.54 = (f32[3,8,64]{2,1,0:T(8,128)}, f32[3,8,64]{2,1,0:T(8,128)}, f32[3,8,8]{2,1,0:T(8,128)}) custom-call(f32[8,256]{1,0:T(8,128)S(1)} %get-tuple-element.36.refs_4_.vectors, f32[8,256]{1,0:T(8,128)S(1)} %get-tuple-element.43.shifted, f32[2,8,8]{2,1,0:T(8,128)S(1)} %get-tuple-element.44.both, f32[32,1,64]{2,1,0:T(1,128)S(1)} %all_to_all.17.partials), custom_call_target="tpu_custom_call" | custom-call | tf_op jit(solution)/shard_map/pallas_call | solution.py:371
Async XLA Ops:
  16.8 1.4 %collective-permute-start = (f32[32,8,128]{2,1,0:T(8,128)S(1)}, f32[32,8,128]{2,1,0:T(8,128)S(1)}, u32[]{:S(2)}, u32[]{:S(2)}) collective-permute-start(f32[32,8,128]{2,1,0:T(8,128)S(1)} %all_to_all.15.blocks), channel_id=1, source_target_pairs={{0,1},{1,0},{2,3},{3,2},{4,5},{5,4},{6,7},{7,6},{8,9},{9,8},{10,11... | collective-permute-start | bytes 393224 | tf_op jit(solution)/shard_map/ppermute | solution.py:328
  29.3 1.3 %collective-permute-start.1 = (f32[32,8,128]{2,1,0:T(8,128)S(1)}, f32[32,8,128]{2,1,0:T(8,128)S(1)}, u32[]{:S(2)}, u32[]{:S(2)}) collective-permute-start(f32[32,8,128]{2,1,0:T(8,128)S(1)} %all_to_all.16.refs_2_), channel_id=1, source_target_pairs={{0,1},{1,0},{2,3},{3,2},{4,5},{5,4},{6,7},{7,6},{8,9},{9,8},{10,11... | collective-permute-start | bytes 393224 | tf_op jit(solution)/shard_map/ppermute | solution.py:328

commit v23 on v22

--- a/solution.py
+++ b/solution.py
@@ -128,8 +128,8 @@
 def filled_product(columns, source, wide, start, high, low):
     width = high.shape[1]
     products = jnp.zeros((32, high.shape[0]), F32)
-    for at in range(0, width, 512):
-        step = min(512, width - at)
+    for at in range(0, width, 1024):
+        step = min(1024, width - at)
         lanes = pl.ds(at, step)
         both = split_rows(wide[:, pl.ds(pl.multiple_of(start + at, 128), step)])
         pieces = [
@@ -286,7 +286,10 @@
 def last_kernel(size, vectors, shifted, both, partials, basis, residual, coefficients):
     beads = basis.shape[2]
     width = partials.shape[2]
-    total = jnp.sum(partials[...], axis=0) / size
+    parts = [partials[index] for index in range(partials.shape[0])]
+    while len(parts) > 1:
+        parts = [sum(parts[at : at + 2]) for at in range(0, len(parts), 2)]
+    total = parts[0] / size
     spread = jnp.broadcast_to(total, (8, width))
     rows = lax.broadcasted_iota(jnp.int32, spread.shape, 0)
     cols = lax.broadcasted_iota(jnp.int32, spread.shape, 1)

time: 41.3 us -> 41.5 us (level)
  no operation moved by 1% of the time
where the time goes in v23:
time: 41.5 us; the launch traced here: 41.2 us
  blocking collectives  34 us (82%)
  Pallas kernels  5.71 us (14%)
  between operations  0.68 us (2%)
  starting transfers between devices  0.63 us (2%)
    all_to_all x3, blocking collectives, to_all(): return lax.all_to_all(copies, ('row', 'col'), 0, 0, tiled=True)  34 us
    pallas_call x1, Pallas kernels, local(): call(functools.partial(first_stage, size, True), [block, block, copies, w...  1.36 us
    pallas_call x1, Pallas kernels, local(): call(functools.partial(first_stage, size, False), [products, array(4 * ve...  1.09 us
    pallas_call x1, Pallas kernels, local(): call(pack_kernel, [block, copies], [pltpu.VMEM(item.shape, F32) for item...  0.89 us
    pallas_call x1, Pallas kernels, local(): call(functools.partial(third_stage, size, not keep), [products, block, bl...  0.85 us
  transfers between devices with their start and end apart: 2, of which 1 were waited for; matrix products, arithmetic and copies ran while one was open for 0% of the time, Pallas kernels for 5%

profile of v23, /device:TPU:0, one launch (start us, length us, event | category | flops | bytes accessed | tf_op | source)
XLA Modules:
  0.0 41.2 jit_solution(1811725381417501447)
XLA Ops:
  0.6 0.9 %shard_map.49 = (f32[8,256]{1,0:T(8,128)S(1)}, f32[16,2,8,128]{3,2,1,0:T(8,128)S(1)}) custom-call(f32[3,64]{1,0:T(4,128)} %positions.1, f32[3,8,64]{2,1,0:T(8,128)} %bitcast.7), custom_call_target="tpu_custom_call" | custom-call | tf_op jit(solution)/shard_map/pallas_call | solution.py:351
  1.5 15.3 %all_to_all.15.blocks = f32[32,8,128]{2,1,0:T(8,128)S(1)} all-to-all(f32[32,8,128]{2,1,0:T(8,128)S(1)} %bitcast.6), channel_id=1, replica_groups=mesh['row'=4,'col'=8] {'row','col'}, dimensions={0} | all-to-all | bytes 262144 | tf_op jit(solution)/shard_map/all_to_all | solution.py:325
  16.8 0.3 collective-permute-start
  17.1 1.1 %shard_map.50 = (f32[32,384]{1,0:T(8,128)S(1)}, f32[32,32]{1,0:T(8,128)S(1)}, f32[32,1024]{1,0:T(8,128)S(1)}, bf16[384,1024]{1,0:T(8,128)(2,1)S(1)}, bf16[384,1024]{1,0:T(8,128)(2,1)S(1)}) custom-call(f32[8,256]{1,0:T(8,128)S(1)} %get-tuple-element.26.own, f32[32,8,128]{2,1,0:T(8,128)S(1)} %all_to_all.15.blocks), custom_call_target="tpu_custom_call" | custom-call | tf_op jit(solution)/shard_map/pallas_call | solution.py:358
  18.2 0.0 collective-permute-done.blocks
  18.2 1.4 %shard_map.51 = (f32[8,256]{1,0:T(8,128)S(1)}, f32[8,256]{1,0:T(8,128)S(1)}, f32[16,2,8,128]{3,2,1,0:T(8,128)S(1)}, f32[32,1024]{1,0:T(8,128)S(1)}, bf16[384,102...) custom-call(f32[8,256]{1,0:T(8,128)S(1)} %get-tuple-element.26.own, f32[32,8,128]{2,1,0:T(8,128)S(1)} %collective-permute-done.blocks, ...), custom_call_target="tpu_custom_call" | custom-call | tf_op jit(solution)/shard_map/pallas_call | solution.py:361
  19.6 9.9 %all_to_all.16.refs_2_ = f32[32,8,128]{2,1,0:T(8,128)S(1)} all-to-all(f32[32,8,128]{2,1,0:T(8,128)S(1)} %bitcast.5), channel_id=1, replica_groups=mesh['row'=4,'col'=8] {'row','col'}, dimensions={0} | all-to-all | bytes 262144 | tf_op jit(solution)/shard_map/all_to_all | solution.py:325
  29.5 0.3 collective-permute-start.1
  29.8 0.8 %shard_map.52 = (f32[32,384]{1,0:T(8,128)S(1)}, f32[8,256]{1,0:T(8,128)S(1)}, f32[8,256]{1,0:T(8,128)S(1)}, f32[8,8]{1,0:T(8,128)S(1)}, f32[2,8,8]{2,1,0:T(8,128)S(1)}) custom-call(f32[8,256]{1,0:T(8,128)S(1)} %get-tuple-element.26.own, f32[32,1024]{1,0:T(8,128)S(1)} %get-tuple-element.28.wide, bf16[384,1024]{1,0:T(8,128)(2,1)S(1)} %get-tuple-element.29.refs_0_, ...), custom_call_target="tpu_custom_call" | custom-call | tf_op jit(solution)/shard_map/pallas_call | solution.py:365
  30.6 0.2 collective-permute-done.1.refs_2_
  30.8 0.7 %shard_map.53 = (f32[8,256]{1,0:T(8,128)S(1)}, f32[32,1,64]{2,1,0:T(1,128)S(1)}) custom-call(f32[8,256]{1,0:T(8,128)S(1)} %get-tuple-element.26.own, f32[32,1024]{1,0:T(8,128)S(1)} %get-tuple-element.37.wide, bf16[384,1024]{1,0:T(8,128)(2,1)S(1)} %get-tuple-element.38.refs_0_, bf16[384,1024]{1,0:T(8,128)(2,1)S(1)} %get-tuple-element.39.refs_1_, ...), custom_call_target="tpu_custom_call" | custom-call | tf_op jit(solution)/shard_map/pallas_call | solution.py:370
  31.6 8.8 %all_to_all.17.partials = f32[32,1,64]{2,1,0:T(1,128)S(1)} all-to-all(f32[32,1,64]{2,1,0:T(1,128)S(1)} %get-tuple-element.45), channel_id=1, replica_groups=mesh['row'=4,'col'=8] {'row','col'}, dimensions={0} | all-to-all | bytes 16384 | tf_op jit(solution)/shard_map/all_to_all | solution.py:325
  40.4 0.8 %shard_map.54 = (f32[3,8,64]{2,1,0:T(8,128)}, f32[3,8,64]{2,1,0:T(8,128)}, f32[3,8,8]{2,1,0:T(8,128)}) custom-call(f32[8,256]{1,0:T(8,128)S(1)} %get-tuple-element.36.refs_4_.vectors, f32[8,256]{1,0:T(8,128)S(1)} %get-tuple-element.43.shifted, f32[2,8,8]{2,1,0:T(8,128)S(1)} %get-tuple-element.44.both, f32[32,1,64]{2,1,0:T(1,128)S(1)} %all_to_all.17.partials), custom_call_target="tpu_custom_call" | custom-call | tf_op jit(solution)/shard_map/pallas_call | solution.py:374
Async XLA Ops:
  16.8 1.4 %collective-permute-start = (f32[32,8,128]{2,1,0:T(8,128)S(1)}, f32[32,8,128]{2,1,0:T(8,128)S(1)}, u32[]{:S(2)}, u32[]{:S(2)}) collective-permute-start(f32[32,8,128]{2,1,0:T(8,128)S(1)} %all_to_all.15.blocks), channel_id=1, source_target_pairs={{0,1},{1,0},{2,3},{3,2},{4,5},{5,4},{6,7},{7,6},{8,9},{9,8},{10,11... | collective-permute-start | bytes 393224 | tf_op jit(solution)/shard_map/ppermute | solution.py:331
  29.5 1.3 %collective-permute-start.1 = (f32[32,8,128]{2,1,0:T(8,128)S(1)}, f32[32,8,128]{2,1,0:T(8,128)S(1)}, u32[]{:S(2)}, u32[]{:S(2)}) collective-permute-start(f32[32,8,128]{2,1,0:T(8,128)S(1)} %all_to_all.16.refs_2_), channel_id=1, source_target_pairs={{0,1},{1,0},{2,3},{3,2},{4,5},{5,4},{6,7},{7,6},{8,9},{9,8},{10,11... | collective-permute-start | bytes 393224 | tf_op jit(solution)/shard_map/ppermute | solution.py:331

commit v24 on v22

--- a/solution.py
+++ b/solution.py
@@ -231,7 +231,11 @@
 def second_product(fill, own, wide, wide_image, high, low):
     if fill:
         return all_filled(own, wide, wide_image, high, low)
-    return apply_tensor(split_rows(wide_image[...]), high[...], low[...])
+    products = jnp.zeros((32, high.shape[0]), F32)
+    for at in range(0, high.shape[1], 512):
+        lanes = slice(at, min(at + 512, high.shape[1]))
+        products = products + apply_tensor(split_rows(wide_image[:, lanes]), high[:, lanes], low[:, lanes])
+    return products
 
 
 def third_stage(size, fill, own, wide, *refs):

time: 41.3 us -> 41.4 us (level)
  no operation moved by 1% of the time
where the time goes in v24:
time: 41.4 us; the launch traced here: 41.1 us
  blocking collectives  34 us (82%)
  Pallas kernels  5.61 us (14%)
  between operations  0.67 us (2%)
  starting transfers between devices  0.63 us (2%)
    all_to_all x3, blocking collectives, to_all(): return lax.all_to_all(copies, ('row', 'col'), 0, 0, tiled=True)  34 us
    pallas_call x1, Pallas kernels, local(): call(functools.partial(first_stage, size, True), [block, block, copies, w...  1.28 us
    pallas_call x1, Pallas kernels, local(): call(functools.partial(first_stage, size, False), [products, array(4 * ve...  1.03 us
    pallas_call x1, Pallas kernels, local(): call(pack_kernel, [block, copies], [pltpu.VMEM(item.shape, F32) for item...  0.89 us
    pallas_call x1, Pallas kernels, local(): call(functools.partial(third_stage, size, not keep), [products, block, bl...  0.84 us
  transfers between devices with their start and end apart: 2, of which 1 were waited for; matrix products, arithmetic and copies ran while one was open for 0% of the time, Pallas kernels for 5%

profile of v24, /device:TPU:0, one launch (start us, length us, event | category | flops | bytes accessed | tf_op | source)
XLA Modules:
  0.0 41.1 jit_solution(1972958146700365946)
XLA Ops:
  0.6 0.9 %shard_map.49 = (f32[8,256]{1,0:T(8,128)S(1)}, f32[16,2,8,128]{3,2,1,0:T(8,128)S(1)}) custom-call(f32[3,64]{1,0:T(4,128)} %positions.1, f32[3,8,64]{2,1,0:T(8,128)} %bitcast.7), custom_call_target="tpu_custom_call" | custom-call | tf_op jit(solution)/shard_map/pallas_call | solution.py:352
  1.5 15.3 %all_to_all.15.blocks = f32[32,8,128]{2,1,0:T(8,128)S(1)} all-to-all(f32[32,8,128]{2,1,0:T(8,128)S(1)} %bitcast.6), channel_id=1, replica_groups=mesh['row'=4,'col'=8] {'row','col'}, dimensions={0} | all-to-all | bytes 262144 | tf_op jit(solution)/shard_map/all_to_all | solution.py:326
  16.8 0.3 collective-permute-start
  17.1 1.0 %shard_map.50 = (f32[32,384]{1,0:T(8,128)S(1)}, f32[32,32]{1,0:T(8,128)S(1)}, f32[32,1024]{1,0:T(8,128)S(1)}, bf16[384,1024]{1,0:T(8,128)(2,1)S(1)}, bf16[384,1024]{1,0:T(8,128)(2,1)S(1)}) custom-call(f32[8,256]{1,0:T(8,128)S(1)} %get-tuple-element.26.own, f32[32,8,128]{2,1,0:T(8,128)S(1)} %all_to_all.15.blocks), custom_call_target="tpu_custom_call" | custom-call | tf_op jit(solution)/shard_map/pallas_call | solution.py:359
  18.2 0.0 collective-permute-done.blocks
  18.2 1.3 %shard_map.51 = (f32[8,256]{1,0:T(8,128)S(1)}, f32[8,256]{1,0:T(8,128)S(1)}, f32[16,2,8,128]{3,2,1,0:T(8,128)S(1)}, f32[32,1024]{1,0:T(8,128)S(1)}, bf16[384,102...) custom-call(f32[8,256]{1,0:T(8,128)S(1)} %get-tuple-element.26.own, f32[32,8,128]{2,1,0:T(8,128)S(1)} %collective-permute-done.blocks, ...), custom_call_target="tpu_custom_call" | custom-call | tf_op jit(solution)/shard_map/pallas_call | solution.py:362
  19.5 9.9 %all_to_all.16.refs_2_ = f32[32,8,128]{2,1,0:T(8,128)S(1)} all-to-all(f32[32,8,128]{2,1,0:T(8,128)S(1)} %bitcast.5), channel_id=1, replica_groups=mesh['row'=4,'col'=8] {'row','col'}, dimensions={0} | all-to-all | bytes 262144 | tf_op jit(solution)/shard_map/all_to_all | solution.py:326
  29.3 0.3 collective-permute-start.1
  29.7 0.8 %shard_map.52 = (f32[32,384]{1,0:T(8,128)S(1)}, f32[8,256]{1,0:T(8,128)S(1)}, f32[8,256]{1,0:T(8,128)S(1)}, f32[8,8]{1,0:T(8,128)S(1)}, f32[2,8,8]{2,1,0:T(8,128)S(1)}) custom-call(f32[8,256]{1,0:T(8,128)S(1)} %get-tuple-element.26.own, f32[32,1024]{1,0:T(8,128)S(1)} %get-tuple-element.28.wide, bf16[384,1024]{1,0:T(8,128)(2,1)S(1)} %get-tuple-element.29.refs_0_, ...), custom_call_target="tpu_custom_call" | custom-call | tf_op jit(solution)/shard_map/pallas_call | solution.py:366
  30.5 0.2 collective-permute-done.1.refs_2_
  30.7 0.8 %shard_map.53 = (f32[8,256]{1,0:T(8,128)S(1)}, f32[32,1,64]{2,1,0:T(1,128)S(1)}) custom-call(f32[8,256]{1,0:T(8,128)S(1)} %get-tuple-element.26.own, f32[32,1024]{1,0:T(8,128)S(1)} %get-tuple-element.37.wide, bf16[384,1024]{1,0:T(8,128)(2,1)S(1)} %get-tuple-element.38.refs_0_, bf16[384,1024]{1,0:T(8,128)(2,1)S(1)} %get-tuple-element.39.refs_1_, ...), custom_call_target="tpu_custom_call" | custom-call | tf_op jit(solution)/shard_map/pallas_call | solution.py:371
  31.5 8.8 %all_to_all.17.partials = f32[32,1,64]{2,1,0:T(1,128)S(1)} all-to-all(f32[32,1,64]{2,1,0:T(1,128)S(1)} %get-tuple-element.45), channel_id=1, replica_groups=mesh['row'=4,'col'=8] {'row','col'}, dimensions={0} | all-to-all | bytes 16384 | tf_op jit(solution)/shard_map/all_to_all | solution.py:326
  40.3 0.8 %shard_map.54 = (f32[3,8,64]{2,1,0:T(8,128)}, f32[3,8,64]{2,1,0:T(8,128)}, f32[3,8,8]{2,1,0:T(8,128)}) custom-call(f32[8,256]{1,0:T(8,128)S(1)} %get-tuple-element.36.refs_4_.vectors, f32[8,256]{1,0:T(8,128)S(1)} %get-tuple-element.43.shifted, f32[2,8,8]{2,1,0:T(8,128)S(1)} %get-tuple-element.44.both, f32[32,1,64]{2,1,0:T(1,128)S(1)} %all_to_all.17.partials), custom_call_target="tpu_custom_call" | custom-call | tf_op jit(solution)/shard_map/pallas_call | solution.py:375
Async XLA Ops:
  16.8 1.4 %collective-permute-start = (f32[32,8,128]{2,1,0:T(8,128)S(1)}, f32[32,8,128]{2,1,0:T(8,128)S(1)}, u32[]{:S(2)}, u32[]{:S(2)}) collective-permute-start(f32[32,8,128]{2,1,0:T(8,128)S(1)} %all_to_all.15.blocks), channel_id=1, source_target_pairs={{0,1},{1,0},{2,3},{3,2},{4,5},{5,4},{6,7},{7,6},{8,9},{9,8},{10,11... | collective-permute-start | bytes 393224 | tf_op jit(solution)/shard_map/ppermute | solution.py:332
  29.3 1.3 %collective-permute-start.1 = (f32[32,8,128]{2,1,0:T(8,128)S(1)}, f32[32,8,128]{2,1,0:T(8,128)S(1)}, u32[]{:S(2)}, u32[]{:S(2)}) collective-permute-start(f32[32,8,128]{2,1,0:T(8,128)S(1)} %all_to_all.16.refs_2_), channel_id=1, source_target_pairs={{0,1},{1,0},{2,3},{3,2},{4,5},{5,4},{6,7},{7,6},{8,9},{9,8},{10,11... | collective-permute-start | bytes 393224 | tf_op jit(solution)/shard_map/ppermute | solution.py:332

commit v25 on v22

--- a/solution.py
+++ b/solution.py
@@ -127,11 +127,12 @@
 
 def filled_product(columns, source, wide, start, high, low):
     width = high.shape[1]
+    steps = [(at, min(512, width - at)) for at in range(0, width, 512)]
+    vectors = [split_rows(wide[:, pl.ds(pl.multiple_of(start + at, 128), step)]) for at, step in steps]
+    sums = row_sums(vectors)
     products = jnp.zeros((32, high.shape[0]), F32)
-    for at in range(0, width, 512):
-        step = min(512, width - at)
+    for (at, step), both in zip(steps, vectors):
         lanes = pl.ds(at, step)
-        both = split_rows(wide[:, pl.ds(pl.multiple_of(start + at, 128), step)])
         pieces = [
             tensor(columns, source, pl.multiple_of(start + part, 128)) for part in range(at, at + step, 128)
         ]
@@ -139,7 +140,7 @@
         high[:, lanes] = upper
         low[:, lanes] = lower
         products = products + apply_tensor(both, upper, lower)
-    return products
+    return products, sums
 
 
 def all_filled(own, source, wide, high, low):
@@ -148,7 +149,7 @@
     chunk = lambda start: filled_product(columns, source, wide, start, high, low)
     if wide.shape[1] == width:
         return chunk(0)
-    body = lambda index, total: total + chunk(index * width)
+    body = lambda index, totals: tuple(a + b for a, b in zip(totals, chunk(index * width)))
     return lax.fori_loop(1, wide.shape[1] // width, body, chunk(0))
 
 
@@ -157,10 +158,9 @@
     return jnp.where(lanes < block.shape[1] // 4 * 3, block, 0.0)
 
 
-def row_sums(wide):
-    total = jnp.zeros((wide.shape[0], wide.shape[0]), F32)
-    for at in range(0, wide.shape[1], CHUNK):
-        both = split_rows(wide[:, at : min(at + CHUNK, wide.shape[1])])
+def row_sums(vectors):
+    total = 0.0
+    for both in vectors:
         half = both.shape[0] // 2
         first, second = matmul_nt(both, both[:half]), matmul_nt(both, both[half:])
         total = total + ((first[:half] + first[half:]) + (second[:half] + second[half:]))
@@ -174,8 +174,7 @@
     else:
         out, sums_out, wide, high, low = refs
     unpack(blocks, wide)
-    sums = row_sums(wide)
-    products = all_filled(own[...], wide, wide, high, low)
+    products, sums = all_filled(own[...], wide, wide, high, low)
     if not last:
         out[...], sums_out[...] = products, sums
         return
@@ -230,7 +229,7 @@
 
 def second_product(fill, own, wide, wide_image, high, low):
     if fill:
-        return all_filled(own, wide, wide_image, high, low)
+        return all_filled(own, wide, wide_image, high, low)[0]
     return apply_tensor(split_rows(wide_image[...]), high[...], low[...])
 
 

time: 41.3 us -> 41.3 us (level)
  no operation moved by 1% of the time
where the time goes in v25:
time: 41.3 us; the launch traced here: 41 us
  blocking collectives  34 us (82%)
  Pallas kernels  5.55 us (13%)
  between operations  0.67 us (2%)
  starting transfers between devices  0.63 us (2%)
    all_to_all x3, blocking collectives, to_all(): return lax.all_to_all(copies, ('row', 'col'), 0, 0, tiled=True)  34 us
    pallas_call x1, Pallas kernels, local(): call(functools.partial(first_stage, size, True), [block, block, copies, w...  1.24 us
    pallas_call x1, Pallas kernels, local(): call(functools.partial(first_stage, size, False), [products, array(4 * ve...  1.02 us
    pallas_call x1, Pallas kernels, local(): call(pack_kernel, [block, copies], [pltpu.VMEM(item.shape, F32) for item...  0.89 us
    pallas_call x1, Pallas kernels, local(): call(functools.partial(third_stage, size, not keep), [products, block, bl...  0.85 us
  transfers between devices with their start and end apart: 2, of which 1 were waited for; matrix products, arithmetic and copies ran while one was open for 0% of the time, Pallas kernels for 5%

profile of v25, /device:TPU:0, one launch (start us, length us, event | category | flops | bytes accessed | tf_op | source)
XLA Modules:
  0.0 41.0 jit_solution(6179672634028983896)
XLA Ops:
  0.6 0.9 %shard_map.49 = (f32[8,256]{1,0:T(8,128)S(1)}, f32[16,2,8,128]{3,2,1,0:T(8,128)S(1)}) custom-call(f32[3,64]{1,0:T(4,128)} %positions.1, f32[3,8,64]{2,1,0:T(8,128)} %bitcast.7), custom_call_target="tpu_custom_call" | custom-call | tf_op jit(solution)/shard_map/pallas_call | solution.py:347
  1.5 15.3 %all_to_all.15.blocks = f32[32,8,128]{2,1,0:T(8,128)S(1)} all-to-all(f32[32,8,128]{2,1,0:T(8,128)S(1)} %bitcast.6), channel_id=1, replica_groups=mesh['row'=4,'col'=8] {'row','col'}, dimensions={0} | all-to-all | bytes 262144 | tf_op jit(solution)/shard_map/all_to_all | solution.py:321
  16.8 0.3 collective-permute-start
  17.1 1.0 %shard_map.50 = (f32[32,384]{1,0:T(8,128)S(1)}, f32[32,32]{1,0:T(8,128)S(1)}, f32[32,1024]{1,0:T(8,128)S(1)}, bf16[384,1024]{1,0:T(8,128)(2,1)S(1)}, bf16[384,1024]{1,0:T(8,128)(2,1)S(1)}) custom-call(f32[8,256]{1,0:T(8,128)S(1)} %get-tuple-element.26.own, f32[32,8,128]{2,1,0:T(8,128)S(1)} %all_to_all.15.blocks), custom_call_target="tpu_custom_call" | custom-call | tf_op jit(solution)/shard_map/pallas_call | solution.py:354
  18.2 0.0 collective-permute-done.blocks
  18.2 1.2 %shard_map.51 = (f32[8,256]{1,0:T(8,128)S(1)}, f32[8,256]{1,0:T(8,128)S(1)}, f32[16,2,8,128]{3,2,1,0:T(8,128)S(1)}, f32[32,1024]{1,0:T(8,128)S(1)}, bf16[384,102...) custom-call(f32[8,256]{1,0:T(8,128)S(1)} %get-tuple-element.26.own, f32[32,8,128]{2,1,0:T(8,128)S(1)} %collective-permute-done.blocks, ...), custom_call_target="tpu_custom_call" | custom-call | tf_op jit(solution)/shard_map/pallas_call | solution.py:357
  19.4 9.9 %all_to_all.16.refs_2_ = f32[32,8,128]{2,1,0:T(8,128)S(1)} all-to-all(f32[32,8,128]{2,1,0:T(8,128)S(1)} %bitcast.5), channel_id=1, replica_groups=mesh['row'=4,'col'=8] {'row','col'}, dimensions={0} | all-to-all | bytes 262144 | tf_op jit(solution)/shard_map/all_to_all | solution.py:321
  29.3 0.3 collective-permute-start.1
  29.6 0.8 %shard_map.52 = (f32[32,384]{1,0:T(8,128)S(1)}, f32[8,256]{1,0:T(8,128)S(1)}, f32[8,256]{1,0:T(8,128)S(1)}, f32[8,8]{1,0:T(8,128)S(1)}, f32[2,8,8]{2,1,0:T(8,128)S(1)}) custom-call(f32[8,256]{1,0:T(8,128)S(1)} %get-tuple-element.26.own, f32[32,1024]{1,0:T(8,128)S(1)} %get-tuple-element.28.wide, bf16[384,1024]{1,0:T(8,128)(2,1)S(1)} %get-tuple-element.29.refs_0_, ...), custom_call_target="tpu_custom_call" | custom-call | tf_op jit(solution)/shard_map/pallas_call | solution.py:361
  30.5 0.2 collective-permute-done.1.refs_2_
  30.6 0.7 %shard_map.53 = (f32[8,256]{1,0:T(8,128)S(1)}, f32[32,1,64]{2,1,0:T(1,128)S(1)}) custom-call(f32[8,256]{1,0:T(8,128)S(1)} %get-tuple-element.26.own, f32[32,1024]{1,0:T(8,128)S(1)} %get-tuple-element.37.wide, bf16[384,1024]{1,0:T(8,128)(2,1)S(1)} %get-tuple-element.38.refs_0_, bf16[384,1024]{1,0:T(8,128)(2,1)S(1)} %get-tuple-element.39.refs_1_, ...), custom_call_target="tpu_custom_call" | custom-call | tf_op jit(solution)/shard_map/pallas_call | solution.py:366
  31.4 8.8 %all_to_all.17.partials = f32[32,1,64]{2,1,0:T(1,128)S(1)} all-to-all(f32[32,1,64]{2,1,0:T(1,128)S(1)} %get-tuple-element.45), channel_id=1, replica_groups=mesh['row'=4,'col'=8] {'row','col'}, dimensions={0} | all-to-all | bytes 16384 | tf_op jit(solution)/shard_map/all_to_all | solution.py:321
  40.2 0.8 %shard_map.54 = (f32[3,8,64]{2,1,0:T(8,128)}, f32[3,8,64]{2,1,0:T(8,128)}, f32[3,8,8]{2,1,0:T(8,128)}) custom-call(f32[8,256]{1,0:T(8,128)S(1)} %get-tuple-element.36.refs_4_.vectors, f32[8,256]{1,0:T(8,128)S(1)} %get-tuple-element.43.shifted, f32[2,8,8]{2,1,0:T(8,128)S(1)} %get-tuple-element.44.both, f32[32,1,64]{2,1,0:T(1,128)S(1)} %all_to_all.17.partials), custom_call_target="tpu_custom_call" | custom-call | tf_op jit(solution)/shard_map/pallas_call | solution.py:370
Async XLA Ops:
  16.8 1.3 %collective-permute-start = (f32[32,8,128]{2,1,0:T(8,128)S(1)}, f32[32,8,128]{2,1,0:T(8,128)S(1)}, u32[]{:S(2)}, u32[]{:S(2)}) collective-permute-start(f32[32,8,128]{2,1,0:T(8,128)S(1)} %all_to_all.15.blocks), channel_id=1, source_target_pairs={{0,1},{1,0},{2,3},{3,2},{4,5},{5,4},{6,7},{7,6},{8,9},{9,8},{10,11... | collective-permute-start | bytes 393224 | tf_op jit(solution)/shard_map/ppermute | solution.py:327
  29.3 1.3 %collective-permute-start.1 = (f32[32,8,128]{2,1,0:T(8,128)S(1)}, f32[32,8,128]{2,1,0:T(8,128)S(1)}, u32[]{:S(2)}, u32[]{:S(2)}) collective-permute-start(f32[32,8,128]{2,1,0:T(8,128)S(1)} %all_to_all.16.refs_2_), channel_id=1, source_target_pairs={{0,1},{1,0},{2,3},{3,2},{4,5},{5,4},{6,7},{7,6},{8,9},{9,8},{10,11... | collective-permute-start | bytes 393224 | tf_op jit(solution)/shard_map/ppermute | solution.py:327

commit v26 on v22

--- a/solution.py
+++ b/solution.py
@@ -59,12 +59,12 @@
     return total
 
 
-def unpack(blocks, wide):
+def unpack(blocks, wide, parts=4):
     count, vecs, lanes = blocks.shape
     width = lanes // 4
     for at in range(0, count, 4):
         four = [blocks[at + index] for index in range(4)]
-        for part in range(4):
+        for part in range(parts):
             wide[part * vecs : (part + 1) * vecs, pl.ds(at * width, 4 * width)] = jnp.concatenate(
                 [block[:, part * width : (part + 1) * width] for block in four], axis=1
             )
@@ -269,7 +269,8 @@
     if fill:
         high, low = refs[7:9]
     wide_image = refs[-1]
-    unpack(images, wide_image)
+    unpack(images, wide_image, 3)
+    wide_image[24:] = jnp.zeros((8, wide_image.shape[1]), F32)
     products = second_product(fill, own[...], wide, wide_image, high, low) + before[...]
     vectors = vectors_in[...]
     shift = small_matmul(small[...], assemble(products)) - known[...]

time: 41.3 us -> 41.3 us (level)
  no operation moved by 1% of the time
where the time goes in v26:
time: 41.3 us; the launch traced here: 41.1 us
  blocking collectives  34 us (82%)
  Pallas kernels  5.6 us (14%)
  between operations  0.67 us (2%)
  starting transfers between devices  0.63 us (2%)
    all_to_all x3, blocking collectives, to_all(): return lax.all_to_all(copies, ('row', 'col'), 0, 0, tiled=True)  34 us
    pallas_call x1, Pallas kernels, local(): call(functools.partial(first_stage, size, True), [block, block, copies, w...  1.28 us
    pallas_call x1, Pallas kernels, local(): call(functools.partial(first_stage, size, False), [products, array(4 * ve...  1.03 us
    pallas_call x1, Pallas kernels, local(): call(pack_kernel, [block, copies], [pltpu.VMEM(item.shape, F32) for item...  0.89 us
    pallas_call x1, Pallas kernels, local(): call(functools.partial(third_stage, size, not keep), [products, block, bl...  0.85 us
  transfers between devices with their start and end apart: 2, of which 1 were waited for; matrix products, arithmetic and copies ran while one was open for 0% of the time, Pallas kernels for 5%

profile of v26, /device:TPU:0, one launch (start us, length us, event | category | flops | bytes accessed | tf_op | source)
XLA Modules:
  0.0 41.1 jit_solution(13812160813339239582)
XLA Ops:
  0.6 0.9 %shard_map.49 = (f32[8,256]{1,0:T(8,128)S(1)}, f32[16,2,8,128]{3,2,1,0:T(8,128)S(1)}) custom-call(f32[3,64]{1,0:T(4,128)} %positions.1, f32[3,8,64]{2,1,0:T(8,128)} %bitcast.7), custom_call_target="tpu_custom_call" | custom-call | tf_op jit(solution)/shard_map/pallas_call | solution.py:349
  1.5 15.3 %all_to_all.15.blocks = f32[32,8,128]{2,1,0:T(8,128)S(1)} all-to-all(f32[32,8,128]{2,1,0:T(8,128)S(1)} %bitcast.6), channel_id=1, replica_groups=mesh['row'=4,'col'=8] {'row','col'}, dimensions={0} | all-to-all | bytes 262144 | tf_op jit(solution)/shard_map/all_to_all | solution.py:323
  16.8 0.3 collective-permute-start
  17.1 1.0 %shard_map.50 = (f32[32,384]{1,0:T(8,128)S(1)}, f32[32,32]{1,0:T(8,128)S(1)}, f32[32,1024]{1,0:T(8,128)S(1)}, bf16[384,1024]{1,0:T(8,128)(2,1)S(1)}, bf16[384,1024]{1,0:T(8,128)(2,1)S(1)}) custom-call(f32[8,256]{1,0:T(8,128)S(1)} %get-tuple-element.26.own, f32[32,8,128]{2,1,0:T(8,128)S(1)} %all_to_all.15.blocks), custom_call_target="tpu_custom_call" | custom-call | tf_op jit(solution)/shard_map/pallas_call | solution.py:356
  18.2 0.0 collective-permute-done.blocks
  18.2 1.3 %shard_map.51 = (f32[8,256]{1,0:T(8,128)S(1)}, f32[8,256]{1,0:T(8,128)S(1)}, f32[16,2,8,128]{3,2,1,0:T(8,128)S(1)}, f32[32,1024]{1,0:T(8,128)S(1)}, bf16[384,102...) custom-call(f32[8,256]{1,0:T(8,128)S(1)} %get-tuple-element.26.own, f32[32,8,128]{2,1,0:T(8,128)S(1)} %collective-permute-done.blocks, ...), custom_call_target="tpu_custom_call" | custom-call | tf_op jit(solution)/shard_map/pallas_call | solution.py:359
  19.5 9.9 %all_to_all.16.refs_2_ = f32[32,8,128]{2,1,0:T(8,128)S(1)} all-to-all(f32[32,8,128]{2,1,0:T(8,128)S(1)} %bitcast.5), channel_id=1, replica_groups=mesh['row'=4,'col'=8] {'row','col'}, dimensions={0} | all-to-all | bytes 262144 | tf_op jit(solution)/shard_map/all_to_all | solution.py:323
  29.3 0.3 collective-permute-start.1
  29.7 0.8 %shard_map.52 = (f32[32,384]{1,0:T(8,128)S(1)}, f32[8,256]{1,0:T(8,128)S(1)}, f32[8,256]{1,0:T(8,128)S(1)}, f32[8,8]{1,0:T(8,128)S(1)}, f32[2,8,8]{2,1,0:T(8,128)S(1)}) custom-call(f32[8,256]{1,0:T(8,128)S(1)} %get-tuple-element.26.own, f32[32,1024]{1,0:T(8,128)S(1)} %get-tuple-element.28.wide, bf16[384,1024]{1,0:T(8,128)(2,1)S(1)} %get-tuple-element.29.refs_0_, ...), custom_call_target="tpu_custom_call" | custom-call | tf_op jit(solution)/shard_map/pallas_call | solution.py:363
  30.5 0.2 collective-permute-done.1.refs_2_
  30.7 0.8 %shard_map.53 = (f32[8,256]{1,0:T(8,128)S(1)}, f32[32,1,64]{2,1,0:T(1,128)S(1)}) custom-call(f32[8,256]{1,0:T(8,128)S(1)} %get-tuple-element.26.own, f32[32,1024]{1,0:T(8,128)S(1)} %get-tuple-element.37.wide, bf16[384,1024]{1,0:T(8,128)(2,1)S(1)} %get-tuple-element.38.refs_0_, bf16[384,1024]{1,0:T(8,128)(2,1)S(1)} %get-tuple-element.39.refs_1_, ...), custom_call_target="tpu_custom_call" | custom-call | tf_op jit(solution)/shard_map/pallas_call | solution.py:368
  31.5 8.8 %all_to_all.17.partials = f32[32,1,64]{2,1,0:T(1,128)S(1)} all-to-all(f32[32,1,64]{2,1,0:T(1,128)S(1)} %get-tuple-element.45), channel_id=1, replica_groups=mesh['row'=4,'col'=8] {'row','col'}, dimensions={0} | all-to-all | bytes 16384 | tf_op jit(solution)/shard_map/all_to_all | solution.py:323
  40.3 0.8 %shard_map.54 = (f32[3,8,64]{2,1,0:T(8,128)}, f32[3,8,64]{2,1,0:T(8,128)}, f32[3,8,8]{2,1,0:T(8,128)}) custom-call(f32[8,256]{1,0:T(8,128)S(1)} %get-tuple-element.36.refs_4_.vectors, f32[8,256]{1,0:T(8,128)S(1)} %get-tuple-element.43.shifted, f32[2,8,8]{2,1,0:T(8,128)S(1)} %get-tuple-element.44.both, f32[32,1,64]{2,1,0:T(1,128)S(1)} %all_to_all.17.partials), custom_call_target="tpu_custom_call" | custom-call | tf_op jit(solution)/shard_map/pallas_call | solution.py:372
Async XLA Ops:
  16.8 1.4 %collective-permute-start = (f32[32,8,128]{2,1,0:T(8,128)S(1)}, f32[32,8,128]{2,1,0:T(8,128)S(1)}, u32[]{:S(2)}, u32[]{:S(2)}) collective-permute-start(f32[32,8,128]{2,1,0:T(8,128)S(1)} %all_to_all.15.blocks), channel_id=1, source_target_pairs={{0,1},{1,0},{2,3},{3,2},{4,5},{5,4},{6,7},{7,6},{8,9},{9,8},{10,11... | collective-permute-start | bytes 393224 | tf_op jit(solution)/shard_map/ppermute | solution.py:329
  29.3 1.3 %collective-permute-start.1 = (f32[32,8,128]{2,1,0:T(8,128)S(1)}, f32[32,8,128]{2,1,0:T(8,128)S(1)}, u32[]{:S(2)}, u32[]{:S(2)}) collective-permute-start(f32[32,8,128]{2,1,0:T(8,128)S(1)} %all_to_all.16.refs_2_), channel_id=1, source_target_pairs={{0,1},{1,0},{2,3},{3,2},{4,5},{5,4},{6,7},{7,6},{8,9},{9,8},{10,11... | collective-permute-start | bytes 393224 | tf_op jit(solution)/shard_map/ppermute | solution.py:329
